TPU v7x, 32 devices: a whole 2x2x4 slice. The times are simulated.
32 devices in a mesh: rows: 8 (over z, y), cols: 4 (over x, core).
Axes of the slice: x: 2, y: 2, z: 4, core: 2. Of those that a mesh axis runs over, the one named last changes fastest.
Arguments:
- features: bfloat16 [2, 8, 128, 512], P(None, 'rows', 'cols'), may hold values from -6 to 6
- skip_feat: bfloat16 [2, 16, 256, 512], P(None, 'rows', 'cols'), may hold values from -6 to 6
- labels: int32 [2, 16, 256], P(None, 'rows', 'cols'), may hold values from 0 to 1
- pixel_weight: int32 [2, 16, 256], P(None, 'rows', 'cols'), may hold values from 1 to 10
- valid_mask: int32 [2, 16, 256], P(None, 'rows', 'cols'), may hold values from 0 to 1, as said below
- conv_first: float32 [4718592], P(('rows', 'cols')), may hold values from -0.09375 to 0.09375
- conv_first_mom: float32 [4718592], P(('rows', 'cols')), may hold values from -3.8146973e-06 to 3.8146973e-06
- conv_first_sec: float32 [4718592], P(('rows', 'cols')), may hold values from 5.2981907e-15 to 2.1192763e-14
- conv_second: float32 [9437184], P(('rows', 'cols')), may hold values from -0.0625 to 0.0625
- conv_second_mom: float32 [9437184], P(('rows', 'cols')), may hold values from -3.8146973e-06 to 3.8146973e-06
- conv_second_sec: float32 [9437184], P(('rows', 'cols')), may hold values from 5.9339736e-15 to 2.3841858e-14
- up_conv: float32 [2097152], P(('rows', 'cols')), may hold values from -0.1875 to 0.1875
- up_conv_mom: float32 [2097152], P(('rows', 'cols')), may hold values from -1.1444092e-05 to 1.1444092e-05
- up_conv_sec: float32 [2097152], P(('rows', 'cols')), may hold values from 4.7683716e-14 to 1.9073487e-13
- conv_merge: float32 [4718592], P(('rows', 'cols')), may hold values from -0.0625 to 0.0625
- conv_merge_mom: float32 [4718592], P(('rows', 'cols')), may hold values from -2.670288e-05 to 2.670288e-05
- conv_merge_sec: float32 [4718592], P(('rows', 'cols')), may hold values from 2.5431314e-13 to 1.0384454e-12
- head_weight: float32 [512, 2], replicated, may hold values from -0.25 to 0.25
- head_mom: float32 [512, 2], replicated, may hold values from -0.0007324219 to 0.0007324219
- head_sec: float32 [512, 2], replicated, may hold values from 2.1972656e-10 to 8.789062e-10
- biases: float32 [3074], replicated, may hold values from -0.75 to 0.75
- biases_mom: float32 [3074], replicated, may hold values from -0.00015258789 to 0.00015258789
- biases_sec: float32 [3074], replicated, may hold values from 8.132726e-12 to 3.2530905e-11
Outputs:
- first_mom_out: float32 [4718592], P(('rows', 'cols'))
- first_sec_out: float32 [4718592], P(('rows', 'cols'))
- first_new: float32 [4718592], P(('rows', 'cols'))
- second_mom_out: float32 [9437184], P(('rows', 'cols'))
- second_sec_out: float32 [9437184], P(('rows', 'cols'))
- second_new: float32 [9437184], P(('rows', 'cols'))
- up_mom_out: float32 [2097152], P(('rows', 'cols'))
- up_sec_out: float32 [2097152], P(('rows', 'cols'))
- up_new: float32 [2097152], P(('rows', 'cols'))
- merge_mom_out: float32 [4718592], P(('rows', 'cols'))
- merge_sec_out: float32 [4718592], P(('rows', 'cols'))
- merge_new: float32 [4718592], P(('rows', 'cols'))
- head_mom_out: float32 [512, 2], replicated
- head_sec_out: float32 [512, 2], replicated
- head_new: float32 [512, 2], replicated
- biases_mom_out: float32 [3074], replicated
- biases_sec_out: float32 [3074], replicated
- biases_new: float32 [3074], replicated
- loss_sum: float32 [], replicated
- valid_count: float32 [], replicated
- grad_norm: float32 [], replicated
Inputs may be any that keep to these rules, and one draw needn't show every extreme that they name: `valid_mask`: 1 at the last pixel of every image.
All inputs are finite; a program needn't handle non-finite values.
Results may differ from a plain program's by a relative error of at most 0.011.
Values may be sent and summed in bfloat16 or wider, within the bound.
No kernel may reach another device: no remote copies, remote signals or barrier semaphores. Data moves between devices by JAX's collectives and lax.ppermute only.
A program may use at most 384 MiB of HBM per device.

v0:
```python
import jax
import jax.numpy as jnp
from jax import lax
from jax.sharding import PartitionSpec as P

C0 = 512
C1 = 1024
CLASSES = 2
STEP = 10


clip_norm = 0.05
learn_rate = 0.02
beta_first = 0.9
beta_second = 0.999
epsilon = 1e-08
weight_decay = 0.1


def extended(cells, sides, width):
    for axis, dim in sides:
        count = lax.axis_size(axis)
        ends = count - 1
        head = lax.slice_in_dim(cells, 0, width, axis=dim)
        tail = lax.slice_in_dim(cells, cells.shape[dim] - width, cells.shape[dim], axis=dim)
        cells = jnp.concatenate(
            [
                lax.ppermute(tail, axis, [(i, (i + 1) % count) for i in range(ends)]),
                cells,
                lax.ppermute(head, axis, [((i + 1) % count, i) for i in range(ends)]),
            ],
            axis=dim,
        )
    return cells


def padded_input(values):
    return extended(values, (("rows", 1), ("cols", 2)), 1)


def convolve(padded, kernel):
    return lax.conv_general_dilated(
        padded,
        kernel,
        (1, 1),
        "VALID",
        dimension_numbers=("NHWC", "HWIO", "NHWC"),
        preferred_element_type=jnp.float32,
    )


def kernel_grad(padded, grad):
    rows_in, cols_in = (grad.shape[1], grad.shape[2])
    terms = [
        jnp.einsum(
            "nhwc,nhwo->co",
            padded[:, shift_h : shift_h + rows_in, shift_w : shift_w + cols_in],
            grad,
            preferred_element_type=jnp.float32,
        )
        for shift_h in range(3)
        for shift_w in range(3)
    ]
    return jnp.stack(terms).reshape(-1)


def input_grad(grad, kernel):
    border = extended(grad, (("rows", 1), ("cols", 2)), 1)
    flipped = jnp.swapaxes(kernel[::-1, ::-1], 2, 3)
    return convolve(border, flipped)


def gelu_back(pre_act, upstream):
    return jax.vjp(jax.nn.gelu, pre_act)[1](upstream)[0]


def column_sum(values):
    return jnp.sum(values, axis=(0, 1, 2), dtype=jnp.float32)


def upsample(values, kernel):
    images, rows_in, cols_in = (values.shape[0], values.shape[1], values.shape[2])
    expanded = jnp.einsum("nhwc,abco->nhawbo", values, kernel, preferred_element_type=jnp.float32)
    return expanded.reshape(images, 2 * rows_in, 2 * cols_in, kernel.shape[3])


def forward(kernels, biases, head_low, features, skip_feat):
    kernel_one, kernel_two, kernel_up, kernel_merge = kernels
    feat_pad = padded_input(features)
    pre_one = convolve(feat_pad, kernel_one) + biases[:C1]
    act_one = jax.nn.gelu(pre_one).astype(jnp.bfloat16)
    act_one_pad = padded_input(act_one)
    pre_two = convolve(act_one_pad, kernel_two) + biases[C1 : 2 * C1]
    act_two = jax.nn.gelu(pre_two).astype(jnp.bfloat16)
    upsampled = (upsample(act_two, kernel_up) + biases[2 * C1 : 2 * C1 + C0]).astype(jnp.bfloat16)
    joined_pad = padded_input(jnp.concatenate([upsampled, skip_feat], axis=3))
    pre_three = convolve(joined_pad, kernel_merge) + biases[2 * C1 + C0 : 2 * C1 + 2 * C0]
    act_three = jax.nn.gelu(pre_three).astype(jnp.bfloat16)
    logits = (
        jnp.einsum("nhwc,ck->nhwk", act_three, head_low, preferred_element_type=jnp.float32)
        + biases[2 * C1 + 2 * C0 :]
    )
    return (
        feat_pad,
        pre_one,
        act_one_pad,
        pre_two,
        act_two,
        joined_pad,
        pre_three,
        act_three,
        logits,
    )


def adamw(weight, moment, second, grad, decay):
    new_mom = beta_first * moment + (1.0 - beta_first) * grad
    new_sec = beta_second * second + (1.0 - beta_second) * grad * grad
    corrected = new_mom / (1.0 - beta_first**STEP)
    spread = jnp.sqrt(new_sec / (1.0 - beta_second**STEP))
    return (
        new_mom,
        new_sec,
        weight - learn_rate * (corrected / (spread + epsilon) + decay * weight),
    )


def shards(
    features,
    skip_feat,
    labels,
    pixel_weight,
    valid_mask,
    conv_first,
    conv_first_mom,
    conv_first_sec,
    conv_second,
    conv_second_mom,
    conv_second_sec,
    up_conv,
    up_conv_mom,
    up_conv_sec,
    conv_merge,
    conv_merge_mom,
    conv_merge_sec,
    head_weight,
    head_mom,
    head_sec,
    biases,
    biases_mom,
    biases_sec,
):
    count_all = lax.psum(jnp.sum(valid_mask.astype(jnp.float32)), ("rows", "cols"))
    low_one = conv_first.astype(jnp.bfloat16)
    low_two = conv_second.astype(jnp.bfloat16)
    low_up = up_conv.astype(jnp.bfloat16)
    low_merge = conv_merge.astype(jnp.bfloat16)
    whole = (
        lax.all_gather(low_one, ("rows", "cols"), axis=0, tiled=True),
        lax.all_gather(low_two, ("rows", "cols"), axis=0, tiled=True),
        lax.all_gather(low_up, ("rows", "cols"), axis=0, tiled=True),
        lax.all_gather(low_merge, ("rows", "cols"), axis=0, tiled=True),
    )
    kernel_one = whole[0].reshape(3, 3, C0, C1)
    kernel_two = whole[1].reshape(3, 3, C1, C1)
    kernel_up = whole[2].reshape(2, 2, C1, C0)
    kernel_merge = whole[3].reshape(3, 3, 2 * C0, C0)
    kernels = (kernel_one, kernel_two, kernel_up, kernel_merge)
    head_low = head_weight.astype(jnp.bfloat16)
    first_pass = forward(kernels, biases, head_low, features, skip_feat)
    logits = first_pass[8]
    saved = forward(lax.optimization_barrier(kernels), biases, head_low, features, skip_feat)
    (
        feat_pad,
        pre_one,
        act_one_pad,
        pre_two,
        act_two,
        joined_pad,
        pre_three,
        act_three,
        unused_logits,
    ) = saved
    scaled = (valid_mask * pixel_weight).astype(jnp.float32)
    onehot = (labels[..., None] == jnp.arange(CLASSES, dtype=jnp.int32)).astype(jnp.float32)
    log_probs = jax.nn.log_softmax(logits, axis=-1)
    loss_part = -jnp.sum(scaled * jnp.sum(onehot * log_probs, axis=-1))
    grad_logits = ((jnp.exp(log_probs) - onehot) * (scaled / count_all)[..., None]).astype(
        jnp.bfloat16
    )
    head_part = jnp.einsum(
        "nhwc,nhwk->ck", act_three, grad_logits, preferred_element_type=jnp.float32
    )
    grad_act_three = jnp.einsum(
        "nhwk,ck->nhwc", grad_logits, head_low, preferred_element_type=jnp.float32
    )
    grad_pre_three = gelu_back(pre_three, grad_act_three).astype(jnp.bfloat16)
    merge_grad = kernel_grad(joined_pad, grad_pre_three)
    grad_joined = input_grad(grad_pre_three, kernel_merge)
    grad_upper = grad_joined[..., :C0].astype(jnp.bfloat16)
    images, rows_in, cols_in = (act_two.shape[0], act_two.shape[1], act_two.shape[2])
    grad_blocks = grad_upper.reshape(images, rows_in, 2, cols_in, 2, C0)
    up_grad = jnp.einsum(
        "nhwc,nhawbo->abco", act_two, grad_blocks, preferred_element_type=jnp.float32
    ).reshape(-1)
    grad_act_two = jnp.einsum(
        "nhawbo,abco->nhwc", grad_blocks, kernel_up, preferred_element_type=jnp.float32
    )
    grad_pre_two = gelu_back(pre_two, grad_act_two).astype(jnp.bfloat16)
    second_grad = kernel_grad(act_one_pad, grad_pre_two)
    grad_act_one = input_grad(grad_pre_two, kernel_two)
    grad_pre_one = gelu_back(pre_one, grad_act_one).astype(jnp.bfloat16)
    first_grad = kernel_grad(feat_pad, grad_pre_one)
    bias_part = jnp.concatenate(
        [
            column_sum(grad_pre_one),
            column_sum(grad_pre_two),
            column_sum(grad_upper),
            column_sum(grad_pre_three),
            column_sum(grad_logits),
        ]
    )
    share_one, share_two, share_up, share_merge = (
        lax.psum_scatter(first_grad, ("rows", "cols"), scatter_dimension=0, tiled=True),
        lax.psum_scatter(second_grad, ("rows", "cols"), scatter_dimension=0, tiled=True),
        lax.psum_scatter(up_grad, ("rows", "cols"), scatter_dimension=0, tiled=True),
        lax.psum_scatter(merge_grad, ("rows", "cols"), scatter_dimension=0, tiled=True),
    )
    share_sq = (
        jnp.sum(share_one * share_one)
        + jnp.sum(share_two * share_two)
        + jnp.sum(share_up * share_up)
        + jnp.sum(share_merge * share_merge)
    )
    bias_total, head_total, sq_total, loss_total = lax.psum(
        (bias_part, head_part, share_sq, loss_part), ("rows", "cols")
    )
    grad_norm = jnp.sqrt(
        sq_total + jnp.sum(bias_total * bias_total) + jnp.sum(head_total * head_total)
    )
    factor = clip_norm / jnp.maximum(grad_norm, clip_norm)
    one_m, one_v, one_w = adamw(
        conv_first, conv_first_mom, conv_first_sec, share_one * factor, weight_decay
    )
    two_m, two_v, two_w = adamw(
        conv_second, conv_second_mom, conv_second_sec, share_two * factor, weight_decay
    )
    up_m, up_v, up_w = adamw(up_conv, up_conv_mom, up_conv_sec, share_up * factor, weight_decay)
    mer_m, mer_v, mer_w = adamw(
        conv_merge, conv_merge_mom, conv_merge_sec, share_merge * factor, weight_decay
    )
    head_m, head_v, head_w = adamw(
        head_weight, head_mom, head_sec, head_total * factor, weight_decay
    )
    bias_m, bias_v, bias_w = adamw(biases, biases_mom, biases_sec, bias_total * factor, 0.0)
    return (
        one_m,
        one_v,
        one_w,
        two_m,
        two_v,
        two_w,
        up_m,
        up_v,
        up_w,
        mer_m,
        mer_v,
        mer_w,
        head_m,
        head_v,
        head_w,
        bias_m,
        bias_v,
        bias_w,
        loss_total,
        count_all,
        grad_norm,
    )


def solution(mesh):
    placed = (
        P(None, "rows", "cols", None),
        P(None, "rows", "cols", None),
        P(None, "rows", "cols"),
        P(None, "rows", "cols"),
        P(None, "rows", "cols"),
        P(("rows", "cols")),
        P(("rows", "cols")),
        P(("rows", "cols")),
        P(("rows", "cols")),
        P(("rows", "cols")),
        P(("rows", "cols")),
        P(("rows", "cols")),
        P(("rows", "cols")),
        P(("rows", "cols")),
        P(("rows", "cols")),
        P(("rows", "cols")),
        P(("rows", "cols")),
        P(),
        P(),
        P(),
        P(),
        P(),
        P(),
    )
    return jax.shard_map(
        shards,
        mesh=mesh,
        in_specs=placed,
        out_specs=(
            P(("rows", "cols")),
            P(("rows", "cols")),
            P(("rows", "cols")),
            P(("rows", "cols")),
            P(("rows", "cols")),
            P(("rows", "cols")),
            P(("rows", "cols")),
            P(("rows", "cols")),
            P(("rows", "cols")),
            P(("rows", "cols")),
            P(("rows", "cols")),
            P(("rows", "cols")),
            P(),
            P(),
            P(),
            P(),
            P(),
            P(),
            P(),
            P(),
            P(),
        ),
        check_vma=False,
    )
```

profile of v0, /device:TPU:0, one launch (start us, length us, event | category | flops | bytes accessed | tf_op | source)
XLA Modules:
  0.0 1980.0 jit_solution(11166815598065321090)
XLA Ops:
  15.1 5.5 collective-permute-start
  23.9 3.0 collective-permute-start.2
  29.2 66.8 %all-gather.5.cloned.1.call-done = bf16[4718592]{0:T(1024)(128)(2,1)} async-done(((bf16[147456]{0:T(1024)(128)(2,1)}), bf16[4718592]{0:T(1024)(128)(2,1)}) %all-gather.5.cloned.1.call-update) | async-done | bytes 9437200 | tf_op jit(solution)/shard_map/all_gather | solution.py:159
  96.0 14.8 reshape.182
  110.9 5.5 fusion.141
  117.9 4.6 collective-permute-start.4
  124.2 4.6 collective-permute-done.4
  132.6 27.5 %all-gather.9.cloned.1.call-done = bf16[2097152]{0:T(1024)(128)(2,1)} async-done(((bf16[65536]{0:T(1024)(128)(2,1)}), bf16[2097152]{0:T(1024)(128)(2,1)}) %all-gather.9.cloned.1.call-update) | async-done | bytes 4194320 | tf_op jit(solution)/shard_map/all_gather | solution.py:161
  160.1 7.5 reshape.334
  167.6 7.6 reshape.185
  175.2 69.0 %all-gather.11.cloned.1.call-done = bf16[4718592]{0:T(1024)(128)(2,1)} async-done(((bf16[147456]{0:T(1024)(128)(2,1)}), bf16[4718592]{0:T(1024)(128)(2,1)}) %all-gather.11.cloned.1.call-update) | async-done | bytes 9437200 | tf_op jit(solution)/shard_map/all_gather | solution.py:162
  244.2 15.6 reshape.187
  261.5 109.3 %all-gather.7.cloned.1.call-done = bf16[9437184]{0:T(1024)(128)(2,1)} async-done(((bf16[294912]{0:T(1024)(128)(2,1)}), bf16[9437184]{0:T(1024)(128)(2,1)}) %all-gather.7.cloned.1.call-update) | async-done | bytes 18874384 | tf_op jit(solution)/shard_map/all_gather | solution.py:160
  370.8 28.4 %reshape.183 = bf16[3,3,1024,1024]{3,2,1,0:T(8,128)(2,1)} reshape(bf16[9437184]{0:T(1024)(128)(2,1)} %all-gather.7.cloned.1.call-done) | data formatting | bytes 37748736 | tf_op jit(solution)/shard_map/reshape | solution.py:165
  399.2 5.5 multiply_convert_fusion.2
  406.2 4.6 collective-permute-start.12
  410.8 9.8 fusion.153
  424.0 3.0 convolution_bitcast_fusion.1
  429.2 10.9 multiply_convert_fusion.1
  440.9 3.0 fusion.19
  445.0 4.3 collective-permute-start.8
  451.9 5.2 collective-permute-start.16
  457.1 9.5 collective-permute-done.8
  466.6 5.6 collective-permute-done.16
  476.4 3.6 collective-permute-start.18
  481.9 7.8 reverse_bitcast_fusion
  499.6 6.7 fusion.99
  507.8 43.2 %psum.35 = f32[]{:T(128)} all-reduce(f32[]{:T(128)} %get-tuple-element.30), channel_id=1, replica_groups=mesh['rows'=8,'cols'=4] {'rows','cols'}, use_global_device_ids=true, to_apply=%region_3.0 | all-reduce | flops 1 | bytes 8 | tf_op jit(solution)/shard_map/psum | solution.py:153
  555.0 7.5 multiply_convert_fusion
  566.4 4.4 collective-permute-start.20
  580.8 9.0 copy.245
  597.8 5.0 collective-permute-start.24
  605.5 2.8 bitcast_dynamic-update-slice_fusion.7
  610.9 2.8 bitcast_dynamic-update-slice_fusion.5
  616.4 2.8 bitcast_dynamic-update-slice_fusion.3
  621.9 2.8 bitcast_dynamic-update-slice_fusion.1
  624.7 2.7 bitcast_dynamic-update-slice_fusion
  627.5 4.5 collective-permute-start.26
  633.3 4.6 convolution_bitcast_fusion
  637.9 8.7 copy.190
  646.6 8.9 copy.244
  655.5 32.9 %copy.243 = f32[1152,8,8,128]{3,1,2,0:T(8,128)} copy(f32[1152,8,8,128]{3,2,1,0:T(8,128)} %bitcast.201) | data formatting | bytes 75497472
  690.1 12.4 select_reduce_fusion.1
  707.0 8.9 copy.242
  724.3 1181.7 %all-reduce.8.cloned.1.call-done = (f32[4718592]{0:T(1024)}, f32[9437184]{0:T(1024)}, f32[2097152]{0:T(1024)}, f32[4718592]{0:T(1024)}) async-done(((f32[4718592]{0:T(1024)}, f32[9437184]{0:T(1024)}, f32[2097152]{0:T(1024)}, f32[4718592]{0:T(1024)}), (f32[4718592]{0:T(1024)}, f32[9437184]{0:T(1024)}, f32[2097152]{0:T(1024)}, f32[4718592]{0:T(1024)})) %all-reduce.8.cloned.1.call-update) | async-done | bytes 83886096
  1916.1 41.1 %all-reduce.4 = (f32[]{:T(128)}, f32[3074]{0:T(1024)S(1)}, f32[512,2]{0,1:T(2,128)}, f32[]{:T(128)}) all-reduce(f32[]{:T(128)S(6)} %add.254, f32[3074]{0:T(1024)} %constant_dynamic-update-slice_fusion.1, f32[512,2]{0,1:T(2,128)} %convolution_bitcast_fusion.3, f32[]{:T(128)S(6)} %neg.3), channel_id=1, replica_groups=mesh['rows'=8,'cols'=4] {'rows','cols'}, use_global_device_ids=true, to_apply=%region_12.13 | all-reduce | flops 4100 | bytes 32800 | tf_op jit(solution)/shard_map/psum | solution.py:235
  1961.3 3.8 multiply_subtract_fusion
  1968.5 3.6 multiply_subtract_fusion.1
  (311 shorter events, 114.5 us)
Async XLA Ops:
  7.2 88.8 %all-gather.5.cloned.1.call-start = ((), (), s32[]{:S(2)}) async-start(), calls=%async_computation | async-start | bytes 9732096 | tf_op jit(solution)/shard_map/all_gather | solution.py:159
  9.1 17.8 copy-start.38
  9.2 150.9 %all-gather.9.cloned.1.call-start = ((), (), s32[]{:S(2)}) async-start(), calls=%async_computation.2 | async-start | bytes 4325376 | tf_op jit(solution)/shard_map/all_gather | solution.py:161
  10.9 233.4 %all-gather.11.cloned.1.call-start = ((), (), s32[]{:S(2)}) async-start(), calls=%async_computation.3 | async-start | bytes 9732096 | tf_op jit(solution)/shard_map/all_gather | solution.py:162
  12.8 358.1 %all-gather.7.cloned.1.call-start = ((), (), s32[]{:S(2)}) async-start(), calls=%async_computation.1 | async-start | bytes 19464192 | tf_op jit(solution)/shard_map/all_gather | solution.py:160
  13.7 1892.3 %all-reduce.8.cloned.1.call-start = ((), (), s32[]{:S(2)}) async-start(), calls=%async_computation.4 | async-start | bytes 167772160
  13.8 7.1 collective-permute-start.1
  15.1 7.5 collective-permute-start
  22.6 4.4 collective-permute-start.3
  23.9 3.9 collective-permute-start.2
  29.2 81.6 %copy-start.40 = (pred[16,5]{0,1:T(8,128)(4,1)S(1)}, pred[16,5]{0,1:T(8,128)(4,1)}, u32[]{:S(2)}) copy-start(pred[16,5]{0,1:T(8,128)(4,1)} %constant.131) | copy-start | bytes 244
  116.6 7.6 collective-permute-start.5
  117.9 10.9 collective-permute-start.4
  128.8 131.0 %collective-permute-start.6 = (bf16[2,3,1,1024]{3,2,0,1:T(2,128)(2,1)S(1)}, bf16[2,3,1,1024]{3,2,0,1:T(2,128)(2,1)S(1)}, u32[]{:S(2)}, u32[]{:S(2)}) collective-permute-start(bf16[2,3,1,1024]{3,2,0,1:T(2,128)(2,1)S(1)} %get-tuple-element.77), channel_id=1, source_target_pairs={{0,1},{1,2},{2,3},{4,5},{5,6},{6,7},{8,9},{9,10},{10,11},{12,13},{... | collective-permute-start | bytes 36872 | tf_op jit(solution)/shard_map/ppermute | solution.py:28
  130.8 129.0 %collective-permute-start.7 = (bf16[2,3,1,1024]{3,2,0,1:T(2,128)(2,1)S(1)}, bf16[2,3,1,1024]{3,2,0,1:T(2,128)(2,1)S(1)}, u32[]{:S(2)}, u32[]{:S(2)}) collective-permute-start(bf16[2,3,1,1024]{3,2,0,1:T(2,128)(2,1)S(1)} %get-tuple-element.78), channel_id=1, source_target_pairs={{1,0},{2,1},{3,2},{5,4},{6,5},{7,6},{9,8},{10,9},{11,10},{13,12},{... | collective-permute-start | bytes 36872 | tf_op jit(solution)/shard_map/ppermute | solution.py:30
  404.9 15.9 collective-permute-start.13
  406.2 14.6 collective-permute-start.12
  420.9 6.6 collective-permute-start.14
  422.5 5.0 collective-permute-start.15
  445.0 21.6 %collective-permute-start.8 = (bf16[2,1,64,1024]{3,2,0,1:T(8,128)(2,1)S(1)}, bf16[2,1,64,1024]{3,2,0,1:T(8,128)(2,1)S(1)}, u32[]{:S(2)}, u32[]{:S(2)}) collective-permute-start(bf16[2,1,64,1024]{3,2,0,1:T(8,128)(2,1)S(1)} %get-tuple-element.71), channel_id=1, source_target_pairs={{0,4},{4,8},{8,12},{12,16},{16,20},{20,24},{24,28},{1,5},{5,9},{9,... | collective-permute-start | bytes 786440 | tf_op jit(solution)/shard_map/ppermute | solution.py:28
  449.3 17.3 collective-permute-start.9
  450.6 16.0 collective-permute-start.17
  451.9 20.3 %collective-permute-start.16 = (bf16[2,1,64,1024]{3,2,0,1:T(8,128)(2,1)S(1)}, bf16[2,1,64,1024]{3,2,0,1:T(8,128)(2,1)S(1)}, u32[]{:S(2)}, u32[]{:S(2)}) collective-permute-start(bf16[2,1,64,1024]{3,2,0,1:T(8,128)(2,1)S(1)} %get-tuple-element.92), channel_id=1, source_target_pairs={{0,4},{4,8},{8,12},{12,16},{16,20},{20,24},{24,28},{1,5},{5,9},{9,... | collective-permute-start | bytes 786440 | tf_op jit(solution)/shard_map/ppermute | solution.py:28
  466.6 13.4 copy-start.22
  466.6 13.4 copy-start.24
  472.5 22.6 %collective-permute-start.10 = (bf16[2,4,1,1024]{3,2,0,1:T(2,128)(2,1)S(1)}, bf16[2,4,1,1024]{3,2,0,1:T(2,128)(2,1)S(1)}, u32[]{:S(2)}, u32[]{:S(2)}) collective-permute-start(bf16[2,4,1,1024]{3,2,0,1:T(2,128)(2,1)S(1)} %get-tuple-element.61), channel_id=1, source_target_pairs={{0,1},{1,2},{2,3},{4,5},{5,6},{6,7},{8,9},{9,10},{10,11},{12,13},{... | collective-permute-start | bytes 49160 | tf_op jit(solution)/shard_map/ppermute | solution.py:28
  475.1 20.0 %collective-permute-start.11 = (bf16[2,4,1,1024]{3,2,0,1:T(2,128)(2,1)S(1)}, bf16[2,4,1,1024]{3,2,0,1:T(2,128)(2,1)S(1)}, u32[]{:S(2)}, u32[]{:S(2)}) collective-permute-start(bf16[2,4,1,1024]{3,2,0,1:T(2,128)(2,1)S(1)} %get-tuple-element.62), channel_id=1, source_target_pairs={{1,0},{2,1},{3,2},{5,4},{6,5},{7,6},{9,8},{10,9},{11,10},{13,12},{... | collective-permute-start | bytes 49160 | tf_op jit(solution)/shard_map/ppermute | solution.py:30
  476.4 18.6 collective-permute-start.18
  480.0 11.8 copy-start.14
  480.0 15.0 collective-permute-start.19
  566.4 10.2 collective-permute-start.20
  570.8 6.9 collective-permute-start.21
  577.7 12.1 collective-permute-start.22
  579.0 10.8 collective-permute-start.23
  580.8 10.9 slice-start
  580.8 10.9 slice-start.1
  580.8 10.9 slice-start.2
  596.5 30.9 %collective-permute-start.25 = (bf16[2,1,32,1024]{3,2,0,1:T(8,128)(2,1)S(1)}, bf16[2,1,32,1024]{3,2,0,1:T(8,128)(2,1)S(1)}, u32[]{:S(2)}, u32[]{:S(2)}) collective-permute-start(bf16[2,1,32,1024]{3,2,0,1:T(8,128)(2,1)S(1)} %get-tuple-element.110), channel_id=1, source_target_pairs={{4,0},{8,4},{12,8},{16,12},{20,16},{24,20},{28,24},{5,1},{9,5},{13... | collective-permute-start | bytes 393224 | tf_op jit(solution)/shard_map/ppermute | solution.py:30
  597.8 29.6 %collective-permute-start.24 = (bf16[2,1,32,1024]{3,2,0,1:T(8,128)(2,1)S(1)}, bf16[2,1,32,1024]{3,2,0,1:T(8,128)(2,1)S(1)}, u32[]{:S(2)}, u32[]{:S(2)}) collective-permute-start(bf16[2,1,32,1024]{3,2,0,1:T(8,128)(2,1)S(1)} %get-tuple-element.110), channel_id=1, source_target_pairs={{0,4},{4,8},{8,12},{12,16},{16,20},{20,24},{24,28},{1,5},{5,9},{9,... | collective-permute-start | bytes 393224 | tf_op jit(solution)/shard_map/ppermute | solution.py:28
  627.5 60.9 %collective-permute-start.26 = (bf16[2,3,1,1024]{3,2,0,1:T(2,128)(2,1)S(1)}, bf16[2,3,1,1024]{3,2,0,1:T(2,128)(2,1)S(1)}, u32[]{:S(2)}, u32[]{:S(2)}) collective-permute-start(bf16[2,3,1,1024]{3,2,0,1:T(2,128)(2,1)S(1)} %get-tuple-element.75), channel_id=1, source_target_pairs={{0,1},{1,2},{2,3},{4,5},{5,6},{6,7},{8,9},{9,10},{10,11},{12,13},{... | collective-permute-start | bytes 36872 | tf_op jit(solution)/shard_map/ppermute | solution.py:28
  632.0 56.4 %collective-permute-start.27 = (bf16[2,3,1,1024]{3,2,0,1:T(2,128)(2,1)S(1)}, bf16[2,3,1,1024]{3,2,0,1:T(2,128)(2,1)S(1)}, u32[]{:S(2)}, u32[]{:S(2)}) collective-permute-start(bf16[2,3,1,1024]{3,2,0,1:T(2,128)(2,1)S(1)} %get-tuple-element.76), channel_id=1, source_target_pairs={{1,0},{2,1},{3,2},{5,4},{6,5},{7,6},{9,8},{10,9},{11,10},{13,12},{... | collective-permute-start | bytes 36872 | tf_op jit(solution)/shard_map/ppermute | solution.py:30
  690.1 12.6 copy-start.2
  690.1 12.6 copy-start.4
  690.1 12.6 copy-start.6
  690.1 12.6 copy-start.37
  715.9 1245.2 %copy-start.8 = (f32[294912]{0:T(1024)S(1)}, f32[294912]{0:T(1024)}, u32[]{:S(2)}) copy-start(f32[294912]{0:T(1024)} %param.31) | copy-start | bytes 3538948
  715.9 1245.2 %copy-start.15 = (f32[294912]{0:T(1024)S(1)}, f32[294912]{0:T(1024)}, u32[]{:S(2)}) copy-start(f32[294912]{0:T(1024)} %param.33) | copy-start | bytes 3538948
  715.9 1245.2 %copy-start.16 = (f32[294912]{0:T(1024)S(1)}, f32[294912]{0:T(1024)}, u32[]{:S(2)}) copy-start(f32[294912]{0:T(1024)} %param.32) | copy-start | bytes 3538948
  (47 other events, 218.1 us)
Sparse Core Ops, SparseCore 0:
  11.5 84.4 all-gather.4
  99.4 60.6 all-gather.8
  163.6 80.5 all-gather.10
  247.6 123.2 all-gather.6
  716.0 1189.9 all-reduce.7
where the time goes:
time: 1990 us; the launch traced here: 1980 us
  waiting for transfers between devices  1480 us (74%)
  local copies, waits for them, and re-layouts  178 us (9%)
  matrix products  108 us (5%)
  blocking collectives  84.3 us (4%)
  starting transfers between devices  71.2 us (4%)
  other arithmetic  36.1 us (2%)
  between operations  22.3 us (1%)
    unnamed x6, waiting for transfers between devices  1180 us
    all_gather x1, waiting for transfers between devices, shards(): lax.all_gather(low_two, ('rows', 'cols'), axis=0, tiled=True)  109 us
    unnamed x137, local copies, waits for them, and re-layouts  69.6 us
    all_gather x1, waiting for transfers between devices, shards(): lax.all_gather(low_merge, ('rows', 'cols'), axis=0, tiled=True)  69 us
    all_gather x1, waiting for transfers between devices, shards(): lax.all_gather(low_one, ('rows', 'cols'), axis=0, tiled=True)  66.8 us
    conv_general_dilated x8, matrix products, convolve(): lax.conv_general_dilated(padded, kernel, (1, 1), 'VALID', dimension_numbe...  60.5 us
    ppermute x14, starting transfers between devices, extended(): lax.ppermute(tail, axis, [(i, (i + 1) % count) for i in range(ends)])  51.9 us
    psum x1, blocking collectives, shards(): lax.psum(jnp.sum(valid_mask.astype(jnp.float32)), ('rows', 'cols'))  43.2 us
  transfers between devices with their start and end apart: 33, of which 13 were waited for; matrix products, arithmetic and copies ran while one was open for 9% of the time, Pallas kernels for 0%

commit v1 on v0

v1 whole, which is shorter than its diff:
```python
import jax
import jax.numpy as jnp
from jax import lax
from jax.sharding import Mesh
from jax.sharding import PartitionSpec as P

C0 = 512
C1 = 1024
CLASSES = 2
STEP = 10

clip_norm = 0.05
learn_rate = 0.02
beta_first = 0.9
beta_second = 0.999
epsilon = 1e-08
weight_decay = 0.1

AXES = ("zh", "zl", "y", "x", "core")
MEMBERS = ("zl", "y", "core")
CHIPS = ("zh", "zl", "y", "x")
ROWS = ("zh", "zl", "y")
bf16 = jnp.bfloat16
f32 = jnp.float32


def size_of(axis):
    return lax.axis_size(axis)


def shifted(values, axis, step):
    count = size_of(axis)
    return lax.ppermute(
        values, axis, [(i, i + step) for i in range(count) if 0 <= i + step < count]
    )


def swapped(values, axis):
    return lax.ppermute(values, axis, [(0, 1), (1, 0)])


def padded(cells, axis, dim, width):
    head = lax.slice_in_dim(cells, 0, width, axis=dim)
    tail = lax.slice_in_dim(cells, cells.shape[dim] - width, cells.shape[dim], axis=dim)
    return jnp.concatenate(
        [shifted(tail, axis, 1), cells, shifted(head, axis, -1)], axis=dim
    )


def in_order(own, other, axis, dim):
    first = lax.axis_index(axis) == 0
    return jnp.concatenate(
        [jnp.where(first, own, other), jnp.where(first, other, own)], axis=dim
    )


def pair_gather(own, axis, dim):
    return in_order(own, swapped(own, axis), axis, dim)


def pair_half(values, axis, dim, index):
    width = values.shape[dim] // 2
    return lax.dynamic_slice_in_dim(values, index * width, width, axis=dim)


def pair_scatter(values, axis, dim, kind):
    me = lax.axis_index(axis)
    away = pair_half(values, axis, dim, 1 - me).astype(kind)
    return pair_half(values, axis, dim, me).astype(f32) + swapped(away, axis).astype(f32)


def total(values):
    for axis in ("core", "x", "y", "zl"):
        values = values + swapped(values, axis)
    if size_of("zh") == 2:
        return values + swapped(values, "zh")
    return lax.psum(values, "zh")


def convolve(values, kernel, pad=0):
    return lax.conv_general_dilated(
        values,
        kernel,
        (1, 1),
        ((pad, pad), (pad, pad)),
        dimension_numbers=("NHWC", "HWIO", "NHWC"),
        preferred_element_type=f32,
    )


def kernel_grad(cells, grad):
    rows_in, cols_in = (grad.shape[1], grad.shape[2])
    terms = [
        jnp.einsum(
            "nhwc,nhwo->co",
            cells[:, shift_h : shift_h + rows_in, shift_w : shift_w + cols_in],
            grad,
            preferred_element_type=f32,
        )
        for shift_h in range(3)
        for shift_w in range(3)
    ]
    return jnp.concatenate(terms, axis=0)


def turned(kernel):
    return jnp.swapaxes(kernel[::-1, ::-1], 2, 3)


def gelu_back(pre_act, upstream):
    return jax.vjp(jax.nn.gelu, pre_act)[1](upstream)[0]


def column_sum(values):
    return jnp.sum(values, axis=(0, 1, 2), dtype=f32)


def group_gather(block):
    n, _, w, c = block.shape
    sent = jnp.broadcast_to(block[None], (8,) + block.shape)
    got = lax.all_to_all(sent, MEMBERS, 0, 0, tiled=True)
    got = got.reshape(4, 2, n, w, c)
    return got.transpose(2, 0, 1, 3, 4).reshape(n, 4, 2 * w, c)


def group_scatter(partial):
    n, _, w2, c = partial.shape
    sent = partial.astype(bf16).reshape(n, 4, 2, w2 // 2, c).transpose(1, 2, 0, 3, 4)
    got = lax.all_to_all(sent.reshape(8, n, w2 // 2, c), MEMBERS, 0, 0, tiled=True)
    return jnp.sum(got.astype(f32), axis=0)[:, None]


def far_gather(part):
    got = (
        pair_gather(part[None], "zh", 0)
        if size_of("zh") == 2
        else lax.all_gather(part, "zh", axis=0)
    )
    got = pair_gather(got[:, None], "x", 1)
    zh, _, _, r, o = got.shape
    got = got.reshape(zh, 2, 2, 2, 2, r, o).transpose(0, 2, 3, 1, 4, 5, 6)
    return got.reshape(zh * 16 * r, o)


def far_scatter(grad, kind=bf16):
    zh = size_of("zh")
    o = grad.shape[1]
    r = grad.shape[0] // (16 * zh)
    split = grad.reshape(zh, 2, 2, 2, 2, r, o).transpose(3, 0, 1, 2, 4, 5, 6)
    split = pair_scatter(split, "x", 0, kind)[0]
    if zh == 2:
        split = pair_scatter(split, "zh", 0, kind)[0]
    else:
        split = lax.psum_scatter(split, "zh", scatter_dimension=0)
    return split.reshape(8, r, o)


def adamw(weight, moment, second, grad, decay):
    new_mom = beta_first * moment + (1.0 - beta_first) * grad
    new_sec = beta_second * second + (1.0 - beta_second) * grad * grad
    corrected = new_mom / (1.0 - beta_first**STEP)
    spread = jnp.sqrt(new_sec / (1.0 - beta_second**STEP))
    return (
        new_mom,
        new_sec,
        weight - learn_rate * (corrected / (spread + epsilon) + decay * weight),
    )


def shards(
    features,
    skip_feat,
    labels,
    pixel_weight,
    valid_mask,
    conv_first,
    conv_first_mom,
    conv_first_sec,
    conv_second,
    conv_second_mom,
    conv_second_sec,
    up_conv,
    up_conv_mom,
    up_conv_sec,
    conv_merge,
    conv_merge_mom,
    conv_merge_sec,
    head_weight,
    head_mom,
    head_sec,
    biases,
    biases_mom,
    biases_sec,
):
    core = lax.axis_index("core")
    member = (lax.axis_index("zl") * 2 + lax.axis_index("y")) * 2 + core
    zh, x = lax.axis_index("zh"), lax.axis_index("x")

    r1 = conv_first.shape[0] // C1
    low_one = conv_first.astype(bf16).reshape(r1, C1 // 8, 8).transpose(2, 0, 1)
    low_one = lax.all_to_all(low_one, MEMBERS, 0, 0, tiled=True)
    kernel_one = far_gather(low_one).reshape(3, 3, C0, C1 // 8)
    r2 = conv_second.shape[0] // C1
    low_two = conv_second.astype(bf16).reshape(r2, C1)
    if r2 % 8 == 0:
        low_two = low_two.reshape(r2 // 8, 8, C1).transpose(1, 0, 2)
        low_two = lax.all_to_all(low_two, MEMBERS, 0, 0, tiled=True)
        kernel_two = far_gather(low_two)
    else:
        low_two = lax.all_gather(low_two, AXES, axis=0, tiled=True).reshape(-1, 8, C1)
        kernel_two = lax.dynamic_index_in_dim(low_two, member, axis=1, keepdims=False)
    kernel_two = kernel_two.reshape(3, 3, C1 // 8, C1)

    def chip_kernel(flat):
        rows_in = flat.shape[0] // C0
        cut = flat.astype(bf16).reshape(rows_in, 2, C0 // 2).transpose(1, 0, 2)
        cut = pair_swap(cut).reshape(2 * rows_in, C0 // 2)
        return lax.all_gather(cut, CHIPS, axis=0, tiled=True)

    def pair_swap(cut):
        own = lax.dynamic_slice_in_dim(cut, core, 1, axis=0)
        away = lax.dynamic_slice_in_dim(cut, 1 - core, 1, axis=0)
        return in_order(own, swapped(away, "core"), "core", 0)

    kernel_up = chip_kernel(up_conv).reshape(2, 2, C1, C0 // 2)
    kernel_merge = chip_kernel(conv_merge).reshape(3, 3, 2 * C0, C0 // 2)

    bias_one = lax.dynamic_index_in_dim(
        biases[:C1].reshape(C1 // 8, 8), member, axis=1, keepdims=False
    )
    bias_two = biases[C1 : 2 * C1]
    bias_up = lax.dynamic_slice_in_dim(biases[2 * C1 : 2 * C1 + C0], core * (C0 // 2), C0 // 2)
    bias_three = lax.dynamic_slice_in_dim(
        biases[2 * C1 + C0 : 2 * C1 + 2 * C0], core * (C0 // 2), C0 // 2
    )
    bias_head = biases[2 * C1 + 2 * C0 :]
    head_low = lax.dynamic_slice_in_dim(
        head_weight.astype(bf16), core * (C0 // 2), C0 // 2, axis=0
    )

    count_all = total(jnp.sum(valid_mask.astype(f32)))

    feat = group_gather(features)
    feat = padded(feat, "zh", 1, 2)
    feat = padded(feat, "x", 2, 2)
    pre_one = convolve(feat, kernel_one) + bias_one
    high, wide = pre_one.shape[1], pre_one.shape[2]
    row_at = jnp.arange(high)
    col_at = jnp.arange(wide)
    row_in = ((row_at > 0) | (zh > 0)) & ((row_at < high - 1) | (zh < size_of("zh") - 1))
    col_in = ((col_at > 0) | (x > 0)) & ((col_at < wide - 1) | (x < size_of("x") - 1))
    inside = (row_in[:, None] & col_in[None, :])[None, :, :, None]
    act_one = jnp.where(inside, jax.nn.gelu(pre_one), 0.0).astype(bf16)
    pre_two = group_scatter(convolve(act_one, kernel_two)) + bias_two
    act_two = jax.nn.gelu(pre_two).astype(bf16)

    skip = padded(pair_gather(skip_feat, "core", 2), ROWS, 1, 1)
    skip = padded(skip, "x", 2, 1)
    act_chip = pair_gather(act_two, "core", 2)
    images, rows_in, cols_in = act_chip.shape[:3]
    ups = jnp.einsum("nhwc,abco->nhawbo", act_chip, kernel_up, preferred_element_type=f32)
    ups = ups.reshape(images, 2 * rows_in, 2 * cols_in, C0 // 2) + bias_up
    ups = padded(ups.astype(bf16), ROWS, 1, 1)
    ups = padded(ups, "x", 2, 1)
    joined = jnp.concatenate([pair_gather(ups, "core", 3), skip], axis=3)
    pre_three = convolve(joined, kernel_merge) + bias_three
    act_three = jax.nn.gelu(pre_three).astype(bf16)
    logits = jnp.einsum("nhwc,ck->nhwk", act_three, head_low, preferred_element_type=f32)
    logits = logits + swapped(logits, "core") + bias_head

    marks = jnp.stack([labels, valid_mask * pixel_weight])
    marks = pair_gather(marks, "core", 3)
    scaled = marks[1].astype(f32)
    onehot = (marks[0][..., None] == jnp.arange(CLASSES, dtype=jnp.int32)).astype(f32)
    log_probs = jax.nn.log_softmax(logits, axis=-1)
    loss_part = -0.5 * jnp.sum(scaled * jnp.sum(onehot * log_probs, axis=-1))
    grad_logits = ((jnp.exp(log_probs) - onehot) * (scaled / count_all)[..., None]).astype(bf16)

    head_part = jnp.einsum("nhwc,nhwk->ck", act_three, grad_logits, preferred_element_type=f32)
    grad_act_three = jnp.einsum("nhwk,ck->nhwc", grad_logits, head_low, preferred_element_type=f32)
    grad_pre_three = gelu_back(pre_three, grad_act_three).astype(bf16)
    merge_grad = kernel_grad(joined, grad_pre_three)
    border = padded(grad_pre_three, ROWS, 1, 1)
    border = padded(border, "x", 2, 1)
    grad_ups = convolve(border, turned(kernel_merge[:, :, :C0]))
    grad_upper = pair_scatter(grad_ups, "core", 3, bf16).astype(bf16)
    grad_blocks = grad_upper.reshape(images, rows_in, 2, cols_in, 2, C0 // 2)
    up_grad = jnp.einsum(
        "nhwc,nhawbo->abco", act_chip, grad_blocks, preferred_element_type=f32
    ).reshape(-1, C0 // 2)
    grad_act_two = jnp.einsum(
        "nhawbo,abco->nhwc", grad_blocks, kernel_up, preferred_element_type=f32
    )
    grad_act_two = pair_scatter(grad_act_two, "core", 2, f32)
    grad_pre_two = gelu_back(pre_two, grad_act_two).astype(bf16)

    grad_two = group_gather(grad_pre_two)
    second_grad = kernel_grad(act_one, grad_two)
    spill = convolve(grad_two, turned(kernel_two), 2)
    inner = spill[:, 1:-1]
    inner = inner.at[:, :1].add(shifted(spill[:, -1:], "zh", 1))
    inner = inner.at[:, -1:].add(shifted(spill[:, :1], "zh", -1))
    core_part = inner[:, :, 1:-1]
    core_part = core_part.at[:, :, :1].add(shifted(inner[:, :, -1:], "x", 1))
    core_part = core_part.at[:, :, -1:].add(shifted(inner[:, :, :1], "x", -1))
    grad_pre_one = gelu_back(pre_one[:, 1:-1, 1:-1], core_part).astype(bf16)
    first_grad = kernel_grad(feat[:, 1:-1, 1:-1], grad_pre_one)

    def chip_grad(grad):
        mine = lax.psum_scatter(grad.astype(bf16), CHIPS, scatter_dimension=0, tiled=True)
        rows_out = mine.shape[0] // 2
        cut = pair_swap(mine.reshape(2, rows_out, C0 // 2))
        return cut.transpose(1, 0, 2).reshape(-1).astype(f32)

    share_merge = chip_grad(merge_grad)
    share_up = chip_grad(up_grad)
    if r2 % 8 == 0:
        part_two = far_scatter(second_grad).astype(bf16)
        part_two = lax.all_to_all(part_two, MEMBERS, 0, 0, tiled=True)
        share_two = part_two.transpose(1, 0, 2).reshape(-1).astype(f32)
    else:
        mine = jnp.arange(8)[None, :, None] == member
        part_two = jnp.where(mine, second_grad.astype(bf16)[:, None], 0)
        share_two = lax.psum_scatter(
            part_two.reshape(-1, C1), AXES, scatter_dimension=0, tiled=True
        ).reshape(-1).astype(f32)
    part_one = far_scatter(first_grad).astype(bf16)
    part_one = lax.all_to_all(part_one, MEMBERS, 0, 0, tiled=True)
    share_one = part_one.transpose(1, 2, 0).reshape(-1).astype(f32)

    share_sq = (
        jnp.sum(share_one * share_one)
        + jnp.sum(share_two * share_two)
        + jnp.sum(share_up * share_up)
        + jnp.sum(share_merge * share_merge)
    )
    spread_one = (
        jnp.where(jnp.arange(8)[None, :] == member, column_sum(grad_pre_one)[:, None], 0.0)
    ).reshape(-1)

    def half_of(values):
        shape = (2 * values.shape[0],) + values.shape[1:]
        return lax.dynamic_update_slice_in_dim(
            jnp.zeros(shape, f32), values, core * values.shape[0], axis=0
        )

    packed = jnp.concatenate(
        [
            spread_one,
            column_sum(grad_pre_two),
            half_of(column_sum(grad_upper)),
            half_of(column_sum(grad_pre_three)),
            0.5 * column_sum(grad_logits),
            half_of(head_part).reshape(-1),
            share_sq[None],
            loss_part[None],
        ]
    )
    packed = total(packed)
    bias_total = packed[: biases.shape[0]]
    head_total = packed[biases.shape[0] : -2].reshape(head_weight.shape)
    sq_total, loss_total = packed[-2], packed[-1]
    grad_norm = jnp.sqrt(
        sq_total + jnp.sum(bias_total * bias_total) + jnp.sum(head_total * head_total)
    )
    factor = clip_norm / jnp.maximum(grad_norm, clip_norm)
    outs = ()
    for weight, moment, second, grad, decay in (
        (conv_first, conv_first_mom, conv_first_sec, share_one, weight_decay),
        (conv_second, conv_second_mom, conv_second_sec, share_two, weight_decay),
        (up_conv, up_conv_mom, up_conv_sec, share_up, weight_decay),
        (conv_merge, conv_merge_mom, conv_merge_sec, share_merge, weight_decay),
        (head_weight, head_mom, head_sec, head_total, weight_decay),
        (biases, biases_mom, biases_sec, bias_total, 0.0),
    ):
        outs += adamw(weight, moment, second, grad * factor, decay)
    return outs + (loss_total, count_all, grad_norm)


def solution(mesh):
    rows, cols = mesh.shape["rows"], mesh.shape["cols"]
    split = Mesh(mesh.devices.reshape(rows // 4, 2, 2, cols // 2, 2), AXES)
    image = P(None, ROWS, ("x", "core"))
    flat = P(AXES)
    return jax.shard_map(
        shards,
        mesh=split,
        in_specs=(image,) * 5 + (flat,) * 12 + (P(),) * 6,
        out_specs=(flat,) * 12 + (P(),) * 9,
        check_vma=False,
    )
```

time: 1990 us -> 682 us (0.34)
  waiting for transfers between devices: 1480 us -> 267 us
  blocking collectives: 84.3 us -> 13.6 us
  local copies, waits for them, and re-layouts: 178 us -> 115 us
  matrix products: 108 us -> 56.6 us
  starting transfers between devices: 71.2 us -> 117 us
  other arithmetic: 36.1 us -> 77.5 us
    unnamed x6 -> x4, waiting for transfers between devices: 1180 us -> 0.07 us
    all_gather x4 -> x2, waiting for transfers between devices: 273 us -> 0.04 us  [chip_kernel(): return lax.all_gather(cut, CHIPS, axis=0, tiled=True)]
    ppermute x28 -> x49, waiting for transfers between devices: 25.3 us -> 146 us  [the longest x29 92.8 us: swapped(): return lax.ppermute(values, axis, [(0, 1), (1, 0)])]
    psum x2 -> x0, blocking collectives: 84.3 us -> none  [the longest x1 43.2 us: shards(): lax.psum(jnp.sum(valid_mask.astype(jnp.float32)), ('rows', 'cols'))]
    all_to_all x0 -> x6, waiting for transfers between devices: none -> 62.1 us  [the longest x1 22.2 us: group_scatter(): lax.all_to_all(sent.reshape(8, n, w2 // 2, c), MEMBERS, 0, 0, tiled=True)]
    reshape x5 -> x9, local copies, waits for them, and re-layouts: 73.9 us -> 14.5 us  [the longest x1 6.37 us: shards(): low_one = conv_first.astype(bf16).reshape(r1, C1 // 8, 8).transpose(2, 0, 1)]
    reduce_scatter x0 -> x2, waiting for transfers between devices: none -> 58.4 us  [chip_grad(): lax.psum_scatter(grad.astype(bf16), CHIPS, scatter_dimension=0, tiled=True)]
    unnamed x137 -> x173, local copies, waits for them, and re-layouts: 69.6 us -> 23.1 us
  transfers between devices with their start and end apart: 33 -> 59, of which waited for: 13 -> 30; matrix products, arithmetic and copies ran while one was open for 9% -> 27% of each run, Pallas kernels for 0% -> 0%
where the time goes in v1:
time: 682 us; the launch traced here: 674 us
  waiting for transfers between devices  267 us (39%)
  starting transfers between devices  117 us (17%)
  local copies, waits for them, and re-layouts  115 us (17%)
  other arithmetic  77.5 us (11%)
  matrix products  56.6 us (8%)
  between operations  27.6 us (4%)
  blocking collectives  13.6 us (2%)
    ppermute x29, waiting for transfers between devices, swapped(): return lax.ppermute(values, axis, [(0, 1), (1, 0)])  92.8 us
    ppermute x20, starting transfers between devices, shifted(): lax.ppermute(values, axis, [(i, i + step) for i in range(count) if 0 <= i...  61.9 us
    reduce_scatter x2, waiting for transfers between devices, chip_grad(): lax.psum_scatter(grad.astype(bf16), CHIPS, scatter_dimension=0, tiled=True)  58.4 us
    ppermute x20, waiting for transfers between devices, shifted(): lax.ppermute(values, axis, [(i, i + step) for i in range(count) if 0 <= i...  53.4 us
    ppermute x29, starting transfers between devices, swapped(): return lax.ppermute(values, axis, [(0, 1), (1, 0)])  31.1 us
    dot_general x27, matrix products, kernel_grad(): jnp.einsum('nhwc,nhwo->co', cells[:, shift_h:shift_h + rows_in, shift_w:s...  28.3 us
    unnamed x173, local copies, waits for them, and re-layouts  23.1 us
    all_to_all x1, waiting for transfers between devices, group_scatter(): lax.all_to_all(sent.reshape(8, n, w2 // 2, c), MEMBERS, 0, 0, tiled=True)  22.2 us
  transfers between devices with their start and end apart: 59, of which 30 were waited for; matrix products, arithmetic and copies ran while one was open for 27% of the time, Pallas kernels for 0%

profile of v1, /device:TPU:0, one launch (start us, length us, event | category | flops | bytes accessed | tf_op | source)
XLA Modules:
  0.0 674.3 jit_solution(6842999015834087872)
XLA Ops:
  10.9 6.4 reshape.518
  17.2 4.0 copy.616
  21.2 13.6 %all_to_all.35 = bf16[8,144,128]{2,1,0:T(8,128)(2,1)S(1)} all-to-all(bf16[8,144,128]{2,1,0:T(8,128)(2,1)S(1)} %copy.616), channel_id=1, replica_groups=mesh['zh'=2,'zl'=2,'y'=2,'x'=2,'core'=2] {'zl','y','core'}, dimensions={0} | all-to-all | bytes 589824 | tf_op jit(solution)/shard_map/all_to_all | solution.py:201
  35.7 3.5 all-to-all-start
  42.3 9.9 %all-to-all-done = bf16[8,2,1,32,512]{4,3,1,2,0:T(8,128)(2,1)S(1)} async-done(((bf16[8,2,1,32,512]{4,3,1,2,0:T(8,128)(2,1)}), bf16[8,2,1,32,512]{4,3,1,2,0:T(8,128)(2,1)S(1)}, u32[]{:S(2)}, u32[]{:S(2)}) %all-to-all-start) | async-done | bytes 524320 | tf_op jit(solution)/shard_map/all_to_all | solution.py:121
  52.2 3.5 all-to-all-start.2
  59.8 5.5 collective-permute-start
  66.1 18.1 %all-to-all-done.2 = bf16[8,36,1024]{2,1,0:T(8,128)(2,1)S(1)} async-done(((bf16[8,36,1024]{2,1,0:T(8,128)(2,1)}), bf16[8,36,1024]{2,1,0:T(8,128)(2,1)S(1)}, u32[]{:S(2)}, u32[]{:S(2)}) %all-to-all-start.2) | async-done | bytes 589856 | tf_op jit(solution)/shard_map/all_to_all | solution.py:207
  84.7 23.6 %collective-permute-done.1 = bf16[2,2,64,512]{3,2,0,1:T(8,128)(2,1)S(1)} collective-permute-done((bf16[2,2,64,512]{3,2,0,1:T(8,128)(2,1)S(1)}, bf16[2,2,64,512]{3,2,0,1:T(8,128)(2,1)S(1)}, u32[]{:S(2)}, u32[]{:S(2)}) %collective-permute-start.1) | collective-permute-done | bytes 262176 | tf_op jit(solution)/shard_map/ppermute | solution.py:33
  109.7 4.7 collective-permute-start.2
  123.3 9.5 %collective-permute-done.6 = bf16[2,1,8,144,128]{4,3,2,1,0:T(8,128)(2,1)S(1)} collective-permute-done((bf16[2,1,8,144,128]{4,3,2,1,0:T(8,128)(2,1)S(1)}, bf16[2,1,8,144,128]{4,3,2,1,0:T(8,128)(2,1)S(1)}, u32[]{:S(2)}, u32[]{:S(2)}) %collective-permute-start.6) | collective-permute-done | bytes 589856 | tf_op jit(solution)/shard_map/ppermute | solution.py:39
  133.7 3.3 fusion.133
  138.6 25.4 %collective-permute-done.8 = bf16[2,1,8,36,1024]{4,2,3,1,0:T(8,128)(2,1)S(1)} collective-permute-done((bf16[2,1,8,36,1024]{4,2,3,1,0:T(8,128)(2,1)S(1)}, bf16[2,1,8,36,1024]{4,2,3,1,0:T(8,128)(2,1)S(1)}, u32[]{:S(2)}, u32[]{:S(2)}) %collective-permute-start.8) | collective-permute-done | bytes 1179680 | tf_op jit(solution)/shard_map/ppermute | solution.py:39
  171.3 3.4 select_convert_fusion
  177.2 3.7 all-to-all-start.3
  183.1 22.2 %all-to-all-done.3 = bf16[8,2,32,1024]{3,2,1,0:T(8,128)(2,1)S(1)} async-done(((bf16[8,2,32,1024]{3,2,1,0:T(8,128)(2,1)}), bf16[8,2,32,1024]{3,2,1,0:T(8,128)(2,1)S(1)}, u32[]{:S(2)}, u32[]{:S(2)}) %all-to-all-start.3) | async-done | bytes 1048608 | tf_op jit(solution)/shard_map/all_to_all | solution.py:129
  211.3 4.6 collective-permute-start.10
  219.4 5.3 collective-permute-start.16
  227.2 5.4 collective-permute-start.12
  235.1 7.1 %collective-permute-start.24 = (f32[]{:T(128)}, f32[]{:T(128)}, u32[]{:S(2)}, u32[]{:S(2)}) collective-permute-start(f32[]{:T(128)} %add.398), channel_id=1, source_target_pairs={{0,2},{2,0},{1,3},{3,1},{4,6},{6,4},{5,7},{7,5},{8,10},{10,8},{9,1... | collective-permute-start | bytes 20 | tf_op jit(solution)/shard_map/ppermute | solution.py:39
  268.5 5.1 collective-permute-start.18
  284.0 9.2 %fusion.247 = bf16[4,2,130,1024]{2,3,1,0:T(8,128)(2,1)} fusion(bf16[2,4,1,512]{2,3,0,1:T(8,128)(2,1)S(1)} %copy-done.3, bf16[2,1,128,512]{2,3,0,1:T(8,128)(2,1)S(1)} %collective-permute-done.17, bf16[2,2,64,512]{2,3,0,1:T(8,128)(2,1)S(1)} %get-tuple-element.238, bf16[2,2,64,512]{2,3,0,1:T(8,128)(2,1)S(1)} %get-tuple-element.237, ...), kind=kLoop, calls=%fused_computation.401 | loop fusion | flops 17039360 | bytes 4259840 | tf_op jit(solution)/shard_map/concatenate | solution.py:265
  293.2 8.9 %copy.762 = bf16[4,2,130,1024]{3,1,2,0:T(2,128)(2,1)} copy(bf16[4,2,130,1024]{2,3,1,0:T(8,128)(2,1)} %fusion.247) | data formatting | bytes 4259840
  302.1 3.3 pad.12.clone
  305.5 6.0 fusion.3
  311.6 6.0 multiply_convert_fusion
  324.7 4.6 collective-permute-start.28
  335.7 5.1 collective-permute-start.30
  356.8 4.3 copy.693
  366.4 8.3 %maximum_maximum_fusion = bf16[2,4,130,1024]{2,3,0,1:T(8,128)(2,1)S(1)} fusion(bf16[2,4,1,512]{2,3,0,1:T(8,128)(2,1)S(1)} %copy-done.4, bf16[2,1,128,512]{2,3,0,1:T(8,128)(2,1)S(1)} %copy-done.20, bf16[2,2,64,512]{2,3,0,1:T(8,128)(2,1)S(1)} %get-tuple-element.238, bf16[2,2,64,512]{2,3,0,1:T(8,128)(2,1)S(1)} %get-tuple-element.237, ...), kind=kLoop, calls=%fused_computation.4 | loop fusion | flops 17039360 | bytes 4259840 | tf_op jit(solution)/shard_map/concatenate | solution.py:265
  381.8 4.0 all-to-all-start.4
  398.3 7.9 %all-to-all-done.4 = bf16[8,2,1,32,1024]{4,3,1,2,0:T(8,128)(2,1)S(1)} async-done(((bf16[8,2,1,32,1024]{4,3,1,2,0:T(8,128)(2,1)}), bf16[8,2,1,32,1024]{4,3,1,2,0:T(8,128)(2,1)S(1)}, u32[]{:S(2)}, u32[]{:S(2)}) %all-to-all-start.4) | async-done | bytes 1048608 | tf_op jit(solution)/shard_map/all_to_all | solution.py:121
  409.6 4.3 fusion.51
  414.2 5.3 collective-permute-start.34
  431.5 5.2 reshape.534
  436.7 3.4 collective-permute-start.36
  447.8 22.7 %collective-permute-done.37 = f32[2,4,1,128]{3,2,1,0:T(1,128)S(1)} collective-permute-done((f32[2,4,1,128]{3,2,1,0:T(1,128)S(1)}, f32[2,4,1,128]{3,2,1,0:T(1,128)S(1)}, u32[]{:S(2)}, u32[]{:S(2)}) %collective-permute-start.37) | collective-permute-done | bytes 4128 | tf_op jit(solution)/shard_map/ppermute | solution.py:33
  481.5 9.2 %collective-permute-done.38 = bf16[1,2,2,2,2,144,128]{6,5,4,3,2,1,0:T(8,128)(2,1)S(1)} collective-permute-done((bf16[1,2,2,2,2,144,128]{6,5,4,3,2,1,0:T(8,128)(2,1)S(1)}, bf16[1,2,2,2,2,144,128]{6,5,4,3,2,1,0:T(8,128)(2,1)S(1)}, u32[]{:S(2)}, u32[]{:S(2)}) %collective-permute-start.38) | collective-permute-done | bytes 589856 | tf_op jit(solution)/shard_map/ppermute | solution.py:39
  491.6 4.2 collective-permute-start.39
  495.7 3.7 bitcast_add_fusion
  500.7 25.0 %collective-permute-done.39 = bf16[1,2,2,2,144,128]{5,4,3,2,1,0:T(8,128)(2,1)} collective-permute-done((bf16[1,2,2,2,144,128]{5,4,3,2,1,0:T(8,128)(2,1)}, bf16[1,2,2,2,144,128]{5,4,3,2,1,0:T(8,128)(2,1)}, u32[]{:S(2)}, u32[]{:S(2)}) %collective-permute-start.39) | collective-permute-done | bytes 294944 | tf_op jit(solution)/shard_map/ppermute | solution.py:39
  527.4 5.4 all-to-all-start.5
  537.9 4.0 all-to-all-done.5
  542.0 3.5 all-to-all-start.6
  549.7 58.3 %reduce-scatter.5.cloned.1.call-done = bf16[576,256]{1,0:T(8,128)(2,1)} async-done(((bf16[9216,256]{1,0:T(8,128)(2,1)}), bf16[576,256]{1,0:T(8,128)(2,1)}) %reduce-scatter.5.cloned.1.call-update) | async-done | bytes 294928 | tf_op jit(solution)/shard_map/reduce_scatter | solution.py:310
  637.9 5.2 copy.703
  643.1 7.0 %mul.611 = f32[147456]{0:T(1024)S(1)} reshape(f32[144,128,8]{2,1,0:T(8,128)} %copy.703) | data formatting | bytes 1179648 | tf_op jit(solution)/shard_map/mul | solution.py:376
  657.1 4.1 multiply_subtract_fusion
  (486 shorter events, 220.9 us)
Async XLA Ops:
  7.2 199.9 %all-gather.3.cloned.1.call-start = ((), (), s32[]{:S(2)}) async-start(), calls=%async_computation.9 | async-start | bytes 2228224 | tf_op jit(solution)/shard_map/all_gather | solution.py:218
  35.7 16.5 %all-to-all-start = ((bf16[8,2,1,32,512]{4,3,1,2,0:T(8,128)(2,1)}), bf16[8,2,1,32,512]{4,3,1,2,0:T(8,128)(2,1)S(1)}, u32[]{:S(2)}, u32[]{:S(2)}) async-start(bf16[8,2,1,32,512]{4,3,1,2,0:T(8,128)(2,1)} %broadcast_in_dim.87), calls=%async_computation | async-start | bytes 1048576 | tf_op jit(solution)/shard_map/all_to_all | solution.py:121
  40.1 15.8 %collective-permute-start.20 = (bf16[1,288,256]{2,1,0:T(8,128)(2,1)S(1)}, bf16[1,288,256]{2,1,0:T(8,128)(2,1)S(1)}, u32[]{:S(2)}, u32[]{:S(2)}) collective-permute-start(bf16[1,288,256]{2,1,0:T(8,128)(2,1)S(1)} %bitcast.577), channel_id=1, source_target_pairs={{0,1},{1,0},{2,3},{3,2},{4,5},{5,4},{6,7},{7,6},{8,9},{9,8},{10,11... | collective-permute-start | bytes 442376 | tf_op jit(solution)/shard_map/ppermute | solution.py:39
  52.2 32.0 %all-to-all-start.2 = ((bf16[8,36,1024]{2,1,0:T(8,128)(2,1)}), bf16[8,36,1024]{2,1,0:T(8,128)(2,1)S(1)}, u32[]{:S(2)}, u32[]{:S(2)}) async-start(bf16[8,36,1024]{2,1,0:T(8,128)(2,1)} %copy.622), calls=%async_computation.2 | async-start | bytes 1310720 | tf_op jit(solution)/shard_map/all_to_all | solution.py:207
  55.7 255.9 %all-gather.5.cloned.1.call-start = ((), (), s32[]{:S(2)}) async-start(), calls=%async_computation.10 | async-start | bytes 5013504 | tf_op jit(solution)/shard_map/all_gather | solution.py:218
  55.9 28.7 %collective-permute-start.5 = (bf16[1,8,144,128]{3,2,1,0:T(8,128)(2,1)S(1)}, bf16[1,8,144,128]{3,2,1,0:T(8,128)(2,1)S(1)}, u32[]{:S(2)}, u32[]{:S(2)}) collective-permute-start(bf16[1,8,144,128]{3,2,1,0:T(8,128)(2,1)S(1)} %bitcast.560), channel_id=1, source_target_pairs={{0,16},{16,0},{1,17},{17,1},{2,18},{18,2},{3,19},{19,3},{4,20},{20... | collective-permute-start | bytes 884744 | tf_op jit(solution)/shard_map/ppermute | solution.py:39
  58.5 49.8 %collective-permute-start.1 = (bf16[2,2,64,512]{3,2,0,1:T(8,128)(2,1)S(1)}, bf16[2,2,64,512]{3,2,0,1:T(8,128)(2,1)S(1)}, u32[]{:S(2)}, u32[]{:S(2)}) collective-permute-start(bf16[2,2,64,512]{3,2,0,1:T(8,128)(2,1)S(1)} %get-tuple-element.252), channel_id=1, source_target_pairs={{16,0},{17,1},{18,2},{19,3},{20,4},{21,5},{22,6},{23,7},{24,8},{25... | collective-permute-start | bytes 786440 | tf_op jit(solution)/shard_map/ppermute | solution.py:33
  59.8 48.5 %collective-permute-start = (bf16[2,2,64,512]{3,2,0,1:T(8,128)(2,1)S(1)}, bf16[2,2,64,512]{3,2,0,1:T(8,128)(2,1)S(1)}, u32[]{:S(2)}, u32[]{:S(2)}) collective-permute-start(bf16[2,2,64,512]{3,2,0,1:T(8,128)(2,1)S(1)} %get-tuple-element.251), channel_id=1, source_target_pairs={{0,16},{1,17},{2,18},{3,19},{4,20},{5,21},{6,22},{7,23},{8,24},{9,... | collective-permute-start | bytes 786440 | tf_op jit(solution)/shard_map/ppermute | solution.py:33
  84.5 35.9 %collective-permute-start.7 = (bf16[1,8,36,1024]{3,1,2,0:T(8,128)(2,1)S(1)}, bf16[1,8,36,1024]{3,1,2,0:T(8,128)(2,1)S(1)}, u32[]{:S(2)}, u32[]{:S(2)}) collective-permute-start(bf16[1,8,36,1024]{3,1,2,0:T(8,128)(2,1)S(1)} %copy.623), channel_id=1, source_target_pairs={{0,16},{16,0},{1,17},{17,1},{2,18},{18,2},{3,19},{19,3},{4,20},{20... | collective-permute-start | bytes 1769480 | tf_op jit(solution)/shard_map/ppermute | solution.py:39
  108.4 6.2 collective-permute-start.4
  109.7 6.4 collective-permute-start.2
  114.4 18.4 %collective-permute-start.6 = (bf16[2,1,8,144,128]{4,3,2,1,0:T(8,128)(2,1)S(1)}, bf16[2,1,8,144,128]{4,3,2,1,0:T(8,128)(2,1)S(1)}, u32[]{:S(2)}, u32[]{:S(2)}) collective-permute-start(bf16[2,1,8,144,128]{4,3,2,1,0:T(8,128)(2,1)S(1)} %maximum_bitcast_fusion.2), channel_id=1, source_target_pairs={{0,2},{2,0},{1,3},{3,1},{4,6},{6,4},{5,7},{7,5},{8,10},{10,8},{9,1... | collective-permute-start | bytes 1769480 | tf_op jit(solution)/shard_map/ppermute | solution.py:39
  121.9 42.1 %collective-permute-start.8 = (bf16[2,1,8,36,1024]{4,2,3,1,0:T(8,128)(2,1)S(1)}, bf16[2,1,8,36,1024]{4,2,3,1,0:T(8,128)(2,1)S(1)}, u32[]{:S(2)}, u32[]{:S(2)}) collective-permute-start(bf16[2,1,8,36,1024]{4,2,3,1,0:T(8,128)(2,1)S(1)} %copy.626), channel_id=1, source_target_pairs={{0,2},{2,0},{1,3},{3,1},{4,6},{6,4},{5,7},{7,5},{8,10},{10,8},{9,1... | collective-permute-start | bytes 3538952 | tf_op jit(solution)/shard_map/ppermute | solution.py:39
  177.2 28.0 %all-to-all-start.3 = ((bf16[8,2,32,1024]{3,2,1,0:T(8,128)(2,1)}), bf16[8,2,32,1024]{3,2,1,0:T(8,128)(2,1)S(1)}, u32[]{:S(2)}, u32[]{:S(2)}) async-start(bf16[8,2,32,1024]{3,2,1,0:T(8,128)(2,1)} %bitcast.29), calls=%async_computation.3 | async-start | bytes 2097152 | tf_op jit(solution)/shard_map/all_to_all | solution.py:129
  180.9 365.1 %reduce-scatter.3.cloned.1.call-start = ((), (), s32[]{:S(2)}) async-start(), calls=%async_computation.11 | async-start | bytes 2228224 | tf_op jit(solution)/shard_map/reduce_scatter | solution.py:310
  181.3 34.6 %collective-permute-start.15 = (bf16[2,2,64,512]{2,3,0,1:T(8,128)(2,1)S(1)}, bf16[2,2,64,512]{2,3,0,1:T(8,128)(2,1)}, u32[]{:S(2)}, u32[]{:S(2)}) collective-permute-start(bf16[2,2,64,512]{2,3,0,1:T(8,128)(2,1)S(1)} %copy.639), channel_id=1, source_target_pairs={{0,1},{1,0},{2,3},{3,2},{4,5},{5,4},{6,7},{7,6},{8,9},{9,8},{10,11... | collective-permute-start | bytes 786440 | tf_op jit(solution)/shard_map/ppermute | solution.py:39
  182.3 51.5 %collective-permute-start.23 = (f32[]{:T(128)}, f32[]{:T(128)}, u32[]{:S(2)}, u32[]{:S(2)}) collective-permute-start(f32[]{:T(128)} %convert_reduce_fusion.6), channel_id=1, source_target_pairs={{0,1},{1,0},{2,3},{3,2},{4,5},{5,4},{6,7},{7,6},{8,9},{9,8},{10,11... | collective-permute-start | bytes 20 | tf_op jit(solution)/shard_map/ppermute | solution.py:39
  210.0 14.7 %collective-permute-start.11 = (bf16[2,1,128,256]{2,3,0,1:T(8,128)(2,1)S(1)}, bf16[2,1,128,256]{2,3,0,1:T(8,128)(2,1)S(1)}, u32[]{:S(2)}, u32[]{:S(2)}) collective-permute-start(bf16[2,1,128,256]{2,3,0,1:T(8,128)(2,1)S(1)} %get-tuple-element.267), channel_id=1, source_target_pairs={{4,0},{8,4},{12,8},{16,12},{20,16},{24,20},{28,24},{5,1},{9,5},{13... | collective-permute-start | bytes 393224 | tf_op jit(solution)/shard_map/ppermute | solution.py:33
  211.3 13.4 %collective-permute-start.10 = (bf16[2,1,128,256]{2,3,0,1:T(8,128)(2,1)S(1)}, bf16[2,1,128,256]{2,3,0,1:T(8,128)(2,1)S(1)}, u32[]{:S(2)}, u32[]{:S(2)}) collective-permute-start(bf16[2,1,128,256]{2,3,0,1:T(8,128)(2,1)S(1)} %get-tuple-element.266), channel_id=1, source_target_pairs={{0,4},{4,8},{8,12},{12,16},{16,20},{20,24},{24,28},{1,5},{5,9},{9,... | collective-permute-start | bytes 393224 | tf_op jit(solution)/shard_map/ppermute | solution.py:33
  218.1 43.2 %collective-permute-start.17 = (bf16[2,1,128,512]{2,3,0,1:T(8,128)(2,1)}, bf16[2,1,128,512]{2,3,0,1:T(8,128)(2,1)S(1)}, u32[]{:S(2)}, u32[]{:S(2)}) collective-permute-start(bf16[2,1,128,512]{2,3,0,1:T(8,128)(2,1)} %get-tuple-element.236), channel_id=1, source_target_pairs={{4,0},{8,4},{12,8},{16,12},{20,16},{24,20},{28,24},{5,1},{9,5},{13... | collective-permute-start | bytes 786440 | tf_op jit(solution)/shard_map/ppermute | solution.py:33
  219.4 41.9 %collective-permute-start.16 = (bf16[2,1,128,512]{2,3,0,1:T(8,128)(2,1)}, bf16[2,1,128,512]{2,3,0,1:T(8,128)(2,1)}, u32[]{:S(2)}, u32[]{:S(2)}) collective-permute-start(bf16[2,1,128,512]{2,3,0,1:T(8,128)(2,1)} %get-tuple-element.235), channel_id=1, source_target_pairs={{0,4},{4,8},{8,12},{12,16},{16,20},{20,24},{24,28},{1,5},{5,9},{9,... | collective-permute-start | bytes 786440 | tf_op jit(solution)/shard_map/ppermute | solution.py:33
  225.9 30.9 %collective-permute-start.13 = (bf16[2,4,1,256]{2,3,0,1:T(8,128)(2,1)}, bf16[2,4,1,256]{2,3,0,1:T(8,128)(2,1)S(1)}, u32[]{:S(2)}, u32[]{:S(2)}) collective-permute-start(bf16[2,4,1,256]{2,3,0,1:T(8,128)(2,1)} %get-tuple-element.250), channel_id=1, source_target_pairs={{2,0},{3,1},{6,4},{7,5},{10,8},{11,9},{14,12},{15,13},{18,16},{19,... | collective-permute-start | bytes 12296 | tf_op jit(solution)/shard_map/ppermute | solution.py:33
  227.2 30.4 %collective-permute-start.12 = (bf16[2,4,1,256]{2,3,0,1:T(8,128)(2,1)}, bf16[2,4,1,256]{2,3,0,1:T(8,128)(2,1)}, u32[]{:S(2)}, u32[]{:S(2)}) collective-permute-start(bf16[2,4,1,256]{2,3,0,1:T(8,128)(2,1)} %get-tuple-element.249), channel_id=1, source_target_pairs={{0,2},{1,3},{4,6},{5,7},{8,10},{9,11},{12,14},{13,15},{16,18},{17,... | collective-permute-start | bytes 12296 | tf_op jit(solution)/shard_map/ppermute | solution.py:33
  235.1 7.1 %collective-permute-start.24 = (f32[]{:T(128)}, f32[]{:T(128)}, u32[]{:S(2)}, u32[]{:S(2)}) collective-permute-start(f32[]{:T(128)} %add.398), channel_id=1, source_target_pairs={{0,2},{2,0},{1,3},{3,1},{4,6},{6,4},{5,7},{7,5},{8,10},{10,8},{9,1... | collective-permute-start | bytes 20 | tf_op jit(solution)/shard_map/ppermute | solution.py:39
  251.5 4.6 collective-permute-start.27
  256.1 17.5 %collective-permute-start.22 = (s32[2,2,2,64]{3,2,1,0:T(2,128)}, s32[2,2,2,64]{3,2,1,0:T(2,128)}, u32[]{:S(2)}, u32[]{:S(2)}) collective-permute-start(s32[2,2,2,64]{3,2,1,0:T(2,128)} %pad_add_fusion), channel_id=1, source_target_pairs={{0,1},{1,0},{2,3},{3,2},{4,5},{5,4},{6,7},{7,6},{8,9},{9,8},{10,11... | collective-permute-start | bytes 6152 | tf_op jit(solution)/shard_map/ppermute | solution.py:39
  260.8 17.0 %collective-permute-start.14 = (bf16[2,4,130,256]{3,1,2,0:T(4,128)(2,1)}, bf16[2,4,130,256]{3,1,2,0:T(4,128)(2,1)}, u32[]{:S(2)}, u32[]{:S(2)}) collective-permute-start(bf16[2,4,130,256]{3,1,2,0:T(4,128)(2,1)} %copy.635), channel_id=1, source_target_pairs={{0,1},{1,0},{2,3},{3,2},{4,5},{5,4},{6,7},{7,6},{8,9},{9,8},{10,11... | collective-permute-start | bytes 1597448 | tf_op jit(solution)/shard_map/ppermute | solution.py:39
  266.3 8.1 %collective-permute-start.19 = (bf16[2,4,1,512]{3,1,2,0:T(4,128)(2,1)}, bf16[2,4,1,512]{3,1,2,0:T(4,128)(2,1)}, u32[]{:S(2)}, u32[]{:S(2)}) collective-permute-start(bf16[2,4,1,512]{3,1,2,0:T(4,128)(2,1)} %copy.642), channel_id=1, source_target_pairs={{2,0},{3,1},{6,4},{7,5},{10,8},{11,9},{14,12},{15,13},{18,16},{19,... | collective-permute-start | bytes 24584 | tf_op jit(solution)/shard_map/ppermute | solution.py:33
  268.5 7.9 %collective-permute-start.18 = (bf16[2,4,1,512]{3,1,2,0:T(4,128)(2,1)}, bf16[2,4,1,512]{3,1,2,0:T(4,128)(2,1)S(1)}, u32[]{:S(2)}, u32[]{:S(2)}) collective-permute-start(bf16[2,4,1,512]{3,1,2,0:T(4,128)(2,1)} %copy.641), channel_id=1, source_target_pairs={{0,2},{1,3},{4,6},{5,7},{8,10},{9,11},{12,14},{13,15},{16,18},{17,... | collective-permute-start | bytes 24584 | tf_op jit(solution)/shard_map/ppermute | solution.py:33
  323.4 7.8 %collective-permute-start.29 = (bf16[2,1,128,256]{3,2,1,0:T(8,128)(2,1)S(1)}, bf16[2,1,128,256]{3,2,1,0:T(8,128)(2,1)S(1)}, u32[]{:S(2)}, u32[]{:S(2)}) collective-permute-start(bf16[2,1,128,256]{3,2,1,0:T(8,128)(2,1)S(1)} %get-tuple-element.265), channel_id=1, source_target_pairs={{4,0},{8,4},{12,8},{16,12},{20,16},{24,20},{28,24},{5,1},{9,5},{13... | collective-permute-start | bytes 393224 | tf_op jit(solution)/shard_map/ppermute | solution.py:33
  324.7 9.2 %collective-permute-start.28 = (bf16[2,1,128,256]{3,2,1,0:T(8,128)(2,1)S(1)}, bf16[2,1,128,256]{3,2,1,0:T(8,128)(2,1)S(1)}, u32[]{:S(2)}, u32[]{:S(2)}) collective-permute-start(bf16[2,1,128,256]{3,2,1,0:T(8,128)(2,1)S(1)} %get-tuple-element.264), channel_id=1, source_target_pairs={{0,4},{4,8},{8,12},{12,16},{16,20},{20,24},{24,28},{1,5},{5,9},{9,... | collective-permute-start | bytes 393224 | tf_op jit(solution)/shard_map/ppermute | solution.py:33
  334.5 6.4 collective-permute-start.31
  335.7 6.1 collective-permute-start.30
  381.8 24.3 %all-to-all-start.4 = ((bf16[8,2,1,32,1024]{4,3,1,2,0:T(8,128)(2,1)}), bf16[8,2,1,32,1024]{4,3,1,2,0:T(8,128)(2,1)S(1)}, u32[]{:S(2)}, u32[]{:S(2)}) async-start(bf16[8,2,1,32,1024]{4,3,1,2,0:T(8,128)(2,1)} %broadcast_in_dim.95), calls=%async_computation.4 | async-start | bytes 2097152 | tf_op jit(solution)/shard_map/all_to_all | solution.py:121
  385.9 222.1 %reduce-scatter.5.cloned.1.call-start = ((), (), s32[]{:S(2)}) async-start(), calls=%async_computation.12 | async-start | bytes 5013504 | tf_op jit(solution)/shard_map/reduce_scatter | solution.py:310
  414.2 22.4 %collective-permute-start.34 = (f32[2,1,66,128]{3,2,1,0:T(8,128)S(1)}, f32[2,1,66,128]{3,2,1,0:T(8,128)S(1)}, u32[]{:S(2)}, u32[]{:S(2)}) collective-permute-start(f32[2,1,66,128]{3,2,1,0:T(8,128)S(1)} %slice_bitcast_fusion.1), channel_id=1, source_target_pairs={{0,16},{1,17},{2,18},{3,19},{4,20},{5,21},{6,22},{7,23},{8,24},{9,... | collective-permute-start | bytes 202760 | tf_op jit(solution)/shard_map/ppermute | solution.py:33
  419.7 17.0 %collective-permute-start.35 = (f32[2,1,66,128]{3,2,1,0:T(8,128)S(1)}, f32[2,1,66,128]{3,2,1,0:T(8,128)S(1)}, u32[]{:S(2)}, u32[]{:S(2)}) collective-permute-start(f32[2,1,66,128]{3,2,1,0:T(8,128)S(1)} %slice_bitcast_fusion), channel_id=1, source_target_pairs={{16,0},{17,1},{18,2},{19,3},{20,4},{21,5},{22,6},{23,7},{24,8},{25... | collective-permute-start | bytes 202760 | tf_op jit(solution)/shard_map/ppermute | solution.py:33
  436.7 9.6 %collective-permute-start.36 = (f32[2,4,1,128]{3,2,1,0:T(1,128)S(1)}, f32[2,4,1,128]{3,2,1,0:T(1,128)S(1)}, u32[]{:S(2)}, u32[]{:S(2)}) collective-permute-start(f32[2,4,1,128]{3,2,1,0:T(1,128)S(1)} %get-tuple-element.261), channel_id=1, source_target_pairs={{0,2},{1,3},{4,6},{5,7},{8,10},{9,11},{12,14},{13,15},{16,18},{17,... | collective-permute-start | bytes 12296 | tf_op jit(solution)/shard_map/ppermute | solution.py:33
  444.3 51.4 %collective-permute-start.40 = (bf16[1,2,2,2,2,36,1024]{6,4,5,3,2,1,0:T(2,128)(2,1)}, bf16[1,2,2,2,2,36,1024]{6,4,5,3,2,1,0:T(2,128)(2,1)}, u32[]{:S(2)}, u32[]{:S(2)}) collective-permute-start(bf16[1,2,2,2,2,36,1024]{6,4,5,3,2,1,0:T(2,128)(2,1)} %copy.689), channel_id=1, source_target_pairs={{0,2},{2,0},{1,3},{3,1},{4,6},{6,4},{5,7},{7,5},{8,10},{10,8},{9,1... | collective-permute-start | bytes 3538952 | tf_op jit(solution)/shard_map/ppermute | solution.py:39
  445.1 25.4 %collective-permute-start.37 = (f32[2,4,1,128]{3,2,1,0:T(1,128)S(1)}, f32[2,4,1,128]{3,2,1,0:T(1,128)S(1)}, u32[]{:S(2)}, u32[]{:S(2)}) collective-permute-start(f32[2,4,1,128]{3,2,1,0:T(1,128)S(1)} %get-tuple-element.260), channel_id=1, source_target_pairs={{2,0},{3,1},{6,4},{7,5},{10,8},{11,9},{14,12},{15,13},{18,16},{19,... | collective-permute-start | bytes 12296 | tf_op jit(solution)/shard_map/ppermute | solution.py:33
  479.2 11.5 %collective-permute-start.38 = (bf16[1,2,2,2,2,144,128]{6,5,4,3,2,1,0:T(8,128)(2,1)S(1)}, bf16[1,2,2,2,2,144,128]{6,5,4,3,2,1,0:T(8,128)(2,1)S(1)}, u32[]{:S(2)}, u32[]{:S(2)}) collective-permute-start(bf16[1,2,2,2,2,144,128]{6,5,4,3,2,1,0:T(8,128)(2,1)S(1)} %fusion.106), channel_id=1, source_target_pairs={{0,2},{2,0},{1,3},{3,1},{4,6},{6,4},{5,7},{7,5},{8,10},{10,8},{9,1... | collective-permute-start | bytes 1769480 | tf_op jit(solution)/shard_map/ppermute | solution.py:39
  491.6 34.1 %collective-permute-start.39 = (bf16[1,2,2,2,144,128]{5,4,3,2,1,0:T(8,128)(2,1)}, bf16[1,2,2,2,144,128]{5,4,3,2,1,0:T(8,128)(2,1)}, u32[]{:S(2)}, u32[]{:S(2)}) collective-permute-start(bf16[1,2,2,2,144,128]{5,4,3,2,1,0:T(8,128)(2,1)} %fusion.135), channel_id=1, source_target_pairs={{0,16},{16,0},{1,17},{17,1},{2,18},{18,2},{3,19},{19,3},{4,20},{20... | collective-permute-start | bytes 884744 | tf_op jit(solution)/shard_map/ppermute | solution.py:39
  500.7 34.6 %collective-permute-start.41 = (bf16[1,2,2,2,36,1024]{5,3,4,2,1,0:T(2,128)(2,1)}, bf16[1,2,2,2,36,1024]{5,3,4,2,1,0:T(2,128)(2,1)}, u32[]{:S(2)}, u32[]{:S(2)}) collective-permute-start(bf16[1,2,2,2,36,1024]{5,3,4,2,1,0:T(2,128)(2,1)} %fusion.105), channel_id=1, source_target_pairs={{0,16},{16,0},{1,17},{17,1},{2,18},{18,2},{3,19},{19,3},{4,20},{20... | collective-permute-start | bytes 1769480 | tf_op jit(solution)/shard_map/ppermute | solution.py:39
  527.4 14.6 %all-to-all-start.5 = ((bf16[8,144,128]{2,1,0:T(8,128)(2,1)}), bf16[8,144,128]{2,1,0:T(8,128)(2,1)S(1)}, u32[]{:S(2)}, u32[]{:S(2)}) async-start(bf16[8,144,128]{2,1,0:T(8,128)(2,1)} %bitcast.561), calls=%async_computation.5 | async-start | bytes 589824 | tf_op jit(solution)/shard_map/all_to_all | solution.py:328
  542.0 67.1 %all-to-all-start.6 = ((bf16[8,36,1024]{2,1,0:T(8,128)(2,1)}), bf16[8,36,1024]{2,1,0:T(8,128)(2,1)S(1)}, u32[]{:S(2)}, u32[]{:S(2)}) async-start(bf16[8,36,1024]{2,1,0:T(8,128)(2,1)} %bitcast.138), calls=%async_computation.6 | async-start | bytes 1310720 | tf_op jit(solution)/shard_map/all_to_all | solution.py:319
  619.5 3.8 collective-permute-start.46
  623.3 3.8 collective-permute-start.47
  627.1 4.7 collective-permute-start.48
  (92 other events, 774.0 us)
Sparse Core Ops, SparseCore 0:
  11.4 95.4 all-gather.2
  110.3 96.9 all-gather.4
  361.3 85.2 reduce-scatter.2
  451.7 156.3 reduce-scatter.4

commit v2 on v1

--- a/solution.py
+++ b/solution.py
@@ -1,6 +1,8 @@
 import jax
 import jax.numpy as jnp
 from jax import lax
+from jax.experimental import pallas as pl
+from jax.experimental.pallas import tpu as pltpu
 from jax.sharding import Mesh
 from jax.sharding import PartitionSpec as P
 
@@ -69,12 +71,13 @@
     return pair_half(values, axis, dim, me).astype(f32) + swapped(away, axis).astype(f32)
 
 
-def total(values):
-    for axis in ("core", "x", "y", "zl"):
-        values = values + swapped(values, axis)
-    if size_of("zh") == 2:
-        return values + swapped(values, "zh")
-    return lax.psum(values, "zh")
+def total(values, axes=("core", "x", "y", "zl", "zh")):
+    for axis in axes:
+        if size_of(axis) == 2:
+            values = values + swapped(values, axis)
+        else:
+            values = lax.psum(values, axis)
+    return values
 
 
 def convolve(values, kernel, pad=0):
@@ -112,7 +115,7 @@
 
 
 def column_sum(values):
-    return jnp.sum(values, axis=(0, 1, 2), dtype=f32)
+    return jnp.sum(values, axis=tuple(range(values.ndim - 1)), dtype=f32)
 
 
 def group_gather(block):
@@ -130,16 +133,16 @@
     return jnp.sum(got.astype(f32), axis=0)[:, None]
 
 
-def far_gather(part):
-    got = (
-        pair_gather(part[None], "zh", 0)
-        if size_of("zh") == 2
-        else lax.all_gather(part, "zh", axis=0)
-    )
-    got = pair_gather(got[:, None], "x", 1)
-    zh, _, _, r, o = got.shape
-    got = got.reshape(zh, 2, 2, 2, 2, r, o).transpose(0, 2, 3, 1, 4, 5, 6)
-    return got.reshape(zh * 16 * r, o)
+def over_zh(part):
+    if size_of("zh") == 2:
+        return pair_gather(part[None], "zh", 0)
+    return lax.all_gather(part, "zh", axis=0)
+
+
+def over_x(part):
+    part = pair_gather(part[:, None], "x", 1)
+    zh, _, _, r, o = part.shape
+    return part.reshape(zh, 2, 2, 2, 2, r, o).transpose(0, 2, 3, 1, 4, 5, 6)
 
 
 def far_scatter(grad, kind=bf16):
@@ -153,6 +156,361 @@
     else:
         split = lax.psum_scatter(split, "zh", scatter_dimension=0)
     return split.reshape(8, r, o)
+
+
+VMEM_LIMIT = 60 * 1024 * 1024
+HALF = C0 // 2
+
+
+def joined_on(values, axis):
+    return jnp.concatenate([values, swapped(values, axis)], axis=0)
+
+
+def kept_on(own, away, axis):
+    got = swapped(away, axis)
+    half = own.shape[0] // 2
+    sums = [
+        v.astype(f32) + w.astype(f32)
+        for v, w in ((own[:half], got[:half]), (own[half:], got[half:]))
+    ]
+    return sums[0].astype(bf16), sums[1].astype(bf16)
+
+
+def place(chunk, me, first):
+    bits = [me[i] if not (chunk >> (4 - i)) & 1 else 1 - me[i] for i in range(5)]
+    zh, zl, y, x, core = bits
+    high, low = (zl, y) if first == "y" else (y, zl)
+    return high * 16 + low * 8 + x * 4 + zh * 2 + core
+
+
+def pieces_of(rows, cut, zhs):
+    if zhs != 2:
+        return [(0, None, 0, rows, 0)]
+    return cut
+
+
+def chunk_list(r3, ru, zhs):
+    cut = (r3 + ru) // 2
+    merge, up = [], []
+    for chunk in range(32):
+        merge.append((0, (chunk, "y"), 0, cut, r3 * chunk))
+        merge.append((1, (chunk, "zl"), 0, r3 - cut, r3 * chunk + cut))
+        up.append((0, (chunk, "zl"), r3 - cut, ru, ru * chunk))
+    return pieces_of(32 * r3, merge, zhs), pieces_of(32 * ru, up, zhs)
+
+
+def copies(pieces, me, sources, target, sems):
+    made = []
+    for i, (which, spot, start, count, to) in enumerate(pieces):
+        at = 0 if spot is None else place(spot[0], me, spot[1])
+        there = sources[which].at[at, pl.ds(start, count), :]
+        here = target.at[pl.ds(to, count), :]
+        made.append(pltpu.make_async_copy(there, here, sems.at[i]))
+    return made
+
+
+def send_out(pieces, me, targets, source, sems):
+    made = []
+    for i, (which, spot, _, count, to) in enumerate(pieces):
+        at = 0 if spot is None else place(spot[0], me, spot[1])
+        here = source.at[pl.ds(to, count), :]
+        if spot is None:
+            pltpu.make_async_copy(here, targets[which].at[0], sems.at[i]).start()
+        else:
+            for side in range(2):
+                inside = at - 16 * side
+
+                @pl.when((inside >= 0) & (inside < 16))
+                def _(here=here, there=targets[which + side], inside=inside, i=i):
+                    pltpu.make_async_copy(here, there.at[inside], sems.at[i]).start()
+
+        made.append(pltpu.make_async_copy(here, targets[which].at[0], sems.at[i]))
+    for copy in made:
+        copy.wait()
+
+
+def on_chip(body, ins, outs, scratch, spaces, flops):
+    kinds = {"v": pltpu.VMEM, "s": pltpu.SMEM, "a": pl.ANY}
+    moved = sum(v.size * v.dtype.itemsize for v in list(ins) + list(outs))
+    return pl.pallas_call(
+        body,
+        out_shape=outs,
+        in_specs=[pl.BlockSpec(memory_space=kinds[k]) for k in spaces[0]],
+        out_specs=[pl.BlockSpec(memory_space=kinds[k]) for k in spaces[1]],
+        scratch_shapes=scratch,
+        compiler_params=pltpu.CompilerParams(vmem_limit_bytes=VMEM_LIMIT),
+        cost_estimate=pl.CostEstimate(flops=flops, bytes_accessed=moved, transcendentals=0),
+    )(*ins)
+
+
+def up_on_chip(me, own, other, source, bias, pieces):
+    def body(me_ref, own_ref, other_ref, source_ref, bias_ref, ups_ref, kernel_ref, act_ref, sems):
+        made = copies(pieces, me_ref, (source_ref,), kernel_ref, sems)
+        for copy in made:
+            copy.start()
+        core = me_ref[4]
+        mine = pl.ds(pl.multiple_of(core * 32, 32), 32)
+        yours = pl.ds(pl.multiple_of((1 - core) * 32, 32), 32)
+        for image in range(2):
+            act_ref[image, mine, :] = own_ref[image]
+            act_ref[image, yours, :] = other_ref[image]
+        for copy in made:
+            copy.wait()
+        values = act_ref[...].reshape(128, C1)
+        for tap in range(4):
+            got = jnp.dot(
+                values, kernel_ref[tap * C1 : (tap + 1) * C1, :], preferred_element_type=f32
+            )
+            got = (got + bias_ref[...]).astype(bf16).reshape(2, 64, HALF)
+            for image in range(2):
+                ups_ref[image, tap // 2, tap % 2] = got[image]
+
+    return on_chip(
+        body,
+        (me, own, other, source, bias),
+        (
+            jax.ShapeDtypeStruct((2, 2, 2, 64, HALF), bf16),
+            jax.ShapeDtypeStruct((4 * C1, HALF), bf16),
+            jax.ShapeDtypeStruct((2, 64, C1), bf16),
+        ),
+        [pltpu.SemaphoreType.DMA((len(pieces),))],
+        ("svvav", "vvv"),
+        2 * 128 * C1 * 4 * HALF,
+    )
+
+
+def planes_in(target, lanes, rows_ref, sides_ref):
+    line = lax.broadcasted_iota(jnp.int32, (64, 1), 0)
+    for image in range(2):
+        for row in range(4):
+            even = rows_ref[image, row, 0]
+            odd = rows_ref[image, row, 1]
+            target[image, row, 1, :, lanes] = even
+            target[image, row, 2, :, lanes] = odd
+            left = sides_ref[0, image, row : row + 1, :].astype(f32)
+            right = sides_ref[1, image, row : row + 1, :].astype(f32)
+            moved = pltpu.roll(odd.astype(f32), 1, 0)
+            target[image, row, 0, :, lanes] = jnp.where(line == 0, left, moved).astype(bf16)
+            moved = pltpu.roll(even.astype(f32), 63, 0)
+            target[image, row, 3, :, lanes] = jnp.where(line == 63, right, moved).astype(bf16)
+
+
+def tapped(planes, image, tap, lanes):
+    high, wide = tap // 3, tap % 3
+    cells = planes[image, high : high + 2, wide : wide + 2, :, lanes]
+    return cells.reshape(256, cells.shape[-1])
+
+
+def merge_on_chip(me, own, other, own_sides, other_sides, skip, sources, bias, head, pieces):
+    count = len(sources)
+
+    def body(me_ref, own_ref, other_ref, own_sides_ref, other_sides_ref, skip_ref, bias_ref, head_ref, *rest):
+        source_refs = rest[:count]
+        pre_ref, logits_ref, planes_ref, kernel, sems = rest[count:]
+        made = copies(pieces, me_ref, source_refs, kernel, sems)
+        for copy in made:
+            copy.start()
+        core = me_ref[4]
+        planes_in(planes_ref, slice(0, HALF), own_ref, own_sides_ref)
+        planes_in(planes_ref, slice(HALF, C0), other_ref, other_sides_ref)
+        planes_ref[:, :, :, :, C0:] = skip_ref[...]
+        for copy in made:
+            copy.wait()
+        for image in range(2):
+            total = jnp.broadcast_to(bias_ref[...], (256, HALF))
+            for tap in range(9):
+                base = tap * 2 * C0
+                for lanes, start, size in (
+                    (slice(0, HALF), pl.multiple_of(base + core * HALF, HALF), HALF),
+                    (slice(HALF, C0), pl.multiple_of(base + (1 - core) * HALF, HALF), HALF),
+                    (slice(C0, 2 * C0), base + C0, C0),
+                ):
+                    total = total + jnp.dot(
+                        tapped(planes_ref, image, tap, lanes),
+                        kernel[pl.ds(start, size), :],
+                        preferred_element_type=f32,
+                    )
+            rows = slice(image * 256, (image + 1) * 256)
+            pre_ref[rows, :] = total
+            act = jax.nn.gelu(total).astype(bf16)
+            logits_ref[rows, :] = jnp.dot(act, head_ref[...], preferred_element_type=f32)
+
+    return on_chip(
+        body,
+        (me, own, other, own_sides, other_sides, skip, bias, head, *sources),
+        (
+            jax.ShapeDtypeStruct((512, HALF), f32),
+            jax.ShapeDtypeStruct((512, 128), f32),
+            jax.ShapeDtypeStruct((2, 4, 4, 64, 2 * C0), bf16),
+        ),
+        [pltpu.VMEM((18 * C0, HALF), bf16), pltpu.SemaphoreType.DMA((len(pieces),))],
+        ("svvvvvvv" + "a" * count, "vvv"),
+        2 * 512 * 18 * C0 * HALF,
+    )
+
+
+def ups_grad_on_chip(me, rows, sides, sources, pieces):
+    count = len(sources)
+
+    def body(me_ref, rows_ref, sides_ref, *rest):
+        source_refs = rest[:count]
+        own_ref, away_ref, planes, kernel, sems = rest[count:]
+        made = copies(pieces, me_ref, source_refs, kernel, sems)
+        for copy in made:
+            copy.start()
+        core = me_ref[4]
+        planes_in(planes, slice(0, HALF), rows_ref, sides_ref)
+        for copy in made:
+            copy.wait()
+        for image in range(2):
+            lines = slice(image * 256, (image + 1) * 256)
+            for target, half in ((own_ref, core), (away_ref, 1 - core)):
+                total = jnp.zeros((256, HALF), f32)
+                for tap in range(9):
+                    start = pl.multiple_of((8 - tap) * 2 * C0 + half * HALF, HALF)
+                    total = total + lax.dot_general(
+                        tapped(planes, image, tap, slice(0, HALF)),
+                        kernel[pl.ds(start, HALF), :],
+                        (((1,), (1,)), ((), ())),
+                        preferred_element_type=f32,
+                    )
+                target[lines, :] = total.astype(target.dtype)
+
+    return on_chip(
+        body,
+        (me, rows, sides, *sources),
+        (jax.ShapeDtypeStruct((512, HALF), f32), jax.ShapeDtypeStruct((512, HALF), bf16)),
+        [
+            pltpu.VMEM((2, 4, 4, 64, HALF), bf16),
+            pltpu.VMEM((18 * C0, HALF), bf16),
+            pltpu.SemaphoreType.DMA((len(pieces),)),
+        ],
+        ("svv" + "a" * count, "vv"),
+        2 * 512 * 9 * C0 * HALF,
+    )
+
+
+def merge_grad_on_chip(me, planes, grad, pieces, shapes):
+    def body(me_ref, planes_ref, grad_ref, *rest):
+        out_refs = rest[: len(shapes)]
+        whole, sems = rest[len(shapes) :]
+        core = me_ref[4]
+        for tap in range(9):
+            base = tap * 2 * C0
+            for lanes, start, size in (
+                (slice(0, HALF), pl.multiple_of(base + core * HALF, HALF), HALF),
+                (slice(HALF, C0), pl.multiple_of(base + (1 - core) * HALF, HALF), HALF),
+                (slice(C0, 2 * C0), base + C0, C0),
+            ):
+                total = jnp.zeros((size, HALF), f32)
+                for image in range(2):
+                    total = total + lax.dot_general(
+                        tapped(planes_ref, image, tap, lanes),
+                        grad_ref[image * 256 : (image + 1) * 256, :],
+                        (((0,), (0,)), ((), ())),
+                        preferred_element_type=f32,
+                    )
+                whole[pl.ds(start, size), :] = total.astype(bf16)
+        send_out(pieces, me_ref, out_refs, whole, sems)
+
+    return on_chip(
+        body,
+        (me, planes, grad),
+        tuple(jax.ShapeDtypeStruct(shape, bf16) for shape in shapes),
+        [pltpu.VMEM((18 * C0, HALF), bf16), pltpu.SemaphoreType.DMA((len(pieces),))],
+        ("svv", "a" * len(shapes)),
+        2 * 512 * 18 * C0 * HALF,
+    )
+
+
+def up_grad_on_chip(me, act, grad, pieces, shapes):
+    def body(me_ref, act_ref, grad_ref, *rest):
+        out_refs = rest[: len(shapes)]
+        whole, sems = rest[len(shapes) :]
+        values = act_ref[...].reshape(128, C1)
+        for tap in range(4):
+            cells = grad_ref[:, tap // 2, tap % 2].reshape(128, HALF)
+            total = lax.dot_general(
+                values, cells, (((0,), (0,)), ((), ())), preferred_element_type=f32
+            )
+            whole[tap * C1 : (tap + 1) * C1, :] = total.astype(bf16)
+        send_out(pieces, me_ref, out_refs, whole, sems)
+
+    return on_chip(
+        body,
+        (me, act, grad),
+        tuple(jax.ShapeDtypeStruct(shape, bf16) for shape in shapes),
+        [pltpu.VMEM((4 * C1, HALF), bf16), pltpu.SemaphoreType.DMA((len(pieces),))],
+        ("svv", "a" * len(shapes)),
+        2 * 128 * C1 * 4 * HALF,
+    )
+
+
+def split_list(rows, zhs):
+    if zhs != 2:
+        return [(0, None, 0, 32 * rows, 0)], [(1, 32 * rows, HALF)]
+    half = rows // 2
+    pieces = []
+    for chunk in range(32):
+        pieces.append((0, (chunk, "y"), 0, half, rows * chunk))
+        pieces.append((2, (chunk, "zl"), 0, half, rows * chunk + half))
+    return pieces, [(16, half, HALF)] * 4
+
+
+def first_sum(parts):
+    if len(parts) == 1:
+        return parts
+    return kept_on(*parts[:2], "zl") + kept_on(*parts[2:], "y")
+
+
+def second_sum(parts):
+    if len(parts) == 1:
+        return parts
+    first, second = kept_on(*parts[:2], "y"), kept_on(*parts[2:], "zl")
+    return tuple(jnp.concatenate(pair, axis=1) for pair in zip(first, second))
+
+
+def cross_sum(parts):
+    return kept_on(*parts, "x") if len(parts) == 2 else parts
+
+
+def last_sum(parts):
+    if len(parts) == 2:
+        return parts[0].astype(f32) + swapped(parts[1], "zh").astype(f32)
+    whole = parts[0].reshape(8 * size_of("zh"), 2, -1, HALF)
+    whole = lax.psum_scatter(whole, CHIPS, scatter_dimension=0)
+    return in_order_back(whole).astype(f32)
+
+
+def in_order_back(pair):
+    own = lax.dynamic_index_in_dim(pair, lax.axis_index("core"), axis=0)
+    away = lax.dynamic_index_in_dim(pair, 1 - lax.axis_index("core"), axis=0)
+    return jnp.concatenate([own, away], axis=0)
+
+
+def crossed(values, step):
+    count = size_of("zh") * 4
+    moves = [
+        (2 * i + side, 2 * (i + step) + 1 - side)
+        for i in range(count)
+        for side in range(2)
+        if 0 <= i + step < count
+    ]
+    return lax.ppermute(values, ROWS + ("x",), moves)
+
+
+def halo(cells):
+    left_chip = lax.axis_index("x") == 0
+    edge = jnp.where(left_chip, cells[:, :, 1, 63], cells[:, :, 0, 0])
+    above = shifted(cells[:, 1:], ROWS, 1)
+    below = shifted(cells[:, :1], ROWS, -1)
+    beside = jnp.concatenate(
+        [crossed(edge[:, 1:], 1), swapped(edge, "x"), crossed(edge[:, :1], -1)], axis=1
+    )
+    rows = jnp.concatenate([above, cells, below], axis=1)
+    none = jnp.zeros_like(beside)
+    sides = jnp.stack([jnp.where(left_chip, none, beside), jnp.where(left_chip, beside, none)])
+    return rows, sides
 
 
 def adamw(weight, moment, second, grad, decay):
@@ -196,35 +554,113 @@
     member = (lax.axis_index("zl") * 2 + lax.axis_index("y")) * 2 + core
     zh, x = lax.axis_index("zh"), lax.axis_index("x")
 
+    channel = jnp.arange(8)[:, None] + 8 * jnp.arange(C1 // 8)[None, :]
+    sorting = (jnp.arange(C1)[:, None, None] == channel[None]).astype(bf16)
     r1 = conv_first.shape[0] // C1
-    low_one = conv_first.astype(bf16).reshape(r1, C1 // 8, 8).transpose(2, 0, 1)
-    low_one = lax.all_to_all(low_one, MEMBERS, 0, 0, tiled=True)
-    kernel_one = far_gather(low_one).reshape(3, 3, C0, C1 // 8)
     r2 = conv_second.shape[0] // C1
-    low_two = conv_second.astype(bf16).reshape(r2, C1)
-    if r2 % 8 == 0:
-        low_two = low_two.reshape(r2 // 8, 8, C1).transpose(1, 0, 2)
-        low_two = lax.all_to_all(low_two, MEMBERS, 0, 0, tiled=True)
-        kernel_two = far_gather(low_two)
+    even = r2 % 8 == 0
+    count_own = jnp.sum(valid_mask).astype(bf16)
+    low_one = jnp.einsum("rc,cqm->qrm", conv_first.astype(bf16).reshape(r1, C1), sorting)
+    low_two = conv_second.astype(bf16)
+    block = features.reshape(1, -1, 128)
+    lead = [jnp.full((8, 16, 128), count_own, bf16), low_one]
+    early = 0
+    if even:
+        low_two = low_two.reshape(r2 // 8, 8, C1 // 128, 128).transpose(1, 0, 2, 3)
+        low_two = low_two.reshape(8, r2, 128)
+        early = (r2 - r1 - 16) // 2 // 16 * 16
+        lead.append(low_two[:, :early])
+    lead_rows = 16 + r1 + early
+    lead = jnp.concatenate(lead + [jnp.broadcast_to(block, (8,) + block.shape[1:])], axis=1)
+    lead, low_two, conv_merge, up_conv, skip_feat, labels, pixel_weight = lax.optimization_barrier(
+        (lead, low_two, conv_merge, up_conv, skip_feat, labels, pixel_weight)
+    )
+
+    lead = lax.all_to_all(lead, MEMBERS, 0, 0, tiled=True)
+    tail = lax.all_to_all(low_two[:, early:], MEMBERS, 0, 0, tiled=True) if even else low_two
+    r3 = conv_merge.shape[0] // C0
+    ru = up_conv.shape[0] // C0
+    zhs = size_of("zh")
+    me = jnp.stack([lax.axis_index(axis) for axis in AXES]).astype(jnp.int32)
+    low_chip = jnp.concatenate(
+        [conv_merge.astype(bf16).reshape(r3, C0), up_conv.astype(bf16).reshape(ru, C0)], axis=0
+    )
+    low_chip = in_order_back(low_chip.reshape(r3 + ru, 2, HALF).transpose(1, 0, 2))
+    low_chip = jnp.concatenate([low_chip[:1], swapped(low_chip[1:], "core")], axis=0)
+    merge_pieces, up_pieces = chunk_list(r3 * zhs // 2, ru * zhs // 2, zhs)
+    if zhs == 2:
+        low_chip = joined_on(low_chip, "zh")
+    skip = padded(pair_gather(skip_feat, "core", 2), ROWS, 1, 1)
+    marks = pair_gather(jnp.stack([labels, valid_mask * pixel_weight]), "core", 3)
+    lead, low_chip, skip, marks = lax.optimization_barrier((lead, low_chip, skip, marks))
+
+    feat = lead[:, lead_rows:].reshape((4, 2) + features.shape[:1] + features.shape[2:])
+    feat = feat.transpose(2, 0, 1, 3, 4)
+    feat = feat.reshape(feat.shape[0], 4, 2 * feat.shape[3], C0)
+    lead = lead[:, :lead_rows].reshape(-1, 128)
+    if zhs == 2:
+        edge = jnp.where(zh == 0, feat[:, -2:], feat[:, :2])
+        got = swapped(jnp.concatenate([lead, edge.reshape(-1, 128)], axis=0), "zh")
+        edge = got[8 * lead_rows :].reshape(edge.shape)
+        none = jnp.zeros_like(edge)
+        feat = jnp.concatenate(
+            [jnp.where(zh == 0, none, edge), feat, jnp.where(zh == 0, edge, none)], axis=1
+        )
+        lead = in_order(lead, got[: 8 * lead_rows], "zh", 0)
     else:
-        low_two = lax.all_gather(low_two, AXES, axis=0, tiled=True).reshape(-1, 8, C1)
+        feat = padded(feat, "zh", 1, 2)
+        lead = lax.all_gather(lead, "zh", axis=0, tiled=True)
+    skip = padded(skip, "x", 2, 1)
+    skip = jnp.stack(
+        [skip[:, :, 0:128:2], skip[:, :, 1:129:2], skip[:, :, 2:130:2], skip[:, :, 3:130:2]], axis=2
+    )
+    marks = marks.reshape(2, 2, 2, 64, 2).swapaxes(3, 4)
+    first = second = jnp.zeros((), bf16)
+    if zhs == 2:
+        low_chip = joined_on(low_chip, "x")
+        cut = (r3 + ru) // 2
+        first, second = low_chip[:, :cut], low_chip[:, cut:]
+    feat, skip, lead, tail, first, second, marks = lax.optimization_barrier(
+        (feat, skip, lead, tail, first, second, marks)
+    )
+
+    edge = jnp.where(x == 0, feat[:, :, -2:], feat[:, :, :2])
+    got = swapped(jnp.concatenate([lead, edge.reshape(-1, 128)], axis=0), "x")
+    edge = got[lead.shape[0] :].reshape(edge.shape)
+    none = jnp.zeros_like(edge)
+    feat = jnp.concatenate(
+        [jnp.where(x == 0, none, edge), feat, jnp.where(x == 0, edge, none)], axis=2
+    )
+
+    def ordered(own, other):
+        both = jnp.stack([own, other]).reshape(2, zhs, 2, 2, 2, -1, 128)
+        return jnp.where(x == 0, both, both[::-1]).transpose(1, 2, 3, 0, 4, 5, 6)
+
+    lead = ordered(lead, got[: lead.shape[0]])
+    if even:
+        tail = tail.reshape(-1, 128)
+        if zhs == 2:
+            tail = in_order(tail, swapped(tail, "zh"), "zh", 0)
+        else:
+            tail = lax.all_gather(tail, "zh", axis=0, tiled=True)
+    if zhs == 2:
+        first = joined_on(first, "y")
+        second = joined_on(second, "zl")
+    feat, lead, tail, first, second = lax.optimization_barrier((feat, lead, tail, first, second))
+
+    count_all = jnp.sum(lead[..., 0, 0].astype(f32))
+    kernel_one = lead[..., 16 : 16 + r1, :].reshape(3, 3, C0, C1 // 8)
+    if even:
+        tail = ordered(tail, swapped(tail, "x"))
+        kernel_two = jnp.concatenate([lead[..., 16 + r1 :, :], tail], axis=5)
+    else:
+        low_two = lax.all_gather(tail.reshape(r2, C1), AXES, axis=0, tiled=True)
+        low_two = low_two.reshape(-1, 8, C1)
         kernel_two = lax.dynamic_index_in_dim(low_two, member, axis=1, keepdims=False)
     kernel_two = kernel_two.reshape(3, 3, C1 // 8, C1)
-
-    def chip_kernel(flat):
-        rows_in = flat.shape[0] // C0
-        cut = flat.astype(bf16).reshape(rows_in, 2, C0 // 2).transpose(1, 0, 2)
-        cut = pair_swap(cut).reshape(2 * rows_in, C0 // 2)
-        return lax.all_gather(cut, CHIPS, axis=0, tiled=True)
-
-    def pair_swap(cut):
-        own = lax.dynamic_slice_in_dim(cut, core, 1, axis=0)
-        away = lax.dynamic_slice_in_dim(cut, 1 - core, 1, axis=0)
-        return in_order(own, swapped(away, "core"), "core", 0)
-
-    kernel_up = chip_kernel(up_conv).reshape(2, 2, C1, C0 // 2)
-    kernel_merge = chip_kernel(conv_merge).reshape(3, 3, 2 * C0, C0 // 2)
-
+    if zhs == 2:
+        first = joined_on(first, "zl")
+        second = joined_on(second, "y")
     bias_one = lax.dynamic_index_in_dim(
         biases[:C1].reshape(C1 // 8, 8), member, axis=1, keepdims=False
     )
@@ -238,11 +674,6 @@
         head_weight.astype(bf16), core * (C0 // 2), C0 // 2, axis=0
     )
 
-    count_all = total(jnp.sum(valid_mask.astype(f32)))
-
-    feat = group_gather(features)
-    feat = padded(feat, "zh", 1, 2)
-    feat = padded(feat, "x", 2, 2)
     pre_one = convolve(feat, kernel_one) + bias_one
     high, wide = pre_one.shape[1], pre_one.shape[2]
     row_at = jnp.arange(high)
@@ -251,73 +682,126 @@
     col_in = ((col_at > 0) | (x > 0)) & ((col_at < wide - 1) | (x < size_of("x") - 1))
     inside = (row_in[:, None] & col_in[None, :])[None, :, :, None]
     act_one = jnp.where(inside, jax.nn.gelu(pre_one), 0.0).astype(bf16)
-    pre_two = group_scatter(convolve(act_one, kernel_two)) + bias_two
+    part_two = convolve(act_one, kernel_two)
+    part_two, first, second = lax.optimization_barrier((part_two, first, second))
+    if zhs == 2:
+        merge_sources, up_source = (first, second), second
+    else:
+        low_chip = jnp.where(core == 0, low_chip, low_chip[::-1])
+        low_chip = lax.all_gather(low_chip, CHIPS, axis=0, tiled=True)
+        merge_sources = (low_chip[:, :r3].reshape(1, -1, HALF),)
+        up_source = low_chip[:, r3:].reshape(1, -1, HALF)
+    pre_two = group_scatter(part_two) + bias_two
     act_two = jax.nn.gelu(pre_two).astype(bf16)
 
-    skip = padded(pair_gather(skip_feat, "core", 2), ROWS, 1, 1)
-    skip = padded(skip, "x", 2, 1)
-    act_chip = pair_gather(act_two, "core", 2)
-    images, rows_in, cols_in = act_chip.shape[:3]
-    ups = jnp.einsum("nhwc,abco->nhawbo", act_chip, kernel_up, preferred_element_type=f32)
-    ups = ups.reshape(images, 2 * rows_in, 2 * cols_in, C0 // 2) + bias_up
-    ups = padded(ups.astype(bf16), ROWS, 1, 1)
-    ups = padded(ups, "x", 2, 1)
-    joined = jnp.concatenate([pair_gather(ups, "core", 3), skip], axis=3)
-    pre_three = convolve(joined, kernel_merge) + bias_three
+    act_own = act_two[:, 0]
+    ups, kernel_up, act_chip = up_on_chip(
+        me, act_own, swapped(act_own, "core"), up_source, bias_up[None], up_pieces
+    )
+    ups, sides = halo(ups)
+    head_wide = jnp.pad(head_low, ((0, 0), (0, 128 - CLASSES)))
+    pre_three, logits, planes = merge_on_chip(
+        me,
+        ups,
+        swapped(ups, "core"),
+        sides,
+        swapped(sides, "core"),
+        skip,
+        merge_sources,
+        bias_three[None],
+        head_wide,
+        merge_pieces,
+    )
+    logits = (logits + swapped(logits, "core"))[:, :CLASSES] + bias_head
+    logits = logits.reshape(2, 2, 2, 64, CLASSES)
+    pre_three = pre_three.reshape(2, 2, 2, 64, HALF)
     act_three = jax.nn.gelu(pre_three).astype(bf16)
-    logits = jnp.einsum("nhwc,ck->nhwk", act_three, head_low, preferred_element_type=f32)
-    logits = logits + swapped(logits, "core") + bias_head
-
-    marks = jnp.stack([labels, valid_mask * pixel_weight])
-    marks = pair_gather(marks, "core", 3)
+
     scaled = marks[1].astype(f32)
     onehot = (marks[0][..., None] == jnp.arange(CLASSES, dtype=jnp.int32)).astype(f32)
     log_probs = jax.nn.log_softmax(logits, axis=-1)
     loss_part = -0.5 * jnp.sum(scaled * jnp.sum(onehot * log_probs, axis=-1))
     grad_logits = ((jnp.exp(log_probs) - onehot) * (scaled / count_all)[..., None]).astype(bf16)
 
-    head_part = jnp.einsum("nhwc,nhwk->ck", act_three, grad_logits, preferred_element_type=f32)
-    grad_act_three = jnp.einsum("nhwk,ck->nhwc", grad_logits, head_low, preferred_element_type=f32)
+    head_part = jnp.einsum("iabwc,iabwk->ck", act_three, grad_logits, preferred_element_type=f32)
+    grad_act_three = jnp.einsum(
+        "iabwk,ck->iabwc", grad_logits, head_low, preferred_element_type=f32
+    )
     grad_pre_three = gelu_back(pre_three, grad_act_three).astype(bf16)
-    merge_grad = kernel_grad(joined, grad_pre_three)
-    border = padded(grad_pre_three, ROWS, 1, 1)
-    border = padded(border, "x", 2, 1)
-    grad_ups = convolve(border, turned(kernel_merge[:, :, :C0]))
-    grad_upper = pair_scatter(grad_ups, "core", 3, bf16).astype(bf16)
-    grad_blocks = grad_upper.reshape(images, rows_in, 2, cols_in, 2, C0 // 2)
-    up_grad = jnp.einsum(
-        "nhwc,nhawbo->abco", act_chip, grad_blocks, preferred_element_type=f32
-    ).reshape(-1, C0 // 2)
+    border, border_sides = halo(grad_pre_three)
+    split_three, shape_three = split_list(r3 * zhs // 2, zhs)
+    merge_grad = merge_grad_on_chip(
+        me, planes, grad_pre_three.reshape(512, HALF), split_three, shape_three
+    )
+    border, border_sides, merge_grad = lax.optimization_barrier((border, border_sides, merge_grad))
+    merge_grad = first_sum(merge_grad)
+    own_grad, away_grad = ups_grad_on_chip(me, border, border_sides, merge_sources, merge_pieces)
+    grad_upper = (own_grad + swapped(away_grad, "core").astype(f32)).astype(bf16)
+    grad_upper = grad_upper.reshape(2, 2, 2, 64, HALF)
     grad_act_two = jnp.einsum(
-        "nhawbo,abco->nhwc", grad_blocks, kernel_up, preferred_element_type=f32
-    )
+        "iabwo,abco->iwc",
+        grad_upper,
+        kernel_up.reshape(2, 2, C1, HALF),
+        preferred_element_type=f32,
+    )[:, None]
     grad_act_two = pair_scatter(grad_act_two, "core", 2, f32)
     grad_pre_two = gelu_back(pre_two, grad_act_two).astype(bf16)
 
     grad_two = group_gather(grad_pre_two)
-    second_grad = kernel_grad(act_one, grad_two)
+    split_up, shape_up = split_list(ru * zhs // 2, zhs)
+    up_grad = up_grad_on_chip(me, act_chip, grad_upper, split_up, shape_up)
+    grad_two, merge_grad, up_grad = lax.optimization_barrier((grad_two, merge_grad, up_grad))
     spill = convolve(grad_two, turned(kernel_two), 2)
     inner = spill[:, 1:-1]
     inner = inner.at[:, :1].add(shifted(spill[:, -1:], "zh", 1))
     inner = inner.at[:, -1:].add(shifted(spill[:, :1], "zh", -1))
+    inner, merge_grad, up_grad = lax.optimization_barrier((inner, merge_grad, up_grad))
+    merge_grad, up_grad = second_sum(merge_grad), first_sum(up_grad)
     core_part = inner[:, :, 1:-1]
     core_part = core_part.at[:, :, :1].add(shifted(inner[:, :, -1:], "x", 1))
     core_part = core_part.at[:, :, -1:].add(shifted(inner[:, :, :1], "x", -1))
+    core_part, grad_two, act_late = lax.optimization_barrier((core_part, grad_two, act_one))
     grad_pre_one = gelu_back(pre_one[:, 1:-1, 1:-1], core_part).astype(bf16)
+    second_grad = kernel_grad(act_late, grad_two)
     first_grad = kernel_grad(feat[:, 1:-1, 1:-1], grad_pre_one)
-
-    def chip_grad(grad):
-        mine = lax.psum_scatter(grad.astype(bf16), CHIPS, scatter_dimension=0, tiled=True)
-        rows_out = mine.shape[0] // 2
-        cut = pair_swap(mine.reshape(2, rows_out, C0 // 2))
-        return cut.transpose(1, 0, 2).reshape(-1).astype(f32)
-
-    share_merge = chip_grad(merge_grad)
-    share_up = chip_grad(up_grad)
-    if r2 % 8 == 0:
-        part_two = far_scatter(second_grad).astype(bf16)
+    first_grad, merge_grad, up_grad = lax.optimization_barrier((first_grad, merge_grad, up_grad))
+    up_grad = second_sum(up_grad)
+    if zhs == 2:
+        chip_parts = tuple(jnp.concatenate(pair, axis=1) for pair in zip(merge_grad, up_grad))
+    else:
+        chip_parts = (merge_grad[0], up_grad[0])
+
+    if even:
+        part_two = far_scatter(second_grad.astype(bf16).reshape(-1, 128))
+        sq_two = jnp.sum(part_two * part_two)
+        part_two = lax.all_to_all(part_two.astype(bf16), MEMBERS, 0, 0, tiled=True)
+        part_two = part_two.reshape(8, r2 // 8, C1 // 128, 128).transpose(1, 0, 2, 3)
+        share_two = part_two.reshape(-1).astype(f32)
+    else:
+        mine = jnp.arange(8)[None, :, None] == member
+        part_two = jnp.where(mine, second_grad.astype(bf16)[:, None], 0)
+        share_two = lax.psum_scatter(
+            part_two.reshape(-1, C1), AXES, scatter_dimension=0, tiled=True
+        ).reshape(-1).astype(f32)
+        sq_two = jnp.sum(share_two * share_two)
+    part_one = far_scatter(first_grad)
+    sq_one = jnp.sum(part_one * part_one)
+    part_one = lax.all_to_all(part_one.astype(bf16), MEMBERS, 0, 0, tiled=True)
+    share_one = jnp.einsum("qrm,cqm->rc", part_one, sorting, preferred_element_type=f32).reshape(-1)
+    if zhs == 2:
+        part_chip = last_sum(cross_sum(chip_parts))
+    else:
+        part_chip = jnp.concatenate([last_sum(chip_parts[:1]), last_sum(chip_parts[1:])], axis=1)
+    sq_chip = jnp.sum(part_chip * part_chip)
+    part_chip = part_chip.astype(bf16)
+    part_chip = in_order(part_chip[0], swapped(part_chip[1], "core"), "core", 1).astype(f32)
+    share_merge = part_chip[:r3].reshape(-1)
+    share_up = part_chip[r3:].reshape(-1)
+    if even:
+        part_two = far_scatter(second_grad.astype(bf16).reshape(-1, 128)).astype(bf16)
         part_two = lax.all_to_all(part_two, MEMBERS, 0, 0, tiled=True)
-        share_two = part_two.transpose(1, 0, 2).reshape(-1).astype(f32)
+        part_two = part_two.reshape(8, r2 // 8, C1 // 128, 128).transpose(1, 0, 2, 3)
+        share_two = part_two.reshape(-1).astype(f32)
     else:
         mine = jnp.arange(8)[None, :, None] == member
         part_two = jnp.where(mine, second_grad.astype(bf16)[:, None], 0)
@@ -326,14 +810,9 @@
         ).reshape(-1).astype(f32)
     part_one = far_scatter(first_grad).astype(bf16)
     part_one = lax.all_to_all(part_one, MEMBERS, 0, 0, tiled=True)
-    share_one = part_one.transpose(1, 2, 0).reshape(-1).astype(f32)
-
-    share_sq = (
-        jnp.sum(share_one * share_one)
-        + jnp.sum(share_two * share_two)
-        + jnp.sum(share_up * share_up)
-        + jnp.sum(share_merge * share_merge)
-    )
+    share_one = jnp.einsum("qrm,cqm->rc", part_one, sorting, preferred_element_type=f32).reshape(-1)
+
+    share_sq = sq_one + sq_two + sq_chip
     spread_one = (
         jnp.where(jnp.arange(8)[None, :] == member, column_sum(grad_pre_one)[:, None], 0.0)
     ).reshape(-1)
@@ -356,7 +835,9 @@
             loss_part[None],
         ]
     )
-    packed = total(packed)
+    packed = total(packed, ("core", "x", "y"))
+    packed, share_one, share_two = lax.optimization_barrier((packed, share_one, share_two))
+    packed = total(packed, ("zl", "zh"))
     bias_total = packed[: biases.shape[0]]
     head_total = packed[biases.shape[0] : -2].reshape(head_weight.shape)
     sq_total, loss_total = packed[-2], packed[-1]

time: 682 us -> 536 us (0.79)
  waiting for transfers between devices: 267 us -> 172 us
  local copies, waits for them, and re-layouts: 115 us -> 58.7 us
  Pallas kernels: 0 us -> 34.6 us
  matrix products: 56.6 us -> 37.5 us
  between operations: 27.6 us -> 9.15 us
  other arithmetic: 77.5 us -> 86 us
    reduce_scatter x2 -> x0, waiting for transfers between devices: 58.4 us -> none  [chip_grad(): lax.psum_scatter(grad.astype(bf16), CHIPS, scatter_dimension=0, tiled=True)]
    ppermute x29 -> x41, waiting for transfers between devices: 92.8 us -> 148 us  [swapped(): return lax.ppermute(values, axis, [(0, 1), (1, 0)])]
    all_to_all x2, waiting for transfers between devices: 40.3 us -> 0.01 us  [the longest x1 0.01 us: shards(): lax.all_to_all(low_two[:, early:], MEMBERS, 0, 0, tiled=True)]
    pallas_call x0 -> x5, Pallas kernels: none -> 34.6 us  [on_chip(): pl.pallas_call(body, out_shape=outs, in_specs=[pl.BlockSpec(memory_space=...]
    ppermute x20 -> x12, waiting for transfers between devices: 53.4 us -> 22.7 us  [shifted(): lax.ppermute(values, axis, [(i, i + step) for i in range(count) if 0 <= i...]
    ppermute x20 -> x12, starting transfers between devices: 61.9 us -> 32.3 us  [shifted(): lax.ppermute(values, axis, [(i, i + step) for i in range(count) if 0 <= i...]
    convert_element_type x8 -> x16, other arithmetic: 3.17 us -> 21.9 us  [the longest x9 15.9 us: kept_on(): return (sums[0].astype(bf16), sums[1].astype(bf16))]
    all_to_all x2 -> x1, waiting for transfers between devices: 17.8 us -> 0.01 us  [group_gather(): got = lax.all_to_all(sent, MEMBERS, 0, 0, tiled=True)]
  transfers between devices with their start and end apart: 59 -> 62, of which waited for: 30 -> 29; matrix products, arithmetic and copies ran while one was open for 27% -> 23% of each run, Pallas kernels for 0% -> 2%
where the time goes in v2:
time: 536 us; the launch traced here: 528 us
  waiting for transfers between devices  172 us (32%)
  starting transfers between devices  113 us (21%)
  other arithmetic  86 us (16%)
  local copies, waits for them, and re-layouts  58.7 us (11%)
  matrix products  37.5 us (7%)
  Pallas kernels  34.6 us (6%)
  blocking collectives  17.2 us (3%)
  between operations  9.15 us (2%)
    ppermute x41, waiting for transfers between devices, swapped(): return lax.ppermute(values, axis, [(0, 1), (1, 0)])  148 us
    ppermute x41, starting transfers between devices, swapped(): return lax.ppermute(values, axis, [(0, 1), (1, 0)])  42.9 us
    pallas_call x5, Pallas kernels, on_chip(): pl.pallas_call(body, out_shape=outs, in_specs=[pl.BlockSpec(memory_space=...  34.6 us
    ppermute x12, starting transfers between devices, shifted(): lax.ppermute(values, axis, [(i, i + step) for i in range(count) if 0 <= i...  32.3 us
    ppermute x12, waiting for transfers between devices, shifted(): lax.ppermute(values, axis, [(i, i + step) for i in range(count) if 0 <= i...  22.7 us
    dot_general x18, matrix products, kernel_grad(): jnp.einsum('nhwc,nhwo->co', cells[:, shift_h:shift_h + rows_in, shift_w:s...  18.8 us
    all_to_all x1, blocking collectives, group_scatter(): lax.all_to_all(sent.reshape(8, n, w2 // 2, c), MEMBERS, 0, 0, tiled=True)  17.2 us
    convert_element_type x9, other arithmetic, kept_on(): return (sums[0].astype(bf16), sums[1].astype(bf16))  15.9 us
  transfers between devices with their start and end apart: 62, of which 29 were waited for; matrix products, arithmetic and copies ran while one was open for 23% of the time, Pallas kernels for 2%

profile of v2, /device:TPU:0, one launch (start us, length us, event | category | flops | bytes accessed | tf_op | source)
XLA Modules:
  0.0 528.4 jit_solution(14721382902756026320)
XLA Ops:
  7.3 5.3 all-to-all-start
  19.3 3.8 collective-permute-start.3
  24.5 6.0 %collective-permute-done.3 = bf16[2,1,128,512]{3,2,1,0:T(8,128)(2,1)S(1)} collective-permute-done((bf16[2,1,128,512]{3,2,1,0:T(8,128)(2,1)S(1)}, bf16[2,1,128,512]{3,2,1,0:T(8,128)(2,1)S(1)}, u32[]{:S(2)}, u32[]{:S(2)}) %collective-permute-start.3) | collective-permute-done | bytes 262176 | tf_op jit(solution)/shard_map/ppermute | solution.py:35
  30.5 3.9 collective-permute-done.4
  34.5 4.8 collective-permute-done.1
  40.3 8.2 %all-to-all-start.1 = ((bf16[8,224,128]{2,1,0:T(8,128)(2,1)}), bf16[8,224,128]{2,1,0:T(8,128)(2,1)}, u32[]{:S(2)}, u32[]{:S(2)}) async-start(bf16[8,224,128]{2,1,0:T(8,128)(2,1)} %slice.493), calls=%async_computation.1 | async-start | bytes 917504 | tf_op jit(solution)/shard_map/all_to_all | solution.py:580
  50.1 4.8 collective-permute-start.6
  55.2 3.4 collective-permute-start.7
  65.0 2.9 slice.489
  69.3 3.0 slice.490
  77.9 9.5 %collective-permute-done.6 = bf16[2816,128]{1,0:T(8,128)(2,1)} collective-permute-done((bf16[2816,128]{1,0:T(8,128)(2,1)}, bf16[2816,128]{1,0:T(8,128)(2,1)}, u32[]{:S(2)}, u32[]{:S(2)}) %collective-permute-start.6) | collective-permute-done | bytes 720928 | tf_op jit(solution)/shard_map/ppermute | solution.py:41
  96.9 4.0 collective-permute-start.13
  102.6 15.9 %collective-permute-done.11 = bf16[1792,128]{1,0:T(8,128)(2,1)S(1)} collective-permute-done((bf16[1792,128]{1,0:T(8,128)(2,1)}, bf16[1792,128]{1,0:T(8,128)(2,1)S(1)}, u32[]{:S(2)}, u32[]{:S(2)}) %collective-permute-start.11) | collective-permute-done | bytes 458784 | tf_op jit(solution)/shard_map/ppermute | solution.py:41
  121.9 6.3 %collective-permute-done.13 = bf16[8,208,256]{2,1,0:T(8,128)(2,1)S(1)} collective-permute-done((bf16[8,208,256]{2,1,0:T(8,128)(2,1)S(1)}, bf16[8,208,256]{2,1,0:T(8,128)(2,1)S(1)}, u32[]{:S(2)}, u32[]{:S(2)}) %collective-permute-start.13) | collective-permute-done | bytes 852000 | tf_op jit(solution)/shard_map/ppermute | solution.py:41
  134.1 3.9 fusion.44
  138.9 14.3 %collective-permute-done.14 = bf16[3584,128]{1,0:T(8,128)(2,1)S(1)} collective-permute-done((bf16[3584,128]{1,0:T(8,128)(2,1)S(1)}, bf16[3584,128]{1,0:T(8,128)(2,1)S(1)}, u32[]{:S(2)}, u32[]{:S(2)}) %collective-permute-start.14) | collective-permute-done | bytes 917536 | tf_op jit(solution)/shard_map/ppermute | solution.py:41
  156.0 3.6 reshape.766
  159.7 4.0 fusion.99
  163.7 7.9 %collective-permute-done.15 = bf16[16,208,256]{2,1,0:T(8,128)(2,1)} collective-permute-done((bf16[16,208,256]{2,1,0:T(8,128)(2,1)}, bf16[16,208,256]{2,1,0:T(8,128)(2,1)}, u32[]{:S(2)}, u32[]{:S(2)}) %collective-permute-start.15) | collective-permute-done | bytes 1703968 | tf_op jit(solution)/shard_map/ppermute | solution.py:41
  171.7 4.1 pad_maximum_fusion.rest_0_
  175.7 4.0 pad_maximum_fusion.1.source_ref.rest_1_
  179.7 17.2 %all_to_all.30 = bf16[8,2,32,1024]{3,1,2,0:T(2,128)(2,1)S(1)} all-to-all(bf16[8,2,32,1024]{3,1,2,0:T(2,128)(2,1)S(1)} %bitcast.391), channel_id=1, replica_groups=mesh['zh'=2,'zl'=2,'y'=2,'x'=2,'core'=2] {'zl','y','core'}, dimensions={0} | all-to-all | bytes 2097152 | tf_op jit(solution)/shard_map/all_to_all | solution.py:132
  201.5 4.3 shard_map.382
  208.8 3.4 collective-permute-start.18
  212.2 4.2 collective-permute-start.21
  220.0 5.3 collective-permute-done.19
  228.1 12.4 %shard_map.383 = (f32[512,256]{1,0:T(8,128)}, f32[512,128]{1,0:T(8,128)}, bf16[2,4,4,64,1024]{4,3,2,1,0:T(8,128)(2,1)}) custom-call(s32[5]{0:T(128)} %stack.75.me_ref, bf16[2,4,2,64,256]{4,3,2,1,0:T(8,128)(2,1)} %copy-done.35, bf16[2,4,2,64,256]{4,3,2,1,0:T(8,128)(2,1)} %copy-done.45, bf16[2,2,4,256]{3,2,1,0:T(4,128)(2,1)} %copy-done.53, ...), custom_call_target="tpu_custom_call" | custom-call | flops 2415919104 | bytes 15025172 | tf_op jit(solution)/shard_map/pallas_call | solution.py:235
  245.3 3.7 convert_reduce_fusion.1
  252.4 4.7 collective-permute-start.28
  258.4 5.5 %collective-permute-start.26 = (bf16[2,1,2,64,256]{4,1,0,3,2:T(2,128)(2,1)}, bf16[2,1,2,64,256]{4,1,0,3,2:T(2,128)(2,1)S(1)}, u32[]{:S(2)}, u32[]{:S(2)}) collective-permute-start(bf16[2,1,2,64,256]{4,1,0,3,2:T(2,128)(2,1)} %get-tuple-element.391), channel_id=1, source_target_pairs={{0,4},{4,8},{8,12},{12,16},{16,20},{20,24},{24,28},{1,5},{5,9},{9,... | collective-permute-start | bytes 393224 | tf_op jit(solution)/shard_map/ppermute | solution.py:35
  265.7 7.9 %shard_map.384 = (bf16[16,144,256]{2,1,0:T(8,128)(2,1)}, bf16[16,144,256]{2,1,0:T(8,128)(2,1)}, bf16[16,144,256]{2,1,0:T(8,128)(2,1)}, bf16[16,144,256]{2,1,0:T(8,128)(2,1)}) custom-call(s32[5]{0:T(128)} %stack.75.me_ref, bf16[2,4,4,64,1024]{4,3,2,1,0:T(8,128)(2,1)} %get-tuple-element.177.planes_ref, bf16[512,256]{1,0:T(8,128)(2,1)} %bitcast.399), custom_call_target="tpu_custom_call" | custom-call | flops 2415919104 | bytes 9175060 | tf_op jit(solution)/shard_map/pallas_call | solution.py:235
  276.9 6.3 %shard_map.385 = (f32[512,256]{1,0:T(8,128)}, bf16[512,256]{1,0:T(8,128)(2,1)}) custom-call(s32[5]{0:T(128)} %stack.75.me_ref, bf16[2,4,2,64,256]{4,3,2,1,0:T(8,128)(2,1)} %copy.524.rows_ref, bf16[2,2,4,256]{3,2,1,0:T(4,128)(2,1)} %pad_maximum_fusion.27.sides_ref, bf16[32,208,256]{2,1,0:T(8,128)(2,1)} %pad_maximum_fusion.rest_0_, ...), custom_call_target="tpu_custom_call" | custom-call | flops 1207959552 | bytes 8134676 | tf_op jit(solution)/shard_map/pallas_call | solution.py:235
  295.3 4.9 all-to-all-start.3
  300.2 2.9 collective-permute-start.33
  306.3 3.6 shard_map.386
  309.9 30.9 %collective-permute-done.33 = bf16[16,144,256]{2,1,0:T(8,128)(2,1)} collective-permute-done((bf16[16,144,256]{2,1,0:T(8,128)(2,1)}, bf16[16,144,256]{2,1,0:T(8,128)(2,1)}, u32[]{:S(2)}, u32[]{:S(2)}) %collective-permute-start.33) | collective-permute-done | bytes 1179680 | tf_op jit(solution)/shard_map/ppermute | solution.py:41
  351.8 4.3 fusion.11
  356.2 5.3 %collective-permute-start.35 = (f32[2,1,66,128]{3,2,1,0:T(8,128)S(1)}, f32[2,1,66,128]{3,2,1,0:T(8,128)S(1)}, u32[]{:S(2)}, u32[]{:S(2)}) collective-permute-start(f32[2,1,66,128]{3,2,1,0:T(8,128)S(1)} %slice_bitcast_fusion.3), channel_id=1, source_target_pairs={{0,16},{1,17},{2,18},{3,19},{4,20},{5,21},{6,22},{7,23},{8,24},{9,... | collective-permute-start | bytes 202760 | tf_op jit(solution)/shard_map/ppermute | solution.py:35
  363.6 6.4 %collective-permute-done.36 = f32[2,1,66,128]{3,2,1,0:T(8,128)S(1)} collective-permute-done((f32[2,1,66,128]{3,2,1,0:T(8,128)S(1)}, f32[2,1,66,128]{3,2,1,0:T(8,128)S(1)}, u32[]{:S(2)}, u32[]{:S(2)}) %collective-permute-start.36) | collective-permute-done | bytes 67616 | tf_op jit(solution)/shard_map/ppermute | solution.py:35
  388.3 3.6 convert_element_type.444
  424.3 11.1 %collective-permute-done.43 = bf16[1,2,2,2,2,144,128]{6,5,4,3,2,1,0:T(8,128)(2,1)S(1)} collective-permute-done((bf16[1,2,2,2,2,144,128]{6,5,4,3,2,1,0:T(8,128)(2,1)S(1)}, bf16[1,2,2,2,2,144,128]{6,5,4,3,2,1,0:T(8,128)(2,1)S(1)}, u32[]{:S(2)}, u32[]{:S(2)}) %collective-permute-start.43) | collective-permute-done | bytes 589856 | tf_op jit(solution)/shard_map/ppermute | solution.py:41
  440.8 2.9 collective-permute-start.46
  443.7 16.8 %collective-permute-done.44 = bf16[1,2,2,2,144,128]{5,4,3,2,1,0:T(8,128)(2,1)S(1)} collective-permute-done((bf16[1,2,2,2,144,128]{5,4,3,2,1,0:T(8,128)(2,1)S(1)}, bf16[1,2,2,2,144,128]{5,4,3,2,1,0:T(8,128)(2,1)S(1)}, u32[]{:S(2)}, u32[]{:S(2)}) %collective-permute-start.44) | collective-permute-done | bytes 294944 | tf_op jit(solution)/shard_map/ppermute | solution.py:41
  461.9 4.2 all-to-all-start.4
  476.1 3.8 all-to-all-start.5
  483.1 8.6 %collective-permute-done.50 = bf16[2,416,256]{2,1,0:T(8,128)(2,1)} collective-permute-done((bf16[2,416,256]{2,1,0:T(8,128)(2,1)}, bf16[2,416,256]{2,1,0:T(8,128)(2,1)}, u32[]{:S(2)}, u32[]{:S(2)}) %collective-permute-start.50) | collective-permute-done | bytes 426016 | tf_op jit(solution)/shard_map/ppermute | solution.py:41
  503.5 3.8 collective-permute-done.54
  507.4 4.5 collective-permute-done.55
  (460 shorter events, 203.2 us)
Async XLA Ops:
  7.3 33.0 %all-to-all-start = ((bf16[8,480,128]{2,1,0:T(8,128)(2,1)}), bf16[8,480,128]{2,1,0:T(8,128)(2,1)S(1)}, u32[]{:S(2)}, u32[]{:S(2)}) async-start(bf16[8,480,128]{2,1,0:T(8,128)(2,1)} %pad_maximum_fusion.12), calls=%async_computation | async-start | bytes 1966080 | tf_op jit(solution)/shard_map/all_to_all | solution.py:579
  12.6 11.8 %collective-permute-start.5 = (s32[2,2,2,64]{3,2,1,0:T(2,128)S(1)}, s32[2,2,2,64]{3,2,1,0:T(2,128)S(1)}, u32[]{:S(2)}, u32[]{:S(2)}) collective-permute-start(s32[2,2,2,64]{3,2,1,0:T(2,128)S(1)} %pad_add_fusion), channel_id=1, source_target_pairs={{0,1},{1,0},{2,3},{3,2},{4,5},{5,4},{6,7},{7,6},{8,9},{9,8},{10,11... | collective-permute-start | bytes 6152 | tf_op jit(solution)/shard_map/ppermute | solution.py:41
  16.5 22.8 %collective-permute-start.1 = (bf16[2,416,256]{2,1,0:T(8,128)(2,1)S(1)}, bf16[2,416,256]{2,1,0:T(8,128)(2,1)S(1)}, u32[]{:S(2)}, u32[]{:S(2)}) collective-permute-start(bf16[2,416,256]{2,1,0:T(8,128)(2,1)S(1)} %pad_maximum_fusion.23), channel_id=1, source_target_pairs={{0,16},{16,0},{1,17},{17,1},{2,18},{18,2},{3,19},{19,3},{4,20},{20... | collective-permute-start | bytes 1277960 | tf_op jit(solution)/shard_map/ppermute | solution.py:41
  19.3 11.2 %collective-permute-start.3 = (bf16[2,1,128,512]{3,2,1,0:T(8,128)(2,1)S(1)}, bf16[2,1,128,512]{3,2,1,0:T(8,128)(2,1)S(1)}, u32[]{:S(2)}, u32[]{:S(2)}) collective-permute-start(bf16[2,1,128,512]{3,2,1,0:T(8,128)(2,1)S(1)} %get-tuple-element.378), channel_id=1, source_target_pairs={{0,4},{4,8},{8,12},{12,16},{16,20},{20,24},{24,28},{1,5},{5,9},{9,... | collective-permute-start | bytes 786440 | tf_op jit(solution)/shard_map/ppermute | solution.py:35
  23.1 11.3 %collective-permute-start.4 = (bf16[2,1,128,512]{3,2,1,0:T(8,128)(2,1)S(1)}, bf16[2,1,128,512]{3,2,1,0:T(8,128)(2,1)S(1)}, u32[]{:S(2)}, u32[]{:S(2)}) collective-permute-start(bf16[2,1,128,512]{3,2,1,0:T(8,128)(2,1)S(1)} %get-tuple-element.379), channel_id=1, source_target_pairs={{4,0},{8,4},{12,8},{16,12},{20,16},{24,20},{28,24},{5,1},{9,5},{13... | collective-permute-start | bytes 786440 | tf_op jit(solution)/shard_map/ppermute | solution.py:35
  40.3 54.7 %all-to-all-start.1 = ((bf16[8,224,128]{2,1,0:T(8,128)(2,1)}), bf16[8,224,128]{2,1,0:T(8,128)(2,1)}, u32[]{:S(2)}, u32[]{:S(2)}) async-start(bf16[8,224,128]{2,1,0:T(8,128)(2,1)} %slice.493), calls=%async_computation.1 | async-start | bytes 917504 | tf_op jit(solution)/shard_map/all_to_all | solution.py:580
  50.1 37.3 %collective-permute-start.6 = (bf16[2816,128]{1,0:T(8,128)(2,1)}, bf16[2816,128]{1,0:T(8,128)(2,1)}, u32[]{:S(2)}, u32[]{:S(2)}) collective-permute-start(bf16[2816,128]{1,0:T(8,128)(2,1)} %pad_maximum_fusion.19), channel_id=1, source_target_pairs={{0,16},{16,0},{1,17},{17,1},{2,18},{18,2},{3,19},{19,3},{4,20},{20... | collective-permute-start | bytes 2162696 | tf_op jit(solution)/shard_map/ppermute | solution.py:41
  55.2 12.9 %collective-permute-start.7 = (bf16[2,4,1,512]{3,2,1,0:T(2,128)(2,1)S(1)}, bf16[2,4,1,512]{3,2,1,0:T(2,128)(2,1)S(1)}, u32[]{:S(2)}, u32[]{:S(2)}) collective-permute-start(bf16[2,4,1,512]{3,2,1,0:T(2,128)(2,1)S(1)} %get-tuple-element.364), channel_id=1, source_target_pairs={{0,2},{1,3},{4,6},{5,7},{8,10},{9,11},{12,14},{13,15},{16,18},{17,... | collective-permute-start | bytes 24584 | tf_op jit(solution)/shard_map/ppermute | solution.py:35
  58.7 9.5 %collective-permute-start.8 = (bf16[2,4,1,512]{3,2,1,0:T(2,128)(2,1)S(1)}, bf16[2,4,1,512]{3,2,1,0:T(2,128)(2,1)S(1)}, u32[]{:S(2)}, u32[]{:S(2)}) collective-permute-start(bf16[2,4,1,512]{3,2,1,0:T(2,128)(2,1)S(1)} %get-tuple-element.365), channel_id=1, source_target_pairs={{2,0},{3,1},{6,4},{7,5},{10,8},{11,9},{14,12},{15,13},{18,16},{19,... | collective-permute-start | bytes 24584 | tf_op jit(solution)/shard_map/ppermute | solution.py:35
  60.1 32.3 %collective-permute-start.9 = (bf16[4,416,256]{2,1,0:T(8,128)(2,1)}, bf16[4,416,256]{2,1,0:T(8,128)(2,1)}, u32[]{:S(2)}, u32[]{:S(2)}) collective-permute-start(bf16[4,416,256]{2,1,0:T(8,128)(2,1)} %pad_maximum_fusion.16), channel_id=1, source_target_pairs={{0,2},{2,0},{1,3},{3,1},{4,6},{6,4},{5,7},{7,5},{8,10},{10,8},{9,1... | collective-permute-start | bytes 2555912 | tf_op jit(solution)/shard_map/ppermute | solution.py:41
  95.1 23.3 %collective-permute-start.11 = (bf16[1792,128]{1,0:T(8,128)(2,1)}, bf16[1792,128]{1,0:T(8,128)(2,1)S(1)}, u32[]{:S(2)}, u32[]{:S(2)}) collective-permute-start(bf16[1792,128]{1,0:T(8,128)(2,1)} %bitcast.27), channel_id=1, source_target_pairs={{0,16},{16,0},{1,17},{17,1},{2,18},{18,2},{3,19},{19,3},{4,20},{20... | collective-permute-start | bytes 1376264 | tf_op jit(solution)/shard_map/ppermute | solution.py:41
  95.2 25.3 %collective-permute-start.12 = (bf16[8,208,256]{2,1,0:T(8,128)(2,1)}, bf16[8,208,256]{2,1,0:T(8,128)(2,1)S(1)}, u32[]{:S(2)}, u32[]{:S(2)}) collective-permute-start(bf16[8,208,256]{2,1,0:T(8,128)(2,1)} %get-tuple-element.162), channel_id=1, source_target_pairs={{0,4},{4,0},{1,5},{5,1},{2,6},{6,2},{3,7},{7,3},{8,12},{12,8},{9,1... | collective-permute-start | bytes 2555912 | tf_op jit(solution)/shard_map/ppermute | solution.py:41
  96.9 31.2 %collective-permute-start.13 = (bf16[8,208,256]{2,1,0:T(8,128)(2,1)S(1)}, bf16[8,208,256]{2,1,0:T(8,128)(2,1)S(1)}, u32[]{:S(2)}, u32[]{:S(2)}) collective-permute-start(bf16[8,208,256]{2,1,0:T(8,128)(2,1)S(1)} %get-tuple-element.163), channel_id=1, source_target_pairs={{0,8},{8,0},{1,9},{9,1},{2,10},{10,2},{3,11},{11,3},{4,12},{12,4},... | collective-permute-start | bytes 2555912 | tf_op jit(solution)/shard_map/ppermute | solution.py:41
  101.0 28.5 %collective-permute-start.10 = (bf16[3712,128]{1,0:T(8,128)(2,1)S(1)}, bf16[3712,128]{1,0:T(8,128)(2,1)S(1)}, u32[]{:S(2)}, u32[]{:S(2)}) collective-permute-start(bf16[3712,128]{1,0:T(8,128)(2,1)S(1)} %pad_maximum_fusion.13), channel_id=1, source_target_pairs={{0,2},{2,0},{1,3},{3,1},{4,6},{6,4},{5,7},{7,5},{8,10},{10,8},{9,1... | collective-permute-start | bytes 2850824 | tf_op jit(solution)/shard_map/ppermute | solution.py:41
  132.1 21.1 %collective-permute-start.14 = (bf16[3584,128]{1,0:T(8,128)(2,1)S(1)}, bf16[3584,128]{1,0:T(8,128)(2,1)S(1)}, u32[]{:S(2)}, u32[]{:S(2)}) collective-permute-start(bf16[3584,128]{1,0:T(8,128)(2,1)S(1)} %copy-done.11), channel_id=1, source_target_pairs={{0,2},{2,0},{1,3},{3,1},{4,6},{6,4},{5,7},{7,5},{8,10},{10,8},{9,1... | collective-permute-start | bytes 2752520 | tf_op jit(solution)/shard_map/ppermute | solution.py:41
  133.6 38.0 %collective-permute-start.15 = (bf16[16,208,256]{2,1,0:T(8,128)(2,1)}, bf16[16,208,256]{2,1,0:T(8,128)(2,1)}, u32[]{:S(2)}, u32[]{:S(2)}) collective-permute-start(bf16[16,208,256]{2,1,0:T(8,128)(2,1)} %pad_maximum_fusion.6), channel_id=1, source_target_pairs={{0,8},{8,0},{1,9},{9,1},{2,10},{10,2},{3,11},{11,3},{4,12},{12,4},... | collective-permute-start | bytes 5111816 | tf_op jit(solution)/shard_map/ppermute | solution.py:41
  133.8 41.9 %collective-permute-start.16 = (bf16[16,208,256]{2,1,0:T(8,128)(2,1)}, bf16[16,208,256]{2,1,0:T(8,128)(2,1)}, u32[]{:S(2)}, u32[]{:S(2)}) collective-permute-start(bf16[16,208,256]{2,1,0:T(8,128)(2,1)} %pad_maximum_fusion.7), channel_id=1, source_target_pairs={{0,4},{4,0},{1,5},{5,1},{2,6},{6,2},{3,7},{7,3},{8,12},{12,8},{9,1... | collective-permute-start | bytes 5111816 | tf_op jit(solution)/shard_map/ppermute | solution.py:41
  208.2 17.2 %collective-permute-start.22 = (bf16[2,2,256]{2,1,0:T(2,128)(2,1)S(1)}, bf16[2,2,256]{2,1,0:T(2,128)(2,1)S(1)}, u32[]{:S(2)}, u32[]{:S(2)}) collective-permute-start(bf16[2,2,256]{2,1,0:T(2,128)(2,1)S(1)} %fusion.138), channel_id=1, source_target_pairs={{0,2},{2,0},{1,3},{3,1},{4,6},{6,4},{5,7},{7,5},{8,10},{10,8},{9,1... | collective-permute-start | bytes 6152 | tf_op jit(solution)/shard_map/ppermute | solution.py:41
  208.8 10.2 %collective-permute-start.18 = (bf16[2,1,2,64,256]{4,3,2,1,0:T(8,128)(2,1)S(1)}, bf16[2,1,2,64,256]{4,3,2,1,0:T(8,128)(2,1)S(1)}, u32[]{:S(2)}, u32[]{:S(2)}) collective-permute-start(bf16[2,1,2,64,256]{4,3,2,1,0:T(8,128)(2,1)S(1)} %get-tuple-element.394), channel_id=1, source_target_pairs={{0,4},{4,8},{8,12},{12,16},{16,20},{20,24},{24,28},{1,5},{5,9},{9,... | collective-permute-start | bytes 393224 | tf_op jit(solution)/shard_map/ppermute | solution.py:35
  212.2 13.2 %collective-permute-start.21 = (bf16[2,1,256]{2,1,0:T(2,128)(2,1)S(1)}, bf16[2,1,256]{2,1,0:T(2,128)(2,1)S(1)}, u32[]{:S(2)}, u32[]{:S(2)}) collective-permute-start(bf16[2,1,256]{2,1,0:T(2,128)(2,1)S(1)} %get-tuple-element.420), channel_id=1, source_target_pairs={{0,6},{2,4},{4,10},{6,8},{8,14},{10,12},{12,18},{14,16},{16,22},{1... | collective-permute-start | bytes 3080 | tf_op jit(solution)/shard_map/ppermute | solution.py:499
  216.4 9.0 %collective-permute-start.23 = (bf16[2,1,256]{2,1,0:T(2,128)(2,1)S(1)}, bf16[2,1,256]{2,1,0:T(2,128)(2,1)S(1)}, u32[]{:S(2)}, u32[]{:S(2)}) collective-permute-start(bf16[2,1,256]{2,1,0:T(2,128)(2,1)S(1)} %get-tuple-element.421), channel_id=1, source_target_pairs={{4,2},{6,0},{8,6},{10,4},{12,10},{14,8},{16,14},{18,12},{20,18},{2... | collective-permute-start | bytes 3080 | tf_op jit(solution)/shard_map/ppermute | solution.py:499
  217.7 7.6 %collective-permute-start.19 = (bf16[2,1,2,64,256]{4,3,2,1,0:T(8,128)(2,1)S(1)}, bf16[2,1,2,64,256]{4,3,2,1,0:T(8,128)(2,1)S(1)}, u32[]{:S(2)}, u32[]{:S(2)}) collective-permute-start(bf16[2,1,2,64,256]{4,3,2,1,0:T(8,128)(2,1)S(1)} %get-tuple-element.393), channel_id=1, source_target_pairs={{4,0},{8,4},{12,8},{16,12},{20,16},{24,20},{28,24},{5,1},{9,5},{13... | collective-permute-start | bytes 393224 | tf_op jit(solution)/shard_map/ppermute | solution.py:35
  249.0 24.6 %collective-permute-start.29 = (bf16[2,2,256]{2,1,0:T(2,128)(2,1)S(1)}, bf16[2,2,256]{2,1,0:T(2,128)(2,1)S(1)}, u32[]{:S(2)}, u32[]{:S(2)}) collective-permute-start(bf16[2,2,256]{2,1,0:T(2,128)(2,1)S(1)} %fusion.139), channel_id=1, source_target_pairs={{0,2},{2,0},{1,3},{3,1},{4,6},{6,4},{5,7},{7,5},{8,10},{10,8},{9,1... | collective-permute-start | bytes 6152 | tf_op jit(solution)/shard_map/ppermute | solution.py:41
  252.4 21.1 %collective-permute-start.28 = (bf16[2,1,256]{2,1,0:T(2,128)(2,1)S(1)}, bf16[2,1,256]{2,1,0:T(2,128)(2,1)S(1)}, u32[]{:S(2)}, u32[]{:S(2)}) collective-permute-start(bf16[2,1,256]{2,1,0:T(2,128)(2,1)S(1)} %get-tuple-element.418), channel_id=1, source_target_pairs={{0,6},{2,4},{4,10},{6,8},{8,14},{10,12},{12,18},{14,16},{16,22},{1... | collective-permute-start | bytes 3080 | tf_op jit(solution)/shard_map/ppermute | solution.py:499
  257.1 16.4 %collective-permute-start.30 = (bf16[2,1,256]{2,1,0:T(2,128)(2,1)S(1)}, bf16[2,1,256]{2,1,0:T(2,128)(2,1)S(1)}, u32[]{:S(2)}, u32[]{:S(2)}) collective-permute-start(bf16[2,1,256]{2,1,0:T(2,128)(2,1)S(1)} %get-tuple-element.419), channel_id=1, source_target_pairs={{4,2},{6,0},{8,6},{10,4},{12,10},{14,8},{16,14},{18,12},{20,18},{2... | collective-permute-start | bytes 3080 | tf_op jit(solution)/shard_map/ppermute | solution.py:499
  258.4 16.6 %collective-permute-start.26 = (bf16[2,1,2,64,256]{4,1,0,3,2:T(2,128)(2,1)}, bf16[2,1,2,64,256]{4,1,0,3,2:T(2,128)(2,1)S(1)}, u32[]{:S(2)}, u32[]{:S(2)}) collective-permute-start(bf16[2,1,2,64,256]{4,1,0,3,2:T(2,128)(2,1)} %get-tuple-element.391), channel_id=1, source_target_pairs={{0,4},{4,8},{8,12},{12,16},{16,20},{20,24},{24,28},{1,5},{5,9},{9,... | collective-permute-start | bytes 393224 | tf_op jit(solution)/shard_map/ppermute | solution.py:35
  263.9 11.2 %collective-permute-start.27 = (bf16[2,1,2,64,256]{4,1,0,3,2:T(2,128)(2,1)}, bf16[2,1,2,64,256]{4,1,0,3,2:T(2,128)(2,1)S(1)}, u32[]{:S(2)}, u32[]{:S(2)}) collective-permute-start(bf16[2,1,2,64,256]{4,1,0,3,2:T(2,128)(2,1)} %get-tuple-element.392), channel_id=1, source_target_pairs={{4,0},{8,4},{12,8},{16,12},{20,16},{24,20},{28,24},{5,1},{9,5},{13... | collective-permute-start | bytes 393224 | tf_op jit(solution)/shard_map/ppermute | solution.py:35
  295.3 50.8 %all-to-all-start.3 = ((bf16[8,2,1,32,1024]{4,3,1,2,0:T(8,128)(2,1)}), bf16[8,2,1,32,1024]{4,3,1,2,0:T(8,128)(2,1)}, u32[]{:S(2)}, u32[]{:S(2)}) async-start(bf16[8,2,1,32,1024]{4,3,1,2,0:T(8,128)(2,1)} %broadcast_in_dim.102), calls=%async_computation.3 | async-start | bytes 2097152 | tf_op jit(solution)/shard_map/all_to_all | solution.py:124
  300.2 40.6 %collective-permute-start.33 = (bf16[16,144,256]{2,1,0:T(8,128)(2,1)}, bf16[16,144,256]{2,1,0:T(8,128)(2,1)}, u32[]{:S(2)}, u32[]{:S(2)}) collective-permute-start(bf16[16,144,256]{2,1,0:T(8,128)(2,1)} %get-tuple-element.188), channel_id=1, source_target_pairs={{0,8},{8,0},{1,9},{9,1},{2,10},{10,2},{3,11},{11,3},{4,12},{12,4},... | collective-permute-start | bytes 3538952 | tf_op jit(solution)/shard_map/ppermute | solution.py:41
  303.1 40.4 %collective-permute-start.34 = (bf16[16,144,256]{2,1,0:T(8,128)(2,1)}, bf16[16,144,256]{2,1,0:T(8,128)(2,1)}, u32[]{:S(2)}, u32[]{:S(2)}) collective-permute-start(bf16[16,144,256]{2,1,0:T(8,128)(2,1)} %get-tuple-element.190), channel_id=1, source_target_pairs={{0,4},{4,0},{1,5},{5,1},{2,6},{6,2},{3,7},{7,3},{8,12},{12,8},{9,1... | collective-permute-start | bytes 3538952 | tf_op jit(solution)/shard_map/ppermute | solution.py:41
  356.2 7.3 %collective-permute-start.35 = (f32[2,1,66,128]{3,2,1,0:T(8,128)S(1)}, f32[2,1,66,128]{3,2,1,0:T(8,128)S(1)}, u32[]{:S(2)}, u32[]{:S(2)}) collective-permute-start(f32[2,1,66,128]{3,2,1,0:T(8,128)S(1)} %slice_bitcast_fusion.3), channel_id=1, source_target_pairs={{0,16},{1,17},{2,18},{3,19},{4,20},{5,21},{6,22},{7,23},{8,24},{9,... | collective-permute-start | bytes 202760 | tf_op jit(solution)/shard_map/ppermute | solution.py:35
  361.9 8.0 %collective-permute-start.36 = (f32[2,1,66,128]{3,2,1,0:T(8,128)S(1)}, f32[2,1,66,128]{3,2,1,0:T(8,128)S(1)}, u32[]{:S(2)}, u32[]{:S(2)}) collective-permute-start(f32[2,1,66,128]{3,2,1,0:T(8,128)S(1)} %slice_bitcast_fusion.2), channel_id=1, source_target_pairs={{16,0},{17,1},{18,2},{19,3},{20,4},{21,5},{22,6},{23,7},{24,8},{25... | collective-permute-start | bytes 202760 | tf_op jit(solution)/shard_map/ppermute | solution.py:35
  370.0 6.4 %collective-permute-start.37 = (f32[2,4,1,128]{3,2,1,0:T(1,128)S(1)}, f32[2,4,1,128]{3,2,1,0:T(1,128)S(1)}, u32[]{:S(2)}, u32[]{:S(2)}) collective-permute-start(f32[2,4,1,128]{3,2,1,0:T(1,128)S(1)} %get-tuple-element.390), channel_id=1, source_target_pairs={{0,2},{1,3},{4,6},{5,7},{8,10},{9,11},{12,14},{13,15},{16,18},{17,... | collective-permute-start | bytes 12296 | tf_op jit(solution)/shard_map/ppermute | solution.py:35
  374.2 31.2 %collective-permute-start.41 = (bf16[16,64,256]{2,1,0:T(8,128)(2,1)}, bf16[16,64,256]{2,1,0:T(8,128)(2,1)}, u32[]{:S(2)}, u32[]{:S(2)}) collective-permute-start(bf16[16,64,256]{2,1,0:T(8,128)(2,1)} %get-tuple-element.212), channel_id=1, source_target_pairs={{0,8},{8,0},{1,9},{9,1},{2,10},{10,2},{3,11},{11,3},{4,12},{12,4},... | collective-permute-start | bytes 1572872 | tf_op jit(solution)/shard_map/ppermute | solution.py:41
  374.3 33.1 %collective-permute-start.42 = (bf16[16,64,256]{2,1,0:T(8,128)(2,1)}, bf16[16,64,256]{2,1,0:T(8,128)(2,1)}, u32[]{:S(2)}, u32[]{:S(2)}) collective-permute-start(bf16[16,64,256]{2,1,0:T(8,128)(2,1)} %get-tuple-element.214), channel_id=1, source_target_pairs={{0,4},{4,0},{1,5},{5,1},{2,6},{6,2},{3,7},{7,3},{8,12},{12,8},{9,1... | collective-permute-start | bytes 1572872 | tf_op jit(solution)/shard_map/ppermute | solution.py:41
  375.8 33.6 %collective-permute-start.39 = (bf16[8,144,256]{2,1,0:T(8,128)(2,1)}, bf16[8,144,256]{2,1,0:T(8,128)(2,1)}, u32[]{:S(2)}, u32[]{:S(2)}) collective-permute-start(bf16[8,144,256]{2,1,0:T(8,128)(2,1)} %get-tuple-element.208), channel_id=1, source_target_pairs={{0,4},{4,0},{1,5},{5,1},{2,6},{6,2},{3,7},{7,3},{8,12},{12,8},{9,1... | collective-permute-start | bytes 1769480 | tf_op jit(solution)/shard_map/ppermute | solution.py:41
  376.4 34.3 %collective-permute-start.40 = (bf16[8,144,256]{2,1,0:T(8,128)(2,1)}, bf16[8,144,256]{2,1,0:T(8,128)(2,1)}, u32[]{:S(2)}, u32[]{:S(2)}) collective-permute-start(bf16[8,144,256]{2,1,0:T(8,128)(2,1)} %get-tuple-element.210), channel_id=1, source_target_pairs={{0,8},{8,0},{1,9},{9,1},{2,10},{10,2},{3,11},{11,3},{4,12},{12,4},... | collective-permute-start | bytes 1769480 | tf_op jit(solution)/shard_map/ppermute | solution.py:41
  393.1 43.9 %collective-permute-start.45 = (bf16[1,2,2,2,2,288,128]{6,5,4,3,2,1,0:T(8,128)(2,1)}, bf16[1,2,2,2,2,288,128]{6,5,4,3,2,1,0:T(8,128)(2,1)}, u32[]{:S(2)}, u32[]{:S(2)}) collective-permute-start(bf16[1,2,2,2,2,288,128]{6,5,4,3,2,1,0:T(8,128)(2,1)} %dynamic-slice_bitcast_fusion), channel_id=1, source_target_pairs={{0,2},{2,0},{1,3},{3,1},{4,6},{6,4},{5,7},{7,5},{8,10},{10,8},{9,1... | collective-permute-start | bytes 3538952 | tf_op jit(solution)/shard_map/ppermute | solution.py:41
  412.8 6.7 %collective-permute-start.47 = (bf16[8,64,256]{2,1,0:T(8,128)(2,1)}, bf16[8,64,256]{2,1,0:T(8,128)(2,1)}, u32[]{:S(2)}, u32[]{:S(2)}) collective-permute-start(bf16[8,64,256]{2,1,0:T(8,128)(2,1)} %get-tuple-element.220), channel_id=1, source_target_pairs={{0,4},{4,0},{1,5},{5,1},{2,6},{6,2},{3,7},{7,3},{8,12},{12,8},{9,1... | collective-permute-start | bytes 786440 | tf_op jit(solution)/shard_map/ppermute | solution.py:41
  415.4 6.6 %collective-permute-start.48 = (bf16[8,64,256]{2,1,0:T(8,128)(2,1)}, bf16[8,64,256]{2,1,0:T(8,128)(2,1)S(1)}, u32[]{:S(2)}, u32[]{:S(2)}) collective-permute-start(bf16[8,64,256]{2,1,0:T(8,128)(2,1)} %get-tuple-element.222), channel_id=1, source_target_pairs={{0,8},{8,0},{1,9},{9,1},{2,10},{10,2},{3,11},{11,3},{4,12},{12,4},... | collective-permute-start | bytes 786440 | tf_op jit(solution)/shard_map/ppermute | solution.py:41
  416.9 18.5 %collective-permute-start.43 = (bf16[1,2,2,2,2,144,128]{6,5,4,3,2,1,0:T(8,128)(2,1)S(1)}, bf16[1,2,2,2,2,144,128]{6,5,4,3,2,1,0:T(8,128)(2,1)S(1)}, u32[]{:S(2)}, u32[]{:S(2)}) collective-permute-start(bf16[1,2,2,2,2,144,128]{6,5,4,3,2,1,0:T(8,128)(2,1)S(1)} %fusion.50), channel_id=1, source_target_pairs={{0,2},{2,0},{1,3},{3,1},{4,6},{6,4},{5,7},{7,5},{8,10},{10,8},{9,1... | collective-permute-start | bytes 1769480 | tf_op jit(solution)/shard_map/ppermute | solution.py:41
  423.8 43.5 %collective-permute-start.49 = (bf16[4,416,256]{2,1,0:T(8,128)(2,1)}, bf16[4,416,256]{2,1,0:T(8,128)(2,1)}, u32[]{:S(2)}, u32[]{:S(2)}) collective-permute-start(bf16[4,416,256]{2,1,0:T(8,128)(2,1)} %pad_maximum_fusion.18), channel_id=1, source_target_pairs={{0,2},{2,0},{1,3},{3,1},{4,6},{6,4},{5,7},{7,5},{8,10},{10,8},{9,1... | collective-permute-start | bytes 2555912 | tf_op jit(solution)/shard_map/ppermute | solution.py:41
  436.9 23.6 %collective-permute-start.44 = (bf16[1,2,2,2,144,128]{5,4,3,2,1,0:T(8,128)(2,1)S(1)}, bf16[1,2,2,2,144,128]{5,4,3,2,1,0:T(8,128)(2,1)S(1)}, u32[]{:S(2)}, u32[]{:S(2)}) collective-permute-start(bf16[1,2,2,2,144,128]{5,4,3,2,1,0:T(8,128)(2,1)S(1)} %fusion.71), channel_id=1, source_target_pairs={{0,16},{16,0},{1,17},{17,1},{2,18},{18,2},{3,19},{19,3},{4,20},{20... | collective-permute-start | bytes 884744 | tf_op jit(solution)/shard_map/ppermute | solution.py:41
  440.8 31.0 %collective-permute-start.46 = (bf16[1,2,2,2,288,128]{5,4,3,2,1,0:T(8,128)(2,1)}, bf16[1,2,2,2,288,128]{5,4,3,2,1,0:T(8,128)(2,1)}, u32[]{:S(2)}, u32[]{:S(2)}) collective-permute-start(bf16[1,2,2,2,288,128]{5,4,3,2,1,0:T(8,128)(2,1)} %fusion.51), channel_id=1, source_target_pairs={{0,16},{16,0},{1,17},{17,1},{2,18},{18,2},{3,19},{19,3},{4,20},{20... | collective-permute-start | bytes 1769480 | tf_op jit(solution)/shard_map/ppermute | solution.py:41
  461.9 14.2 %all-to-all-start.4 = ((bf16[8,144,128]{2,1,0:T(8,128)(2,1)}), bf16[8,144,128]{2,1,0:T(8,128)(2,1)}, u32[]{:S(2)}, u32[]{:S(2)}) async-start(bf16[8,144,128]{2,1,0:T(8,128)(2,1)} %bitcast.131), calls=%async_computation.4 | async-start | bytes 589824 | tf_op jit(solution)/shard_map/all_to_all | solution.py:812
  469.1 22.6 %collective-permute-start.50 = (bf16[2,416,256]{2,1,0:T(8,128)(2,1)}, bf16[2,416,256]{2,1,0:T(8,128)(2,1)}, u32[]{:S(2)}, u32[]{:S(2)}) collective-permute-start(bf16[2,416,256]{2,1,0:T(8,128)(2,1)} %add_convert_fusion.4), channel_id=1, source_target_pairs={{0,16},{16,0},{1,17},{17,1},{2,18},{18,2},{3,19},{19,3},{4,20},{20... | collective-permute-start | bytes 1277960 | tf_op jit(solution)/shard_map/ppermute | solution.py:41
  476.1 27.1 %all-to-all-start.5 = ((bf16[8,288,128]{2,1,0:T(8,128)(2,1)}), bf16[8,288,128]{2,1,0:T(8,128)(2,1)S(1)}, u32[]{:S(2)}, u32[]{:S(2)}) async-start(bf16[8,288,128]{2,1,0:T(8,128)(2,1)} %bitcast.376), calls=%async_computation.5 | async-start | bytes 1179648 | tf_op jit(solution)/shard_map/all_to_all | solution.py:802
  501.0 6.4 %collective-permute-start.56 = (bf16[416,256]{1,0:T(8,128)(2,1)S(1)}, bf16[416,256]{1,0:T(8,128)(2,1)S(1)}, u32[]{:S(2)}, u32[]{:S(2)}) collective-permute-start(bf16[416,256]{1,0:T(8,128)(2,1)S(1)} %slice_bitcast_fusion), channel_id=1, source_target_pairs={{0,1},{1,0},{2,3},{3,2},{4,5},{5,4},{6,7},{7,6},{8,9},{9,8},{10,11... | collective-permute-start | bytes 638984 | tf_op jit(solution)/shard_map/ppermute | solution.py:41
  (79 other events, 419.8 us)

commit v3 on v2

--- a/solution.py
+++ b/solution.py
@@ -166,14 +166,31 @@
     return jnp.concatenate([values, swapped(values, axis)], axis=0)
 
 
-def kept_on(own, away, axis):
-    got = swapped(away, axis)
-    half = own.shape[0] // 2
-    sums = [
-        v.astype(f32) + w.astype(f32)
-        for v, w in ((own[:half], got[:half]), (own[half:], got[half:]))
-    ]
-    return sums[0].astype(bf16), sums[1].astype(bf16)
+def sent(parts, first_axis, second_axis):
+    if len(parts) == 1:
+        return parts
+    return parts[0], swapped(parts[1], first_axis), parts[2], swapped(parts[3], second_axis)
+
+
+def added(parts):
+    out = ()
+    for own, got in (parts[:2], parts[2:]):
+        half = own.shape[0] // 2
+        for v, w in ((own[:half], got[:half]), (own[half:], got[half:])):
+            out += ((v.astype(f32) + w.astype(f32)).astype(bf16),)
+    return out
+
+
+def after(earlier, *parts):
+    own = [part[::2] if isinstance(part, tuple) else (part,) for part in parts]
+    earlier, own = lax.optimization_barrier((earlier, own))
+    out = [earlier]
+    for part, kept in zip(parts, own):
+        if isinstance(part, tuple):
+            out.append((kept[0], part[1], kept[1], part[3]))
+        else:
+            out.append(kept[0])
+    return out
 
 
 def place(chunk, me, first):
@@ -183,30 +200,50 @@
     return high * 16 + low * 8 + x * 4 + zh * 2 + core
 
 
-def pieces_of(rows, cut, zhs):
-    if zhs != 2:
-        return [(0, None, 0, rows, 0)]
-    return cut
-
-
-def chunk_list(r3, ru, zhs):
+def chunk_list(r3, ru):
     cut = (r3 + ru) // 2
     merge, up = [], []
     for chunk in range(32):
         merge.append((0, (chunk, "y"), 0, cut, r3 * chunk))
-        merge.append((1, (chunk, "zl"), 0, r3 - cut, r3 * chunk + cut))
-        up.append((0, (chunk, "zl"), r3 - cut, ru, ru * chunk))
-    return pieces_of(32 * r3, merge, zhs), pieces_of(32 * ru, up, zhs)
-
-
-def copies(pieces, me, sources, target, sems):
-    made = []
-    for i, (which, spot, start, count, to) in enumerate(pieces):
-        at = 0 if spot is None else place(spot[0], me, spot[1])
-        there = sources[which].at[at, pl.ds(start, count), :]
-        here = target.at[pl.ds(to, count), :]
-        made.append(pltpu.make_async_copy(there, here, sems.at[i]))
-    return made
+        merge.append((2, (chunk, "zl"), 0, r3 - cut, r3 * chunk + cut))
+        up.append((2, (chunk, "zl"), r3 - cut, ru, ru * chunk))
+    return merge, up
+
+
+def in_place(me, sources, merge_pieces, up_pieces):
+    lists = (merge_pieces, up_pieces)
+    count = len(merge_pieces) + len(up_pieces)
+
+    def body(me_ref, *rest):
+        source_refs, targets, sems = rest[:4], rest[4:6], rest[6]
+        waits = []
+        for pieces, target in zip(lists, targets):
+            for which, spot, start, rows, to in pieces:
+                sem = sems.at[len(waits)]
+                here = target.at[pl.ds(to, rows), :]
+                at = place(spot[0], me_ref, spot[1])
+                for side in range(2):
+                    inside = at - 16 * side
+
+                    @pl.when((inside >= 0) & (inside < 16))
+                    def _(source=source_refs[which + side], inside=inside, start=start, rows=rows, here=here, sem=sem):
+                        there = source.at[inside, pl.ds(start, rows), :]
+                        pltpu.make_async_copy(there, here, sem).start()
+
+                there = source_refs[which].at[0, pl.ds(start, rows), :]
+                waits.append(pltpu.make_async_copy(there, here, sem))
+        for copy in waits:
+            copy.wait()
+
+    rows = [sum(piece[3] for piece in pieces) for pieces in lists]
+    return on_chip(
+        body,
+        (me, *sources),
+        tuple(jax.ShapeDtypeStruct((n, HALF), bf16) for n in rows),
+        [pltpu.SemaphoreType.DMA((count,))],
+        ("saaaa", "vv"),
+        0,
+    )
 
 
 def send_out(pieces, me, targets, source, sems):
@@ -243,19 +280,14 @@
     )(*ins)
 
 
-def up_on_chip(me, own, other, source, bias, pieces):
-    def body(me_ref, own_ref, other_ref, source_ref, bias_ref, ups_ref, kernel_ref, act_ref, sems):
-        made = copies(pieces, me_ref, (source_ref,), kernel_ref, sems)
-        for copy in made:
-            copy.start()
+def up_on_chip(me, own, other, kernel, bias):
+    def body(me_ref, own_ref, other_ref, kernel_ref, bias_ref, ups_ref, act_ref):
         core = me_ref[4]
         mine = pl.ds(pl.multiple_of(core * 32, 32), 32)
         yours = pl.ds(pl.multiple_of((1 - core) * 32, 32), 32)
         for image in range(2):
             act_ref[image, mine, :] = own_ref[image]
             act_ref[image, yours, :] = other_ref[image]
-        for copy in made:
-            copy.wait()
         values = act_ref[...].reshape(128, C1)
         for tap in range(4):
             got = jnp.dot(
@@ -267,14 +299,13 @@
 
     return on_chip(
         body,
-        (me, own, other, source, bias),
+        (me, own, other, kernel, bias),
         (
             jax.ShapeDtypeStruct((2, 2, 2, 64, HALF), bf16),
-            jax.ShapeDtypeStruct((4 * C1, HALF), bf16),
             jax.ShapeDtypeStruct((2, 64, C1), bf16),
         ),
-        [pltpu.SemaphoreType.DMA((len(pieces),))],
-        ("svvav", "vvv"),
+        [],
+        ("svvvv", "vv"),
         2 * 128 * C1 * 4 * HALF,
     )
 
@@ -301,35 +332,29 @@
     return cells.reshape(256, cells.shape[-1])
 
 
-def merge_on_chip(me, own, other, own_sides, other_sides, skip, sources, bias, head, pieces):
-    count = len(sources)
-
-    def body(me_ref, own_ref, other_ref, own_sides_ref, other_sides_ref, skip_ref, bias_ref, head_ref, *rest):
-        source_refs = rest[:count]
-        pre_ref, logits_ref, planes_ref, kernel, sems = rest[count:]
-        made = copies(pieces, me_ref, source_refs, kernel, sems)
-        for copy in made:
-            copy.start()
-        core = me_ref[4]
-        planes_in(planes_ref, slice(0, HALF), own_ref, own_sides_ref)
-        planes_in(planes_ref, slice(HALF, C0), other_ref, other_sides_ref)
-        planes_ref[:, :, :, :, C0:] = skip_ref[...]
-        for copy in made:
-            copy.wait()
+def merge_on_chip(me, own, other, own_sides, other_sides, skip, skip_sides, kernel, bias, head):
+    def body(me_ref, own_ref, other_ref, own_sides_ref, other_sides_ref, skip_ref, skip_sides_ref, kernel_ref, bias_ref, head_ref, pre_ref, logits_ref, planes_ref):
+        low, high = slice(0, HALF), slice(HALF, C0)
+
+        @pl.when(me_ref[4] == 0)
+        def _():
+            planes_in(planes_ref, low, own_ref, own_sides_ref)
+            planes_in(planes_ref, high, other_ref, other_sides_ref)
+
+        @pl.when(me_ref[4] == 1)
+        def _():
+            planes_in(planes_ref, high, own_ref, own_sides_ref)
+            planes_in(planes_ref, low, other_ref, other_sides_ref)
+
+        planes_in(planes_ref, slice(C0, 2 * C0), skip_ref, skip_sides_ref)
         for image in range(2):
             total = jnp.broadcast_to(bias_ref[...], (256, HALF))
             for tap in range(9):
-                base = tap * 2 * C0
-                for lanes, start, size in (
-                    (slice(0, HALF), pl.multiple_of(base + core * HALF, HALF), HALF),
-                    (slice(HALF, C0), pl.multiple_of(base + (1 - core) * HALF, HALF), HALF),
-                    (slice(C0, 2 * C0), base + C0, C0),
-                ):
-                    total = total + jnp.dot(
-                        tapped(planes_ref, image, tap, lanes),
-                        kernel[pl.ds(start, size), :],
-                        preferred_element_type=f32,
-                    )
+                total = total + jnp.dot(
+                    tapped(planes_ref, image, tap, slice(0, 2 * C0)),
+                    kernel_ref[tap * 2 * C0 : (tap + 1) * 2 * C0, :],
+                    preferred_element_type=f32,
+                )
             rows = slice(image * 256, (image + 1) * 256)
             pre_ref[rows, :] = total
             act = jax.nn.gelu(total).astype(bf16)
@@ -337,31 +362,22 @@
 
     return on_chip(
         body,
-        (me, own, other, own_sides, other_sides, skip, bias, head, *sources),
+        (me, own, other, own_sides, other_sides, skip, skip_sides, kernel, bias, head),
         (
             jax.ShapeDtypeStruct((512, HALF), f32),
             jax.ShapeDtypeStruct((512, 128), f32),
             jax.ShapeDtypeStruct((2, 4, 4, 64, 2 * C0), bf16),
         ),
-        [pltpu.VMEM((18 * C0, HALF), bf16), pltpu.SemaphoreType.DMA((len(pieces),))],
-        ("svvvvvvv" + "a" * count, "vvv"),
+        [],
+        ("svvvvvvvvv", "vvv"),
         2 * 512 * 18 * C0 * HALF,
     )
 
 
-def ups_grad_on_chip(me, rows, sides, sources, pieces):
-    count = len(sources)
-
-    def body(me_ref, rows_ref, sides_ref, *rest):
-        source_refs = rest[:count]
-        own_ref, away_ref, planes, kernel, sems = rest[count:]
-        made = copies(pieces, me_ref, source_refs, kernel, sems)
-        for copy in made:
-            copy.start()
+def ups_grad_on_chip(me, rows, sides, kernel):
+    def body(me_ref, rows_ref, sides_ref, kernel_ref, own_ref, away_ref, planes):
         core = me_ref[4]
         planes_in(planes, slice(0, HALF), rows_ref, sides_ref)
-        for copy in made:
-            copy.wait()
         for image in range(2):
             lines = slice(image * 256, (image + 1) * 256)
             for target, half in ((own_ref, core), (away_ref, 1 - core)):
@@ -370,7 +386,7 @@
                     start = pl.multiple_of((8 - tap) * 2 * C0 + half * HALF, HALF)
                     total = total + lax.dot_general(
                         tapped(planes, image, tap, slice(0, HALF)),
-                        kernel[pl.ds(start, HALF), :],
+                        kernel_ref[pl.ds(start, HALF), :],
                         (((1,), (1,)), ((), ())),
                         preferred_element_type=f32,
                     )
@@ -378,14 +394,10 @@
 
     return on_chip(
         body,
-        (me, rows, sides, *sources),
+        (me, rows, sides, kernel),
         (jax.ShapeDtypeStruct((512, HALF), f32), jax.ShapeDtypeStruct((512, HALF), bf16)),
-        [
-            pltpu.VMEM((2, 4, 4, 64, HALF), bf16),
-            pltpu.VMEM((18 * C0, HALF), bf16),
-            pltpu.SemaphoreType.DMA((len(pieces),)),
-        ],
-        ("svv" + "a" * count, "vv"),
+        [pltpu.VMEM((2, 4, 4, 64, HALF), bf16)],
+        ("svvv", "vv"),
         2 * 512 * 9 * C0 * HALF,
     )
 
@@ -394,23 +406,16 @@
     def body(me_ref, planes_ref, grad_ref, *rest):
         out_refs = rest[: len(shapes)]
         whole, sems = rest[len(shapes) :]
-        core = me_ref[4]
         for tap in range(9):
-            base = tap * 2 * C0
-            for lanes, start, size in (
-                (slice(0, HALF), pl.multiple_of(base + core * HALF, HALF), HALF),
-                (slice(HALF, C0), pl.multiple_of(base + (1 - core) * HALF, HALF), HALF),
-                (slice(C0, 2 * C0), base + C0, C0),
-            ):
-                total = jnp.zeros((size, HALF), f32)
-                for image in range(2):
-                    total = total + lax.dot_general(
-                        tapped(planes_ref, image, tap, lanes),
-                        grad_ref[image * 256 : (image + 1) * 256, :],
-                        (((0,), (0,)), ((), ())),
-                        preferred_element_type=f32,
-                    )
-                whole[pl.ds(start, size), :] = total.astype(bf16)
+            total = jnp.zeros((2 * C0, HALF), f32)
+            for image in range(2):
+                total = total + lax.dot_general(
+                    tapped(planes_ref, image, tap, slice(0, 2 * C0)),
+                    grad_ref[image * 256 : (image + 1) * 256, :],
+                    (((0,), (0,)), ((), ())),
+                    preferred_element_type=f32,
+                )
+            whole[tap * 2 * C0 : (tap + 1) * 2 * C0, :] = total.astype(bf16)
         send_out(pieces, me_ref, out_refs, whole, sems)
 
     return on_chip(
@@ -446,6 +451,89 @@
     )
 
 
+def side_list(first_rows, rows, chunks):
+    return [
+        ((chunk >> 1) & 1, (chunk >> 2) * 2 + (chunk & 1), rows * chunk, rows, first_rows)
+        for chunk in range(chunks)
+    ]
+
+
+def two_ways(pieces, me, stays, goes, source, sems):
+    for i, (side, at, start, count, to) in enumerate(pieces):
+        here = source.at[pl.ds(start, count), :]
+        for target, wanted in ((stays, side), (goes, 1 - side)):
+
+            @pl.when(me[3] == wanted)
+            def _(here=here, target=target, at=at, to=to, count=count, i=i):
+                there = target.at[at, pl.ds(to, count), :]
+                pltpu.make_async_copy(here, there, sems.at[i]).start()
+
+    for i, (side, at, start, count, to) in enumerate(pieces):
+        here = source.at[pl.ds(start, count), :]
+        pltpu.make_async_copy(here, stays.at[at, pl.ds(to, count), :], sems.at[i]).wait()
+
+
+def second_grad_on_chip(me, cells, grad, rows, chunks):
+    images, width, outs = cells.shape[1], cells.shape[4], grad.shape[3]
+    tiles = outs // 128
+    pieces = side_list(0, rows, chunks)
+
+    def body(me_ref, cells_ref, grad_ref, stays_ref, goes_ref, wide, narrow, sems):
+        upstream = grad_ref[...].reshape(images * 256, outs)
+        for tap in range(9):
+            values = cells_ref[tap % 3, :, tap // 3 : tap // 3 + 4].reshape(images * 256, width)
+            got = lax.dot_general(
+                values, upstream, (((0,), (0,)), ((), ())), preferred_element_type=f32
+            )
+            for tile in range(tiles):
+                wide[:, tile, :] = got[:, tile * 128 : (tile + 1) * 128]
+            narrow[tap * width * tiles : (tap + 1) * width * tiles, :] = (
+                wide[...].reshape(width * tiles, 128).astype(bf16)
+            )
+        two_ways(pieces, me_ref, stays_ref, goes_ref, narrow, sems)
+
+    return on_chip(
+        body,
+        (me, cells, grad),
+        (jax.ShapeDtypeStruct((chunks // 2, rows, 128), bf16),) * 2,
+        [
+            pltpu.VMEM((width, tiles, 128), f32),
+            pltpu.VMEM((9 * width * tiles, 128), bf16),
+            pltpu.SemaphoreType.DMA((chunks,)),
+        ],
+        ("svv", "aa"),
+        2 * images * 256 * 9 * width * outs,
+    )
+
+
+def first_grad_on_chip(me, cells, grad, rows, chunks):
+    images, width, outs = cells.shape[1], cells.shape[4], grad.shape[3]
+    pieces = side_list(0, rows, chunks)
+
+    def body(me_ref, cells_ref, grad_ref, stays_ref, goes_ref, narrow, sems):
+        upstream = grad_ref[...].reshape(images * 256, outs)
+        for tap in range(9):
+            values = cells_ref[tap % 3, :, tap // 3 : tap // 3 + 4].reshape(images * 256, width)
+            got = lax.dot_general(
+                values, upstream, (((0,), (0,)), ((), ())), preferred_element_type=f32
+            )
+            narrow[tap * width : (tap + 1) * width, :] = got.astype(bf16)
+        two_ways(pieces, me_ref, stays_ref, goes_ref, narrow, sems)
+
+    return on_chip(
+        body,
+        (me, cells, grad),
+        (jax.ShapeDtypeStruct((chunks // 2, rows, 128), bf16),) * 2,
+        [pltpu.VMEM((9 * width, 128), bf16), pltpu.SemaphoreType.DMA((chunks,))],
+        ("svv", "aa"),
+        2 * images * 256 * 9 * width * outs,
+    )
+
+
+def by_shift(cells):
+    return jnp.stack([cells[:, :, shift : shift + 64] for shift in range(3)])
+
+
 def split_list(rows, zhs):
     if zhs != 2:
         return [(0, None, 0, 32 * rows, 0)], [(1, 32 * rows, HALF)]
@@ -457,27 +545,8 @@
     return pieces, [(16, half, HALF)] * 4
 
 
-def first_sum(parts):
-    if len(parts) == 1:
-        return parts
-    return kept_on(*parts[:2], "zl") + kept_on(*parts[2:], "y")
-
-
-def second_sum(parts):
-    if len(parts) == 1:
-        return parts
-    first, second = kept_on(*parts[:2], "y"), kept_on(*parts[2:], "zl")
-    return tuple(jnp.concatenate(pair, axis=1) for pair in zip(first, second))
-
-
-def cross_sum(parts):
-    return kept_on(*parts, "x") if len(parts) == 2 else parts
-
-
-def last_sum(parts):
-    if len(parts) == 2:
-        return parts[0].astype(f32) + swapped(parts[1], "zh").astype(f32)
-    whole = parts[0].reshape(8 * size_of("zh"), 2, -1, HALF)
+def last_sum(whole):
+    whole = whole.reshape(8 * size_of("zh"), 2, -1, HALF)
     whole = lax.psum_scatter(whole, CHIPS, scatter_dimension=0)
     return in_order_back(whole).astype(f32)
 
@@ -488,26 +557,26 @@
     return jnp.concatenate([own, away], axis=0)
 
 
-def crossed(values, step):
-    count = size_of("zh") * 4
-    moves = [
-        (2 * i + side, 2 * (i + step) + 1 - side)
-        for i in range(count)
-        for side in range(2)
-        if 0 <= i + step < count
-    ]
-    return lax.ppermute(values, ROWS + ("x",), moves)
-
-
 def halo(cells):
+    width = cells.shape[-1]
     left_chip = lax.axis_index("x") == 0
     edge = jnp.where(left_chip, cells[:, :, 1, 63], cells[:, :, 0, 0])
-    above = shifted(cells[:, 1:], ROWS, 1)
-    below = shifted(cells[:, :1], ROWS, -1)
+    beside = swapped(edge, "x")
+
+    def with_side(row):
+        return jnp.concatenate(
+            [cells[:, row].reshape(-1, width), beside[:, row], jnp.zeros((14, width), bf16)], axis=0
+        )
+
+    above = shifted(with_side(1), ROWS, 1)
+    below = shifted(with_side(0), ROWS, -1)
+    shape = (2, 1, 2, 64, width)
+    rows = jnp.concatenate(
+        [above[:256].reshape(shape), cells, below[:256].reshape(shape)], axis=1
+    )
     beside = jnp.concatenate(
-        [crossed(edge[:, 1:], 1), swapped(edge, "x"), crossed(edge[:, :1], -1)], axis=1
-    )
-    rows = jnp.concatenate([above, cells, below], axis=1)
+        [above[256:258, None], beside, below[256:258, None]], axis=1
+    )
     none = jnp.zeros_like(beside)
     sides = jnp.stack([jnp.where(left_chip, none, beside), jnp.where(left_chip, beside, none)])
     return rows, sides
@@ -563,21 +632,18 @@
     low_one = jnp.einsum("rc,cqm->qrm", conv_first.astype(bf16).reshape(r1, C1), sorting)
     low_two = conv_second.astype(bf16)
     block = features.reshape(1, -1, 128)
-    lead = [jnp.full((8, 16, 128), count_own, bf16), low_one]
-    early = 0
+    bundle = [jnp.full((8, 16, 128), count_own, bf16), low_one]
+    kernel_rows = 16 + r1
     if even:
         low_two = low_two.reshape(r2 // 8, 8, C1 // 128, 128).transpose(1, 0, 2, 3)
-        low_two = low_two.reshape(8, r2, 128)
-        early = (r2 - r1 - 16) // 2 // 16 * 16
-        lead.append(low_two[:, :early])
-    lead_rows = 16 + r1 + early
-    lead = jnp.concatenate(lead + [jnp.broadcast_to(block, (8,) + block.shape[1:])], axis=1)
-    lead, low_two, conv_merge, up_conv, skip_feat, labels, pixel_weight = lax.optimization_barrier(
-        (lead, low_two, conv_merge, up_conv, skip_feat, labels, pixel_weight)
-    )
-
-    lead = lax.all_to_all(lead, MEMBERS, 0, 0, tiled=True)
-    tail = lax.all_to_all(low_two[:, early:], MEMBERS, 0, 0, tiled=True) if even else low_two
+        bundle.append(low_two.reshape(8, r2, 128))
+        kernel_rows += r2
+    bundle.append(jnp.broadcast_to(block, (8,) + block.shape[1:]))
+    bundle, conv_merge, up_conv, skip_feat, labels, pixel_weight = lax.optimization_barrier(
+        (jnp.concatenate(bundle, axis=1), conv_merge, up_conv, skip_feat, labels, pixel_weight)
+    )
+
+    bundle = lax.all_to_all(bundle, MEMBERS, 0, 0, tiled=True)
     r3 = conv_merge.shape[0] // C0
     ru = up_conv.shape[0] // C0
     zhs = size_of("zh")
@@ -587,45 +653,43 @@
     )
     low_chip = in_order_back(low_chip.reshape(r3 + ru, 2, HALF).transpose(1, 0, 2))
     low_chip = jnp.concatenate([low_chip[:1], swapped(low_chip[1:], "core")], axis=0)
-    merge_pieces, up_pieces = chunk_list(r3 * zhs // 2, ru * zhs // 2, zhs)
+    merge_pieces, up_pieces = chunk_list(r3, ru)
     if zhs == 2:
         low_chip = joined_on(low_chip, "zh")
-    skip = padded(pair_gather(skip_feat, "core", 2), ROWS, 1, 1)
+    skip = skip_feat.reshape(2, 2, 32, 2, C0).swapaxes(2, 3)
+    skip_cells = pair_gather(skip, "core", 3)
     marks = pair_gather(jnp.stack([labels, valid_mask * pixel_weight]), "core", 3)
-    lead, low_chip, skip, marks = lax.optimization_barrier((lead, low_chip, skip, marks))
-
-    feat = lead[:, lead_rows:].reshape((4, 2) + features.shape[:1] + features.shape[2:])
+    marks = marks.reshape(2, 2, 2, 64, 2).swapaxes(3, 4)
+    bundle, low_chip, skip_cells = lax.optimization_barrier((bundle, low_chip, skip_cells))
+
+    feat = bundle[:, kernel_rows:].reshape((4, 2) + features.shape[:1] + features.shape[2:])
     feat = feat.transpose(2, 0, 1, 3, 4)
     feat = feat.reshape(feat.shape[0], 4, 2 * feat.shape[3], C0)
-    lead = lead[:, :lead_rows].reshape(-1, 128)
+    kernels = bundle[:, :kernel_rows].reshape(-1, 128)
     if zhs == 2:
         edge = jnp.where(zh == 0, feat[:, -2:], feat[:, :2])
-        got = swapped(jnp.concatenate([lead, edge.reshape(-1, 128)], axis=0), "zh")
-        edge = got[8 * lead_rows :].reshape(edge.shape)
+        got = swapped(jnp.concatenate([kernels, edge.reshape(-1, 128)], axis=0), "zh")
+        low_chip = joined_on(low_chip, "x")
+        cut = (r3 + ru) // 2
+        first, second = low_chip[:, :cut], low_chip[:, cut:]
+        first, second = (first, swapped(first, "y")), (second, swapped(second, "zl"))
+        feat, kernels, got = lax.optimization_barrier((feat, kernels, got))
+        edge = got[8 * kernel_rows :].reshape(edge.shape)
         none = jnp.zeros_like(edge)
         feat = jnp.concatenate(
             [jnp.where(zh == 0, none, edge), feat, jnp.where(zh == 0, edge, none)], axis=1
         )
-        lead = in_order(lead, got[: 8 * lead_rows], "zh", 0)
+        kernels = in_order(kernels, got[: 8 * kernel_rows], "zh", 0)
     else:
         feat = padded(feat, "zh", 1, 2)
-        lead = lax.all_gather(lead, "zh", axis=0, tiled=True)
-    skip = padded(skip, "x", 2, 1)
-    skip = jnp.stack(
-        [skip[:, :, 0:128:2], skip[:, :, 1:129:2], skip[:, :, 2:130:2], skip[:, :, 3:130:2]], axis=2
-    )
-    marks = marks.reshape(2, 2, 2, 64, 2).swapaxes(3, 4)
-    first = second = jnp.zeros((), bf16)
-    if zhs == 2:
-        low_chip = joined_on(low_chip, "x")
-        cut = (r3 + ru) // 2
-        first, second = low_chip[:, :cut], low_chip[:, cut:]
-    feat, skip, lead, tail, first, second, marks = lax.optimization_barrier(
-        (feat, skip, lead, tail, first, second, marks)
-    )
-
+        kernels = lax.all_gather(kernels, "zh", axis=0, tiled=True)
+
+    kernels = kernels.reshape(8 * zhs, kernel_rows, 128)
+    lead = kernels[:, : 16 + r1].reshape(-1, 128)
     edge = jnp.where(x == 0, feat[:, :, -2:], feat[:, :, :2])
     got = swapped(jnp.concatenate([lead, edge.reshape(-1, 128)], axis=0), "x")
+    if zhs == 2:
+        got, first, second = lax.optimization_barrier((got, first, second))
     edge = got[lead.shape[0] :].reshape(edge.shape)
     none = jnp.zeros_like(edge)
     feat = jnp.concatenate(
@@ -637,30 +701,23 @@
         return jnp.where(x == 0, both, both[::-1]).transpose(1, 2, 3, 0, 4, 5, 6)
 
     lead = ordered(lead, got[: lead.shape[0]])
+    count_all = jnp.sum(lead[..., 0, 0].astype(f32))
+    kernel_one = lead[..., 16:, :].reshape(3, 3, C0, C1 // 8)
     if even:
-        tail = tail.reshape(-1, 128)
-        if zhs == 2:
-            tail = in_order(tail, swapped(tail, "zh"), "zh", 0)
-        else:
-            tail = lax.all_gather(tail, "zh", axis=0, tiled=True)
-    if zhs == 2:
-        first = joined_on(first, "y")
-        second = joined_on(second, "zl")
-    feat, lead, tail, first, second = lax.optimization_barrier((feat, lead, tail, first, second))
-
-    count_all = jnp.sum(lead[..., 0, 0].astype(f32))
-    kernel_one = lead[..., 16 : 16 + r1, :].reshape(3, 3, C0, C1 // 8)
-    if even:
-        tail = ordered(tail, swapped(tail, "x"))
-        kernel_two = jnp.concatenate([lead[..., 16 + r1 :, :], tail], axis=5)
+        kernel_two = kernels[:, 16 + r1 :].reshape(-1, 128)
+        kernel_two = ordered(kernel_two, swapped(kernel_two, "x"))
     else:
-        low_two = lax.all_gather(tail.reshape(r2, C1), AXES, axis=0, tiled=True)
+        low_two = lax.all_gather(low_two.reshape(r2, C1), AXES, axis=0, tiled=True)
         low_two = low_two.reshape(-1, 8, C1)
         kernel_two = lax.dynamic_index_in_dim(low_two, member, axis=1, keepdims=False)
     kernel_two = kernel_two.reshape(3, 3, C1 // 8, C1)
     if zhs == 2:
-        first = joined_on(first, "zl")
-        second = joined_on(second, "y")
+        first, second = jnp.concatenate(first, axis=0), jnp.concatenate(second, axis=0)
+        first = (first, swapped(first, "zl"))
+        second = (second, swapped(second, "y"))
+    else:
+        first = second = jnp.zeros((), bf16)
+
     bias_one = lax.dynamic_index_in_dim(
         biases[:C1].reshape(C1 // 8, 8), member, axis=1, keepdims=False
     )
@@ -683,21 +740,24 @@
     inside = (row_in[:, None] & col_in[None, :])[None, :, :, None]
     act_one = jnp.where(inside, jax.nn.gelu(pre_one), 0.0).astype(bf16)
     part_two = convolve(act_one, kernel_two)
-    part_two, first, second = lax.optimization_barrier((part_two, first, second))
+    feat_shifts, act_shifts = by_shift(feat[:, 1:-1, 1:-1]), by_shift(act_one)
+    skip, skip_sides = halo(skip_cells)
+    part_two, first, second, skip, skip_sides, marks = lax.optimization_barrier(
+        (part_two, first, second, skip, skip_sides, marks)
+    )
     if zhs == 2:
-        merge_sources, up_source = (first, second), second
+        kernel_merge, kernel_up = in_place(me, first + second, merge_pieces, up_pieces)
     else:
         low_chip = jnp.where(core == 0, low_chip, low_chip[::-1])
         low_chip = lax.all_gather(low_chip, CHIPS, axis=0, tiled=True)
-        merge_sources = (low_chip[:, :r3].reshape(1, -1, HALF),)
-        up_source = low_chip[:, r3:].reshape(1, -1, HALF)
+        kernel_merge = low_chip[:, :r3].reshape(-1, HALF)
+        kernel_up = low_chip[:, r3:].reshape(-1, HALF)
     pre_two = group_scatter(part_two) + bias_two
     act_two = jax.nn.gelu(pre_two).astype(bf16)
+    act_two, kernel_merge, kernel_up = lax.optimization_barrier((act_two, kernel_merge, kernel_up))
 
     act_own = act_two[:, 0]
-    ups, kernel_up, act_chip = up_on_chip(
-        me, act_own, swapped(act_own, "core"), up_source, bias_up[None], up_pieces
-    )
+    ups, act_chip = up_on_chip(me, act_own, swapped(act_own, "core"), kernel_up, bias_up[None])
     ups, sides = halo(ups)
     head_wide = jnp.pad(head_low, ((0, 0), (0, 128 - CLASSES)))
     pre_three, logits, planes = merge_on_chip(
@@ -707,10 +767,10 @@
         sides,
         swapped(sides, "core"),
         skip,
-        merge_sources,
+        skip_sides,
+        kernel_merge,
         bias_three[None],
         head_wide,
-        merge_pieces,
     )
     logits = (logits + swapped(logits, "core"))[:, :CLASSES] + bias_head
     logits = logits.reshape(2, 2, 2, 64, CLASSES)
@@ -734,8 +794,7 @@
         me, planes, grad_pre_three.reshape(512, HALF), split_three, shape_three
     )
     border, border_sides, merge_grad = lax.optimization_barrier((border, border_sides, merge_grad))
-    merge_grad = first_sum(merge_grad)
-    own_grad, away_grad = ups_grad_on_chip(me, border, border_sides, merge_sources, merge_pieces)
+    own_grad, away_grad = ups_grad_on_chip(me, border, border_sides, kernel_merge)
     grad_upper = (own_grad + swapped(away_grad, "core").astype(f32)).astype(bf16)
     grad_upper = grad_upper.reshape(2, 2, 2, 64, HALF)
     grad_act_two = jnp.einsum(
@@ -751,68 +810,88 @@
     split_up, shape_up = split_list(ru * zhs // 2, zhs)
     up_grad = up_grad_on_chip(me, act_chip, grad_upper, split_up, shape_up)
     grad_two, merge_grad, up_grad = lax.optimization_barrier((grad_two, merge_grad, up_grad))
+    if zhs == 2:
+        second_grad = second_grad_on_chip(me, act_shifts, grad_two, r2, 16 * zhs)
+    else:
+        second_grad = kernel_grad(act_one, grad_two)
     spill = convolve(grad_two, turned(kernel_two), 2)
-    inner = spill[:, 1:-1]
-    inner = inner.at[:, :1].add(shifted(spill[:, -1:], "zh", 1))
-    inner = inner.at[:, -1:].add(shifted(spill[:, :1], "zh", -1))
-    inner, merge_grad, up_grad = lax.optimization_barrier((inner, merge_grad, up_grad))
-    merge_grad, up_grad = second_sum(merge_grad), first_sum(up_grad)
-    core_part = inner[:, :, 1:-1]
-    core_part = core_part.at[:, :, :1].add(shifted(inner[:, :, -1:], "x", 1))
-    core_part = core_part.at[:, :, -1:].add(shifted(inner[:, :, :1], "x", -1))
-    core_part, grad_two, act_late = lax.optimization_barrier((core_part, grad_two, act_one))
+    if zhs == 2:
+        row = jnp.where(zh == 0, spill[:, -1:], spill[:, :1])
+        column = jnp.where(x == 0, spill[:, 1:-1, -1:], spill[:, 1:-1, :1])
+        corner = jnp.where(x == 0, row[:, :, -1:], row[:, :, :1])
+        corner = lax.ppermute(corner, ("zh", "x"), [(i, 3 - i) for i in range(4)])
+        row = swapped(row[:, :, 1:-1], "zh")
+        column = swapped(column, "x")
+        row, column, corner, merge_grad, up_grad = lax.optimization_barrier(
+            (row, column, corner, merge_grad, up_grad)
+        )
+        at_row = jnp.arange(4)[None, :, None, None] == jnp.where(zh == 0, 3, 0)
+        at_column = jnp.arange(64)[None, None, :, None] == jnp.where(x == 0, 63, 0)
+        core_part = (
+            spill[:, 1:-1, 1:-1]
+            + jnp.where(at_row, row, 0.0)
+            + jnp.where(at_column, column, 0.0)
+            + jnp.where(at_row & at_column, corner, 0.0)
+        )
+    else:
+        inner = spill[:, 1:-1]
+        inner = inner.at[:, :1].add(shifted(spill[:, -1:], "zh", 1))
+        inner = inner.at[:, -1:].add(shifted(spill[:, :1], "zh", -1))
+        core_part = inner[:, :, 1:-1]
+        core_part = core_part.at[:, :, :1].add(shifted(inner[:, :, -1:], "x", 1))
+        core_part = core_part.at[:, :, -1:].add(shifted(inner[:, :, :1], "x", -1))
+    merge_grad, up_grad = sent(merge_grad, "zl", "y"), sent(up_grad, "zl", "y")
     grad_pre_one = gelu_back(pre_one[:, 1:-1, 1:-1], core_part).astype(bf16)
-    second_grad = kernel_grad(act_late, grad_two)
-    first_grad = kernel_grad(feat[:, 1:-1, 1:-1], grad_pre_one)
-    first_grad, merge_grad, up_grad = lax.optimization_barrier((first_grad, merge_grad, up_grad))
-    up_grad = second_sum(up_grad)
-    if zhs == 2:
-        chip_parts = tuple(jnp.concatenate(pair, axis=1) for pair in zip(merge_grad, up_grad))
-    else:
-        chip_parts = (merge_grad[0], up_grad[0])
-
-    if even:
-        part_two = far_scatter(second_grad.astype(bf16).reshape(-1, 128))
-        sq_two = jnp.sum(part_two * part_two)
-        part_two = lax.all_to_all(part_two.astype(bf16), MEMBERS, 0, 0, tiled=True)
+    tiled = zhs == 2
+    if tiled:
+        grad_pre_one, second_grad = lax.optimization_barrier((grad_pre_one, second_grad))
+        first_grad = first_grad_on_chip(me, feat_shifts, grad_pre_one, r1, 16 * zhs)
+        stays, goes = (jnp.concatenate(pair, axis=1) for pair in zip(first_grad, second_grad))
+        part = stays.astype(f32) + swapped(goes, "x").astype(f32)
+        part = part.reshape(2, 8, r1 + r2, 128)
+        away = lax.dynamic_index_in_dim(part, 1 - zh, axis=0, keepdims=False).astype(bf16)
+        own = lax.dynamic_index_in_dim(part, zh, axis=0, keepdims=False)
+        got = swapped(away, "zh")
+        merge_grad, up_grad = added(merge_grad), added(up_grad)
+        merge_grad, up_grad = sent(merge_grad, "y", "zl"), sent(up_grad, "y", "zl")
+        away, merge_grad, up_grad = after(away, merge_grad, up_grad)
+        merge_grad, up_grad = added(merge_grad), added(up_grad)
+        chip_stays, chip_goes = (
+            jnp.concatenate([merge_grad[i], merge_grad[i + 2], up_grad[i], up_grad[i + 2]], axis=1)
+            for i in range(2)
+        )
+        chip_got = swapped(chip_goes, "x")
+        own = after(chip_goes, own)[1]
+        part = own + got.astype(f32)
+        part_low = part.astype(bf16)
+        chip_stays = after(part_low, chip_stays)[1]
+        chip_parts = chip_stays.astype(f32) + chip_got.astype(f32)
+        part_chip = chip_parts[:2] + swapped(chip_parts[2:].astype(bf16), "zh").astype(f32)
+        sq_kernels = jnp.sum(part * part)
+        part = lax.all_to_all(part_low, MEMBERS, 0, 0, tiled=True)
+        part_one, part_two = part[:, :r1], part[:, r1:]
         part_two = part_two.reshape(8, r2 // 8, C1 // 128, 128).transpose(1, 0, 2, 3)
         share_two = part_two.reshape(-1).astype(f32)
     else:
+        first_grad = kernel_grad(feat[:, 1:-1, 1:-1], grad_pre_one)
         mine = jnp.arange(8)[None, :, None] == member
         part_two = jnp.where(mine, second_grad.astype(bf16)[:, None], 0)
         share_two = lax.psum_scatter(
             part_two.reshape(-1, C1), AXES, scatter_dimension=0, tiled=True
         ).reshape(-1).astype(f32)
-        sq_two = jnp.sum(share_two * share_two)
-    part_one = far_scatter(first_grad)
-    sq_one = jnp.sum(part_one * part_one)
-    part_one = lax.all_to_all(part_one.astype(bf16), MEMBERS, 0, 0, tiled=True)
+        part_one = far_scatter(first_grad)
+        sq_kernels = jnp.sum(share_two * share_two) + jnp.sum(part_one * part_one)
+        part_one = lax.all_to_all(part_one.astype(bf16), MEMBERS, 0, 0, tiled=True)
+        part_chip = jnp.concatenate(
+            [last_sum(merge_grad[0]), last_sum(up_grad[0])], axis=1
+        )
     share_one = jnp.einsum("qrm,cqm->rc", part_one, sorting, preferred_element_type=f32).reshape(-1)
-    if zhs == 2:
-        part_chip = last_sum(cross_sum(chip_parts))
-    else:
-        part_chip = jnp.concatenate([last_sum(chip_parts[:1]), last_sum(chip_parts[1:])], axis=1)
     sq_chip = jnp.sum(part_chip * part_chip)
     part_chip = part_chip.astype(bf16)
     part_chip = in_order(part_chip[0], swapped(part_chip[1], "core"), "core", 1).astype(f32)
     share_merge = part_chip[:r3].reshape(-1)
     share_up = part_chip[r3:].reshape(-1)
-    if even:
-        part_two = far_scatter(second_grad.astype(bf16).reshape(-1, 128)).astype(bf16)
-        part_two = lax.all_to_all(part_two, MEMBERS, 0, 0, tiled=True)
-        part_two = part_two.reshape(8, r2 // 8, C1 // 128, 128).transpose(1, 0, 2, 3)
-        share_two = part_two.reshape(-1).astype(f32)
-    else:
-        mine = jnp.arange(8)[None, :, None] == member
-        part_two = jnp.where(mine, second_grad.astype(bf16)[:, None], 0)
-        share_two = lax.psum_scatter(
-            part_two.reshape(-1, C1), AXES, scatter_dimension=0, tiled=True
-        ).reshape(-1).astype(f32)
-    part_one = far_scatter(first_grad).astype(bf16)
-    part_one = lax.all_to_all(part_one, MEMBERS, 0, 0, tiled=True)
-    share_one = jnp.einsum("qrm,cqm->rc", part_one, sorting, preferred_element_type=f32).reshape(-1)
-
-    share_sq = sq_one + sq_two + sq_chip
+    share_sq = sq_kernels + sq_chip
     spread_one = (
         jnp.where(jnp.arange(8)[None, :] == member, column_sum(grad_pre_one)[:, None], 0.0)
     ).reshape(-1)

time: 536 us -> 485 us (0.905)
  starting transfers between devices: 113 us -> 74.8 us
  waiting for transfers between devices: 172 us -> 201 us
  other arithmetic: 86 us -> 65.3 us
  blocking collectives: 17.2 us -> 0 us
  Pallas kernels: 34.6 us -> 49 us
  matrix products: 37.5 us -> 24.2 us
    ppermute x41, waiting for transfers between devices: 148 us -> 179 us  [swapped(): return lax.ppermute(values, axis, [(0, 1), (1, 0)])]
    dot_general x18 -> x0, matrix products: 18.8 us -> none  [kernel_grad(): jnp.einsum('nhwc,nhwo->co', cells[:, shift_h:shift_h + rows_in, shift_w:s...]
    all_to_all x1 -> x0, blocking collectives: 17.2 us -> none  [group_scatter(): lax.all_to_all(sent.reshape(8, n, w2 // 2, c), MEMBERS, 0, 0, tiled=True)]
    ppermute x12 -> x6, starting transfers between devices: 32.3 us -> 16 us  [shifted(): lax.ppermute(values, axis, [(i, i + step) for i in range(count) if 0 <= i...]
    ppermute x12 -> x6, waiting for transfers between devices: 22.7 us -> 7.66 us  [shifted(): lax.ppermute(values, axis, [(i, i + step) for i in range(count) if 0 <= i...]
    pallas_call x5 -> x8, Pallas kernels: 34.6 us -> 49 us  [on_chip(): pl.pallas_call(body, out_shape=outs, in_specs=[pl.BlockSpec(memory_space=...]
    convert_element_type x11 -> x10, other arithmetic: 20.1 us -> 8.77 us  [the longest x8 5.9 us: added(): out += ((v.astype(f32) + w.astype(f32)).astype(bf16),)]
    concatenate x5 -> x1, other arithmetic: 11.7 us -> 1.09 us  [joined_on(): return jnp.concatenate([values, swapped(values, axis)], axis=0)]
  transfers between devices with their start and end apart: 62 -> 52, of which waited for: 29 -> 29; matrix products, arithmetic and copies ran while one was open for 23% -> 18% of each run, Pallas kernels for 2% -> 5%
where the time goes in v3:
time: 485 us; the launch traced here: 477 us
  waiting for transfers between devices  201 us (41%)
  starting transfers between devices  74.8 us (15%)
  other arithmetic  65.3 us (13%)
  local copies, waits for them, and re-layouts  54 us (11%)
  Pallas kernels  49 us (10%)
  matrix products  24.2 us (5%)
  between operations  8.7 us (2%)
    ppermute x41, waiting for transfers between devices, swapped(): return lax.ppermute(values, axis, [(0, 1), (1, 0)])  179 us
    pallas_call x8, Pallas kernels, on_chip(): pl.pallas_call(body, out_shape=outs, in_specs=[pl.BlockSpec(memory_space=...  49 us
    ppermute x41, starting transfers between devices, swapped(): return lax.ppermute(values, axis, [(0, 1), (1, 0)])  38.4 us
    conv_general_dilated x3, matrix products, convolve(): lax.conv_general_dilated(values, kernel, (1, 1), ((pad, pad), (pad, pad))...  20 us
    ppermute x6, starting transfers between devices, shifted(): lax.ppermute(values, axis, [(i, i + step) for i in range(count) if 0 <= i...  16 us
    unnamed x193, local copies, waits for them, and re-layouts  12.8 us
  transfers between devices with their start and end apart: 52, of which 29 were waited for; matrix products, arithmetic and copies ran while one was open for 18% of the time, Pallas kernels for 5%

profile of v3, /device:TPU:0, one launch (start us, length us, event | category | flops | bytes accessed | tf_op | source)
XLA Modules:
  0.0 476.6 jit_solution(2070386100191853719)
XLA Ops:
  6.6 5.4 %all-to-all-start = ((bf16[8,704,128]{2,1,0:T(8,128)(2,1)}), bf16[8,704,128]{2,1,0:T(8,128)(2,1)S(1)}, u32[]{:S(2)}, u32[]{:S(2)}) async-start(bf16[8,704,128]{2,1,0:T(8,128)(2,1)} %pad_maximum_fusion.4), calls=%async_computation | async-start | bytes 2883584 | tf_op jit(solution)/shard_map/all_to_all | solution.py:646
  19.2 2.6 collective-permute-start.1
  23.3 14.5 %collective-permute-done.1 = bf16[2,416,256]{2,1,0:T(8,128)(2,1)} collective-permute-done((bf16[2,416,256]{2,1,0:T(8,128)(2,1)}, bf16[2,416,256]{2,1,0:T(8,128)(2,1)}, u32[]{:S(2)}, u32[]{:S(2)}) %collective-permute-start.1) | collective-permute-done | bytes 426016 | tf_op jit(solution)/shard_map/ppermute | solution.py:41
  48.5 2.7 collective-permute-start.3
  52.5 4.2 collective-permute-start.12
  58.3 9.8 %collective-permute-done.5 = bf16[4,416,256]{2,1,0:T(8,128)(2,1)S(1)} collective-permute-done((bf16[4,416,256]{2,1,0:T(8,128)(2,1)S(1)}, bf16[4,416,256]{2,1,0:T(8,128)(2,1)S(1)}, u32[]{:S(2)}, u32[]{:S(2)}) %collective-permute-start.5) | collective-permute-done | bytes 852000 | tf_op jit(solution)/shard_map/ppermute | solution.py:41
  70.9 3.8 collective-permute-start.7
  74.7 29.0 %collective-permute-done.3 = bf16[4608,128]{1,0:T(8,128)(2,1)S(1)} collective-permute-done((bf16[4608,128]{1,0:T(8,128)(2,1)S(1)}, bf16[4608,128]{1,0:T(8,128)(2,1)S(1)}, u32[]{:S(2)}, u32[]{:S(2)}) %collective-permute-start.3) | collective-permute-done | bytes 1179680 | tf_op jit(solution)/shard_map/ppermute | solution.py:41
  113.3 2.7 pad_maximum_fusion.8
  116.7 8.6 %collective-permute-done.4 = bf16[2688,128]{1,0:T(8,128)(2,1)S(1)} collective-permute-done((bf16[2688,128]{1,0:T(8,128)(2,1)S(1)}, bf16[2688,128]{1,0:T(8,128)(2,1)S(1)}, u32[]{:S(2)}, u32[]{:S(2)}) %collective-permute-start.4) | collective-permute-done | bytes 688160 | tf_op jit(solution)/shard_map/ppermute | solution.py:41
  125.3 2.1 constant_dynamic-update-slice_fusion.10
  129.5 2.2 constant_dynamic-update-slice_fusion.8
  131.7 2.1 constant_dynamic-update-slice_fusion.7.rest_0_
  139.6 4.0 fusion.11
  148.4 3.0 reshape.744
  151.4 7.1 %fusion.52 = bf16[2,4,64,1024]{3,0,2,1:T(2,128)(2,1)} fusion(bf16[3,3,128,1024]{3,2,1,0:T(8,128)(2,1)} %reshape.744, bf16[2,6,66,128]{3,2,1,0:T(8,128)(2,1)} %get-tuple-element.348), kind=kOutput, calls=%fused_computation.162 | convolution fusion | flops 1207959552 | bytes 3610624 | tf_op jit(solution)/shard_map/conv_general_dilated | solution.py:84
  158.6 2.7 collective-permute-done.10.rest_3_
  161.3 8.3 %collective-permute-done.9.rest_1_ = bf16[16,208,256]{2,1,0:T(8,128)(2,1)} collective-permute-done((bf16[16,208,256]{2,1,0:T(8,128)(2,1)}, bf16[16,208,256]{2,1,0:T(8,128)(2,1)}, u32[]{:S(2)}, u32[]{:S(2)}) %collective-permute-start.9) | collective-permute-done | bytes 1703968 | tf_op jit(solution)/shard_map/ppermute | solution.py:41
  169.6 3.6 all-to-all-start.1
  173.8 7.4 %shard_map.382 = (bf16[9216,256]{1,0:T(8,128)(2,1)}, bf16[4096,256]{1,0:T(8,128)(2,1)}) custom-call(s32[5]{0:T(128)} %stack.87.me_ref, bf16[16,208,256]{2,1,0:T(8,128)(2,1)} %constant_dynamic-update-slice_fusion.7.rest_0_, bf16[16,208,256]{2,1,0:T(8,128)(2,1)} %collective-permute-done.9.rest_1_, ...), custom_call_target="tpu_custom_call" | custom-call | bytes 13631508 | tf_op jit(solution)/shard_map/pallas_call | solution.py:272
  181.2 6.4 %all-to-all-done.1 = bf16[8,2,32,1024]{3,1,2,0:T(2,128)(2,1)S(1)} async-done(((bf16[8,2,32,1024]{3,1,2,0:T(2,128)(2,1)}), bf16[8,2,32,1024]{3,1,2,0:T(2,128)(2,1)S(1)}, u32[]{:S(2)}, u32[]{:S(2)}) %all-to-all-start.1) | async-done | bytes 1048608 | tf_op jit(solution)/shard_map/all_to_all | solution.py:132
  192.3 2.9 shard_map.383
  200.4 3.4 collective-permute-start.17
  214.3 11.1 %shard_map.384 = (f32[512,256]{1,0:T(8,128)}, f32[512,128]{1,0:T(8,128)}, bf16[2,4,4,64,1024]{4,3,2,1,0:T(8,128)(2,1)}) custom-call(s32[5]{0:T(128)} %stack.87.me_ref, bf16[2,4,2,64,256]{4,3,2,1,0:T(8,128)(2,1)} %copy-done.40, bf16[2,4,2,64,256]{4,3,2,1,0:T(8,128)(2,1)} %copy-done.86, bf16[2,2,4,256]{3,2,1,0:T(4,128)(2,1)} %copy-done.71, ...), custom_call_target="tpu_custom_call" | custom-call | flops 2415919104 | bytes 11895828 | tf_op jit(solution)/shard_map/pallas_call | solution.py:272
  229.3 3.1 convert_reduce_fusion.1
  236.2 4.3 collective-permute-start.23
  240.5 7.6 %shard_map.385 = (bf16[16,144,256]{2,1,0:T(8,128)(2,1)}, bf16[16,144,256]{2,1,0:T(8,128)(2,1)}, bf16[16,144,256]{2,1,0:T(8,128)(2,1)}, bf16[16,144,256]{2,1,0:T(8,128)(2,1)}) custom-call(s32[5]{0:T(128)} %stack.87.me_ref, bf16[2,4,4,64,1024]{4,3,2,1,0:T(8,128)(2,1)} %get-tuple-element.141.planes_ref, bf16[512,256]{1,0:T(8,128)(2,1)} %bitcast.272), custom_call_target="tpu_custom_call" | custom-call | flops 2415919104 | bytes 9175060 | tf_op jit(solution)/shard_map/pallas_call | solution.py:272
  249.5 5.6 %collective-permute-done.24 = bf16[272,256]{1,0:T(8,128)(2,1)S(1)} collective-permute-done((bf16[272,256]{1,0:T(8,128)(2,1)S(1)}, bf16[272,256]{1,0:T(8,128)(2,1)S(1)}, u32[]{:S(2)}, u32[]{:S(2)}) %collective-permute-start.24) | collective-permute-done | bytes 139296 | tf_op jit(solution)/shard_map/ppermute | solution.py:35
  258.0 5.0 %shard_map.386 = (f32[512,256]{1,0:T(8,128)}, bf16[512,256]{1,0:T(8,128)(2,1)}) custom-call(s32[5]{0:T(128)} %stack.87.me_ref, bf16[2,4,2,64,256]{4,3,2,1,0:T(8,128)(2,1)} %copy.389.rows_ref, bf16[2,2,4,256]{3,2,1,0:T(4,128)(2,1)} %pad_maximum_fusion.24.sides_ref, bf16[9216,256]{1,0:T(8,128)(2,1)} %get-tuple-element.137.kernel_ref), custom_call_target="tpu_custom_call" | custom-call | flops 1207959552 | bytes 6037524 | tf_op jit(solution)/shard_map/pallas_call | solution.py:272
  272.8 5.4 %all-to-all-start.2 = ((bf16[8,2,1,32,1024]{4,3,1,2,0:T(8,128)(2,1)}), bf16[8,2,1,32,1024]{4,3,1,2,0:T(8,128)(2,1)S(1)}, u32[]{:S(2)}, u32[]{:S(2)}) async-start(bf16[8,2,1,32,1024]{4,3,1,2,0:T(8,128)(2,1)} %broadcast_in_dim.176), calls=%async_computation.2 | async-start | bytes 2097152 | tf_op jit(solution)/shard_map/all_to_all | solution.py:124
  282.1 3.6 shard_map.387
  285.8 6.7 %all-to-all-done.2 = bf16[8,2,1,32,1024]{4,3,1,2,0:T(8,128)(2,1)S(1)} async-done(((bf16[8,2,1,32,1024]{4,3,1,2,0:T(8,128)(2,1)}), bf16[8,2,1,32,1024]{4,3,1,2,0:T(8,128)(2,1)S(1)}, u32[]{:S(2)}, u32[]{:S(2)}) %all-to-all-start.2) | async-done | bytes 1048608 | tf_op jit(solution)/shard_map/all_to_all | solution.py:124
  292.5 8.8 %fusion.13 = f32[2,6,66,128]{3,0,2,1:T(2,128)S(1)} fusion(bf16[3,3,128,1024]{3,2,1,0:T(8,128)(2,1)} %reshape.744, bf16[2,4,64,1024]{3,2,1,0:T(8,128)(2,1)S(1)} %bitcast.256), kind=kOutput, calls=%fused_computation.41 | convolution fusion | flops 1207959552 | bytes 3813376 | tf_op jit(solution)/shard_map/conv_general_dilated | solution.py:84
  303.2 2.1 collective-permute-start.29
  305.9 7.0 %shard_map.388 = (bf16[16,288,128]{2,1,0:T(8,128)(2,1)}, bf16[16,288,128]{2,1,0:T(8,128)(2,1)}) custom-call(s32[5]{0:T(128)} %stack.87.me_ref, bf16[3,2,6,64,128]{4,3,2,1,0:T(8,128)(2,1)} %pad_maximum_fusion.15.cells_ref, bf16[2,4,64,1024]{3,2,1,0:T(8,128)(2,1)} %bitcast.257), custom_call_target="tpu_custom_call" | custom-call | flops 1207959552 | bytes 3997716 | tf_op jit(solution)/shard_map/pallas_call | solution.py:272
  314.0 4.4 shard_map.389
  318.5 2.4 pad_maximum_fusion.3
  328.7 31.7 %collective-permute-done.33 = bf16[16,64,256]{2,1,0:T(8,128)(2,1)} collective-permute-done((bf16[16,64,256]{2,1,0:T(8,128)(2,1)}, bf16[16,64,256]{2,1,0:T(8,128)(2,1)}, u32[]{:S(2)}, u32[]{:S(2)}) %collective-permute-start.33) | collective-permute-done | bytes 524320 | tf_op jit(solution)/shard_map/ppermute | solution.py:41
  372.6 8.0 %collective-permute-done.35 = bf16[8,144,256]{2,1,0:T(8,128)(2,1)S(1)} collective-permute-done((bf16[8,144,256]{2,1,0:T(8,128)(2,1)S(1)}, bf16[8,144,256]{2,1,0:T(8,128)(2,1)S(1)}, u32[]{:S(2)}, u32[]{:S(2)}) %collective-permute-start.35) | collective-permute-done | bytes 589856 | tf_op jit(solution)/shard_map/ppermute | solution.py:41
  380.7 5.9 %collective-permute-done.38 = bf16[8,64,256]{2,1,0:T(8,128)(2,1)S(1)} collective-permute-done((bf16[8,64,256]{2,1,0:T(8,128)(2,1)S(1)}, bf16[8,64,256]{2,1,0:T(8,128)(2,1)S(1)}, u32[]{:S(2)}, u32[]{:S(2)}) %collective-permute-start.38) | collective-permute-done | bytes 262176 | tf_op jit(solution)/shard_map/ppermute | solution.py:41
  386.7 10.2 %collective-permute-done.36 = bf16[8,144,256]{2,1,0:T(8,128)(2,1)S(1)} collective-permute-done((bf16[8,144,256]{2,1,0:T(8,128)(2,1)S(1)}, bf16[8,144,256]{2,1,0:T(8,128)(2,1)S(1)}, u32[]{:S(2)}, u32[]{:S(2)}) %collective-permute-start.36) | collective-permute-done | bytes 589856 | tf_op jit(solution)/shard_map/ppermute | solution.py:41
  399.2 9.7 %collective-permute-done.39 = bf16[8,432,128]{2,1,0:T(8,128)(2,1)S(1)} collective-permute-done((bf16[8,432,128]{2,1,0:T(8,128)(2,1)S(1)}, bf16[8,432,128]{2,1,0:T(8,128)(2,1)S(1)}, u32[]{:S(2)}, u32[]{:S(2)}) %collective-permute-start.39) | collective-permute-done | bytes 884768 | tf_op jit(solution)/shard_map/ppermute | solution.py:41
  410.8 3.9 all-to-all-start.3
  421.5 18.2 %collective-permute-done.41 = bf16[2,416,256]{2,1,0:T(8,128)(2,1)S(1)} collective-permute-done((bf16[2,416,256]{2,1,0:T(8,128)(2,1)}, bf16[2,416,256]{2,1,0:T(8,128)(2,1)S(1)}, u32[]{:S(2)}, u32[]{:S(2)}) %collective-permute-start.41) | collective-permute-done | bytes 426016 | tf_op jit(solution)/shard_map/ppermute | solution.py:41
  443.6 3.2 collective-permute-done.43
  452.5 3.8 collective-permute-done.45
  457.9 3.1 collective-permute-done.46
  471.5 2.4 multiply_subtract_fusion
  (492 shorter events, 152.3 us)
Async XLA Ops:
  6.6 33.2 %all-to-all-start = ((bf16[8,704,128]{2,1,0:T(8,128)(2,1)}), bf16[8,704,128]{2,1,0:T(8,128)(2,1)S(1)}, u32[]{:S(2)}, u32[]{:S(2)}) async-start(bf16[8,704,128]{2,1,0:T(8,128)(2,1)} %pad_maximum_fusion.4), calls=%async_computation | async-start | bytes 2883584 | tf_op jit(solution)/shard_map/all_to_all | solution.py:646
  13.6 4.8 %collective-permute-start = (bf16[1,416,256]{2,1,0:T(8,128)(2,1)S(1)}, bf16[1,416,256]{2,1,0:T(8,128)(2,1)S(1)}, u32[]{:S(2)}, u32[]{:S(2)}) collective-permute-start(bf16[1,416,256]{2,1,0:T(8,128)(2,1)S(1)} %bitcast.273), channel_id=1, source_target_pairs={{0,1},{1,0},{2,3},{3,2},{4,5},{5,4},{6,7},{7,6},{8,9},{9,8},{10,11... | collective-permute-start | bytes 638984 | tf_op jit(solution)/shard_map/ppermute | solution.py:41
  15.6 6.6 %collective-permute-start.2 = (bf16[2,2,2,32,512]{4,1,0,3,2:T(2,128)(2,1)S(1)}, bf16[2,2,2,32,512]{4,1,0,3,2:T(2,128)(2,1)S(1)}, u32[]{:S(2)}, u32[]{:S(2)}) collective-permute-start(bf16[2,2,2,32,512]{4,1,0,3,2:T(2,128)(2,1)S(1)} %bitcast.271), channel_id=1, source_target_pairs={{0,1},{1,0},{2,3},{3,2},{4,5},{5,4},{6,7},{7,6},{8,9},{9,8},{10,11... | collective-permute-start | bytes 786440 | tf_op jit(solution)/shard_map/ppermute | solution.py:41
  15.7 2.7 collective-permute-start.14
  19.2 18.6 %collective-permute-start.1 = (bf16[2,416,256]{2,1,0:T(8,128)(2,1)}, bf16[2,416,256]{2,1,0:T(8,128)(2,1)}, u32[]{:S(2)}, u32[]{:S(2)}) collective-permute-start(bf16[2,416,256]{2,1,0:T(8,128)(2,1)} %pad_maximum_fusion.19), channel_id=1, source_target_pairs={{0,16},{16,0},{1,17},{17,1},{2,18},{18,2},{3,19},{19,3},{4,20},{20... | collective-permute-start | bytes 1277960 | tf_op jit(solution)/shard_map/ppermute | solution.py:41
  43.9 7.6 %collective-permute-start.11 = (bf16[2,2,512]{2,1,0:T(2,128)(2,1)S(1)}, bf16[2,2,512]{2,1,0:T(2,128)(2,1)S(1)}, u32[]{:S(2)}, u32[]{:S(2)}) collective-permute-start(bf16[2,2,512]{2,1,0:T(2,128)(2,1)S(1)} %fusion.60), channel_id=1, source_target_pairs={{0,2},{2,0},{1,3},{3,1},{4,6},{6,4},{5,7},{7,5},{8,10},{10,8},{9,1... | collective-permute-start | bytes 12296 | tf_op jit(solution)/shard_map/ppermute | solution.py:41
  47.8 20.3 %collective-permute-start.5 = (bf16[4,416,256]{2,1,0:T(8,128)(2,1)S(1)}, bf16[4,416,256]{2,1,0:T(8,128)(2,1)S(1)}, u32[]{:S(2)}, u32[]{:S(2)}) collective-permute-start(bf16[4,416,256]{2,1,0:T(8,128)(2,1)S(1)} %pad_maximum_fusion.9), channel_id=1, source_target_pairs={{0,2},{2,0},{1,3},{3,1},{4,6},{6,4},{5,7},{7,5},{8,10},{10,8},{9,1... | collective-permute-start | bytes 2555912 | tf_op jit(solution)/shard_map/ppermute | solution.py:41
  48.5 55.2 %collective-permute-start.3 = (bf16[4608,128]{1,0:T(8,128)(2,1)S(1)}, bf16[4608,128]{1,0:T(8,128)(2,1)S(1)}, u32[]{:S(2)}, u32[]{:S(2)}) collective-permute-start(bf16[4608,128]{1,0:T(8,128)(2,1)S(1)} %pad_maximum_fusion.6), channel_id=1, source_target_pairs={{0,16},{16,0},{1,17},{17,1},{2,18},{18,2},{3,19},{19,3},{4,20},{20... | collective-permute-start | bytes 3538952 | tf_op jit(solution)/shard_map/ppermute | solution.py:41
  52.5 55.9 %collective-permute-start.12 = (bf16[272,512]{1,0:T(8,128)(2,1)}, bf16[272,512]{1,0:T(8,128)(2,1)}, u32[]{:S(2)}, u32[]{:S(2)}) collective-permute-start(bf16[272,512]{1,0:T(8,128)(2,1)} %get-tuple-element.382), channel_id=1, source_target_pairs={{0,4},{4,8},{8,12},{12,16},{16,20},{20,24},{24,28},{1,5},{5,9},{9,... | collective-permute-start | bytes 835592 | tf_op jit(solution)/shard_map/ppermute | solution.py:35
  56.7 52.4 %collective-permute-start.13 = (bf16[272,512]{1,0:T(8,128)(2,1)}, bf16[272,512]{1,0:T(8,128)(2,1)}, u32[]{:S(2)}, u32[]{:S(2)}) collective-permute-start(bf16[272,512]{1,0:T(8,128)(2,1)} %get-tuple-element.383), channel_id=1, source_target_pairs={{4,0},{8,4},{12,8},{16,12},{20,16},{24,20},{28,24},{5,1},{9,5},{13... | collective-permute-start | bytes 835592 | tf_op jit(solution)/shard_map/ppermute | solution.py:35
  69.5 47.2 %collective-permute-start.6 = (bf16[8,208,256]{2,1,0:T(8,128)(2,1)}, bf16[8,208,256]{2,1,0:T(8,128)(2,1)}, u32[]{:S(2)}, u32[]{:S(2)}) collective-permute-start(bf16[8,208,256]{2,1,0:T(8,128)(2,1)} %get-tuple-element.118), channel_id=1, source_target_pairs={{0,4},{4,0},{1,5},{5,1},{2,6},{6,2},{3,7},{7,3},{8,12},{12,8},{9,1... | collective-permute-start | bytes 2555912 | tf_op jit(solution)/shard_map/ppermute | solution.py:41
  70.9 45.8 %collective-permute-start.7 = (bf16[8,208,256]{2,1,0:T(8,128)(2,1)}, bf16[8,208,256]{2,1,0:T(8,128)(2,1)}, u32[]{:S(2)}, u32[]{:S(2)}) collective-permute-start(bf16[8,208,256]{2,1,0:T(8,128)(2,1)} %get-tuple-element.120), channel_id=1, source_target_pairs={{0,8},{8,0},{1,9},{9,1},{2,10},{10,2},{3,11},{11,3},{4,12},{12,4},... | collective-permute-start | bytes 2555912 | tf_op jit(solution)/shard_map/ppermute | solution.py:41
  106.9 18.4 %collective-permute-start.4 = (bf16[2688,128]{1,0:T(8,128)(2,1)S(1)}, bf16[2688,128]{1,0:T(8,128)(2,1)S(1)}, u32[]{:S(2)}, u32[]{:S(2)}) collective-permute-start(bf16[2688,128]{1,0:T(8,128)(2,1)S(1)} %pad_maximum_fusion.14), channel_id=1, source_target_pairs={{0,2},{2,0},{1,3},{3,1},{4,6},{6,4},{5,7},{7,5},{8,10},{10,8},{9,1... | collective-permute-start | bytes 2064392 | tf_op jit(solution)/shard_map/ppermute | solution.py:41
  116.1 30.2 %collective-permute-start.8 = (bf16[4608,128]{1,0:T(8,128)(2,1)S(1)}, bf16[4608,128]{1,0:T(8,128)(2,1)}, u32[]{:S(2)}, u32[]{:S(2)}) collective-permute-start(bf16[4608,128]{1,0:T(8,128)(2,1)S(1)} %bitcast.235), channel_id=1, source_target_pairs={{0,2},{2,0},{1,3},{3,1},{4,6},{6,4},{5,7},{7,5},{8,10},{10,8},{9,1... | collective-permute-start | bytes 3538952 | tf_op jit(solution)/shard_map/ppermute | solution.py:41
  129.5 31.7 %collective-permute-start.10 = (bf16[16,208,256]{2,1,0:T(8,128)(2,1)}, bf16[16,208,256]{2,1,0:T(8,128)(2,1)}, u32[]{:S(2)}, u32[]{:S(2)}) collective-permute-start(bf16[16,208,256]{2,1,0:T(8,128)(2,1)} %constant_dynamic-update-slice_fusion.9.rest_2_), channel_id=1, source_target_pairs={{0,4},{4,0},{1,5},{5,1},{2,6},{6,2},{3,7},{7,3},{8,12},{12,8},{9,1... | collective-permute-start | bytes 5111816 | tf_op jit(solution)/shard_map/ppermute | solution.py:41
  133.8 35.8 %collective-permute-start.9 = (bf16[16,208,256]{2,1,0:T(8,128)(2,1)}, bf16[16,208,256]{2,1,0:T(8,128)(2,1)}, u32[]{:S(2)}, u32[]{:S(2)}) collective-permute-start(bf16[16,208,256]{2,1,0:T(8,128)(2,1)} %constant_dynamic-update-slice_fusion.7.rest_0_), channel_id=1, source_target_pairs={{0,8},{8,0},{1,9},{9,1},{2,10},{10,2},{3,11},{11,3},{4,12},{12,4},... | collective-permute-start | bytes 5111816 | tf_op jit(solution)/shard_map/ppermute | solution.py:41
  169.6 17.9 %all-to-all-start.1 = ((bf16[8,2,32,1024]{3,1,2,0:T(2,128)(2,1)}), bf16[8,2,32,1024]{3,1,2,0:T(2,128)(2,1)S(1)}, u32[]{:S(2)}, u32[]{:S(2)}) async-start(bf16[8,2,32,1024]{3,1,2,0:T(2,128)(2,1)} %bitcast.38), calls=%async_computation.1 | async-start | bytes 2097152 | tf_op jit(solution)/shard_map/all_to_all | solution.py:132
  196.6 3.7 collective-permute-start.16
  200.4 8.3 %collective-permute-start.17 = (bf16[272,256]{1,0:T(8,128)(2,1)S(1)}, bf16[272,256]{1,0:T(8,128)(2,1)S(1)}, u32[]{:S(2)}, u32[]{:S(2)}) collective-permute-start(bf16[272,256]{1,0:T(8,128)(2,1)S(1)} %get-tuple-element.380), channel_id=1, source_target_pairs={{0,4},{4,8},{8,12},{12,16},{16,20},{20,24},{24,28},{1,5},{5,9},{9,... | collective-permute-start | bytes 417800 | tf_op jit(solution)/shard_map/ppermute | solution.py:35
  203.8 6.9 %collective-permute-start.18 = (bf16[272,256]{1,0:T(8,128)(2,1)S(1)}, bf16[272,256]{1,0:T(8,128)(2,1)S(1)}, u32[]{:S(2)}, u32[]{:S(2)}) collective-permute-start(bf16[272,256]{1,0:T(8,128)(2,1)S(1)} %get-tuple-element.381), channel_id=1, source_target_pairs={{4,0},{8,4},{12,8},{16,12},{20,16},{24,20},{28,24},{5,1},{9,5},{13... | collective-permute-start | bytes 417800 | tf_op jit(solution)/shard_map/ppermute | solution.py:35
  210.8 2.6 collective-permute-start.19
  211.0 2.4 collective-permute-start.20
  225.4 1.9 collective-permute-start.21
  232.4 3.7 collective-permute-start.22
  236.2 13.2 %collective-permute-start.23 = (bf16[272,256]{1,0:T(8,128)(2,1)S(1)}, bf16[272,256]{1,0:T(8,128)(2,1)S(1)}, u32[]{:S(2)}, u32[]{:S(2)}) collective-permute-start(bf16[272,256]{1,0:T(8,128)(2,1)S(1)} %get-tuple-element.378), channel_id=1, source_target_pairs={{0,4},{4,8},{8,12},{12,16},{16,20},{20,24},{24,28},{1,5},{5,9},{9,... | collective-permute-start | bytes 417800 | tf_op jit(solution)/shard_map/ppermute | solution.py:35
  248.1 6.9 %collective-permute-start.24 = (bf16[272,256]{1,0:T(8,128)(2,1)S(1)}, bf16[272,256]{1,0:T(8,128)(2,1)S(1)}, u32[]{:S(2)}, u32[]{:S(2)}) collective-permute-start(bf16[272,256]{1,0:T(8,128)(2,1)S(1)} %get-tuple-element.379), channel_id=1, source_target_pairs={{4,0},{8,4},{12,8},{16,12},{20,16},{24,20},{28,24},{5,1},{9,5},{13... | collective-permute-start | bytes 417800 | tf_op jit(solution)/shard_map/ppermute | solution.py:35
  272.8 19.6 %all-to-all-start.2 = ((bf16[8,2,1,32,1024]{4,3,1,2,0:T(8,128)(2,1)}), bf16[8,2,1,32,1024]{4,3,1,2,0:T(8,128)(2,1)S(1)}, u32[]{:S(2)}, u32[]{:S(2)}) async-start(bf16[8,2,1,32,1024]{4,3,1,2,0:T(8,128)(2,1)} %broadcast_in_dim.176), calls=%async_computation.2 | async-start | bytes 2097152 | tf_op jit(solution)/shard_map/all_to_all | solution.py:124
  301.5 11.5 %collective-permute-start.27 = (f32[2,1,64,128]{3,0,2,1:T(2,128)S(1)}, f32[2,1,64,128]{3,0,2,1:T(2,128)S(1)}, u32[]{:S(2)}, u32[]{:S(2)}) collective-permute-start(f32[2,1,64,128]{3,0,2,1:T(2,128)S(1)} %slice.507), channel_id=1, source_target_pairs={{0,16},{16,0},{1,17},{17,1},{2,18},{18,2},{3,19},{19,3},{4,20},{20... | collective-permute-start | bytes 196616 | tf_op jit(solution)/shard_map/ppermute | solution.py:41
  303.2 9.7 %collective-permute-start.29 = (f32[2,1,1,128]{3,0,2,1:T(2,128)S(1)}, f32[2,1,1,128]{3,0,2,1:T(2,128)S(1)}, u32[]{:S(2)}, u32[]{:S(2)}) collective-permute-start(f32[2,1,1,128]{3,0,2,1:T(2,128)S(1)} %slice_select_fusion.3), channel_id=1, source_target_pairs={{0,18},{2,16},{16,2},{18,0},{1,19},{3,17},{17,3},{19,1},{4,22},{6,... | collective-permute-start | bytes 3080 | tf_op jit(solution)/shard_map/ppermute | solution.py:822
  305.4 7.6 %collective-permute-start.28 = (f32[2,4,1,128]{3,0,2,1:T(2,128)S(1)}, f32[2,4,1,128]{3,0,2,1:T(2,128)S(1)}, u32[]{:S(2)}, u32[]{:S(2)}) collective-permute-start(f32[2,4,1,128]{3,0,2,1:T(2,128)S(1)} %slice_select_fusion.2), channel_id=1, source_target_pairs={{0,2},{2,0},{1,3},{3,1},{4,6},{6,4},{5,7},{7,5},{8,10},{10,8},{9,1... | collective-permute-start | bytes 12296 | tf_op jit(solution)/shard_map/ppermute | solution.py:41
  320.9 49.3 %collective-permute-start.30 = (bf16[16,432,128]{2,1,0:T(8,128)(2,1)}, bf16[16,432,128]{2,1,0:T(8,128)(2,1)S(1)}, u32[]{:S(2)}, u32[]{:S(2)}) collective-permute-start(bf16[16,432,128]{2,1,0:T(8,128)(2,1)} %pad_maximum_fusion.3), channel_id=1, source_target_pairs={{0,2},{2,0},{1,3},{3,1},{4,6},{6,4},{5,7},{7,5},{8,10},{10,8},{9,1... | collective-permute-start | bytes 5308424 | tf_op jit(solution)/shard_map/ppermute | solution.py:41
  322.4 42.5 %collective-permute-start.31 = (bf16[16,144,256]{2,1,0:T(8,128)(2,1)}, bf16[16,144,256]{2,1,0:T(8,128)(2,1)}, u32[]{:S(2)}, u32[]{:S(2)}) collective-permute-start(bf16[16,144,256]{2,1,0:T(8,128)(2,1)} %get-tuple-element.179), channel_id=1, source_target_pairs={{0,8},{8,0},{1,9},{9,1},{2,10},{10,2},{3,11},{11,3},{4,12},{12,4},... | collective-permute-start | bytes 3538952 | tf_op jit(solution)/shard_map/ppermute | solution.py:41
  323.8 36.5 %collective-permute-start.33 = (bf16[16,64,256]{2,1,0:T(8,128)(2,1)}, bf16[16,64,256]{2,1,0:T(8,128)(2,1)}, u32[]{:S(2)}, u32[]{:S(2)}) collective-permute-start(bf16[16,64,256]{2,1,0:T(8,128)(2,1)} %get-tuple-element.183), channel_id=1, source_target_pairs={{0,8},{8,0},{1,9},{9,1},{2,10},{10,2},{3,11},{11,3},{4,12},{12,4},... | collective-permute-start | bytes 1572872 | tf_op jit(solution)/shard_map/ppermute | solution.py:41
  324.4 42.8 %collective-permute-start.32 = (bf16[16,144,256]{2,1,0:T(8,128)(2,1)}, bf16[16,144,256]{2,1,0:T(8,128)(2,1)}, u32[]{:S(2)}, u32[]{:S(2)}) collective-permute-start(bf16[16,144,256]{2,1,0:T(8,128)(2,1)} %get-tuple-element.181), channel_id=1, source_target_pairs={{0,4},{4,0},{1,5},{5,1},{2,6},{6,2},{3,7},{7,3},{8,12},{12,8},{9,1... | collective-permute-start | bytes 3538952 | tf_op jit(solution)/shard_map/ppermute | solution.py:41
  325.9 37.2 %collective-permute-start.34 = (bf16[16,64,256]{2,1,0:T(8,128)(2,1)}, bf16[16,64,256]{2,1,0:T(8,128)(2,1)}, u32[]{:S(2)}, u32[]{:S(2)}) collective-permute-start(bf16[16,64,256]{2,1,0:T(8,128)(2,1)} %get-tuple-element.185), channel_id=1, source_target_pairs={{0,4},{4,0},{1,5},{5,1},{2,6},{6,2},{3,7},{7,3},{8,12},{12,8},{9,1... | collective-permute-start | bytes 1572872 | tf_op jit(solution)/shard_map/ppermute | solution.py:41
  361.5 11.0 %collective-permute-start.37 = (bf16[8,64,256]{2,1,0:T(8,128)(2,1)S(1)}, bf16[8,64,256]{2,1,0:T(8,128)(2,1)S(1)}, u32[]{:S(2)}, u32[]{:S(2)}) collective-permute-start(bf16[8,64,256]{2,1,0:T(8,128)(2,1)S(1)} %get-tuple-element.325), channel_id=1, source_target_pairs={{0,4},{4,0},{1,5},{5,1},{2,6},{6,2},{3,7},{7,3},{8,12},{12,8},{9,1... | collective-permute-start | bytes 786440 | tf_op jit(solution)/shard_map/ppermute | solution.py:41
  364.2 22.4 %collective-permute-start.38 = (bf16[8,64,256]{2,1,0:T(8,128)(2,1)S(1)}, bf16[8,64,256]{2,1,0:T(8,128)(2,1)S(1)}, u32[]{:S(2)}, u32[]{:S(2)}) collective-permute-start(bf16[8,64,256]{2,1,0:T(8,128)(2,1)S(1)} %get-tuple-element.328), channel_id=1, source_target_pairs={{0,8},{8,0},{1,9},{9,1},{2,10},{10,2},{3,11},{11,3},{4,12},{12,4},... | collective-permute-start | bytes 786440 | tf_op jit(solution)/shard_map/ppermute | solution.py:41
  366.5 14.1 %collective-permute-start.35 = (bf16[8,144,256]{2,1,0:T(8,128)(2,1)S(1)}, bf16[8,144,256]{2,1,0:T(8,128)(2,1)S(1)}, u32[]{:S(2)}, u32[]{:S(2)}) collective-permute-start(bf16[8,144,256]{2,1,0:T(8,128)(2,1)S(1)} %get-tuple-element.309), channel_id=1, source_target_pairs={{0,4},{4,0},{1,5},{5,1},{2,6},{6,2},{3,7},{7,3},{8,12},{12,8},{9,1... | collective-permute-start | bytes 1769480 | tf_op jit(solution)/shard_map/ppermute | solution.py:41
  368.8 28.2 %collective-permute-start.36 = (bf16[8,144,256]{2,1,0:T(8,128)(2,1)S(1)}, bf16[8,144,256]{2,1,0:T(8,128)(2,1)S(1)}, u32[]{:S(2)}, u32[]{:S(2)}) collective-permute-start(bf16[8,144,256]{2,1,0:T(8,128)(2,1)S(1)} %get-tuple-element.311), channel_id=1, source_target_pairs={{0,8},{8,0},{1,9},{9,1},{2,10},{10,2},{3,11},{11,3},{4,12},{12,4},... | collective-permute-start | bytes 1769480 | tf_op jit(solution)/shard_map/ppermute | solution.py:41
  370.7 38.2 %collective-permute-start.39 = (bf16[8,432,128]{2,1,0:T(8,128)(2,1)S(1)}, bf16[8,432,128]{2,1,0:T(8,128)(2,1)S(1)}, u32[]{:S(2)}, u32[]{:S(2)}) collective-permute-start(bf16[8,432,128]{2,1,0:T(8,128)(2,1)S(1)} %fusion.15), channel_id=1, source_target_pairs={{0,16},{16,0},{1,17},{17,1},{2,18},{18,2},{3,19},{19,3},{4,20},{20... | collective-permute-start | bytes 2654216 | tf_op jit(solution)/shard_map/ppermute | solution.py:41
  398.1 18.6 %collective-permute-start.40 = (bf16[4,416,256]{2,1,0:T(8,128)(2,1)}, bf16[4,416,256]{2,1,0:T(8,128)(2,1)}, u32[]{:S(2)}, u32[]{:S(2)}) collective-permute-start(bf16[4,416,256]{2,1,0:T(8,128)(2,1)} %pad_maximum_fusion.10), channel_id=1, source_target_pairs={{0,2},{2,0},{1,3},{3,1},{4,6},{6,4},{5,7},{7,5},{8,10},{10,8},{9,1... | collective-permute-start | bytes 2555912 | tf_op jit(solution)/shard_map/ppermute | solution.py:41
  410.8 39.9 %all-to-all-start.3 = ((bf16[8,432,128]{2,1,0:T(8,128)(2,1)}), bf16[8,432,128]{2,1,0:T(8,128)(2,1)S(1)}, u32[]{:S(2)}, u32[]{:S(2)}) async-start(bf16[8,432,128]{2,1,0:T(8,128)(2,1)} %get-tuple-element.307), calls=%async_computation.3 | async-start | bytes 1769472 | tf_op jit(solution)/shard_map/all_to_all | solution.py:871
  418.8 20.9 %collective-permute-start.41 = (bf16[2,416,256]{2,1,0:T(8,128)(2,1)}, bf16[2,416,256]{2,1,0:T(8,128)(2,1)S(1)}, u32[]{:S(2)}, u32[]{:S(2)}) collective-permute-start(bf16[2,416,256]{2,1,0:T(8,128)(2,1)} %slice.643), channel_id=1, source_target_pairs={{0,16},{16,0},{1,17},{17,1},{2,18},{18,2},{3,19},{19,3},{4,20},{20... | collective-permute-start | bytes 1277960 | tf_op jit(solution)/shard_map/ppermute | solution.py:41
  443.1 3.8 collective-permute-start.43
  446.9 3.8 collective-permute-start.44
  448.6 8.2 %collective-permute-start.47 = (bf16[416,256]{1,0:T(8,128)(2,1)S(1)}, bf16[416,256]{1,0:T(8,128)(2,1)}, u32[]{:S(2)}, u32[]{:S(2)}) collective-permute-start(bf16[416,256]{1,0:T(8,128)(2,1)S(1)} %slice_bitcast_fusion.2), channel_id=1, source_target_pairs={{0,1},{1,0},{2,3},{3,2},{4,5},{5,4},{6,7},{7,6},{8,9},{9,8},{10,11... | collective-permute-start | bytes 638984 | tf_op jit(solution)/shard_map/ppermute | solution.py:41
  452.4 3.8 collective-permute-start.45
  456.3 4.7 collective-permute-start.46
  (93 other events, 568.7 us)

commit v4 on v3

--- a/solution.py
+++ b/solution.py
@@ -1,3 +1,5 @@
+import math
+
 import jax
 import jax.numpy as jnp
 from jax import lax
@@ -119,11 +121,9 @@
 
 
 def group_gather(block):
-    n, _, w, c = block.shape
-    sent = jnp.broadcast_to(block[None], (8,) + block.shape)
-    got = lax.all_to_all(sent, MEMBERS, 0, 0, tiled=True)
-    got = got.reshape(4, 2, n, w, c)
-    return got.transpose(2, 0, 1, 3, 4).reshape(n, 4, 2 * w, c)
+    return lax.all_to_all(
+        jnp.broadcast_to(block[None], (8,) + block.shape), MEMBERS, 0, 0, tiled=True
+    )
 
 
 def group_scatter(partial):
@@ -158,7 +158,6 @@
     return split.reshape(8, r, o)
 
 
-VMEM_LIMIT = 60 * 1024 * 1024
 HALF = C0 // 2
 
 
@@ -246,37 +245,19 @@
     )
 
 
-def send_out(pieces, me, targets, source, sems):
-    made = []
-    for i, (which, spot, _, count, to) in enumerate(pieces):
-        at = 0 if spot is None else place(spot[0], me, spot[1])
-        here = source.at[pl.ds(to, count), :]
-        if spot is None:
-            pltpu.make_async_copy(here, targets[which].at[0], sems.at[i]).start()
-        else:
-            for side in range(2):
-                inside = at - 16 * side
-
-                @pl.when((inside >= 0) & (inside < 16))
-                def _(here=here, there=targets[which + side], inside=inside, i=i):
-                    pltpu.make_async_copy(here, there.at[inside], sems.at[i]).start()
-
-        made.append(pltpu.make_async_copy(here, targets[which].at[0], sems.at[i]))
-    for copy in made:
-        copy.wait()
-
-
 def on_chip(body, ins, outs, scratch, spaces, flops):
     kinds = {"v": pltpu.VMEM, "s": pltpu.SMEM, "a": pl.ANY}
-    moved = sum(v.size * v.dtype.itemsize for v in list(ins) + list(outs))
+    held = [v for v, k in zip(list(ins) + list(outs), spaces[0] + spaces[1]) if k == "v"]
+    held += [v for v in scratch if len(v.shape) > 1]
+    room = sum(math.prod(v.shape) * jnp.dtype(v.dtype).itemsize for v in held)
     return pl.pallas_call(
         body,
         out_shape=outs,
         in_specs=[pl.BlockSpec(memory_space=kinds[k]) for k in spaces[0]],
         out_specs=[pl.BlockSpec(memory_space=kinds[k]) for k in spaces[1]],
         scratch_shapes=scratch,
-        compiler_params=pltpu.CompilerParams(vmem_limit_bytes=VMEM_LIMIT),
-        cost_estimate=pl.CostEstimate(flops=flops, bytes_accessed=moved, transcendentals=0),
+        compiler_params=pltpu.CompilerParams(vmem_limit_bytes=int(1.25 * room) + 6 * 1024 * 1024),
+        cost_estimate=pl.CostEstimate(flops=0, bytes_accessed=0, transcendentals=0),
     )(*ins)
 
 
@@ -355,10 +336,9 @@
                     kernel_ref[tap * 2 * C0 : (tap + 1) * 2 * C0, :],
                     preferred_element_type=f32,
                 )
-            rows = slice(image * 256, (image + 1) * 256)
-            pre_ref[rows, :] = total
-            act = jax.nn.gelu(total).astype(bf16)
-            logits_ref[rows, :] = jnp.dot(act, head_ref[...], preferred_element_type=f32)
+            pre_ref[image * 256 : (image + 1) * 256, :] = total
+        act = jax.nn.gelu(pre_ref[...]).astype(bf16)
+        logits_ref[...] = jnp.dot(act, head_ref[...], preferred_element_type=f32)
 
     return on_chip(
         body,
@@ -402,10 +382,24 @@
     )
 
 
-def merge_grad_on_chip(me, planes, grad, pieces, shapes):
-    def body(me_ref, planes_ref, grad_ref, *rest):
-        out_refs = rest[: len(shapes)]
-        whole, sems = rest[len(shapes) :]
+def chip_grads(me, planes, grad, act, ups_grad, r3, ru):
+    high, low = r3 // 2, ru // 2
+    pieces = []
+    for chunk in range(32):
+        pieces.append((0, 0, (chunk, "y"), r3 * chunk, high, 0))
+        pieces.append((0, 2, (chunk, "zl"), r3 * chunk + high, high, 0))
+        pieces.append((1, 0, (chunk, "y"), ru * chunk, low, high))
+        pieces.append((1, 2, (chunk, "zl"), ru * chunk + low, low, high))
+
+    def body(me_ref, planes_ref, grad_ref, act_ref, ups_grad_ref, *rest):
+        targets, wholes, sems = rest[:4], rest[4:6], rest[6]
+        values = act_ref[...].reshape(128, C1)
+        for tap in range(4):
+            cells = ups_grad_ref[:, tap // 2, tap % 2].reshape(128, HALF)
+            total = lax.dot_general(
+                values, cells, (((0,), (0,)), ((), ())), preferred_element_type=f32
+            )
+            wholes[1][tap * C1 : (tap + 1) * C1, :] = total.astype(bf16)
         for tap in range(9):
             total = jnp.zeros((2 * C0, HALF), f32)
             for image in range(2):
@@ -415,39 +409,35 @@
                     (((0,), (0,)), ((), ())),
                     preferred_element_type=f32,
                 )
-            whole[tap * 2 * C0 : (tap + 1) * 2 * C0, :] = total.astype(bf16)
-        send_out(pieces, me_ref, out_refs, whole, sems)
+            wholes[0][tap * 2 * C0 : (tap + 1) * 2 * C0, :] = total.astype(bf16)
+        waits = []
+        for i, (whole, pair, spot, start, rows, to) in enumerate(pieces):
+            here = wholes[whole].at[pl.ds(start, rows), :]
+            at = place(spot[0], me_ref, spot[1])
+            for side in range(2):
+                inside = at - 16 * side
+
+                @pl.when((inside >= 0) & (inside < 16))
+                def _(here=here, target=targets[pair + side], inside=inside, rows=rows, to=to, i=i):
+                    there = target.at[inside, pl.ds(to, rows), :]
+                    pltpu.make_async_copy(here, there, sems.at[i]).start()
+
+            there = targets[pair].at[0, pl.ds(to, rows), :]
+            waits.append(pltpu.make_async_copy(here, there, sems.at[i]))
+        for copy in waits:
+            copy.wait()
 
     return on_chip(
         body,
-        (me, planes, grad),
-        tuple(jax.ShapeDtypeStruct(shape, bf16) for shape in shapes),
-        [pltpu.VMEM((18 * C0, HALF), bf16), pltpu.SemaphoreType.DMA((len(pieces),))],
-        ("svv", "a" * len(shapes)),
-        2 * 512 * 18 * C0 * HALF,
-    )
-
-
-def up_grad_on_chip(me, act, grad, pieces, shapes):
-    def body(me_ref, act_ref, grad_ref, *rest):
-        out_refs = rest[: len(shapes)]
-        whole, sems = rest[len(shapes) :]
-        values = act_ref[...].reshape(128, C1)
-        for tap in range(4):
-            cells = grad_ref[:, tap // 2, tap % 2].reshape(128, HALF)
-            total = lax.dot_general(
-                values, cells, (((0,), (0,)), ((), ())), preferred_element_type=f32
-            )
-            whole[tap * C1 : (tap + 1) * C1, :] = total.astype(bf16)
-        send_out(pieces, me_ref, out_refs, whole, sems)
-
-    return on_chip(
-        body,
-        (me, act, grad),
-        tuple(jax.ShapeDtypeStruct(shape, bf16) for shape in shapes),
-        [pltpu.VMEM((4 * C1, HALF), bf16), pltpu.SemaphoreType.DMA((len(pieces),))],
-        ("svv", "a" * len(shapes)),
-        2 * 128 * C1 * 4 * HALF,
+        (me, planes, grad, act, ups_grad),
+        (jax.ShapeDtypeStruct((16, high + low, HALF), bf16),) * 4,
+        [
+            pltpu.VMEM((18 * C0, HALF), bf16),
+            pltpu.VMEM((4 * C1, HALF), bf16),
+            pltpu.SemaphoreType.DMA((len(pieces),)),
+        ],
+        ("svvvv", "aaaa"),
+        0,
     )
 
 
@@ -530,19 +520,55 @@
     )
 
 
+def second_back_on_chip(grad, kernel):
+    images = grad.shape[1]
+
+    def body(grad_ref, kernel_ref, order_ref, inner_ref, sides_ref, parts):
+        for member in range(8):
+            row, core = member // 2, member % 2
+            for image in range(images):
+                order_ref[image, row, core * 32 : (core + 1) * 32] = grad_ref[member, image, 0]
+        parts[...] = jnp.zeros(parts.shape, f32)
+        for image in range(images):
+            values = order_ref[image].reshape(256, C1)
+            for tap in range(9):
+                got = lax.dot_general(
+                    values,
+                    kernel_ref[tap * 128 : (tap + 1) * 128, :],
+                    (((1,), (1,)), ((), ())),
+                    preferred_element_type=f32,
+                )
+                high = tap // 3
+                parts[tap % 3, image, high : high + 4] += got.reshape(4, 64, 128)
+        line = lax.broadcasted_iota(jnp.int32, (64, 1), 0)
+        for image in range(images):
+            for row in range(6):
+                before = pltpu.roll(parts[0, image, row], 63, 0)
+                later = pltpu.roll(parts[2, image, row], 1, 0)
+                inner_ref[image, row] = (
+                    parts[1, image, row]
+                    + jnp.where(line == 63, 0.0, before)
+                    + jnp.where(line == 0, 0.0, later)
+                )
+                sides_ref[0, image, row : row + 1, :] = parts[0, image, row, 0:1, :]
+                sides_ref[1, image, row : row + 1, :] = parts[2, image, row, 63:64, :]
+
+    return on_chip(
+        body,
+        (grad, kernel),
+        (
+            jax.ShapeDtypeStruct((images, 4, 64, C1), bf16),
+            jax.ShapeDtypeStruct((images, 6, 64, 128), f32),
+            jax.ShapeDtypeStruct((2, images, 6, 128), f32),
+        ),
+        [pltpu.VMEM((3, images, 6, 64, 128), f32)],
+        ("vv", "vvv"),
+        0,
+    )
+
+
 def by_shift(cells):
     return jnp.stack([cells[:, :, shift : shift + 64] for shift in range(3)])
-
-
-def split_list(rows, zhs):
-    if zhs != 2:
-        return [(0, None, 0, 32 * rows, 0)], [(1, 32 * rows, HALF)]
-    half = rows // 2
-    pieces = []
-    for chunk in range(32):
-        pieces.append((0, (chunk, "y"), 0, half, rows * chunk))
-        pieces.append((2, (chunk, "zl"), 0, half, rows * chunk + half))
-    return pieces, [(16, half, HALF)] * 4
 
 
 def last_sum(whole):
@@ -789,11 +815,6 @@
     )
     grad_pre_three = gelu_back(pre_three, grad_act_three).astype(bf16)
     border, border_sides = halo(grad_pre_three)
-    split_three, shape_three = split_list(r3 * zhs // 2, zhs)
-    merge_grad = merge_grad_on_chip(
-        me, planes, grad_pre_three.reshape(512, HALF), split_three, shape_three
-    )
-    border, border_sides, merge_grad = lax.optimization_barrier((border, border_sides, merge_grad))
     own_grad, away_grad = ups_grad_on_chip(me, border, border_sides, kernel_merge)
     grad_upper = (own_grad + swapped(away_grad, "core").astype(f32)).astype(bf16)
     grad_upper = grad_upper.reshape(2, 2, 2, 64, HALF)
@@ -807,69 +828,109 @@
     grad_pre_two = gelu_back(pre_two, grad_act_two).astype(bf16)
 
     grad_two = group_gather(grad_pre_two)
-    split_up, shape_up = split_list(ru * zhs // 2, zhs)
-    up_grad = up_grad_on_chip(me, act_chip, grad_upper, split_up, shape_up)
-    grad_two, merge_grad, up_grad = lax.optimization_barrier((grad_two, merge_grad, up_grad))
     if zhs == 2:
+        grad_two, inner, sides = second_back_on_chip(grad_two, kernel_two.reshape(-1, C1))
+        grad_two, inner, sides, planes = lax.optimization_barrier((grad_two, inner, sides, planes))
+        chip_parts = chip_grads(
+            me, planes, grad_pre_three.reshape(512, HALF), act_chip, grad_upper, r3, ru
+        )
+        chip_parts, act_shifts = lax.optimization_barrier((chip_parts, act_shifts))
         second_grad = second_grad_on_chip(me, act_shifts, grad_two, r2, 16 * zhs)
-    else:
-        second_grad = kernel_grad(act_one, grad_two)
-    spill = convolve(grad_two, turned(kernel_two), 2)
-    if zhs == 2:
-        row = jnp.where(zh == 0, spill[:, -1:], spill[:, :1])
-        column = jnp.where(x == 0, spill[:, 1:-1, -1:], spill[:, 1:-1, :1])
-        corner = jnp.where(x == 0, row[:, :, -1:], row[:, :, :1])
+        row = jnp.where(zh == 0, inner[:, 5:], inner[:, :1])
+        column = jnp.where(x == 0, sides[1], sides[0])
+        corner = jnp.where(zh == 0, column[:, 5:], column[:, :1])[:, :, None]
+        column = swapped(column[:, 1:5, None], "x")
         corner = lax.ppermute(corner, ("zh", "x"), [(i, 3 - i) for i in range(4)])
-        row = swapped(row[:, :, 1:-1], "zh")
-        column = swapped(column, "x")
-        row, column, corner, merge_grad, up_grad = lax.optimization_barrier(
-            (row, column, corner, merge_grad, up_grad)
+        row = swapped(row, "zh")
+        row, column, corner, chip_parts = lax.optimization_barrier(
+            (row, column, corner, chip_parts)
         )
         at_row = jnp.arange(4)[None, :, None, None] == jnp.where(zh == 0, 3, 0)
         at_column = jnp.arange(64)[None, None, :, None] == jnp.where(x == 0, 63, 0)
         core_part = (
-            spill[:, 1:-1, 1:-1]
+            inner[:, 1:5]
             + jnp.where(at_row, row, 0.0)
             + jnp.where(at_column, column, 0.0)
             + jnp.where(at_row & at_column, corner, 0.0)
         )
     else:
+        cells = planes.reshape(2, 4, 4, 64, 2 * C0)
+        chip_parts = (
+            jnp.concatenate(
+                [
+                    jnp.einsum(
+                        "iabwc,iabwo->co",
+                        cells[:, high : high + 2, wide : wide + 2],
+                        grad_pre_three,
+                        preferred_element_type=f32,
+                    )
+                    for high in range(3)
+                    for wide in range(3)
+                ]
+            ).astype(bf16),
+            jnp.einsum(
+                "iwc,iabwo->abco", act_chip, grad_upper, preferred_element_type=f32
+            ).astype(bf16),
+        )
+        images, width = grad_two.shape[1], grad_two.shape[3]
+        grad_two = grad_two.reshape(4, 2, images, width, C1).transpose(2, 0, 1, 3, 4)
+        grad_two = grad_two.reshape(images, 4, 2 * width, C1)
+        second_grad = kernel_grad(act_one, grad_two)
+        spill = convolve(grad_two, turned(kernel_two), 2)
         inner = spill[:, 1:-1]
         inner = inner.at[:, :1].add(shifted(spill[:, -1:], "zh", 1))
         inner = inner.at[:, -1:].add(shifted(spill[:, :1], "zh", -1))
         core_part = inner[:, :, 1:-1]
         core_part = core_part.at[:, :, :1].add(shifted(inner[:, :, -1:], "x", 1))
         core_part = core_part.at[:, :, -1:].add(shifted(inner[:, :, :1], "x", -1))
-    merge_grad, up_grad = sent(merge_grad, "zl", "y"), sent(up_grad, "zl", "y")
     grad_pre_one = gelu_back(pre_one[:, 1:-1, 1:-1], core_part).astype(bf16)
     tiled = zhs == 2
     if tiled:
         grad_pre_one, second_grad = lax.optimization_barrier((grad_pre_one, second_grad))
         first_grad = first_grad_on_chip(me, feat_shifts, grad_pre_one, r1, 16 * zhs)
-        stays, goes = (jnp.concatenate(pair, axis=1) for pair in zip(first_grad, second_grad))
-        part = stays.astype(f32) + swapped(goes, "x").astype(f32)
-        part = part.reshape(2, 8, r1 + r2, 128)
-        away = lax.dynamic_index_in_dim(part, 1 - zh, axis=0, keepdims=False).astype(bf16)
-        own = lax.dynamic_index_in_dim(part, zh, axis=0, keepdims=False)
-        got = swapped(away, "zh")
-        merge_grad, up_grad = added(merge_grad), added(up_grad)
-        merge_grad, up_grad = sent(merge_grad, "y", "zl"), sent(up_grad, "y", "zl")
-        away, merge_grad, up_grad = after(away, merge_grad, up_grad)
-        merge_grad, up_grad = added(merge_grad), added(up_grad)
+        def shard_sum(own, got):
+            return (own.astype(f32) + got.astype(f32)).reshape(2, 8, -1, 128)
+
+        def leave(part):
+            away = lax.dynamic_index_in_dim(part, 1 - zh, axis=0, keepdims=False).astype(bf16)
+            own = lax.dynamic_index_in_dim(part, zh, axis=0, keepdims=False)
+            return own, away, swapped(away, "zh")
+
+        chip_parts = sent(chip_parts, "zl", "y")
+        chip_parts = sent(added(chip_parts), "y", "zl")
+        second_stays = after(chip_parts[0], second_grad[0])[1]
+        two_own, two_away, two_got = leave(shard_sum(second_stays, swapped(second_grad[1], "x")))
+        two_away, first_stays = after(two_away, first_grad[0])
+        one_own, one_away, one_got = leave(shard_sum(first_stays, swapped(first_grad[1], "x")))
+        one_away, chip_parts = after(one_away, chip_parts)
+        chip_parts = added(chip_parts)
         chip_stays, chip_goes = (
-            jnp.concatenate([merge_grad[i], merge_grad[i + 2], up_grad[i], up_grad[i + 2]], axis=1)
-            for i in range(2)
+            jnp.concatenate([chip_parts[i], chip_parts[i + 2]], axis=1) for i in range(2)
         )
         chip_got = swapped(chip_goes, "x")
-        own = after(chip_goes, own)[1]
-        part = own + got.astype(f32)
-        part_low = part.astype(bf16)
-        chip_stays = after(part_low, chip_stays)[1]
+        chip_goes, two_own = after(chip_goes, two_own)
+        part_two = two_own + two_got.astype(f32)
+        two_low, chip_stays, one_own = after(part_two.astype(bf16), chip_stays, one_own)
         chip_parts = chip_stays.astype(f32) + chip_got.astype(f32)
-        part_chip = chip_parts[:2] + swapped(chip_parts[2:].astype(bf16), "zh").astype(f32)
-        sq_kernels = jnp.sum(part * part)
-        part = lax.all_to_all(part_low, MEMBERS, 0, 0, tiled=True)
+        chip_goes = chip_parts[2:].astype(bf16)
+        part_chip = chip_parts[:2] + swapped(chip_goes, "zh").astype(f32)
+        chip_goes, one_own = after(chip_goes, one_own)
+        part_one = one_own + one_got.astype(f32)
+        one_low = part_one.astype(bf16)
+        sq_kernels = jnp.sum(part_one * part_one) + jnp.sum(part_two * part_two)
+        part = jnp.concatenate([one_low, two_low], axis=1)
+        part = lax.all_to_all(part, MEMBERS, 0, 0, tiled=True)
         part_one, part_two = part[:, :r1], part[:, r1:]
+        half = r3 // 2
+        part_chip = jnp.concatenate(
+            [
+                part_chip[:, :half],
+                part_chip[:, half + ru // 2 : r3 + ru // 2],
+                part_chip[:, half : half + ru // 2],
+                part_chip[:, r3 + ru // 2 :],
+            ],
+            axis=1,
+        )
         part_two = part_two.reshape(8, r2 // 8, C1 // 128, 128).transpose(1, 0, 2, 3)
         share_two = part_two.reshape(-1).astype(f32)
     else:
@@ -883,7 +944,7 @@
         sq_kernels = jnp.sum(share_two * share_two) + jnp.sum(part_one * part_one)
         part_one = lax.all_to_all(part_one.astype(bf16), MEMBERS, 0, 0, tiled=True)
         part_chip = jnp.concatenate(
-            [last_sum(merge_grad[0]), last_sum(up_grad[0])], axis=1
+            [last_sum(chip_parts[0]), last_sum(chip_parts[1])], axis=1
         )
     share_one = jnp.einsum("qrm,cqm->rc", part_one, sorting, preferred_element_type=f32).reshape(-1)
     sq_chip = jnp.sum(part_chip * part_chip)
@@ -920,9 +981,7 @@
     bias_total = packed[: biases.shape[0]]
     head_total = packed[biases.shape[0] : -2].reshape(head_weight.shape)
     sq_total, loss_total = packed[-2], packed[-1]
-    grad_norm = jnp.sqrt(
-        sq_total + jnp.sum(bias_total * bias_total) + jnp.sum(head_total * head_total)
-    )
+    grad_norm = jnp.sqrt(sq_total + jnp.sum(jnp.square(packed[:-2])))
     factor = clip_norm / jnp.maximum(grad_norm, clip_norm)
     outs = ()
     for weight, moment, second, grad, decay in (

time: 485 us -> 443 us (0.913)
  waiting for transfers between devices: 201 us -> 168 us
  local copies, waits for them, and re-layouts: 54 us -> 66.4 us
  Pallas kernels: 49 us -> 40.5 us
  matrix products: 24.2 us -> 16 us
  other arithmetic: 65.3 us -> 57.6 us
    ppermute x41 -> x39, waiting for transfers between devices: 179 us -> 151 us  [swapped(): return lax.ppermute(values, axis, [(0, 1), (1, 0)])]
    unnamed x193 -> x157, local copies, waits for them, and re-layouts: 12.8 us -> 23.7 us
    conv_general_dilated x3 -> x2, matrix products: 20 us -> 11.2 us  [convolve(): lax.conv_general_dilated(values, kernel, (1, 1), ((pad, pad), (pad, pad))...]
    pallas_call x8, Pallas kernels: 49 us -> 40.5 us  [on_chip(): pl.pallas_call(body, out_shape=outs, in_specs=[pl.BlockSpec(memory_space=...]
    all_to_all x1, waiting for transfers between devices: 6.36 us -> 1.09 us  [group_scatter(): lax.all_to_all(sent.reshape(8, n, w2 // 2, c), MEMBERS, 0, 0, tiled=True)]
    ppermute x41 -> x39, starting transfers between devices: 38.4 us -> 36.7 us  [swapped(): return lax.ppermute(values, axis, [(0, 1), (1, 0)])]
  transfers between devices with their start and end apart: 52 -> 50, of which waited for: 29 -> 28; matrix products, arithmetic and copies ran while one was open for 18% -> 21% of each run, Pallas kernels for 5% -> 7%
where the time goes in v4:
time: 443 us; the launch traced here: 435 us
  waiting for transfers between devices  168 us (38%)
  starting transfers between devices  77.3 us (17%)
  local copies, waits for them, and re-layouts  66.4 us (15%)
  other arithmetic  57.6 us (13%)
  Pallas kernels  40.5 us (9%)
  matrix products  16 us (4%)
  between operations  8.89 us (2%)
    ppermute x39, waiting for transfers between devices, swapped(): return lax.ppermute(values, axis, [(0, 1), (1, 0)])  151 us
    pallas_call x8, Pallas kernels, on_chip(): pl.pallas_call(body, out_shape=outs, in_specs=[pl.BlockSpec(memory_space=...  40.5 us
    ppermute x39, starting transfers between devices, swapped(): return lax.ppermute(values, axis, [(0, 1), (1, 0)])  36.7 us
    unnamed x157, local copies, waits for them, and re-layouts  23.7 us
    ppermute x6, starting transfers between devices, shifted(): lax.ppermute(values, axis, [(i, i + step) for i in range(count) if 0 <= i...  19.7 us
    conv_general_dilated x2, matrix products, convolve(): lax.conv_general_dilated(values, kernel, (1, 1), ((pad, pad), (pad, pad))...  11.2 us
    all_to_all x1, waiting for transfers between devices, group_gather(): lax.all_to_all(jnp.broadcast_to(block[None], (8,) + block.shape), MEMBERS...  9.36 us
    sub x6, other arithmetic, adamw(): weight - learn_rate * (corrected / (spread + epsilon) + decay * weight)  9.02 us
  transfers between devices with their start and end apart: 50, of which 28 were waited for; matrix products, arithmetic and copies ran while one was open for 21% of the time, Pallas kernels for 7%

profile of v4, /device:TPU:0, one launch (start us, length us, event | category | flops | bytes accessed | tf_op | source)
XLA Modules:
  0.0 434.6 jit_solution(12308702539612859806)
XLA Ops:
  7.4 5.4 %all-to-all-start = ((bf16[8,704,128]{2,1,0:T(8,128)(2,1)}), bf16[8,704,128]{2,1,0:T(8,128)(2,1)}, u32[]{:S(2)}, u32[]{:S(2)}) async-start(bf16[8,704,128]{2,1,0:T(8,128)(2,1)} %pad_maximum_fusion.3), calls=%async_computation | async-start | bytes 2883584 | tf_op jit(solution)/shard_map/all_to_all | solution.py:672
  18.3 3.0 collective-permute-start.1
  22.9 15.6 %collective-permute-done.1 = bf16[2,416,256]{2,1,0:T(8,128)(2,1)S(1)} collective-permute-done((bf16[2,416,256]{2,1,0:T(8,128)(2,1)S(1)}, bf16[2,416,256]{2,1,0:T(8,128)(2,1)S(1)}, u32[]{:S(2)}, u32[]{:S(2)}) %collective-permute-start.1) | collective-permute-done | bytes 426016 | tf_op jit(solution)/shard_map/ppermute | solution.py:43
  48.2 17.5 %collective-permute-done.11 = bf16[2,2,512]{2,1,0:T(2,128)(2,1)S(1)} collective-permute-done((bf16[2,2,512]{2,1,0:T(2,128)(2,1)S(1)}, bf16[2,2,512]{2,1,0:T(2,128)(2,1)S(1)}, u32[]{:S(2)}, u32[]{:S(2)}) %collective-permute-start.11) | collective-permute-done | bytes 4128 | tf_op jit(solution)/shard_map/ppermute | solution.py:43
  68.0 5.5 %collective-permute-start.12 = (bf16[272,512]{1,0:T(8,128)(2,1)}, bf16[272,512]{1,0:T(8,128)(2,1)}, u32[]{:S(2)}, u32[]{:S(2)}) collective-permute-start(bf16[272,512]{1,0:T(8,128)(2,1)} %get-tuple-element.362), channel_id=1, source_target_pairs={{0,4},{4,8},{8,12},{12,16},{16,20},{20,24},{24,28},{1,5},{5,9},{9,... | collective-permute-start | bytes 835592 | tf_op jit(solution)/shard_map/ppermute | solution.py:37
  76.4 2.9 collective-permute-start.7
  79.4 19.4 %collective-permute-done.3 = bf16[4608,128]{1,0:T(8,128)(2,1)S(1)} collective-permute-done((bf16[4608,128]{1,0:T(8,128)(2,1)S(1)}, bf16[4608,128]{1,0:T(8,128)(2,1)S(1)}, u32[]{:S(2)}, u32[]{:S(2)}) %collective-permute-start.3) | collective-permute-done | bytes 1179680 | tf_op jit(solution)/shard_map/ppermute | solution.py:43
  108.5 2.8 pad_maximum_fusion.7
  112.5 5.5 %collective-permute-done.7 = bf16[8,208,256]{2,1,0:T(8,128)(2,1)} collective-permute-done((bf16[8,208,256]{2,1,0:T(8,128)(2,1)}, bf16[8,208,256]{2,1,0:T(8,128)(2,1)}, u32[]{:S(2)}, u32[]{:S(2)}) %collective-permute-start.7) | collective-permute-done | bytes 852000 | tf_op jit(solution)/shard_map/ppermute | solution.py:43
  118.0 2.7 collective-permute-done.4
  128.4 2.4 slice.431
  132.7 4.1 fusion.10
  137.9 4.7 %collective-permute-done.8 = bf16[4608,128]{1,0:T(8,128)(2,1)} collective-permute-done((bf16[4608,128]{1,0:T(8,128)(2,1)}, bf16[4608,128]{1,0:T(8,128)(2,1)}, u32[]{:S(2)}, u32[]{:S(2)}) %collective-permute-start.8) | collective-permute-done | bytes 1179680 | tf_op jit(solution)/shard_map/ppermute | solution.py:43
  144.4 2.1 fusion.2
  146.5 5.3 %reshape.743 = bf16[3,3,128,1024]{3,2,1,0:T(8,128)(2,1)} reshape(bf16[2,2,2,2,2,288,128]{6,5,4,3,2,1,0:T(8,128)(2,1)} %fusion.2) | data formatting | bytes 4718592 | tf_op jit(solution)/shard_map/reshape | solution.py:739
  151.8 7.1 %fusion.50 = bf16[2,4,64,1024]{3,0,2,1:T(2,128)(2,1)} fusion(bf16[3,3,128,1024]{3,2,1,0:T(8,128)(2,1)} %reshape.743, bf16[2,6,66,128]{3,2,1,0:T(8,128)(2,1)} %get-tuple-element.327), kind=kOutput, calls=%fused_computation.157 | convolution fusion | flops 1207959552 | bytes 3610624 | tf_op jit(solution)/shard_map/conv_general_dilated | solution.py:86
  158.9 2.7 collective-permute-done.10.rest_3_
  161.6 3.6 all-to-all-start.1
  168.2 8.0 %shard_map.382 = (bf16[9216,256]{1,0:T(8,128)(2,1)S(1)}, bf16[4096,256]{1,0:T(8,128)(2,1)S(1)}) custom-call(s32[5]{0:T(128)S(1)} %stack.87.me_ref, bf16[16,208,256]{2,1,0:T(8,128)(2,1)S(1)} %copy-done.6, bf16[16,208,256]{2,1,0:T(8,128)(2,1)} %collective-permute-done.9.rest_1_, bf16[16,208,256]{2,1,0:T(8,128)(2,1)S(1)} %copy-done.8, ...), custom_call_target="tpu_custom_call" | custom-call | tf_op jit(solution)/shard_map/pallas_call | solution.py:253
  176.2 2.2 copy-done
  189.1 5.2 %collective-permute-start.17 = (bf16[272,256]{1,0:T(8,128)(2,1)S(1)}, bf16[272,256]{1,0:T(8,128)(2,1)}, u32[]{:S(2)}, u32[]{:S(2)}) collective-permute-start(bf16[272,256]{1,0:T(8,128)(2,1)S(1)} %get-tuple-element.360), channel_id=1, source_target_pairs={{0,4},{4,8},{8,12},{12,16},{16,20},{20,24},{24,28},{1,5},{5,9},{9,... | collective-permute-start | bytes 417800 | tf_op jit(solution)/shard_map/ppermute | solution.py:37
  201.1 2.3 copy-done.1
  203.4 4.0 shard_map.384
  212.0 4.1 convert_reduce_fusion.1
  221.2 5.1 %collective-permute-start.23 = (bf16[272,256]{1,0:T(8,128)(2,1)S(1)}, bf16[272,256]{1,0:T(8,128)(2,1)S(1)}, u32[]{:S(2)}, u32[]{:S(2)}) collective-permute-start(bf16[272,256]{1,0:T(8,128)(2,1)S(1)} %get-tuple-element.358), channel_id=1, source_target_pairs={{0,4},{4,8},{8,12},{12,16},{16,20},{20,24},{24,28},{1,5},{5,9},{9,... | collective-permute-start | bytes 417800 | tf_op jit(solution)/shard_map/ppermute | solution.py:37
  227.8 2.9 collective-permute-done.23
  232.1 2.3 copy-done.2
  242.5 8.1 %all-to-all-start.2 = ((bf16[8,2,1,32,1024]{4,3,2,1,0:T(8,128)(2,1)}), bf16[8,2,1,32,1024]{4,3,2,1,0:T(8,128)(2,1)S(1)}, u32[]{:S(2)}, u32[]{:S(2)}) async-start(bf16[8,2,1,32,1024]{4,3,2,1,0:T(8,128)(2,1)} %broadcast_in_dim.182), calls=%async_computation.2 | async-start | bytes 2097152 | tf_op jit(solution)/shard_map/all_to_all | solution.py:124
  252.0 3.6 reshape_reshape.3.kernel_ref
  255.7 9.4 %all-to-all-done.2.grad_ref = bf16[8,2,1,32,1024]{4,3,2,1,0:T(8,128)(2,1)S(1)} async-done(((bf16[8,2,1,32,1024]{4,3,2,1,0:T(8,128)(2,1)}), bf16[8,2,1,32,1024]{4,3,2,1,0:T(8,128)(2,1)S(1)}, u32[]{:S(2)}, u32[]{:S(2)}) %all-to-all-start.2) | async-done | bytes 1048608 | tf_op jit(solution)/shard_map/all_to_all | solution.py:124
  265.0 2.7 shard_map.386
  267.8 3.9 collective-permute-start.27
  274.7 11.9 %shard_map.387 = (bf16[16,208,256]{2,1,0:T(8,128)(2,1)S(1)}, bf16[16,208,256]{2,1,0:T(8,128)(2,1)}, bf16[16,208,256]{2,1,0:T(8,128)(2,1)S(1)}, bf16[16,208,256]{2,1,0:T(8,128)(2,1)}) custom-call(s32[5]{0:T(128)S(1)} %stack.87.me_ref, bf16[2,4,4,64,1024]{4,3,2,1,0:T(8,128)(2,1)S(1)} %copy-done.4, bf16[512,256]{1,0:T(8,128)(2,1)S(1)} %bitcast.234, ...), custom_call_target="tpu_custom_call" | custom-call | tf_op jit(solution)/shard_map/pallas_call | solution.py:253
  293.0 6.7 %shard_map.388 = (bf16[16,288,128]{2,1,0:T(8,128)(2,1)S(1)}, bf16[16,288,128]{2,1,0:T(8,128)(2,1)}) custom-call(s32[5]{0:T(128)S(1)} %stack.87.me_ref, bf16[3,2,6,64,128]{4,3,2,1,0:T(8,128)(2,1)S(1)} %pad_maximum_fusion.16.cells_ref, bf16[2,4,64,1024]{3,2,1,0:T(8,128)(2,1)S(1)} %copy-done.18), custom_call_target="tpu_custom_call" | custom-call | tf_op jit(solution)/shard_map/pallas_call | solution.py:253
  307.3 4.3 shard_map.389
  312.4 15.4 %collective-permute-done.33 = bf16[16,208,256]{2,1,0:T(8,128)(2,1)} collective-permute-done((bf16[16,208,256]{2,1,0:T(8,128)(2,1)}, bf16[16,208,256]{2,1,0:T(8,128)(2,1)}, u32[]{:S(2)}, u32[]{:S(2)}) %collective-permute-start.33) | collective-permute-done | bytes 1703968 | tf_op jit(solution)/shard_map/ppermute | solution.py:43
  334.8 2.4 collective-permute-start.36
  337.2 3.1 collective-permute-done.32
  340.4 20.9 %collective-permute-done.35 = bf16[8,208,256]{2,1,0:T(8,128)(2,1)S(1)} collective-permute-done((bf16[8,208,256]{2,1,0:T(8,128)(2,1)S(1)}, bf16[8,208,256]{2,1,0:T(8,128)(2,1)S(1)}, u32[]{:S(2)}, u32[]{:S(2)}) %collective-permute-start.35) | collective-permute-done | bytes 852000 | tf_op jit(solution)/shard_map/ppermute | solution.py:43
  364.5 15.4 %collective-permute-done.37 = bf16[4,416,256]{2,1,0:T(8,128)(2,1)S(1)} collective-permute-done((bf16[4,416,256]{2,1,0:T(8,128)(2,1)S(1)}, bf16[4,416,256]{2,1,0:T(8,128)(2,1)S(1)}, u32[]{:S(2)}, u32[]{:S(2)}) %collective-permute-start.37) | collective-permute-done | bytes 852000 | tf_op jit(solution)/shard_map/ppermute | solution.py:43
  382.7 3.8 all-to-all-start.3
  391.0 7.4 %collective-permute-done.39 = bf16[2,416,256]{2,1,0:T(8,128)(2,1)} collective-permute-done((bf16[2,416,256]{2,1,0:T(8,128)(2,1)}, bf16[2,416,256]{2,1,0:T(8,128)(2,1)}, u32[]{:S(2)}, u32[]{:S(2)}) %collective-permute-start.39) | collective-permute-done | bytes 426016 | tf_op jit(solution)/shard_map/ppermute | solution.py:43
  403.9 2.2 collective-permute-done.41
  407.8 2.1 collective-permute-done.42
  411.3 3.8 collective-permute-done.43
  416.1 3.7 collective-permute-done.44
  423.8 2.9 multiply_subtract_fusion.2
  426.7 2.4 multiply_subtract_fusion
  (452 shorter events, 141.2 us)
Async XLA Ops:
  7.4 33.3 %all-to-all-start = ((bf16[8,704,128]{2,1,0:T(8,128)(2,1)}), bf16[8,704,128]{2,1,0:T(8,128)(2,1)}, u32[]{:S(2)}, u32[]{:S(2)}) async-start(bf16[8,704,128]{2,1,0:T(8,128)(2,1)} %pad_maximum_fusion.3), calls=%async_computation | async-start | bytes 2883584 | tf_op jit(solution)/shard_map/all_to_all | solution.py:672
  14.4 3.9 collective-permute-start
  15.4 6.3 %collective-permute-start.2 = (bf16[2,2,2,32,512]{4,1,0,3,2:T(2,128)(2,1)S(1)}, bf16[2,2,2,32,512]{4,1,0,3,2:T(2,128)(2,1)S(1)}, u32[]{:S(2)}, u32[]{:S(2)}) collective-permute-start(bf16[2,2,2,32,512]{4,1,0,3,2:T(2,128)(2,1)S(1)} %bitcast.279), channel_id=1, source_target_pairs={{0,1},{1,0},{2,3},{3,2},{4,5},{5,4},{6,7},{7,6},{8,9},{9,8},{10,11... | collective-permute-start | bytes 786440 | tf_op jit(solution)/shard_map/ppermute | solution.py:43
  15.6 2.7 collective-permute-start.14
  18.3 20.2 %collective-permute-start.1 = (bf16[2,416,256]{2,1,0:T(8,128)(2,1)S(1)}, bf16[2,416,256]{2,1,0:T(8,128)(2,1)S(1)}, u32[]{:S(2)}, u32[]{:S(2)}) collective-permute-start(bf16[2,416,256]{2,1,0:T(8,128)(2,1)S(1)} %pad_maximum_fusion.20), channel_id=1, source_target_pairs={{0,16},{16,0},{1,17},{17,1},{2,18},{18,2},{3,19},{19,3},{4,20},{20... | collective-permute-start | bytes 1277960 | tf_op jit(solution)/shard_map/ppermute | solution.py:43
  43.7 55.2 %collective-permute-start.3 = (bf16[4608,128]{1,0:T(8,128)(2,1)S(1)}, bf16[4608,128]{1,0:T(8,128)(2,1)S(1)}, u32[]{:S(2)}, u32[]{:S(2)}) collective-permute-start(bf16[4608,128]{1,0:T(8,128)(2,1)S(1)} %pad_maximum_fusion.5), channel_id=1, source_target_pairs={{0,16},{16,0},{1,17},{17,1},{2,18},{18,2},{3,19},{19,3},{4,20},{20... | collective-permute-start | bytes 3538952 | tf_op jit(solution)/shard_map/ppermute | solution.py:43
  45.1 28.3 %collective-permute-start.5 = (bf16[4,416,256]{2,1,0:T(8,128)(2,1)S(1)}, bf16[4,416,256]{2,1,0:T(8,128)(2,1)S(1)}, u32[]{:S(2)}, u32[]{:S(2)}) collective-permute-start(bf16[4,416,256]{2,1,0:T(8,128)(2,1)S(1)} %pad_maximum_fusion.9), channel_id=1, source_target_pairs={{0,2},{2,0},{1,3},{3,1},{4,6},{6,4},{5,7},{7,5},{8,10},{10,8},{9,1... | collective-permute-start | bytes 2555912 | tf_op jit(solution)/shard_map/ppermute | solution.py:43
  47.7 18.0 %collective-permute-start.11 = (bf16[2,2,512]{2,1,0:T(2,128)(2,1)S(1)}, bf16[2,2,512]{2,1,0:T(2,128)(2,1)S(1)}, u32[]{:S(2)}, u32[]{:S(2)}) collective-permute-start(bf16[2,2,512]{2,1,0:T(2,128)(2,1)S(1)} %fusion.59), channel_id=1, source_target_pairs={{0,2},{2,0},{1,3},{3,1},{4,6},{6,4},{5,7},{7,5},{8,10},{10,8},{9,1... | collective-permute-start | bytes 12296 | tf_op jit(solution)/shard_map/ppermute | solution.py:43
  66.7 37.5 %collective-permute-start.13 = (bf16[272,512]{1,0:T(8,128)(2,1)}, bf16[272,512]{1,0:T(8,128)(2,1)}, u32[]{:S(2)}, u32[]{:S(2)}) collective-permute-start(bf16[272,512]{1,0:T(8,128)(2,1)} %get-tuple-element.363), channel_id=1, source_target_pairs={{4,0},{8,4},{12,8},{16,12},{20,16},{24,20},{28,24},{5,1},{9,5},{13... | collective-permute-start | bytes 835592 | tf_op jit(solution)/shard_map/ppermute | solution.py:37
  68.0 38.3 %collective-permute-start.12 = (bf16[272,512]{1,0:T(8,128)(2,1)}, bf16[272,512]{1,0:T(8,128)(2,1)}, u32[]{:S(2)}, u32[]{:S(2)}) collective-permute-start(bf16[272,512]{1,0:T(8,128)(2,1)} %get-tuple-element.362), channel_id=1, source_target_pairs={{0,4},{4,8},{8,12},{12,16},{16,20},{20,24},{24,28},{1,5},{5,9},{9,... | collective-permute-start | bytes 835592 | tf_op jit(solution)/shard_map/ppermute | solution.py:37
  74.8 37.6 %collective-permute-start.6 = (bf16[8,208,256]{2,1,0:T(8,128)(2,1)}, bf16[8,208,256]{2,1,0:T(8,128)(2,1)}, u32[]{:S(2)}, u32[]{:S(2)}) collective-permute-start(bf16[8,208,256]{2,1,0:T(8,128)(2,1)} %get-tuple-element.110), channel_id=1, source_target_pairs={{0,4},{4,0},{1,5},{5,1},{2,6},{6,2},{3,7},{7,3},{8,12},{12,8},{9,1... | collective-permute-start | bytes 2555912 | tf_op jit(solution)/shard_map/ppermute | solution.py:43
  76.4 41.5 %collective-permute-start.7 = (bf16[8,208,256]{2,1,0:T(8,128)(2,1)}, bf16[8,208,256]{2,1,0:T(8,128)(2,1)}, u32[]{:S(2)}, u32[]{:S(2)}) collective-permute-start(bf16[8,208,256]{2,1,0:T(8,128)(2,1)} %get-tuple-element.112), channel_id=1, source_target_pairs={{0,8},{8,0},{1,9},{9,1},{2,10},{10,2},{3,11},{11,3},{4,12},{12,4},... | collective-permute-start | bytes 2555912 | tf_op jit(solution)/shard_map/ppermute | solution.py:43
  102.3 18.4 %collective-permute-start.4 = (bf16[2688,128]{1,0:T(8,128)(2,1)S(1)}, bf16[2688,128]{1,0:T(8,128)(2,1)S(1)}, u32[]{:S(2)}, u32[]{:S(2)}) collective-permute-start(bf16[2688,128]{1,0:T(8,128)(2,1)S(1)} %pad_maximum_fusion.15), channel_id=1, source_target_pairs={{0,2},{2,0},{1,3},{3,1},{4,6},{6,4},{5,7},{7,5},{8,10},{10,8},{9,1... | collective-permute-start | bytes 2064392 | tf_op jit(solution)/shard_map/ppermute | solution.py:43
  112.3 30.2 %collective-permute-start.8 = (bf16[4608,128]{1,0:T(8,128)(2,1)}, bf16[4608,128]{1,0:T(8,128)(2,1)}, u32[]{:S(2)}, u32[]{:S(2)}) collective-permute-start(bf16[4608,128]{1,0:T(8,128)(2,1)} %bitcast.22), channel_id=1, source_target_pairs={{0,2},{2,0},{1,3},{3,1},{4,6},{6,4},{5,7},{7,5},{8,10},{10,8},{9,1... | collective-permute-start | bytes 3538952 | tf_op jit(solution)/shard_map/ppermute | solution.py:43
  123.4 35.5 %collective-permute-start.9 = (bf16[16,208,256]{2,1,0:T(8,128)(2,1)S(1)}, bf16[16,208,256]{2,1,0:T(8,128)(2,1)}, u32[]{:S(2)}, u32[]{:S(2)}) collective-permute-start(bf16[16,208,256]{2,1,0:T(8,128)(2,1)S(1)} %constant_dynamic-update-slice_fusion.7.rest_0_), channel_id=1, source_target_pairs={{0,8},{8,0},{1,9},{9,1},{2,10},{10,2},{3,11},{11,3},{4,12},{12,4},... | collective-permute-start | bytes 5111816 | tf_op jit(solution)/shard_map/ppermute | solution.py:43
  126.5 35.1 %collective-permute-start.10 = (bf16[16,208,256]{2,1,0:T(8,128)(2,1)S(1)}, bf16[16,208,256]{2,1,0:T(8,128)(2,1)}, u32[]{:S(2)}, u32[]{:S(2)}) collective-permute-start(bf16[16,208,256]{2,1,0:T(8,128)(2,1)S(1)} %constant_dynamic-update-slice_fusion.9.rest_2_), channel_id=1, source_target_pairs={{0,4},{4,0},{1,5},{5,1},{2,6},{6,2},{3,7},{7,3},{8,12},{12,8},{9,1... | collective-permute-start | bytes 5111816 | tf_op jit(solution)/shard_map/ppermute | solution.py:43
  161.6 17.9 %all-to-all-start.1 = ((bf16[8,2,32,1024]{3,1,2,0:T(2,128)(2,1)}), bf16[8,2,32,1024]{3,1,2,0:T(2,128)(2,1)S(1)}, u32[]{:S(2)}, u32[]{:S(2)}) async-start(bf16[8,2,32,1024]{3,1,2,0:T(2,128)(2,1)} %bitcast.269), calls=%async_computation.1 | async-start | bytes 2097152 | tf_op jit(solution)/shard_map/all_to_all | solution.py:132
  184.0 3.7 collective-permute-start.16
  187.8 8.9 %collective-permute-start.18 = (bf16[272,256]{1,0:T(8,128)(2,1)S(1)}, bf16[272,256]{1,0:T(8,128)(2,1)S(1)}, u32[]{:S(2)}, u32[]{:S(2)}) collective-permute-start(bf16[272,256]{1,0:T(8,128)(2,1)S(1)} %get-tuple-element.361), channel_id=1, source_target_pairs={{4,0},{8,4},{12,8},{16,12},{20,16},{24,20},{28,24},{5,1},{9,5},{13... | collective-permute-start | bytes 417800 | tf_op jit(solution)/shard_map/ppermute | solution.py:37
  189.1 8.0 %collective-permute-start.17 = (bf16[272,256]{1,0:T(8,128)(2,1)S(1)}, bf16[272,256]{1,0:T(8,128)(2,1)}, u32[]{:S(2)}, u32[]{:S(2)}) collective-permute-start(bf16[272,256]{1,0:T(8,128)(2,1)S(1)} %get-tuple-element.360), channel_id=1, source_target_pairs={{0,4},{4,8},{8,12},{12,16},{16,20},{20,24},{24,28},{1,5},{5,9},{9,... | collective-permute-start | bytes 417800 | tf_op jit(solution)/shard_map/ppermute | solution.py:37
  198.1 2.9 collective-permute-start.19
  199.0 2.1 collective-permute-start.20
  209.5 1.5 collective-permute-start.21
  216.1 3.7 collective-permute-start.22
  219.9 7.7 %collective-permute-start.24 = (bf16[272,256]{1,0:T(8,128)(2,1)S(1)}, bf16[272,256]{1,0:T(8,128)(2,1)S(1)}, u32[]{:S(2)}, u32[]{:S(2)}) collective-permute-start(bf16[272,256]{1,0:T(8,128)(2,1)S(1)} %get-tuple-element.359), channel_id=1, source_target_pairs={{4,0},{8,4},{12,8},{16,12},{20,16},{24,20},{28,24},{5,1},{9,5},{13... | collective-permute-start | bytes 417800 | tf_op jit(solution)/shard_map/ppermute | solution.py:37
  221.2 9.5 %collective-permute-start.23 = (bf16[272,256]{1,0:T(8,128)(2,1)S(1)}, bf16[272,256]{1,0:T(8,128)(2,1)S(1)}, u32[]{:S(2)}, u32[]{:S(2)}) collective-permute-start(bf16[272,256]{1,0:T(8,128)(2,1)S(1)} %get-tuple-element.358), channel_id=1, source_target_pairs={{0,4},{4,8},{8,12},{12,16},{16,20},{20,24},{24,28},{1,5},{5,9},{9,... | collective-permute-start | bytes 417800 | tf_op jit(solution)/shard_map/ppermute | solution.py:37
  236.4 1.6 collective-permute-start.25
  239.5 1.6 collective-permute-start.26
  242.5 22.6 %all-to-all-start.2 = ((bf16[8,2,1,32,1024]{4,3,2,1,0:T(8,128)(2,1)}), bf16[8,2,1,32,1024]{4,3,2,1,0:T(8,128)(2,1)S(1)}, u32[]{:S(2)}, u32[]{:S(2)}) async-start(bf16[8,2,1,32,1024]{4,3,2,1,0:T(8,128)(2,1)} %broadcast_in_dim.182), calls=%async_computation.2 | async-start | bytes 2097152 | tf_op jit(solution)/shard_map/all_to_all | solution.py:124
  267.8 21.4 %collective-permute-start.27 = (f32[2,1,64,128]{3,2,1,0:T(8,128)S(1)}, f32[2,1,64,128]{3,2,1,0:T(8,128)S(1)}, u32[]{:S(2)}, u32[]{:S(2)}) collective-permute-start(f32[2,1,64,128]{3,2,1,0:T(8,128)S(1)} %slice_select_fusion.1), channel_id=1, source_target_pairs={{0,16},{16,0},{1,17},{17,1},{2,18},{18,2},{3,19},{19,3},{4,20},{20... | collective-permute-start | bytes 196616 | tf_op jit(solution)/shard_map/ppermute | solution.py:43
  271.7 17.5 %collective-permute-start.28 = (f32[2,4,1,128]{3,1,0,2:T(4,128)S(1)}, f32[2,4,1,128]{3,1,0,2:T(4,128)S(1)}, u32[]{:S(2)}, u32[]{:S(2)}) collective-permute-start(f32[2,4,1,128]{3,1,0,2:T(4,128)S(1)} %slice_bitcast_fusion.7), channel_id=1, source_target_pairs={{0,2},{2,0},{1,3},{3,1},{4,6},{6,4},{5,7},{7,5},{8,10},{10,8},{9,1... | collective-permute-start | bytes 12296 | tf_op jit(solution)/shard_map/ppermute | solution.py:43
  273.4 15.7 %collective-permute-start.29 = (f32[2,1,1,128]{3,0,2,1:T(2,128)S(1)}, f32[2,1,1,128]{3,0,2,1:T(2,128)S(1)}, u32[]{:S(2)}, u32[]{:S(2)}) collective-permute-start(f32[2,1,1,128]{3,0,2,1:T(2,128)S(1)} %bitcast.297), channel_id=1, source_target_pairs={{0,18},{2,16},{16,2},{18,0},{1,19},{3,17},{17,3},{19,1},{4,22},{6,... | collective-permute-start | bytes 3080 | tf_op jit(solution)/shard_map/ppermute | solution.py:843
  289.2 38.6 %collective-permute-start.33 = (bf16[16,208,256]{2,1,0:T(8,128)(2,1)}, bf16[16,208,256]{2,1,0:T(8,128)(2,1)}, u32[]{:S(2)}, u32[]{:S(2)}) collective-permute-start(bf16[16,208,256]{2,1,0:T(8,128)(2,1)} %get-tuple-element.168), channel_id=1, source_target_pairs={{0,4},{4,0},{1,5},{5,1},{2,6},{6,2},{3,7},{7,3},{8,12},{12,8},{9,1... | collective-permute-start | bytes 5111816 | tf_op jit(solution)/shard_map/ppermute | solution.py:43
  290.3 39.9 %collective-permute-start.30 = (bf16[16,208,256]{2,1,0:T(8,128)(2,1)}, bf16[16,208,256]{2,1,0:T(8,128)(2,1)}, u32[]{:S(2)}, u32[]{:S(2)}) collective-permute-start(bf16[16,208,256]{2,1,0:T(8,128)(2,1)} %get-tuple-element.160), channel_id=1, source_target_pairs={{0,8},{8,0},{1,9},{9,1},{2,10},{10,2},{3,11},{11,3},{4,12},{12,4},... | collective-permute-start | bytes 5111816 | tf_op jit(solution)/shard_map/ppermute | solution.py:43
  301.0 32.0 %collective-permute-start.31 = (bf16[16,288,128]{2,1,0:T(8,128)(2,1)}, bf16[16,288,128]{2,1,0:T(8,128)(2,1)}, u32[]{:S(2)}, u32[]{:S(2)}) collective-permute-start(bf16[16,288,128]{2,1,0:T(8,128)(2,1)} %get-tuple-element.163), channel_id=1, source_target_pairs={{0,2},{2,0},{1,3},{3,1},{4,6},{6,4},{5,7},{7,5},{8,10},{10,8},{9,1... | collective-permute-start | bytes 3538952 | tf_op jit(solution)/shard_map/ppermute | solution.py:43
  311.6 28.7 %collective-permute-start.32 = (bf16[16,144,128]{2,1,0:T(8,128)(2,1)S(1)}, bf16[16,144,128]{2,1,0:T(8,128)(2,1)S(1)}, u32[]{:S(2)}, u32[]{:S(2)}) collective-permute-start(bf16[16,144,128]{2,1,0:T(8,128)(2,1)S(1)} %get-tuple-element.166), channel_id=1, source_target_pairs={{0,2},{2,0},{1,3},{3,1},{4,6},{6,4},{5,7},{7,5},{8,10},{10,8},{9,1... | collective-permute-start | bytes 1769480 | tf_op jit(solution)/shard_map/ppermute | solution.py:43
  329.6 31.7 %collective-permute-start.35 = (bf16[8,208,256]{2,1,0:T(8,128)(2,1)S(1)}, bf16[8,208,256]{2,1,0:T(8,128)(2,1)S(1)}, u32[]{:S(2)}, u32[]{:S(2)}) collective-permute-start(bf16[8,208,256]{2,1,0:T(8,128)(2,1)S(1)} %get-tuple-element.294), channel_id=1, source_target_pairs={{0,8},{8,0},{1,9},{9,1},{2,10},{10,2},{3,11},{11,3},{4,12},{12,4},... | collective-permute-start | bytes 2555912 | tf_op jit(solution)/shard_map/ppermute | solution.py:43
  332.0 29.5 %collective-permute-start.34 = (bf16[8,208,256]{2,1,0:T(8,128)(2,1)S(1)}, bf16[8,208,256]{2,1,0:T(8,128)(2,1)S(1)}, u32[]{:S(2)}, u32[]{:S(2)}) collective-permute-start(bf16[8,208,256]{2,1,0:T(8,128)(2,1)S(1)} %get-tuple-element.291), channel_id=1, source_target_pairs={{0,4},{4,0},{1,5},{5,1},{2,6},{6,2},{3,7},{7,3},{8,12},{12,8},{9,1... | collective-permute-start | bytes 2555912 | tf_op jit(solution)/shard_map/ppermute | solution.py:43
  334.8 28.9 %collective-permute-start.36 = (bf16[8,288,128]{2,1,0:T(8,128)(2,1)S(1)}, bf16[8,288,128]{2,1,0:T(8,128)(2,1)S(1)}, u32[]{:S(2)}, u32[]{:S(2)}) collective-permute-start(bf16[8,288,128]{2,1,0:T(8,128)(2,1)S(1)} %fusion.17), channel_id=1, source_target_pairs={{0,16},{16,0},{1,17},{17,1},{2,18},{18,2},{3,19},{19,3},{4,20},{20... | collective-permute-start | bytes 1769480 | tf_op jit(solution)/shard_map/ppermute | solution.py:43
  361.8 18.2 %collective-permute-start.37 = (bf16[4,416,256]{2,1,0:T(8,128)(2,1)S(1)}, bf16[4,416,256]{2,1,0:T(8,128)(2,1)S(1)}, u32[]{:S(2)}, u32[]{:S(2)}) collective-permute-start(bf16[4,416,256]{2,1,0:T(8,128)(2,1)S(1)} %pad_maximum_fusion.10), channel_id=1, source_target_pairs={{0,2},{2,0},{1,3},{3,1},{4,6},{6,4},{5,7},{7,5},{8,10},{10,8},{9,1... | collective-permute-start | bytes 2555912 | tf_op jit(solution)/shard_map/ppermute | solution.py:43
  363.4 17.5 %collective-permute-start.38 = (bf16[8,144,128]{2,1,0:T(8,128)(2,1)S(1)}, bf16[8,144,128]{2,1,0:T(8,128)(2,1)S(1)}, u32[]{:S(2)}, u32[]{:S(2)}) collective-permute-start(bf16[8,144,128]{2,1,0:T(8,128)(2,1)S(1)} %fusion.30), channel_id=1, source_target_pairs={{0,16},{16,0},{1,17},{17,1},{2,18},{18,2},{3,19},{19,3},{4,20},{20... | collective-permute-start | bytes 884744 | tf_op jit(solution)/shard_map/ppermute | solution.py:43
  380.9 17.5 %collective-permute-start.39 = (bf16[2,416,256]{2,1,0:T(8,128)(2,1)}, bf16[2,416,256]{2,1,0:T(8,128)(2,1)}, u32[]{:S(2)}, u32[]{:S(2)}) collective-permute-start(bf16[2,416,256]{2,1,0:T(8,128)(2,1)} %slice.574), channel_id=1, source_target_pairs={{0,16},{16,0},{1,17},{17,1},{2,18},{18,2},{3,19},{19,3},{4,20},{20... | collective-permute-start | bytes 1277960 | tf_op jit(solution)/shard_map/ppermute | solution.py:43
  382.7 27.2 %all-to-all-start.3 = ((bf16[8,432,128]{2,1,0:T(8,128)(2,1)}), bf16[8,432,128]{2,1,0:T(8,128)(2,1)S(1)}, u32[]{:S(2)}, u32[]{:S(2)}) async-start(bf16[8,432,128]{2,1,0:T(8,128)(2,1)} %pad_maximum_fusion.8), calls=%async_computation.3 | async-start | bytes 1769472 | tf_op jit(solution)/shard_map/all_to_all | solution.py:922
  402.3 3.8 collective-permute-start.41
  406.1 3.8 collective-permute-start.42
  407.8 7.3 %collective-permute-start.45 = (bf16[416,256]{1,0:T(8,128)(2,1)}, bf16[416,256]{1,0:T(8,128)(2,1)}, u32[]{:S(2)}, u32[]{:S(2)}) collective-permute-start(bf16[416,256]{1,0:T(8,128)(2,1)} %slice_bitcast_fusion.2), channel_id=1, source_target_pairs={{0,1},{1,0},{2,3},{3,2},{4,5},{5,4},{6,7},{7,6},{8,9},{9,8},{10,11... | collective-permute-start | bytes 638984 | tf_op jit(solution)/shard_map/ppermute | solution.py:43
  411.2 3.8 collective-permute-start.43
  415.1 4.7 %collective-permute-start.44 = (f32[4100]{0:T(1024)S(1)}, f32[4100]{0:T(1024)S(1)}, u32[]{:S(2)}, u32[]{:S(2)}) collective-permute-start(f32[4100]{0:T(1024)S(1)} %add.406), channel_id=1, source_target_pairs={{0,16},{16,0},{1,17},{17,1},{2,18},{18,2},{3,19},{19,3},{4,20},{20... | collective-permute-start | bytes 49208 | tf_op jit(solution)/shard_map/ppermute | solution.py:43
  (74 other events, 336.8 us)

commit v5 on v4

--- a/solution.py
+++ b/solution.py
@@ -245,18 +245,20 @@
     )
 
 
-def on_chip(body, ins, outs, scratch, spaces, flops):
+def on_chip(body, ins, outs, scratch, spaces, flops, aliases=()):
     kinds = {"v": pltpu.VMEM, "s": pltpu.SMEM, "a": pl.ANY}
     held = [v for v, k in zip(list(ins) + list(outs), spaces[0] + spaces[1]) if k == "v"]
     held += [v for v in scratch if len(v.shape) > 1]
     room = sum(math.prod(v.shape) * jnp.dtype(v.dtype).itemsize for v in held)
+    limit = 58 * 1024 * 1024 if "a" in spaces[1] else int(1.25 * room) + 6 * 1024 * 1024
     return pl.pallas_call(
         body,
         out_shape=outs,
         in_specs=[pl.BlockSpec(memory_space=kinds[k]) for k in spaces[0]],
         out_specs=[pl.BlockSpec(memory_space=kinds[k]) for k in spaces[1]],
         scratch_shapes=scratch,
-        compiler_params=pltpu.CompilerParams(vmem_limit_bytes=int(1.25 * room) + 6 * 1024 * 1024),
+        input_output_aliases=dict(aliases),
+        compiler_params=pltpu.CompilerParams(vmem_limit_bytes=limit),
         cost_estimate=pl.CostEstimate(flops=0, bytes_accessed=0, transcendentals=0),
     )(*ins)
 
@@ -382,24 +384,38 @@
     )
 
 
-def chip_grads(me, planes, grad, act, ups_grad, r3, ru):
-    high, low = r3 // 2, ru // 2
+def chunk_writes(me_ref, pieces, whole, targets, sems):
+    waits = []
+    for i, (pair, spot, start, rows, to) in enumerate(pieces):
+        here = whole.at[pl.ds(start, rows), :]
+        at = place(spot[0], me_ref, spot[1])
+        for side in range(2):
+            inside = at - 16 * side
+
+            @pl.when((inside >= 0) & (inside < 16))
+            def _(here=here, target=targets[pair + side], inside=inside, rows=rows, to=to, i=i):
+                there = target.at[inside, pl.ds(to, rows), :]
+                pltpu.make_async_copy(here, there, sems.at[i]).start()
+
+        there = targets[pair].at[0, pl.ds(to, rows), :]
+        waits.append(pltpu.make_async_copy(here, there, sems.at[i]))
+    for copy in waits:
+        copy.wait()
+
+
+def halves(rows, to):
     pieces = []
     for chunk in range(32):
-        pieces.append((0, 0, (chunk, "y"), r3 * chunk, high, 0))
-        pieces.append((0, 2, (chunk, "zl"), r3 * chunk + high, high, 0))
-        pieces.append((1, 0, (chunk, "y"), ru * chunk, low, high))
-        pieces.append((1, 2, (chunk, "zl"), ru * chunk + low, low, high))
-
-    def body(me_ref, planes_ref, grad_ref, act_ref, ups_grad_ref, *rest):
-        targets, wholes, sems = rest[:4], rest[4:6], rest[6]
-        values = act_ref[...].reshape(128, C1)
-        for tap in range(4):
-            cells = ups_grad_ref[:, tap // 2, tap % 2].reshape(128, HALF)
-            total = lax.dot_general(
-                values, cells, (((0,), (0,)), ((), ())), preferred_element_type=f32
-            )
-            wholes[1][tap * C1 : (tap + 1) * C1, :] = total.astype(bf16)
+        pieces.append((0, (chunk, "y"), rows * chunk, rows // 2, to))
+        pieces.append((2, (chunk, "zl"), rows * chunk + rows // 2, rows // 2, to))
+    return pieces
+
+
+def merge_grads(me, planes, grad, r3, ru):
+    pieces = halves(r3, 0)
+
+    def body(me_ref, planes_ref, grad_ref, *rest):
+        targets, whole, sems = rest[:4], rest[4], rest[5]
         for tap in range(9):
             total = jnp.zeros((2 * C0, HALF), f32)
             for image in range(2):
@@ -409,35 +425,41 @@
                     (((0,), (0,)), ((), ())),
                     preferred_element_type=f32,
                 )
-            wholes[0][tap * 2 * C0 : (tap + 1) * 2 * C0, :] = total.astype(bf16)
-        waits = []
-        for i, (whole, pair, spot, start, rows, to) in enumerate(pieces):
-            here = wholes[whole].at[pl.ds(start, rows), :]
-            at = place(spot[0], me_ref, spot[1])
-            for side in range(2):
-                inside = at - 16 * side
-
-                @pl.when((inside >= 0) & (inside < 16))
-                def _(here=here, target=targets[pair + side], inside=inside, rows=rows, to=to, i=i):
-                    there = target.at[inside, pl.ds(to, rows), :]
-                    pltpu.make_async_copy(here, there, sems.at[i]).start()
-
-            there = targets[pair].at[0, pl.ds(to, rows), :]
-            waits.append(pltpu.make_async_copy(here, there, sems.at[i]))
-        for copy in waits:
-            copy.wait()
+            whole[tap * 2 * C0 : (tap + 1) * 2 * C0, :] = total.astype(bf16)
+        chunk_writes(me_ref, pieces, whole, targets, sems)
 
     return on_chip(
         body,
-        (me, planes, grad, act, ups_grad),
-        (jax.ShapeDtypeStruct((16, high + low, HALF), bf16),) * 4,
-        [
-            pltpu.VMEM((18 * C0, HALF), bf16),
-            pltpu.VMEM((4 * C1, HALF), bf16),
-            pltpu.SemaphoreType.DMA((len(pieces),)),
-        ],
-        ("svvvv", "aaaa"),
+        (me, planes, grad),
+        (jax.ShapeDtypeStruct((16, (r3 + ru) // 2, HALF), bf16),) * 4,
+        [pltpu.VMEM((18 * C0, HALF), bf16), pltpu.SemaphoreType.DMA((len(pieces),))],
+        ("svv", "aaaa"),
         0,
+    )
+
+
+def up_grads(me, act, ups_grad, parts, r3, ru):
+    pieces = halves(ru, r3 // 2)
+
+    def body(me_ref, act_ref, ups_grad_ref, *rest):
+        targets, whole, sems = rest[4:8], rest[8], rest[9]
+        values = act_ref[...].reshape(128, C1)
+        for tap in range(4):
+            cells = ups_grad_ref[:, tap // 2, tap % 2].reshape(128, HALF)
+            total = lax.dot_general(
+                values, cells, (((0,), (0,)), ((), ())), preferred_element_type=f32
+            )
+            whole[tap * C1 : (tap + 1) * C1, :] = total.astype(bf16)
+        chunk_writes(me_ref, pieces, whole, targets, sems)
+
+    return on_chip(
+        body,
+        (me, act, ups_grad, *parts),
+        (jax.ShapeDtypeStruct((16, (r3 + ru) // 2, HALF), bf16),) * 4,
+        [pltpu.VMEM((4 * C1, HALF), bf16), pltpu.SemaphoreType.DMA((len(pieces),))],
+        ("svvaaaa", "aaaa"),
+        0,
+        {3 + i: i for i in range(4)},
     )
 
 
@@ -829,11 +851,14 @@
 
     grad_two = group_gather(grad_pre_two)
     if zhs == 2:
+        planes = lax.optimization_barrier((planes, grad_pre_two))[0]
+        chip_parts = merge_grads(me, planes, grad_pre_three.reshape(512, HALF), r3, ru)
+        grad_two, chip_parts = lax.optimization_barrier((grad_two, chip_parts))
         grad_two, inner, sides = second_back_on_chip(grad_two, kernel_two.reshape(-1, C1))
-        grad_two, inner, sides, planes = lax.optimization_barrier((grad_two, inner, sides, planes))
-        chip_parts = chip_grads(
-            me, planes, grad_pre_three.reshape(512, HALF), act_chip, grad_upper, r3, ru
+        grad_two, inner, sides, act_chip = lax.optimization_barrier(
+            (grad_two, inner, sides, act_chip)
         )
+        chip_parts = up_grads(me, act_chip, grad_upper, chip_parts, r3, ru)
         chip_parts, act_shifts = lax.optimization_barrier((chip_parts, act_shifts))
         second_grad = second_grad_on_chip(me, act_shifts, grad_two, r2, 16 * zhs)
         row = jnp.where(zh == 0, inner[:, 5:], inner[:, :1])

time: 443 us -> 435 us (0.982)
  waiting for transfers between devices: 168 us -> 157 us
  starting transfers between devices: 77.3 us -> 84.6 us
    all_to_all x1, waiting for transfers between devices: 9.36 us -> 0.01 us  [group_gather(): lax.all_to_all(jnp.broadcast_to(block[None], (8,) + block.shape), MEMBERS...]
    ppermute x39, starting transfers between devices: 36.7 us -> 43.2 us  [swapped(): return lax.ppermute(values, axis, [(0, 1), (1, 0)])]
    unnamed x157 -> x151, local copies, waits for them, and re-layouts: 23.7 us -> 23.5 us
    pallas_call x8 -> x9, Pallas kernels: 40.5 us -> 40.3 us  [on_chip(): pl.pallas_call(body, out_shape=outs, in_specs=[pl.BlockSpec(memory_space=...]
  transfers between devices with their start and end apart: 50 -> 50, of which waited for: 28 -> 28; matrix products, arithmetic and copies ran while one was open for 21% -> 20% of each run, Pallas kernels for 7% -> 7%
where the time goes in v5:
time: 435 us; the launch traced here: 426 us
  waiting for transfers between devices  157 us (36%)
  starting transfers between devices  84.6 us (19%)
  local copies, waits for them, and re-layouts  65.4 us (15%)
  other arithmetic  53.8 us (12%)
  Pallas kernels  40.3 us (9%)
  matrix products  16.1 us (4%)
  between operations  8.78 us (2%)
    ppermute x39, waiting for transfers between devices, swapped(): return lax.ppermute(values, axis, [(0, 1), (1, 0)])  148 us
    ppermute x39, starting transfers between devices, swapped(): return lax.ppermute(values, axis, [(0, 1), (1, 0)])  43.2 us
    pallas_call x9, Pallas kernels, on_chip(): pl.pallas_call(body, out_shape=outs, in_specs=[pl.BlockSpec(memory_space=...  40.3 us
    unnamed x151, local copies, waits for them, and re-layouts  23.5 us
    ppermute x6, starting transfers between devices, shifted(): lax.ppermute(values, axis, [(i, i + step) for i in range(count) if 0 <= i...  19.7 us
    conv_general_dilated x2, matrix products, convolve(): lax.conv_general_dilated(values, kernel, (1, 1), ((pad, pad), (pad, pad))...  11.2 us
    sub x6, other arithmetic, adamw(): weight - learn_rate * (corrected / (spread + epsilon) + decay * weight)  8.98 us
  transfers between devices with their start and end apart: 50, of which 28 were waited for; matrix products, arithmetic and copies ran while one was open for 20% of the time, Pallas kernels for 7%

profile of v5, /device:TPU:0, one launch (start us, length us, event | category | flops | bytes accessed | tf_op | source)
XLA Modules:
  0.0 426.2 jit_solution(6174030698042735878)
XLA Ops:
  7.4 5.4 %all-to-all-start = ((bf16[8,704,128]{2,1,0:T(8,128)(2,1)}), bf16[8,704,128]{2,1,0:T(8,128)(2,1)}, u32[]{:S(2)}, u32[]{:S(2)}) async-start(bf16[8,704,128]{2,1,0:T(8,128)(2,1)} %pad_maximum_fusion.3), calls=%async_computation | async-start | bytes 2883584 | tf_op jit(solution)/shard_map/all_to_all | solution.py:694
  18.3 3.0 collective-permute-start.1
  22.9 15.6 %collective-permute-done.1 = bf16[2,416,256]{2,1,0:T(8,128)(2,1)S(1)} collective-permute-done((bf16[2,416,256]{2,1,0:T(8,128)(2,1)S(1)}, bf16[2,416,256]{2,1,0:T(8,128)(2,1)S(1)}, u32[]{:S(2)}, u32[]{:S(2)}) %collective-permute-start.1) | collective-permute-done | bytes 426016 | tf_op jit(solution)/shard_map/ppermute | solution.py:43
  48.2 17.5 %collective-permute-done.11 = bf16[2,2,512]{2,1,0:T(2,128)(2,1)S(1)} collective-permute-done((bf16[2,2,512]{2,1,0:T(2,128)(2,1)S(1)}, bf16[2,2,512]{2,1,0:T(2,128)(2,1)S(1)}, u32[]{:S(2)}, u32[]{:S(2)}) %collective-permute-start.11) | collective-permute-done | bytes 4128 | tf_op jit(solution)/shard_map/ppermute | solution.py:43
  68.0 5.4 %collective-permute-start.12 = (bf16[272,512]{1,0:T(8,128)(2,1)}, bf16[272,512]{1,0:T(8,128)(2,1)}, u32[]{:S(2)}, u32[]{:S(2)}) collective-permute-start(bf16[272,512]{1,0:T(8,128)(2,1)} %get-tuple-element.382), channel_id=1, source_target_pairs={{0,4},{4,8},{8,12},{12,16},{16,20},{20,24},{24,28},{1,5},{5,9},{9,... | collective-permute-start | bytes 835592 | tf_op jit(solution)/shard_map/ppermute | solution.py:37
  76.5 2.9 collective-permute-start.7
  79.4 19.4 %collective-permute-done.3 = bf16[4608,128]{1,0:T(8,128)(2,1)S(1)} collective-permute-done((bf16[4608,128]{1,0:T(8,128)(2,1)S(1)}, bf16[4608,128]{1,0:T(8,128)(2,1)S(1)}, u32[]{:S(2)}, u32[]{:S(2)}) %collective-permute-start.3) | collective-permute-done | bytes 1179680 | tf_op jit(solution)/shard_map/ppermute | solution.py:43
  108.5 2.8 pad_maximum_fusion.7
  112.5 5.5 %collective-permute-done.7 = bf16[8,208,256]{2,1,0:T(8,128)(2,1)} collective-permute-done((bf16[8,208,256]{2,1,0:T(8,128)(2,1)}, bf16[8,208,256]{2,1,0:T(8,128)(2,1)}, u32[]{:S(2)}, u32[]{:S(2)}) %collective-permute-start.7) | collective-permute-done | bytes 852000 | tf_op jit(solution)/shard_map/ppermute | solution.py:43
  118.0 2.7 collective-permute-done.4
  132.4 4.1 fusion.10
  137.5 5.1 %collective-permute-done.8 = bf16[4608,128]{1,0:T(8,128)(2,1)} collective-permute-done((bf16[4608,128]{1,0:T(8,128)(2,1)}, bf16[4608,128]{1,0:T(8,128)(2,1)}, u32[]{:S(2)}, u32[]{:S(2)}) %collective-permute-start.8) | collective-permute-done | bytes 1179680 | tf_op jit(solution)/shard_map/ppermute | solution.py:43
  144.4 2.1 fusion.2
  146.6 5.3 %reshape.743 = bf16[3,3,128,1024]{3,2,1,0:T(8,128)(2,1)} reshape(bf16[2,2,2,2,2,288,128]{6,5,4,3,2,1,0:T(8,128)(2,1)} %fusion.2) | data formatting | bytes 4718592 | tf_op jit(solution)/shard_map/reshape | solution.py:761
  151.9 7.1 %fusion.50 = bf16[2,4,64,1024]{3,0,2,1:T(2,128)(2,1)} fusion(bf16[3,3,128,1024]{3,2,1,0:T(8,128)(2,1)} %reshape.743, bf16[2,6,66,128]{3,2,1,0:T(8,128)(2,1)} %get-tuple-element.347), kind=kOutput, calls=%fused_computation.157 | convolution fusion | flops 1207959552 | bytes 3610624 | tf_op jit(solution)/shard_map/conv_general_dilated | solution.py:86
  159.0 2.6 collective-permute-done.10.rest_3_
  161.6 3.6 all-to-all-start.1
  168.2 8.0 %shard_map.382 = (bf16[9216,256]{1,0:T(8,128)(2,1)S(1)}, bf16[4096,256]{1,0:T(8,128)(2,1)S(1)}) custom-call(s32[5]{0:T(128)S(1)} %stack.87.me_ref, bf16[16,208,256]{2,1,0:T(8,128)(2,1)S(1)} %copy-done.5, bf16[16,208,256]{2,1,0:T(8,128)(2,1)} %collective-permute-done.9.rest_1_, bf16[16,208,256]{2,1,0:T(8,128)(2,1)S(1)} %copy-done.7, ...), custom_call_target="tpu_custom_call" | custom-call | tf_op jit(solution)/shard_map/pallas_call | solution.py:254
  176.3 2.1 copy-done
  189.1 5.2 %collective-permute-start.17 = (bf16[272,256]{1,0:T(8,128)(2,1)S(1)}, bf16[272,256]{1,0:T(8,128)(2,1)}, u32[]{:S(2)}, u32[]{:S(2)}) collective-permute-start(bf16[272,256]{1,0:T(8,128)(2,1)S(1)} %get-tuple-element.380), channel_id=1, source_target_pairs={{0,4},{4,8},{8,12},{12,16},{16,20},{20,24},{24,28},{1,5},{5,9},{9,... | collective-permute-start | bytes 417800 | tf_op jit(solution)/shard_map/ppermute | solution.py:37
  201.1 2.3 copy-done.1
  203.5 4.0 shard_map.384
  212.1 3.5 convert_reduce_fusion.1
  220.7 5.1 %collective-permute-start.23 = (bf16[272,256]{1,0:T(8,128)(2,1)S(1)}, bf16[272,256]{1,0:T(8,128)(2,1)S(1)}, u32[]{:S(2)}, u32[]{:S(2)}) collective-permute-start(bf16[272,256]{1,0:T(8,128)(2,1)S(1)} %get-tuple-element.378), channel_id=1, source_target_pairs={{0,4},{4,8},{8,12},{12,16},{16,20},{20,24},{24,28},{1,5},{5,9},{9,... | collective-permute-start | bytes 417800 | tf_op jit(solution)/shard_map/ppermute | solution.py:37
  227.3 2.9 collective-permute-done.23
  231.6 2.3 copy-done.2
  241.4 7.9 %all-to-all-start.2 = ((bf16[8,2,1,32,1024]{4,3,2,1,0:T(8,128)(2,1)}), bf16[8,2,1,32,1024]{4,3,2,1,0:T(8,128)(2,1)S(1)}, u32[]{:S(2)}, u32[]{:S(2)}) async-start(bf16[8,2,1,32,1024]{4,3,2,1,0:T(8,128)(2,1)} %broadcast_in_dim.182), calls=%async_computation.2 | async-start | bytes 2097152 | tf_op jit(solution)/shard_map/all_to_all | solution.py:124
  250.7 3.9 reshape_reshape.3.kernel_ref
  256.2 7.6 %shard_map.386 = (bf16[16,208,256]{2,1,0:T(8,128)(2,1)}, bf16[16,208,256]{2,1,0:T(8,128)(2,1)}, bf16[16,208,256]{2,1,0:T(8,128)(2,1)}, bf16[16,208,256]{2,1,0:T(8,128)(2,1)}) custom-call(s32[5]{0:T(128)} %copy-done.12, bf16[2,4,4,64,1024]{4,3,2,1,0:T(8,128)(2,1)} %copy-done.3, bf16[512,256]{1,0:T(8,128)(2,1)} %bitcast.266), custom_call_target="tpu_custom_call" | custom-call | tf_op jit(solution)/shard_map/pallas_call | solution.py:254
  263.9 2.7 shard_map.387
  268.4 3.7 collective-permute-start.27
  274.8 3.8 shard_map.388
  285.2 6.9 %shard_map.389 = (bf16[16,288,128]{2,1,0:T(8,128)(2,1)}, bf16[16,288,128]{2,1,0:T(8,128)(2,1)}) custom-call(s32[5]{0:T(128)} %copy-done.12, bf16[3,2,6,64,128]{4,3,2,1,0:T(8,128)(2,1)} %pad_maximum_fusion.16.cells_ref, bf16[2,4,64,1024]{3,2,1,0:T(8,128)(2,1)} %copy-done.8), custom_call_target="tpu_custom_call" | custom-call | tf_op jit(solution)/shard_map/pallas_call | solution.py:254
  298.0 4.4 %shard_map.390 = (bf16[16,144,128]{2,1,0:T(8,128)(2,1)}, bf16[16,144,128]{2,1,0:T(8,128)(2,1)}) custom-call(s32[5]{0:T(128)} %copy-done.12, bf16[3,2,6,64,512]{4,3,2,1,0:T(8,128)(2,1)} %pad_maximum_fusion.1.cells_ref, bf16[2,4,64,128]{3,2,1,0:T(8,128)(2,1)} %fusion.45.grad_ref), custom_call_target="tpu_custom_call" | custom-call | tf_op jit(solution)/shard_map/pallas_call | solution.py:254
  303.5 14.4 %collective-permute-done.33 = bf16[16,208,256]{2,1,0:T(8,128)(2,1)S(1)} collective-permute-done((bf16[16,208,256]{2,1,0:T(8,128)(2,1)}, bf16[16,208,256]{2,1,0:T(8,128)(2,1)S(1)}, u32[]{:S(2)}, u32[]{:S(2)}) %collective-permute-start.33) | collective-permute-done | bytes 1703968 | tf_op jit(solution)/shard_map/ppermute | solution.py:43
  325.3 2.4 collective-permute-start.36
  327.6 4.6 %collective-permute-done.32 = bf16[16,144,128]{2,1,0:T(8,128)(2,1)S(1)} collective-permute-done((bf16[16,144,128]{2,1,0:T(8,128)(2,1)}, bf16[16,144,128]{2,1,0:T(8,128)(2,1)S(1)}, u32[]{:S(2)}, u32[]{:S(2)}) %collective-permute-start.32) | collective-permute-done | bytes 589856 | tf_op jit(solution)/shard_map/ppermute | solution.py:43
  332.4 18.0 %collective-permute-done.35 = bf16[8,208,256]{2,1,0:T(8,128)(2,1)S(1)} collective-permute-done((bf16[8,208,256]{2,1,0:T(8,128)(2,1)S(1)}, bf16[8,208,256]{2,1,0:T(8,128)(2,1)S(1)}, u32[]{:S(2)}, u32[]{:S(2)}) %collective-permute-start.35) | collective-permute-done | bytes 852000 | tf_op jit(solution)/shard_map/ppermute | solution.py:43
  350.9 2.2 collective-permute-start.37
  355.4 15.0 %collective-permute-done.37 = bf16[4,416,256]{2,1,0:T(8,128)(2,1)S(1)} collective-permute-done((bf16[4,416,256]{2,1,0:T(8,128)(2,1)S(1)}, bf16[4,416,256]{2,1,0:T(8,128)(2,1)S(1)}, u32[]{:S(2)}, u32[]{:S(2)}) %collective-permute-start.37) | collective-permute-done | bytes 852000 | tf_op jit(solution)/shard_map/ppermute | solution.py:43
  373.7 4.9 %all-to-all-start.3 = ((bf16[8,432,128]{2,1,0:T(8,128)(2,1)}), bf16[8,432,128]{2,1,0:T(8,128)(2,1)S(1)}, u32[]{:S(2)}, u32[]{:S(2)}) async-start(bf16[8,432,128]{2,1,0:T(8,128)(2,1)} %pad_maximum_fusion.8), calls=%async_computation.3 | async-start | bytes 1769472 | tf_op jit(solution)/shard_map/all_to_all | solution.py:947
  383.1 7.1 %collective-permute-done.39 = bf16[2,416,256]{2,1,0:T(8,128)(2,1)S(1)} collective-permute-done((bf16[2,416,256]{2,1,0:T(8,128)(2,1)}, bf16[2,416,256]{2,1,0:T(8,128)(2,1)S(1)}, u32[]{:S(2)}, u32[]{:S(2)}) %collective-permute-start.39) | collective-permute-done | bytes 426016 | tf_op jit(solution)/shard_map/ppermute | solution.py:43
  394.6 2.3 collective-permute-done.41
  398.2 2.5 collective-permute-done.42
  402.1 3.8 collective-permute-done.43
  407.4 3.1 collective-permute-done.44
  415.4 2.9 multiply_subtract_fusion.2
  418.3 2.4 multiply_subtract_fusion
  (447 shorter events, 145.1 us)
Async XLA Ops:
  7.4 33.3 %all-to-all-start = ((bf16[8,704,128]{2,1,0:T(8,128)(2,1)}), bf16[8,704,128]{2,1,0:T(8,128)(2,1)}, u32[]{:S(2)}, u32[]{:S(2)}) async-start(bf16[8,704,128]{2,1,0:T(8,128)(2,1)} %pad_maximum_fusion.3), calls=%async_computation | async-start | bytes 2883584 | tf_op jit(solution)/shard_map/all_to_all | solution.py:694
  14.4 3.9 collective-permute-start
  15.4 6.3 %collective-permute-start.2 = (bf16[2,2,2,32,512]{4,1,0,3,2:T(2,128)(2,1)S(1)}, bf16[2,2,2,32,512]{4,1,0,3,2:T(2,128)(2,1)S(1)}, u32[]{:S(2)}, u32[]{:S(2)}) collective-permute-start(bf16[2,2,2,32,512]{4,1,0,3,2:T(2,128)(2,1)S(1)} %bitcast.279), channel_id=1, source_target_pairs={{0,1},{1,0},{2,3},{3,2},{4,5},{5,4},{6,7},{7,6},{8,9},{9,8},{10,11... | collective-permute-start | bytes 786440 | tf_op jit(solution)/shard_map/ppermute | solution.py:43
  15.6 2.7 collective-permute-start.14
  18.3 20.2 %collective-permute-start.1 = (bf16[2,416,256]{2,1,0:T(8,128)(2,1)S(1)}, bf16[2,416,256]{2,1,0:T(8,128)(2,1)S(1)}, u32[]{:S(2)}, u32[]{:S(2)}) collective-permute-start(bf16[2,416,256]{2,1,0:T(8,128)(2,1)S(1)} %pad_maximum_fusion.20), channel_id=1, source_target_pairs={{0,16},{16,0},{1,17},{17,1},{2,18},{18,2},{3,19},{19,3},{4,20},{20... | collective-permute-start | bytes 1277960 | tf_op jit(solution)/shard_map/ppermute | solution.py:43
  43.7 55.2 %collective-permute-start.3 = (bf16[4608,128]{1,0:T(8,128)(2,1)S(1)}, bf16[4608,128]{1,0:T(8,128)(2,1)S(1)}, u32[]{:S(2)}, u32[]{:S(2)}) collective-permute-start(bf16[4608,128]{1,0:T(8,128)(2,1)S(1)} %pad_maximum_fusion.5), channel_id=1, source_target_pairs={{0,16},{16,0},{1,17},{17,1},{2,18},{18,2},{3,19},{19,3},{4,20},{20... | collective-permute-start | bytes 3538952 | tf_op jit(solution)/shard_map/ppermute | solution.py:43
  45.1 28.3 %collective-permute-start.5 = (bf16[4,416,256]{2,1,0:T(8,128)(2,1)S(1)}, bf16[4,416,256]{2,1,0:T(8,128)(2,1)S(1)}, u32[]{:S(2)}, u32[]{:S(2)}) collective-permute-start(bf16[4,416,256]{2,1,0:T(8,128)(2,1)S(1)} %pad_maximum_fusion.9), channel_id=1, source_target_pairs={{0,2},{2,0},{1,3},{3,1},{4,6},{6,4},{5,7},{7,5},{8,10},{10,8},{9,1... | collective-permute-start | bytes 2555912 | tf_op jit(solution)/shard_map/ppermute | solution.py:43
  47.8 18.0 %collective-permute-start.11 = (bf16[2,2,512]{2,1,0:T(2,128)(2,1)S(1)}, bf16[2,2,512]{2,1,0:T(2,128)(2,1)S(1)}, u32[]{:S(2)}, u32[]{:S(2)}) collective-permute-start(bf16[2,2,512]{2,1,0:T(2,128)(2,1)S(1)} %fusion.59), channel_id=1, source_target_pairs={{0,2},{2,0},{1,3},{3,1},{4,6},{6,4},{5,7},{7,5},{8,10},{10,8},{9,1... | collective-permute-start | bytes 12296 | tf_op jit(solution)/shard_map/ppermute | solution.py:43
  66.7 37.5 %collective-permute-start.13 = (bf16[272,512]{1,0:T(8,128)(2,1)}, bf16[272,512]{1,0:T(8,128)(2,1)}, u32[]{:S(2)}, u32[]{:S(2)}) collective-permute-start(bf16[272,512]{1,0:T(8,128)(2,1)} %get-tuple-element.383), channel_id=1, source_target_pairs={{4,0},{8,4},{12,8},{16,12},{20,16},{24,20},{28,24},{5,1},{9,5},{13... | collective-permute-start | bytes 835592 | tf_op jit(solution)/shard_map/ppermute | solution.py:37
  68.0 38.3 %collective-permute-start.12 = (bf16[272,512]{1,0:T(8,128)(2,1)}, bf16[272,512]{1,0:T(8,128)(2,1)}, u32[]{:S(2)}, u32[]{:S(2)}) collective-permute-start(bf16[272,512]{1,0:T(8,128)(2,1)} %get-tuple-element.382), channel_id=1, source_target_pairs={{0,4},{4,8},{8,12},{12,16},{16,20},{20,24},{24,28},{1,5},{5,9},{9,... | collective-permute-start | bytes 835592 | tf_op jit(solution)/shard_map/ppermute | solution.py:37
  74.9 37.6 %collective-permute-start.6 = (bf16[8,208,256]{2,1,0:T(8,128)(2,1)}, bf16[8,208,256]{2,1,0:T(8,128)(2,1)}, u32[]{:S(2)}, u32[]{:S(2)}) collective-permute-start(bf16[8,208,256]{2,1,0:T(8,128)(2,1)} %get-tuple-element.120), channel_id=1, source_target_pairs={{0,4},{4,0},{1,5},{5,1},{2,6},{6,2},{3,7},{7,3},{8,12},{12,8},{9,1... | collective-permute-start | bytes 2555912 | tf_op jit(solution)/shard_map/ppermute | solution.py:43
  76.5 41.5 %collective-permute-start.7 = (bf16[8,208,256]{2,1,0:T(8,128)(2,1)}, bf16[8,208,256]{2,1,0:T(8,128)(2,1)}, u32[]{:S(2)}, u32[]{:S(2)}) collective-permute-start(bf16[8,208,256]{2,1,0:T(8,128)(2,1)} %get-tuple-element.122), channel_id=1, source_target_pairs={{0,8},{8,0},{1,9},{9,1},{2,10},{10,2},{3,11},{11,3},{4,12},{12,4},... | collective-permute-start | bytes 2555912 | tf_op jit(solution)/shard_map/ppermute | solution.py:43
  102.3 18.4 %collective-permute-start.4 = (bf16[2688,128]{1,0:T(8,128)(2,1)S(1)}, bf16[2688,128]{1,0:T(8,128)(2,1)S(1)}, u32[]{:S(2)}, u32[]{:S(2)}) collective-permute-start(bf16[2688,128]{1,0:T(8,128)(2,1)S(1)} %pad_maximum_fusion.15), channel_id=1, source_target_pairs={{0,2},{2,0},{1,3},{3,1},{4,6},{6,4},{5,7},{7,5},{8,10},{10,8},{9,1... | collective-permute-start | bytes 2064392 | tf_op jit(solution)/shard_map/ppermute | solution.py:43
  112.3 30.2 %collective-permute-start.8 = (bf16[4608,128]{1,0:T(8,128)(2,1)}, bf16[4608,128]{1,0:T(8,128)(2,1)}, u32[]{:S(2)}, u32[]{:S(2)}) collective-permute-start(bf16[4608,128]{1,0:T(8,128)(2,1)} %bitcast.22), channel_id=1, source_target_pairs={{0,2},{2,0},{1,3},{3,1},{4,6},{6,4},{5,7},{7,5},{8,10},{10,8},{9,1... | collective-permute-start | bytes 3538952 | tf_op jit(solution)/shard_map/ppermute | solution.py:43
  123.4 35.6 %collective-permute-start.9 = (bf16[16,208,256]{2,1,0:T(8,128)(2,1)S(1)}, bf16[16,208,256]{2,1,0:T(8,128)(2,1)}, u32[]{:S(2)}, u32[]{:S(2)}) collective-permute-start(bf16[16,208,256]{2,1,0:T(8,128)(2,1)S(1)} %constant_dynamic-update-slice_fusion.7.rest_0_), channel_id=1, source_target_pairs={{0,8},{8,0},{1,9},{9,1},{2,10},{10,2},{3,11},{11,3},{4,12},{12,4},... | collective-permute-start | bytes 5111816 | tf_op jit(solution)/shard_map/ppermute | solution.py:43
  126.5 35.1 %collective-permute-start.10 = (bf16[16,208,256]{2,1,0:T(8,128)(2,1)S(1)}, bf16[16,208,256]{2,1,0:T(8,128)(2,1)}, u32[]{:S(2)}, u32[]{:S(2)}) collective-permute-start(bf16[16,208,256]{2,1,0:T(8,128)(2,1)S(1)} %constant_dynamic-update-slice_fusion.9.rest_2_), channel_id=1, source_target_pairs={{0,4},{4,0},{1,5},{5,1},{2,6},{6,2},{3,7},{7,3},{8,12},{12,8},{9,1... | collective-permute-start | bytes 5111816 | tf_op jit(solution)/shard_map/ppermute | solution.py:43
  161.6 17.9 %all-to-all-start.1 = ((bf16[8,2,32,1024]{3,1,2,0:T(2,128)(2,1)}), bf16[8,2,32,1024]{3,1,2,0:T(2,128)(2,1)S(1)}, u32[]{:S(2)}, u32[]{:S(2)}) async-start(bf16[8,2,32,1024]{3,1,2,0:T(2,128)(2,1)} %bitcast.269), calls=%async_computation.1 | async-start | bytes 2097152 | tf_op jit(solution)/shard_map/all_to_all | solution.py:132
  184.0 3.7 collective-permute-start.16
  187.8 8.3 %collective-permute-start.18 = (bf16[272,256]{1,0:T(8,128)(2,1)S(1)}, bf16[272,256]{1,0:T(8,128)(2,1)S(1)}, u32[]{:S(2)}, u32[]{:S(2)}) collective-permute-start(bf16[272,256]{1,0:T(8,128)(2,1)S(1)} %get-tuple-element.381), channel_id=1, source_target_pairs={{4,0},{8,4},{12,8},{16,12},{20,16},{24,20},{28,24},{5,1},{9,5},{13... | collective-permute-start | bytes 417800 | tf_op jit(solution)/shard_map/ppermute | solution.py:37
  189.1 8.0 %collective-permute-start.17 = (bf16[272,256]{1,0:T(8,128)(2,1)S(1)}, bf16[272,256]{1,0:T(8,128)(2,1)}, u32[]{:S(2)}, u32[]{:S(2)}) collective-permute-start(bf16[272,256]{1,0:T(8,128)(2,1)S(1)} %get-tuple-element.380), channel_id=1, source_target_pairs={{0,4},{4,8},{8,12},{12,16},{16,20},{20,24},{24,28},{1,5},{5,9},{9,... | collective-permute-start | bytes 417800 | tf_op jit(solution)/shard_map/ppermute | solution.py:37
  198.2 2.9 collective-permute-start.19
  199.0 2.1 collective-permute-start.20
  209.5 1.6 collective-permute-start.21
  215.6 3.7 collective-permute-start.22
  219.4 7.7 %collective-permute-start.24 = (bf16[272,256]{1,0:T(8,128)(2,1)S(1)}, bf16[272,256]{1,0:T(8,128)(2,1)S(1)}, u32[]{:S(2)}, u32[]{:S(2)}) collective-permute-start(bf16[272,256]{1,0:T(8,128)(2,1)S(1)} %get-tuple-element.379), channel_id=1, source_target_pairs={{4,0},{8,4},{12,8},{16,12},{20,16},{24,20},{28,24},{5,1},{9,5},{13... | collective-permute-start | bytes 417800 | tf_op jit(solution)/shard_map/ppermute | solution.py:37
  220.7 9.5 %collective-permute-start.23 = (bf16[272,256]{1,0:T(8,128)(2,1)S(1)}, bf16[272,256]{1,0:T(8,128)(2,1)S(1)}, u32[]{:S(2)}, u32[]{:S(2)}) collective-permute-start(bf16[272,256]{1,0:T(8,128)(2,1)S(1)} %get-tuple-element.378), channel_id=1, source_target_pairs={{0,4},{4,8},{8,12},{12,16},{16,20},{20,24},{24,28},{1,5},{5,9},{9,... | collective-permute-start | bytes 417800 | tf_op jit(solution)/shard_map/ppermute | solution.py:37
  235.9 1.6 collective-permute-start.25
  238.4 1.6 collective-permute-start.26
  241.4 22.5 %all-to-all-start.2 = ((bf16[8,2,1,32,1024]{4,3,2,1,0:T(8,128)(2,1)}), bf16[8,2,1,32,1024]{4,3,2,1,0:T(8,128)(2,1)S(1)}, u32[]{:S(2)}, u32[]{:S(2)}) async-start(bf16[8,2,1,32,1024]{4,3,2,1,0:T(8,128)(2,1)} %broadcast_in_dim.182), calls=%async_computation.2 | async-start | bytes 2097152 | tf_op jit(solution)/shard_map/all_to_all | solution.py:124
  268.4 10.8 %collective-permute-start.27 = (f32[2,1,64,128]{3,2,1,0:T(8,128)S(1)}, f32[2,1,64,128]{3,2,1,0:T(8,128)S(1)}, u32[]{:S(2)}, u32[]{:S(2)}) collective-permute-start(f32[2,1,64,128]{3,2,1,0:T(8,128)S(1)} %slice_select_fusion.1), channel_id=1, source_target_pairs={{0,16},{16,0},{1,17},{17,1},{2,18},{18,2},{3,19},{19,3},{4,20},{20... | collective-permute-start | bytes 196616 | tf_op jit(solution)/shard_map/ppermute | solution.py:43
  272.1 7.1 %collective-permute-start.28 = (f32[2,4,1,128]{3,1,0,2:T(4,128)S(1)}, f32[2,4,1,128]{3,1,0,2:T(4,128)S(1)}, u32[]{:S(2)}, u32[]{:S(2)}) collective-permute-start(f32[2,4,1,128]{3,1,0,2:T(4,128)S(1)} %slice_bitcast_fusion.7), channel_id=1, source_target_pairs={{0,2},{2,0},{1,3},{3,1},{4,6},{6,4},{5,7},{7,5},{8,10},{10,8},{9,1... | collective-permute-start | bytes 12296 | tf_op jit(solution)/shard_map/ppermute | solution.py:43
  273.9 5.4 %collective-permute-start.29 = (f32[2,1,1,128]{3,0,2,1:T(2,128)S(1)}, f32[2,1,1,128]{3,0,2,1:T(2,128)S(1)}, u32[]{:S(2)}, u32[]{:S(2)}) collective-permute-start(f32[2,1,1,128]{3,0,2,1:T(2,128)S(1)} %bitcast.297), channel_id=1, source_target_pairs={{0,18},{2,16},{16,2},{18,0},{1,19},{3,17},{17,3},{19,1},{4,22},{6,... | collective-permute-start | bytes 3080 | tf_op jit(solution)/shard_map/ppermute | solution.py:868
  279.2 38.7 %collective-permute-start.33 = (bf16[16,208,256]{2,1,0:T(8,128)(2,1)}, bf16[16,208,256]{2,1,0:T(8,128)(2,1)S(1)}, u32[]{:S(2)}, u32[]{:S(2)}) collective-permute-start(bf16[16,208,256]{2,1,0:T(8,128)(2,1)} %get-tuple-element.188), channel_id=1, source_target_pairs={{0,4},{4,0},{1,5},{5,1},{2,6},{6,2},{3,7},{7,3},{8,12},{12,8},{9,1... | collective-permute-start | bytes 5111816 | tf_op jit(solution)/shard_map/ppermute | solution.py:43
  281.4 38.9 %collective-permute-start.30 = (bf16[16,208,256]{2,1,0:T(8,128)(2,1)}, bf16[16,208,256]{2,1,0:T(8,128)(2,1)}, u32[]{:S(2)}, u32[]{:S(2)}) collective-permute-start(bf16[16,208,256]{2,1,0:T(8,128)(2,1)} %get-tuple-element.180), channel_id=1, source_target_pairs={{0,8},{8,0},{1,9},{9,1},{2,10},{10,2},{3,11},{11,3},{4,12},{12,4},... | collective-permute-start | bytes 5111816 | tf_op jit(solution)/shard_map/ppermute | solution.py:43
  293.1 30.5 %collective-permute-start.31 = (bf16[16,288,128]{2,1,0:T(8,128)(2,1)}, bf16[16,288,128]{2,1,0:T(8,128)(2,1)}, u32[]{:S(2)}, u32[]{:S(2)}) collective-permute-start(bf16[16,288,128]{2,1,0:T(8,128)(2,1)} %get-tuple-element.183), channel_id=1, source_target_pairs={{0,2},{2,0},{1,3},{3,1},{4,6},{6,4},{5,7},{7,5},{8,10},{10,8},{9,1... | collective-permute-start | bytes 3538952 | tf_op jit(solution)/shard_map/ppermute | solution.py:43
  302.4 29.9 %collective-permute-start.32 = (bf16[16,144,128]{2,1,0:T(8,128)(2,1)}, bf16[16,144,128]{2,1,0:T(8,128)(2,1)S(1)}, u32[]{:S(2)}, u32[]{:S(2)}) collective-permute-start(bf16[16,144,128]{2,1,0:T(8,128)(2,1)} %get-tuple-element.186), channel_id=1, source_target_pairs={{0,2},{2,0},{1,3},{3,1},{4,6},{6,4},{5,7},{7,5},{8,10},{10,8},{9,1... | collective-permute-start | bytes 1769480 | tf_op jit(solution)/shard_map/ppermute | solution.py:43
  318.4 32.1 %collective-permute-start.35 = (bf16[8,208,256]{2,1,0:T(8,128)(2,1)S(1)}, bf16[8,208,256]{2,1,0:T(8,128)(2,1)S(1)}, u32[]{:S(2)}, u32[]{:S(2)}) collective-permute-start(bf16[8,208,256]{2,1,0:T(8,128)(2,1)S(1)} %get-tuple-element.314), channel_id=1, source_target_pairs={{0,8},{8,0},{1,9},{9,1},{2,10},{10,2},{3,11},{11,3},{4,12},{12,4},... | collective-permute-start | bytes 2555912 | tf_op jit(solution)/shard_map/ppermute | solution.py:43
  322.2 28.4 %collective-permute-start.34 = (bf16[8,208,256]{2,1,0:T(8,128)(2,1)S(1)}, bf16[8,208,256]{2,1,0:T(8,128)(2,1)S(1)}, u32[]{:S(2)}, u32[]{:S(2)}) collective-permute-start(bf16[8,208,256]{2,1,0:T(8,128)(2,1)S(1)} %get-tuple-element.311), channel_id=1, source_target_pairs={{0,4},{4,0},{1,5},{5,1},{2,6},{6,2},{3,7},{7,3},{8,12},{12,8},{9,1... | collective-permute-start | bytes 2555912 | tf_op jit(solution)/shard_map/ppermute | solution.py:43
  325.3 29.3 %collective-permute-start.36 = (bf16[8,288,128]{2,1,0:T(8,128)(2,1)S(1)}, bf16[8,288,128]{2,1,0:T(8,128)(2,1)S(1)}, u32[]{:S(2)}, u32[]{:S(2)}) collective-permute-start(bf16[8,288,128]{2,1,0:T(8,128)(2,1)S(1)} %fusion.17), channel_id=1, source_target_pairs={{0,16},{16,0},{1,17},{17,1},{2,18},{18,2},{3,19},{19,3},{4,20},{20... | collective-permute-start | bytes 1769480 | tf_op jit(solution)/shard_map/ppermute | solution.py:43
  350.9 19.5 %collective-permute-start.37 = (bf16[4,416,256]{2,1,0:T(8,128)(2,1)S(1)}, bf16[4,416,256]{2,1,0:T(8,128)(2,1)S(1)}, u32[]{:S(2)}, u32[]{:S(2)}) collective-permute-start(bf16[4,416,256]{2,1,0:T(8,128)(2,1)S(1)} %pad_maximum_fusion.10), channel_id=1, source_target_pairs={{0,2},{2,0},{1,3},{3,1},{4,6},{6,4},{5,7},{7,5},{8,10},{10,8},{9,1... | collective-permute-start | bytes 2555912 | tf_op jit(solution)/shard_map/ppermute | solution.py:43
  353.1 18.8 %collective-permute-start.38 = (bf16[8,144,128]{2,1,0:T(8,128)(2,1)S(1)}, bf16[8,144,128]{2,1,0:T(8,128)(2,1)S(1)}, u32[]{:S(2)}, u32[]{:S(2)}) collective-permute-start(bf16[8,144,128]{2,1,0:T(8,128)(2,1)S(1)} %fusion.30), channel_id=1, source_target_pairs={{0,16},{16,0},{1,17},{17,1},{2,18},{18,2},{3,19},{19,3},{4,20},{20... | collective-permute-start | bytes 884744 | tf_op jit(solution)/shard_map/ppermute | solution.py:43
  371.4 18.8 %collective-permute-start.39 = (bf16[2,416,256]{2,1,0:T(8,128)(2,1)}, bf16[2,416,256]{2,1,0:T(8,128)(2,1)S(1)}, u32[]{:S(2)}, u32[]{:S(2)}) collective-permute-start(bf16[2,416,256]{2,1,0:T(8,128)(2,1)} %slice.574), channel_id=1, source_target_pairs={{0,16},{16,0},{1,17},{17,1},{2,18},{18,2},{3,19},{19,3},{4,20},{20... | collective-permute-start | bytes 1277960 | tf_op jit(solution)/shard_map/ppermute | solution.py:43
  373.7 27.0 %all-to-all-start.3 = ((bf16[8,432,128]{2,1,0:T(8,128)(2,1)}), bf16[8,432,128]{2,1,0:T(8,128)(2,1)S(1)}, u32[]{:S(2)}, u32[]{:S(2)}) async-start(bf16[8,432,128]{2,1,0:T(8,128)(2,1)} %pad_maximum_fusion.8), calls=%async_computation.3 | async-start | bytes 1769472 | tf_op jit(solution)/shard_map/all_to_all | solution.py:947
  393.1 3.8 collective-permute-start.41
  396.9 3.8 collective-permute-start.42
  398.1 8.3 %collective-permute-start.45 = (bf16[416,256]{1,0:T(8,128)(2,1)S(1)}, bf16[416,256]{1,0:T(8,128)(2,1)}, u32[]{:S(2)}, u32[]{:S(2)}) collective-permute-start(bf16[416,256]{1,0:T(8,128)(2,1)S(1)} %slice_bitcast_fusion.2), channel_id=1, source_target_pairs={{0,1},{1,0},{2,3},{3,2},{4,5},{5,4},{6,7},{7,6},{8,9},{9,8},{10,11... | collective-permute-start | bytes 638984 | tf_op jit(solution)/shard_map/ppermute | solution.py:43
  402.0 3.8 collective-permute-start.43
  405.9 4.7 %collective-permute-start.44 = (f32[4100]{0:T(1024)S(1)}, f32[4100]{0:T(1024)S(1)}, u32[]{:S(2)}, u32[]{:S(2)}) collective-permute-start(f32[4100]{0:T(1024)S(1)} %add.406), channel_id=1, source_target_pairs={{0,16},{16,0},{1,17},{17,1},{2,18},{18,2},{3,19},{19,3},{4,20},{20... | collective-permute-start | bytes 49208 | tf_op jit(solution)/shard_map/ppermute | solution.py:43
  (71 other events, 385.4 us)

commit v6 on v5

--- a/solution.py
+++ b/solution.py
@@ -171,13 +171,16 @@
     return parts[0], swapped(parts[1], first_axis), parts[2], swapped(parts[3], second_axis)
 
 
+def halves_of(own, got):
+    half = own.shape[0] // 2
+    return tuple(
+        (v.astype(f32) + w.astype(f32)).astype(bf16)
+        for v, w in ((own[:half], got[:half]), (own[half:], got[half:]))
+    )
+
+
 def added(parts):
-    out = ()
-    for own, got in (parts[:2], parts[2:]):
-        half = own.shape[0] // 2
-        for v, w in ((own[:half], got[:half]), (own[half:], got[half:])):
-            out += ((v.astype(f32) + w.astype(f32)).astype(bf16),)
-    return out
+    return halves_of(*parts[:2]) + halves_of(*parts[2:])
 
 
 def after(earlier, *parts):
@@ -928,20 +931,27 @@
         two_away, first_stays = after(two_away, first_grad[0])
         one_own, one_away, one_got = leave(shard_sum(first_stays, swapped(first_grad[1], "x")))
         one_away, chip_parts = after(one_away, chip_parts)
-        chip_parts = added(chip_parts)
-        chip_stays, chip_goes = (
-            jnp.concatenate([chip_parts[i], chip_parts[i + 2]], axis=1) for i in range(2)
-        )
-        chip_got = swapped(chip_goes, "x")
-        chip_goes, two_own = after(chip_goes, two_own)
+        a_stays, a_goes = halves_of(*chip_parts[:2])
+        a_got = swapped(a_goes, "x")
+        a_goes, b_own = after(a_goes, chip_parts[2])
+        b_stays, b_goes = halves_of(b_own, chip_parts[3])
+        b_got = swapped(b_goes, "x")
+        b_goes, a_stays = after(b_goes, a_stays)
+        a_part = a_stays.astype(f32) + a_got.astype(f32)
+        a_goes = a_part[2:].astype(bf16)
+        a_last = swapped(a_goes, "zh")
+        a_goes, two_own = after(a_goes, two_own)
         part_two = two_own + two_got.astype(f32)
-        two_low, chip_stays, one_own = after(part_two.astype(bf16), chip_stays, one_own)
-        chip_parts = chip_stays.astype(f32) + chip_got.astype(f32)
-        chip_goes = chip_parts[2:].astype(bf16)
-        part_chip = chip_parts[:2] + swapped(chip_goes, "zh").astype(f32)
-        chip_goes, one_own = after(chip_goes, one_own)
+        two_low, b_stays = after(part_two.astype(bf16), b_stays)
+        b_part = b_stays.astype(f32) + b_got.astype(f32)
+        b_goes = b_part[2:].astype(bf16)
+        b_last = swapped(b_goes, "zh")
+        a_last, b_goes, one_own = lax.optimization_barrier((a_last, b_goes, one_own))
         part_one = one_own + one_got.astype(f32)
         one_low = part_one.astype(bf16)
+        part_chip = jnp.concatenate(
+            [a_part[:2] + a_last.astype(f32), b_part[:2] + b_last.astype(f32)], axis=1
+        )
         sq_kernels = jnp.sum(part_one * part_one) + jnp.sum(part_two * part_two)
         part = jnp.concatenate([one_low, two_low], axis=1)
         part = lax.all_to_all(part, MEMBERS, 0, 0, tiled=True)

time: 435 us -> 445 us (1.023)
  waiting for transfers between devices: 157 us -> 165 us
  starting transfers between devices: 84.6 us -> 90.3 us
    ppermute x39 -> x41, waiting for transfers between devices: 148 us -> 156 us  [swapped(): return lax.ppermute(values, axis, [(0, 1), (1, 0)])]
    ppermute x39 -> x41, starting transfers between devices: 43.2 us -> 50 us  [swapped(): return lax.ppermute(values, axis, [(0, 1), (1, 0)])]
    unnamed x151 -> x153, local copies, waits for them, and re-layouts: 23.5 us -> 23.4 us
  transfers between devices with their start and end apart: 50 -> 52, of which waited for: 28 -> 30; matrix products, arithmetic and copies ran while one was open for 20% -> 19% of each run, Pallas kernels for 7% -> 7%
where the time goes in v6:
time: 445 us; the launch traced here: 437 us
  waiting for transfers between devices  165 us (37%)
  starting transfers between devices  90.3 us (20%)
  local copies, waits for them, and re-layouts  63.6 us (14%)
  other arithmetic  53.7 us (12%)
  Pallas kernels  39.9 us (9%)
  matrix products  15.5 us (3%)
  between operations  8.83 us (2%)
    ppermute x41, waiting for transfers between devices, swapped(): return lax.ppermute(values, axis, [(0, 1), (1, 0)])  156 us
    ppermute x41, starting transfers between devices, swapped(): return lax.ppermute(values, axis, [(0, 1), (1, 0)])  50 us
    pallas_call x9, Pallas kernels, on_chip(): pl.pallas_call(body, out_shape=outs, in_specs=[pl.BlockSpec(memory_space=...  39.9 us
    unnamed x153, local copies, waits for them, and re-layouts  23.4 us
    ppermute x6, starting transfers between devices, shifted(): lax.ppermute(values, axis, [(i, i + step) for i in range(count) if 0 <= i...  19.6 us
    conv_general_dilated x2, matrix products, convolve(): lax.conv_general_dilated(values, kernel, (1, 1), ((pad, pad), (pad, pad))...  11.2 us
    sub x6, other arithmetic, adamw(): weight - learn_rate * (corrected / (spread + epsilon) + decay * weight)  8.98 us
  transfers between devices with their start and end apart: 52, of which 30 were waited for; matrix products, arithmetic and copies ran while one was open for 19% of the time, Pallas kernels for 7%

profile of v6, /device:TPU:0, one launch (start us, length us, event | category | flops | bytes accessed | tf_op | source)
XLA Modules:
  0.0 436.8 jit_solution(3026357780983267669)
XLA Ops:
  7.4 5.4 %all-to-all-start = ((bf16[8,704,128]{2,1,0:T(8,128)(2,1)}), bf16[8,704,128]{2,1,0:T(8,128)(2,1)}, u32[]{:S(2)}, u32[]{:S(2)}) async-start(bf16[8,704,128]{2,1,0:T(8,128)(2,1)} %pad_maximum_fusion.3), calls=%async_computation | async-start | bytes 2883584 | tf_op jit(solution)/shard_map/all_to_all | solution.py:697
  18.3 3.0 collective-permute-start.1
  22.9 15.6 %collective-permute-done.1 = bf16[2,416,256]{2,1,0:T(8,128)(2,1)S(1)} collective-permute-done((bf16[2,416,256]{2,1,0:T(8,128)(2,1)S(1)}, bf16[2,416,256]{2,1,0:T(8,128)(2,1)S(1)}, u32[]{:S(2)}, u32[]{:S(2)}) %collective-permute-start.1) | collective-permute-done | bytes 426016 | tf_op jit(solution)/shard_map/ppermute | solution.py:43
  48.2 17.5 %collective-permute-done.11 = bf16[2,2,512]{2,1,0:T(2,128)(2,1)S(1)} collective-permute-done((bf16[2,2,512]{2,1,0:T(2,128)(2,1)S(1)}, bf16[2,2,512]{2,1,0:T(2,128)(2,1)S(1)}, u32[]{:S(2)}, u32[]{:S(2)}) %collective-permute-start.11) | collective-permute-done | bytes 4128 | tf_op jit(solution)/shard_map/ppermute | solution.py:43
  68.0 5.4 %collective-permute-start.12 = (bf16[272,512]{1,0:T(8,128)(2,1)}, bf16[272,512]{1,0:T(8,128)(2,1)}, u32[]{:S(2)}, u32[]{:S(2)}) collective-permute-start(bf16[272,512]{1,0:T(8,128)(2,1)} %get-tuple-element.382), channel_id=1, source_target_pairs={{0,4},{4,8},{8,12},{12,16},{16,20},{20,24},{24,28},{1,5},{5,9},{9,... | collective-permute-start | bytes 835592 | tf_op jit(solution)/shard_map/ppermute | solution.py:37
  76.5 2.9 collective-permute-start.7
  79.4 19.4 %collective-permute-done.3 = bf16[4608,128]{1,0:T(8,128)(2,1)S(1)} collective-permute-done((bf16[4608,128]{1,0:T(8,128)(2,1)S(1)}, bf16[4608,128]{1,0:T(8,128)(2,1)S(1)}, u32[]{:S(2)}, u32[]{:S(2)}) %collective-permute-start.3) | collective-permute-done | bytes 1179680 | tf_op jit(solution)/shard_map/ppermute | solution.py:43
  108.5 2.8 pad_maximum_fusion.7
  112.5 5.5 %collective-permute-done.7 = bf16[8,208,256]{2,1,0:T(8,128)(2,1)} collective-permute-done((bf16[8,208,256]{2,1,0:T(8,128)(2,1)}, bf16[8,208,256]{2,1,0:T(8,128)(2,1)}, u32[]{:S(2)}, u32[]{:S(2)}) %collective-permute-start.7) | collective-permute-done | bytes 852000 | tf_op jit(solution)/shard_map/ppermute | solution.py:43
  118.0 2.7 collective-permute-done.4
  132.4 4.1 fusion.10
  137.5 5.1 %collective-permute-done.8 = bf16[4608,128]{1,0:T(8,128)(2,1)} collective-permute-done((bf16[4608,128]{1,0:T(8,128)(2,1)}, bf16[4608,128]{1,0:T(8,128)(2,1)}, u32[]{:S(2)}, u32[]{:S(2)}) %collective-permute-start.8) | collective-permute-done | bytes 1179680 | tf_op jit(solution)/shard_map/ppermute | solution.py:43
  144.4 2.1 fusion.2
  146.5 5.3 %reshape.743 = bf16[3,3,128,1024]{3,2,1,0:T(8,128)(2,1)} reshape(bf16[2,2,2,2,2,288,128]{6,5,4,3,2,1,0:T(8,128)(2,1)} %fusion.2) | data formatting | bytes 4718592 | tf_op jit(solution)/shard_map/reshape | solution.py:764
  151.8 7.1 %fusion.50 = bf16[2,4,64,1024]{3,0,2,1:T(2,128)(2,1)} fusion(bf16[3,3,128,1024]{3,2,1,0:T(8,128)(2,1)} %reshape.743, bf16[2,6,66,128]{3,2,1,0:T(8,128)(2,1)} %get-tuple-element.347), kind=kOutput, calls=%fused_computation.158 | convolution fusion | flops 1207959552 | bytes 3610624 | tf_op jit(solution)/shard_map/conv_general_dilated | solution.py:86
  159.0 2.6 collective-permute-done.10.rest_3_
  161.6 3.6 all-to-all-start.1
  168.2 8.0 %shard_map.382 = (bf16[9216,256]{1,0:T(8,128)(2,1)S(1)}, bf16[4096,256]{1,0:T(8,128)(2,1)S(1)}) custom-call(s32[5]{0:T(128)S(1)} %stack.87.me_ref, bf16[16,208,256]{2,1,0:T(8,128)(2,1)S(1)} %copy-done.5, bf16[16,208,256]{2,1,0:T(8,128)(2,1)} %collective-permute-done.9.rest_1_, bf16[16,208,256]{2,1,0:T(8,128)(2,1)S(1)} %copy-done.7, ...), custom_call_target="tpu_custom_call" | custom-call | tf_op jit(solution)/shard_map/pallas_call | solution.py:257
  176.2 2.2 copy-done
  189.1 5.2 %collective-permute-start.17 = (bf16[272,256]{1,0:T(8,128)(2,1)S(1)}, bf16[272,256]{1,0:T(8,128)(2,1)}, u32[]{:S(2)}, u32[]{:S(2)}) collective-permute-start(bf16[272,256]{1,0:T(8,128)(2,1)S(1)} %get-tuple-element.380), channel_id=1, source_target_pairs={{0,4},{4,8},{8,12},{12,16},{16,20},{20,24},{24,28},{1,5},{5,9},{9,... | collective-permute-start | bytes 417800 | tf_op jit(solution)/shard_map/ppermute | solution.py:37
  201.1 2.3 copy-done.1
  203.4 4.0 shard_map.384
  212.0 4.1 convert_reduce_fusion.1
  221.2 5.1 %collective-permute-start.23 = (bf16[272,256]{1,0:T(8,128)(2,1)S(1)}, bf16[272,256]{1,0:T(8,128)(2,1)S(1)}, u32[]{:S(2)}, u32[]{:S(2)}) collective-permute-start(bf16[272,256]{1,0:T(8,128)(2,1)S(1)} %get-tuple-element.378), channel_id=1, source_target_pairs={{0,4},{4,8},{8,12},{12,16},{16,20},{20,24},{24,28},{1,5},{5,9},{9,... | collective-permute-start | bytes 417800 | tf_op jit(solution)/shard_map/ppermute | solution.py:37
  227.8 2.9 collective-permute-done.23
  232.1 2.3 copy-done.2
  241.9 7.9 %all-to-all-start.2 = ((bf16[8,2,1,32,1024]{4,3,2,1,0:T(8,128)(2,1)}), bf16[8,2,1,32,1024]{4,3,2,1,0:T(8,128)(2,1)S(1)}, u32[]{:S(2)}, u32[]{:S(2)}) async-start(bf16[8,2,1,32,1024]{4,3,2,1,0:T(8,128)(2,1)} %broadcast_in_dim.182), calls=%async_computation.2 | async-start | bytes 2097152 | tf_op jit(solution)/shard_map/all_to_all | solution.py:124
  251.2 3.9 reshape_reshape.3.kernel_ref
  256.7 7.6 %shard_map.386 = (bf16[16,208,256]{2,1,0:T(8,128)(2,1)}, bf16[16,208,256]{2,1,0:T(8,128)(2,1)}, bf16[16,208,256]{2,1,0:T(8,128)(2,1)}, bf16[16,208,256]{2,1,0:T(8,128)(2,1)}) custom-call(s32[5]{0:T(128)} %copy-done.12, bf16[2,4,4,64,1024]{4,3,2,1,0:T(8,128)(2,1)} %copy-done.3, bf16[512,256]{1,0:T(8,128)(2,1)} %bitcast.266), custom_call_target="tpu_custom_call" | custom-call | tf_op jit(solution)/shard_map/pallas_call | solution.py:257
  264.4 2.7 shard_map.387
  268.8 3.7 collective-permute-start.27
  275.2 3.7 shard_map.388
  279.7 2.2 collective-permute-start.30
  282.0 6.6 %shard_map.389 = (bf16[16,288,128]{2,1,0:T(8,128)(2,1)}, bf16[16,288,128]{2,1,0:T(8,128)(2,1)}) custom-call(s32[5]{0:T(128)} %copy-done.12, bf16[3,2,6,64,128]{4,3,2,1,0:T(8,128)(2,1)} %pad_maximum_fusion.14.cells_ref, bf16[2,4,64,1024]{3,2,1,0:T(8,128)(2,1)} %copy-done.8), custom_call_target="tpu_custom_call" | custom-call | tf_op jit(solution)/shard_map/pallas_call | solution.py:257
  297.4 4.4 %shard_map.390 = (bf16[16,144,128]{2,1,0:T(8,128)(2,1)}, bf16[16,144,128]{2,1,0:T(8,128)(2,1)}) custom-call(s32[5]{0:T(128)} %copy-done.12, bf16[3,2,6,64,512]{4,3,2,1,0:T(8,128)(2,1)} %pad_maximum_fusion.1.cells_ref, bf16[2,4,64,128]{3,2,1,0:T(8,128)(2,1)} %fusion.45.grad_ref), custom_call_target="tpu_custom_call" | custom-call | tf_op jit(solution)/shard_map/pallas_call | solution.py:257
  303.0 15.6 %collective-permute-done.30 = bf16[16,208,256]{2,1,0:T(8,128)(2,1)} collective-permute-done((bf16[16,208,256]{2,1,0:T(8,128)(2,1)}, bf16[16,208,256]{2,1,0:T(8,128)(2,1)}, u32[]{:S(2)}, u32[]{:S(2)}) %collective-permute-start.30) | collective-permute-done | bytes 1703968 | tf_op jit(solution)/shard_map/ppermute | solution.py:43
  322.5 2.4 collective-permute-start.38
  324.9 6.0 %collective-permute-done.33 = bf16[16,208,256]{2,1,0:T(8,128)(2,1)} collective-permute-done((bf16[16,208,256]{2,1,0:T(8,128)(2,1)}, bf16[16,208,256]{2,1,0:T(8,128)(2,1)}, u32[]{:S(2)}, u32[]{:S(2)}) %collective-permute-start.33) | collective-permute-done | bytes 1703968 | tf_op jit(solution)/shard_map/ppermute | solution.py:43
  333.2 13.9 %collective-permute-done.34 = bf16[8,208,256]{2,1,0:T(8,128)(2,1)S(1)} collective-permute-done((bf16[8,208,256]{2,1,0:T(8,128)(2,1)S(1)}, bf16[8,208,256]{2,1,0:T(8,128)(2,1)S(1)}, u32[]{:S(2)}, u32[]{:S(2)}) %collective-permute-start.34) | collective-permute-done | bytes 852000 | tf_op jit(solution)/shard_map/ppermute | solution.py:43
  348.0 2.4 collective-permute-start.40
  350.4 17.3 %collective-permute-done.35 = bf16[8,208,256]{2,1,0:T(8,128)(2,1)S(1)} collective-permute-done((bf16[8,208,256]{2,1,0:T(8,128)(2,1)S(1)}, bf16[8,208,256]{2,1,0:T(8,128)(2,1)S(1)}, u32[]{:S(2)}, u32[]{:S(2)}) %collective-permute-start.35) | collective-permute-done | bytes 852000 | tf_op jit(solution)/shard_map/ppermute | solution.py:43
  370.9 5.2 %collective-permute-done.39 = bf16[4,208,256]{2,1,0:T(8,128)(2,1)S(1)} collective-permute-done((bf16[4,208,256]{2,1,0:T(8,128)(2,1)S(1)}, bf16[4,208,256]{2,1,0:T(8,128)(2,1)S(1)}, u32[]{:S(2)}, u32[]{:S(2)}) %collective-permute-start.39) | collective-permute-done | bytes 426016 | tf_op jit(solution)/shard_map/ppermute | solution.py:43
  379.0 3.8 all-to-all-start.3
  386.1 11.8 %collective-permute-done.41 = bf16[2,208,256]{2,1,0:T(8,128)(2,1)S(1)} collective-permute-done((bf16[2,208,256]{2,1,0:T(8,128)(2,1)S(1)}, bf16[2,208,256]{2,1,0:T(8,128)(2,1)S(1)}, u32[]{:S(2)}, u32[]{:S(2)}) %collective-permute-start.41) | collective-permute-done | bytes 213024 | tf_op jit(solution)/shard_map/ppermute | solution.py:43
  411.1 3.7 collective-permute-start.45
  418.3 2.8 collective-permute-done.46
  426.0 2.9 multiply_subtract_fusion.2
  428.9 2.4 multiply_subtract_fusion
  (456 shorter events, 148.6 us)
Async XLA Ops:
  7.4 33.3 %all-to-all-start = ((bf16[8,704,128]{2,1,0:T(8,128)(2,1)}), bf16[8,704,128]{2,1,0:T(8,128)(2,1)}, u32[]{:S(2)}, u32[]{:S(2)}) async-start(bf16[8,704,128]{2,1,0:T(8,128)(2,1)} %pad_maximum_fusion.3), calls=%async_computation | async-start | bytes 2883584 | tf_op jit(solution)/shard_map/all_to_all | solution.py:697
  14.4 3.9 collective-permute-start
  15.4 6.3 %collective-permute-start.2 = (bf16[2,2,2,32,512]{4,1,0,3,2:T(2,128)(2,1)S(1)}, bf16[2,2,2,32,512]{4,1,0,3,2:T(2,128)(2,1)S(1)}, u32[]{:S(2)}, u32[]{:S(2)}) collective-permute-start(bf16[2,2,2,32,512]{4,1,0,3,2:T(2,128)(2,1)S(1)} %bitcast.279), channel_id=1, source_target_pairs={{0,1},{1,0},{2,3},{3,2},{4,5},{5,4},{6,7},{7,6},{8,9},{9,8},{10,11... | collective-permute-start | bytes 786440 | tf_op jit(solution)/shard_map/ppermute | solution.py:43
  15.6 2.7 collective-permute-start.14
  18.3 20.2 %collective-permute-start.1 = (bf16[2,416,256]{2,1,0:T(8,128)(2,1)S(1)}, bf16[2,416,256]{2,1,0:T(8,128)(2,1)S(1)}, u32[]{:S(2)}, u32[]{:S(2)}) collective-permute-start(bf16[2,416,256]{2,1,0:T(8,128)(2,1)S(1)} %pad_maximum_fusion.18), channel_id=1, source_target_pairs={{0,16},{16,0},{1,17},{17,1},{2,18},{18,2},{3,19},{19,3},{4,20},{20... | collective-permute-start | bytes 1277960 | tf_op jit(solution)/shard_map/ppermute | solution.py:43
  43.7 55.2 %collective-permute-start.3 = (bf16[4608,128]{1,0:T(8,128)(2,1)S(1)}, bf16[4608,128]{1,0:T(8,128)(2,1)S(1)}, u32[]{:S(2)}, u32[]{:S(2)}) collective-permute-start(bf16[4608,128]{1,0:T(8,128)(2,1)S(1)} %pad_maximum_fusion.5), channel_id=1, source_target_pairs={{0,16},{16,0},{1,17},{17,1},{2,18},{18,2},{3,19},{19,3},{4,20},{20... | collective-permute-start | bytes 3538952 | tf_op jit(solution)/shard_map/ppermute | solution.py:43
  45.1 28.3 %collective-permute-start.5 = (bf16[4,416,256]{2,1,0:T(8,128)(2,1)S(1)}, bf16[4,416,256]{2,1,0:T(8,128)(2,1)S(1)}, u32[]{:S(2)}, u32[]{:S(2)}) collective-permute-start(bf16[4,416,256]{2,1,0:T(8,128)(2,1)S(1)} %pad_maximum_fusion.9), channel_id=1, source_target_pairs={{0,2},{2,0},{1,3},{3,1},{4,6},{6,4},{5,7},{7,5},{8,10},{10,8},{9,1... | collective-permute-start | bytes 2555912 | tf_op jit(solution)/shard_map/ppermute | solution.py:43
  47.7 18.0 %collective-permute-start.11 = (bf16[2,2,512]{2,1,0:T(2,128)(2,1)S(1)}, bf16[2,2,512]{2,1,0:T(2,128)(2,1)S(1)}, u32[]{:S(2)}, u32[]{:S(2)}) collective-permute-start(bf16[2,2,512]{2,1,0:T(2,128)(2,1)S(1)} %fusion.59), channel_id=1, source_target_pairs={{0,2},{2,0},{1,3},{3,1},{4,6},{6,4},{5,7},{7,5},{8,10},{10,8},{9,1... | collective-permute-start | bytes 12296 | tf_op jit(solution)/shard_map/ppermute | solution.py:43
  66.7 37.5 %collective-permute-start.13 = (bf16[272,512]{1,0:T(8,128)(2,1)}, bf16[272,512]{1,0:T(8,128)(2,1)}, u32[]{:S(2)}, u32[]{:S(2)}) collective-permute-start(bf16[272,512]{1,0:T(8,128)(2,1)} %get-tuple-element.383), channel_id=1, source_target_pairs={{4,0},{8,4},{12,8},{16,12},{20,16},{24,20},{28,24},{5,1},{9,5},{13... | collective-permute-start | bytes 835592 | tf_op jit(solution)/shard_map/ppermute | solution.py:37
  68.0 38.3 %collective-permute-start.12 = (bf16[272,512]{1,0:T(8,128)(2,1)}, bf16[272,512]{1,0:T(8,128)(2,1)}, u32[]{:S(2)}, u32[]{:S(2)}) collective-permute-start(bf16[272,512]{1,0:T(8,128)(2,1)} %get-tuple-element.382), channel_id=1, source_target_pairs={{0,4},{4,8},{8,12},{12,16},{16,20},{20,24},{24,28},{1,5},{5,9},{9,... | collective-permute-start | bytes 835592 | tf_op jit(solution)/shard_map/ppermute | solution.py:37
  74.8 37.7 %collective-permute-start.6 = (bf16[8,208,256]{2,1,0:T(8,128)(2,1)}, bf16[8,208,256]{2,1,0:T(8,128)(2,1)}, u32[]{:S(2)}, u32[]{:S(2)}) collective-permute-start(bf16[8,208,256]{2,1,0:T(8,128)(2,1)} %get-tuple-element.122), channel_id=1, source_target_pairs={{0,4},{4,0},{1,5},{5,1},{2,6},{6,2},{3,7},{7,3},{8,12},{12,8},{9,1... | collective-permute-start | bytes 2555912 | tf_op jit(solution)/shard_map/ppermute | solution.py:43
  76.5 41.5 %collective-permute-start.7 = (bf16[8,208,256]{2,1,0:T(8,128)(2,1)}, bf16[8,208,256]{2,1,0:T(8,128)(2,1)}, u32[]{:S(2)}, u32[]{:S(2)}) collective-permute-start(bf16[8,208,256]{2,1,0:T(8,128)(2,1)} %get-tuple-element.124), channel_id=1, source_target_pairs={{0,8},{8,0},{1,9},{9,1},{2,10},{10,2},{3,11},{11,3},{4,12},{12,4},... | collective-permute-start | bytes 2555912 | tf_op jit(solution)/shard_map/ppermute | solution.py:43
  102.3 18.4 %collective-permute-start.4 = (bf16[2688,128]{1,0:T(8,128)(2,1)S(1)}, bf16[2688,128]{1,0:T(8,128)(2,1)S(1)}, u32[]{:S(2)}, u32[]{:S(2)}) collective-permute-start(bf16[2688,128]{1,0:T(8,128)(2,1)S(1)} %pad_maximum_fusion.13), channel_id=1, source_target_pairs={{0,2},{2,0},{1,3},{3,1},{4,6},{6,4},{5,7},{7,5},{8,10},{10,8},{9,1... | collective-permute-start | bytes 2064392 | tf_op jit(solution)/shard_map/ppermute | solution.py:43
  112.3 30.2 %collective-permute-start.8 = (bf16[4608,128]{1,0:T(8,128)(2,1)}, bf16[4608,128]{1,0:T(8,128)(2,1)}, u32[]{:S(2)}, u32[]{:S(2)}) collective-permute-start(bf16[4608,128]{1,0:T(8,128)(2,1)} %bitcast.22), channel_id=1, source_target_pairs={{0,2},{2,0},{1,3},{3,1},{4,6},{6,4},{5,7},{7,5},{8,10},{10,8},{9,1... | collective-permute-start | bytes 3538952 | tf_op jit(solution)/shard_map/ppermute | solution.py:43
  123.4 35.6 %collective-permute-start.9 = (bf16[16,208,256]{2,1,0:T(8,128)(2,1)S(1)}, bf16[16,208,256]{2,1,0:T(8,128)(2,1)}, u32[]{:S(2)}, u32[]{:S(2)}) collective-permute-start(bf16[16,208,256]{2,1,0:T(8,128)(2,1)S(1)} %constant_dynamic-update-slice_fusion.7.rest_0_), channel_id=1, source_target_pairs={{0,8},{8,0},{1,9},{9,1},{2,10},{10,2},{3,11},{11,3},{4,12},{12,4},... | collective-permute-start | bytes 5111816 | tf_op jit(solution)/shard_map/ppermute | solution.py:43
  126.5 35.1 %collective-permute-start.10 = (bf16[16,208,256]{2,1,0:T(8,128)(2,1)S(1)}, bf16[16,208,256]{2,1,0:T(8,128)(2,1)}, u32[]{:S(2)}, u32[]{:S(2)}) collective-permute-start(bf16[16,208,256]{2,1,0:T(8,128)(2,1)S(1)} %constant_dynamic-update-slice_fusion.9.rest_2_), channel_id=1, source_target_pairs={{0,4},{4,0},{1,5},{5,1},{2,6},{6,2},{3,7},{7,3},{8,12},{12,8},{9,1... | collective-permute-start | bytes 5111816 | tf_op jit(solution)/shard_map/ppermute | solution.py:43
  161.6 17.9 %all-to-all-start.1 = ((bf16[8,2,32,1024]{3,1,2,0:T(2,128)(2,1)}), bf16[8,2,32,1024]{3,1,2,0:T(2,128)(2,1)S(1)}, u32[]{:S(2)}, u32[]{:S(2)}) async-start(bf16[8,2,32,1024]{3,1,2,0:T(2,128)(2,1)} %bitcast.269), calls=%async_computation.1 | async-start | bytes 2097152 | tf_op jit(solution)/shard_map/all_to_all | solution.py:132
  184.0 3.7 collective-permute-start.16
  187.8 8.2 %collective-permute-start.18 = (bf16[272,256]{1,0:T(8,128)(2,1)S(1)}, bf16[272,256]{1,0:T(8,128)(2,1)S(1)}, u32[]{:S(2)}, u32[]{:S(2)}) collective-permute-start(bf16[272,256]{1,0:T(8,128)(2,1)S(1)} %get-tuple-element.381), channel_id=1, source_target_pairs={{4,0},{8,4},{12,8},{16,12},{20,16},{24,20},{28,24},{5,1},{9,5},{13... | collective-permute-start | bytes 417800 | tf_op jit(solution)/shard_map/ppermute | solution.py:37
  189.1 8.0 %collective-permute-start.17 = (bf16[272,256]{1,0:T(8,128)(2,1)S(1)}, bf16[272,256]{1,0:T(8,128)(2,1)}, u32[]{:S(2)}, u32[]{:S(2)}) collective-permute-start(bf16[272,256]{1,0:T(8,128)(2,1)S(1)} %get-tuple-element.380), channel_id=1, source_target_pairs={{0,4},{4,8},{8,12},{12,16},{16,20},{20,24},{24,28},{1,5},{5,9},{9,... | collective-permute-start | bytes 417800 | tf_op jit(solution)/shard_map/ppermute | solution.py:37
  198.1 2.9 collective-permute-start.19
  199.0 2.1 collective-permute-start.20
  216.1 3.7 collective-permute-start.22
  219.9 7.7 %collective-permute-start.24 = (bf16[272,256]{1,0:T(8,128)(2,1)S(1)}, bf16[272,256]{1,0:T(8,128)(2,1)S(1)}, u32[]{:S(2)}, u32[]{:S(2)}) collective-permute-start(bf16[272,256]{1,0:T(8,128)(2,1)S(1)} %get-tuple-element.379), channel_id=1, source_target_pairs={{4,0},{8,4},{12,8},{16,12},{20,16},{24,20},{28,24},{5,1},{9,5},{13... | collective-permute-start | bytes 417800 | tf_op jit(solution)/shard_map/ppermute | solution.py:37
  221.2 9.5 %collective-permute-start.23 = (bf16[272,256]{1,0:T(8,128)(2,1)S(1)}, bf16[272,256]{1,0:T(8,128)(2,1)S(1)}, u32[]{:S(2)}, u32[]{:S(2)}) collective-permute-start(bf16[272,256]{1,0:T(8,128)(2,1)S(1)} %get-tuple-element.378), channel_id=1, source_target_pairs={{0,4},{4,8},{8,12},{12,16},{16,20},{20,24},{24,28},{1,5},{5,9},{9,... | collective-permute-start | bytes 417800 | tf_op jit(solution)/shard_map/ppermute | solution.py:37
  236.4 1.6 collective-permute-start.25
  241.9 22.5 %all-to-all-start.2 = ((bf16[8,2,1,32,1024]{4,3,2,1,0:T(8,128)(2,1)}), bf16[8,2,1,32,1024]{4,3,2,1,0:T(8,128)(2,1)S(1)}, u32[]{:S(2)}, u32[]{:S(2)}) async-start(bf16[8,2,1,32,1024]{4,3,2,1,0:T(8,128)(2,1)} %broadcast_in_dim.182), calls=%async_computation.2 | async-start | bytes 2097152 | tf_op jit(solution)/shard_map/all_to_all | solution.py:124
  268.8 10.9 %collective-permute-start.27 = (f32[2,1,64,128]{3,2,1,0:T(8,128)S(1)}, f32[2,1,64,128]{3,2,1,0:T(8,128)S(1)}, u32[]{:S(2)}, u32[]{:S(2)}) collective-permute-start(f32[2,1,64,128]{3,2,1,0:T(8,128)S(1)} %slice_select_fusion.1), channel_id=1, source_target_pairs={{0,16},{16,0},{1,17},{17,1},{2,18},{18,2},{3,19},{19,3},{4,20},{20... | collective-permute-start | bytes 196616 | tf_op jit(solution)/shard_map/ppermute | solution.py:43
  272.5 7.1 %collective-permute-start.28 = (f32[2,4,1,128]{3,1,0,2:T(4,128)S(1)}, f32[2,4,1,128]{3,1,0,2:T(4,128)S(1)}, u32[]{:S(2)}, u32[]{:S(2)}) collective-permute-start(f32[2,4,1,128]{3,1,0,2:T(4,128)S(1)} %slice_bitcast_fusion.7), channel_id=1, source_target_pairs={{0,2},{2,0},{1,3},{3,1},{4,6},{6,4},{5,7},{7,5},{8,10},{10,8},{9,1... | collective-permute-start | bytes 12296 | tf_op jit(solution)/shard_map/ppermute | solution.py:43
  274.3 5.4 %collective-permute-start.29 = (f32[2,1,1,128]{3,0,2,1:T(2,128)S(1)}, f32[2,1,1,128]{3,0,2,1:T(2,128)S(1)}, u32[]{:S(2)}, u32[]{:S(2)}) collective-permute-start(f32[2,1,1,128]{3,0,2,1:T(2,128)S(1)} %bitcast.297), channel_id=1, source_target_pairs={{0,18},{2,16},{16,2},{18,0},{1,19},{3,17},{17,3},{19,1},{4,22},{6,... | collective-permute-start | bytes 3080 | tf_op jit(solution)/shard_map/ppermute | solution.py:871
  279.7 38.9 %collective-permute-start.30 = (bf16[16,208,256]{2,1,0:T(8,128)(2,1)}, bf16[16,208,256]{2,1,0:T(8,128)(2,1)}, u32[]{:S(2)}, u32[]{:S(2)}) collective-permute-start(bf16[16,208,256]{2,1,0:T(8,128)(2,1)} %get-tuple-element.182), channel_id=1, source_target_pairs={{0,8},{8,0},{1,9},{9,1},{2,10},{10,2},{3,11},{11,3},{4,12},{12,4},... | collective-permute-start | bytes 5111816 | tf_op jit(solution)/shard_map/ppermute | solution.py:43
  289.5 32.5 %collective-permute-start.31 = (bf16[16,288,128]{2,1,0:T(8,128)(2,1)}, bf16[16,288,128]{2,1,0:T(8,128)(2,1)S(1)}, u32[]{:S(2)}, u32[]{:S(2)}) collective-permute-start(bf16[16,288,128]{2,1,0:T(8,128)(2,1)} %get-tuple-element.185), channel_id=1, source_target_pairs={{0,2},{2,0},{1,3},{3,1},{4,6},{6,4},{5,7},{7,5},{8,10},{10,8},{9,1... | collective-permute-start | bytes 3538952 | tf_op jit(solution)/shard_map/ppermute | solution.py:43
  290.5 40.5 %collective-permute-start.33 = (bf16[16,208,256]{2,1,0:T(8,128)(2,1)}, bf16[16,208,256]{2,1,0:T(8,128)(2,1)}, u32[]{:S(2)}, u32[]{:S(2)}) collective-permute-start(bf16[16,208,256]{2,1,0:T(8,128)(2,1)} %get-tuple-element.190), channel_id=1, source_target_pairs={{0,4},{4,0},{1,5},{5,1},{2,6},{6,2},{3,7},{7,3},{8,12},{12,8},{9,1... | collective-permute-start | bytes 5111816 | tf_op jit(solution)/shard_map/ppermute | solution.py:43
  301.9 31.1 %collective-permute-start.32 = (bf16[16,144,128]{2,1,0:T(8,128)(2,1)}, bf16[16,144,128]{2,1,0:T(8,128)(2,1)S(1)}, u32[]{:S(2)}, u32[]{:S(2)}) collective-permute-start(bf16[16,144,128]{2,1,0:T(8,128)(2,1)} %get-tuple-element.188), channel_id=1, source_target_pairs={{0,2},{2,0},{1,3},{3,1},{4,6},{6,4},{5,7},{7,5},{8,10},{10,8},{9,1... | collective-permute-start | bytes 1769480 | tf_op jit(solution)/shard_map/ppermute | solution.py:43
  320.4 26.6 %collective-permute-start.34 = (bf16[8,208,256]{2,1,0:T(8,128)(2,1)S(1)}, bf16[8,208,256]{2,1,0:T(8,128)(2,1)S(1)}, u32[]{:S(2)}, u32[]{:S(2)}) collective-permute-start(bf16[8,208,256]{2,1,0:T(8,128)(2,1)S(1)} %get-tuple-element.318), channel_id=1, source_target_pairs={{0,4},{4,0},{1,5},{5,1},{2,6},{6,2},{3,7},{7,3},{8,12},{12,8},{9,1... | collective-permute-start | bytes 2555912 | tf_op jit(solution)/shard_map/ppermute | solution.py:43
  322.5 47.5 %collective-permute-start.38 = (bf16[8,288,128]{2,1,0:T(8,128)(2,1)S(1)}, bf16[8,288,128]{2,1,0:T(8,128)(2,1)S(1)}, u32[]{:S(2)}, u32[]{:S(2)}) collective-permute-start(bf16[8,288,128]{2,1,0:T(8,128)(2,1)S(1)} %fusion.17), channel_id=1, source_target_pairs={{0,16},{16,0},{1,17},{17,1},{2,18},{18,2},{3,19},{19,3},{4,20},{20... | collective-permute-start | bytes 1769480 | tf_op jit(solution)/shard_map/ppermute | solution.py:43
  332.8 34.9 %collective-permute-start.35 = (bf16[8,208,256]{2,1,0:T(8,128)(2,1)S(1)}, bf16[8,208,256]{2,1,0:T(8,128)(2,1)S(1)}, u32[]{:S(2)}, u32[]{:S(2)}) collective-permute-start(bf16[8,208,256]{2,1,0:T(8,128)(2,1)S(1)} %get-tuple-element.315), channel_id=1, source_target_pairs={{0,8},{8,0},{1,9},{9,1},{2,10},{10,2},{3,11},{11,3},{4,12},{12,4},... | collective-permute-start | bytes 2555912 | tf_op jit(solution)/shard_map/ppermute | solution.py:43
  347.3 20.7 %collective-permute-start.36 = (bf16[4,208,256]{2,1,0:T(8,128)(2,1)S(1)}, bf16[4,208,256]{2,1,0:T(8,128)(2,1)S(1)}, u32[]{:S(2)}, u32[]{:S(2)}) collective-permute-start(bf16[4,208,256]{2,1,0:T(8,128)(2,1)S(1)} %get-tuple-element.326), channel_id=1, source_target_pairs={{0,2},{2,0},{1,3},{3,1},{4,6},{6,4},{5,7},{7,5},{8,10},{10,8},{9,1... | collective-permute-start | bytes 1277960 | tf_op jit(solution)/shard_map/ppermute | solution.py:43
  348.0 29.3 %collective-permute-start.40 = (bf16[8,144,128]{2,1,0:T(8,128)(2,1)S(1)}, bf16[8,144,128]{2,1,0:T(8,128)(2,1)S(1)}, u32[]{:S(2)}, u32[]{:S(2)}) collective-permute-start(bf16[8,144,128]{2,1,0:T(8,128)(2,1)S(1)} %fusion.30), channel_id=1, source_target_pairs={{0,16},{16,0},{1,17},{17,1},{2,18},{18,2},{3,19},{19,3},{4,20},{20... | collective-permute-start | bytes 884744 | tf_op jit(solution)/shard_map/ppermute | solution.py:43
  367.9 8.2 %collective-permute-start.39 = (bf16[4,208,256]{2,1,0:T(8,128)(2,1)S(1)}, bf16[4,208,256]{2,1,0:T(8,128)(2,1)S(1)}, u32[]{:S(2)}, u32[]{:S(2)}) collective-permute-start(bf16[4,208,256]{2,1,0:T(8,128)(2,1)S(1)} %get-tuple-element.324), channel_id=1, source_target_pairs={{0,2},{2,0},{1,3},{3,1},{4,6},{6,4},{5,7},{7,5},{8,10},{10,8},{9,1... | collective-permute-start | bytes 1277960 | tf_op jit(solution)/shard_map/ppermute | solution.py:43
  368.1 9.1 %collective-permute-start.37 = (bf16[2,208,256]{2,1,0:T(8,128)(2,1)S(1)}, bf16[2,208,256]{2,1,0:T(8,128)(2,1)S(1)}, u32[]{:S(2)}, u32[]{:S(2)}) collective-permute-start(bf16[2,208,256]{2,1,0:T(8,128)(2,1)S(1)} %slice.588), channel_id=1, source_target_pairs={{0,16},{16,0},{1,17},{17,1},{2,18},{18,2},{3,19},{19,3},{4,20},{20... | collective-permute-start | bytes 638984 | tf_op jit(solution)/shard_map/ppermute | solution.py:43
  379.0 30.8 %all-to-all-start.3 = ((bf16[8,432,128]{2,1,0:T(8,128)(2,1)}), bf16[8,432,128]{2,1,0:T(8,128)(2,1)S(1)}, u32[]{:S(2)}, u32[]{:S(2)}) async-start(bf16[8,432,128]{2,1,0:T(8,128)(2,1)} %pad_maximum_fusion.8), calls=%async_computation.3 | async-start | bytes 1769472 | tf_op jit(solution)/shard_map/all_to_all | solution.py:957
  384.4 13.5 %collective-permute-start.41 = (bf16[2,208,256]{2,1,0:T(8,128)(2,1)S(1)}, bf16[2,208,256]{2,1,0:T(8,128)(2,1)S(1)}, u32[]{:S(2)}, u32[]{:S(2)}) collective-permute-start(bf16[2,208,256]{2,1,0:T(8,128)(2,1)S(1)} %slice.587), channel_id=1, source_target_pairs={{0,16},{16,0},{1,17},{17,1},{2,18},{18,2},{3,19},{19,3},{4,20},{20... | collective-permute-start | bytes 638984 | tf_op jit(solution)/shard_map/ppermute | solution.py:43
  402.1 3.8 collective-permute-start.43
  405.9 3.8 collective-permute-start.44
  408.3 10.0 %collective-permute-start.47 = (bf16[416,256]{1,0:T(8,128)(2,1)}, bf16[416,256]{1,0:T(8,128)(2,1)S(1)}, u32[]{:S(2)}, u32[]{:S(2)}) collective-permute-start(bf16[416,256]{1,0:T(8,128)(2,1)} %slice_bitcast_fusion.2), channel_id=1, source_target_pairs={{0,1},{1,0},{2,3},{3,2},{4,5},{5,4},{6,7},{7,6},{8,9},{9,8},{10,11... | collective-permute-start | bytes 638984 | tf_op jit(solution)/shard_map/ppermute | solution.py:43
  411.1 5.4 %collective-permute-start.45 = (f32[4100]{0:T(1024)S(1)}, f32[4100]{0:T(1024)S(1)}, u32[]{:S(2)}, u32[]{:S(2)}) collective-permute-start(f32[4100]{0:T(1024)S(1)} %add.413), channel_id=1, source_target_pairs={{0,8},{8,0},{1,9},{9,1},{2,10},{10,2},{3,11},{11,3},{4,12},{12,4},... | collective-permute-start | bytes 49208 | tf_op jit(solution)/shard_map/ppermute | solution.py:43
  416.5 4.7 %collective-permute-start.46 = (f32[4100]{0:T(1024)S(1)}, f32[4100]{0:T(1024)S(1)}, u32[]{:S(2)}, u32[]{:S(2)}) collective-permute-start(f32[4100]{0:T(1024)S(1)} %add.414), channel_id=1, source_target_pairs={{0,16},{16,0},{1,17},{17,1},{2,18},{18,2},{3,19},{19,3},{4,20},{20... | collective-permute-start | bytes 49208 | tf_op jit(solution)/shard_map/ppermute | solution.py:43
  (74 other events, 406.5 us)
